TPU v7x, 128 devices: a whole 4x4x4 slice. The times are simulated.
128 devices in a mesh: ctx: 16 (over z_lo, x, core), ep: 8 (over z_hi, y).
Axes of the slice: x: 4, y: 4, z: 4 (z_hi: 2, z_lo: 2; z = z_hi * 2 + z_lo), core: 2. Of those that a mesh axis runs over, the one named last changes fastest.
Arguments:
- queries: bfloat16 [2048, 12288], P('ctx', 'ep'), may hold values from -8 to 8
- latents: bfloat16 [576, 2048], P(None, 'ctx'), may hold values from -8 to 8
- w_kv: bfloat16 [512, 16384], P(None, 'ep'), may hold values from -0.25 to 0.25
- w_out: bfloat16 [8192, 3584], P(('ep', 'ctx')), may hold values from -0.75 to 0.75
- resid: bfloat16 [2048, 3584], P(('ctx', 'ep')), may hold values from -3 to 3
- norm_gain: float32 [3584], replicated, may hold values from 0.1 to 1.9
- routes: int32 [2048, 8], P(('ctx', 'ep')), may hold values from 0 to 63, all different within a row; in each aligned block of 16 rows (0 to 15, 16 to 31, ...) at most 3 rows name the same one
- codes: int32 [2048, 8], P(('ctx', 'ep')), may hold values from 1 to 64
- w_gate: bfloat16 [128, 3584, 512], P(('ctx', 'ep')), may hold values from -0.09375 to 0.09375
- w_up: bfloat16 [128, 3584, 512], P(('ctx', 'ep')), may hold values from -0.09375 to 0.09375
- w_down: bfloat16 [128, 512, 3584], P(('ctx', 'ep')), may hold values from -0.1875 to 0.1875
Outputs:
- attended: bfloat16 [2048, 3584], P(('ctx', 'ep'))
- layer_out: bfloat16 [2048, 3584], P(('ctx', 'ep'))
Inputs may be any that keep to these rules, and one draw needn't show every extreme that they name: `routes`: each token names 8 different experts; the 16 rows of one device name any one expert at most 3 times.
All inputs are finite; a program needn't handle non-finite values.
Results may differ from a plain program's by a relative error of at most 0.02.
Values may be sent and summed in bfloat16 or wider, within the bound.
No kernel may reach another device: no remote copies, remote signals or barrier semaphores. Data moves between devices by JAX's collectives and lax.ppermute only.
A program may use at most 128 MiB of HBM per device.

v0:
```python
import jax
import jax.numpy as jnp
from jax import lax
from jax.sharding import PartitionSpec as P

NOPE = 128
VD = 128
KV_RANK = 512
TOP = 8
QK = 192


def attend(carry, key_nope, values, key_rotary, query_nope, query_rotary, query_pos):
    peak, total, accum = carry
    count = key_nope.shape[0]
    scores = jnp.einsum("qhd,nhd->hqn", query_nope, key_nope, preferred_element_type=jnp.float32)
    scores = scores + jnp.einsum(
        "qhd,nd->hqn", query_rotary, key_rotary, preferred_element_type=jnp.float32
    )
    scores = scores * QK ** (-0.5)
    key_pos = jnp.arange(count, dtype=jnp.int32)
    allowed = key_pos[None, None, :] <= query_pos[None, :, None]
    masked = jnp.where(allowed, scores, jnp.float32(-1e30))
    new_peak = jnp.maximum(peak, jnp.max(masked, axis=2))
    probs = jnp.where(allowed, jnp.exp(scores - new_peak[:, :, None]), jnp.float32(0.0))
    total = jnp.sum(probs, axis=2)
    accum = jnp.einsum(
        "hqn,nhd->hqd", probs.astype(jnp.bfloat16), values, preferred_element_type=jnp.float32
    )
    return (new_peak, total, accum)


def expert_apply(block, w_gate, w_up, w_down):
    width = block.shape[-1]
    rows = block.reshape(-1, width)
    gate = jnp.dot(rows, w_gate[0], preferred_element_type=jnp.float32)
    upward = jnp.dot(rows, w_up[0], preferred_element_type=jnp.float32)
    hidden = (jax.nn.silu(gate) * upward).astype(jnp.bfloat16)
    produced = jnp.dot(hidden, w_down[0], preferred_element_type=jnp.float32).astype(jnp.bfloat16)
    return produced.reshape(block.shape)


def local(queries, latents, w_kv, w_out, resid, norm_gain, routes, codes, w_gate, w_up, w_down):
    seq_rows = queries.shape[0]
    head_count = queries.shape[1] // QK
    width = resid.shape[1]
    tok_rows = resid.shape[0]
    query_all = queries.reshape(seq_rows, head_count, QK)
    query_nope = query_all[:, :, :NOPE]
    query_rotary = query_all[:, :, NOPE:]
    first_pos = lax.axis_index("ctx") * seq_rows
    query_pos = first_pos + jnp.arange(seq_rows, dtype=jnp.int32)
    last_pos = first_pos + seq_rows - 1
    initial = (
        jnp.full((head_count, seq_rows), -1e30, jnp.float32),
        jnp.zeros((head_count, seq_rows), jnp.float32),
        jnp.zeros((head_count, seq_rows, VD), jnp.float32),
    )
    piece = lax.all_gather(latents, "ctx", axis=1, tiled=True)

    def compute(state):
        count = piece.shape[1]
        expanded = jnp.einsum(
            "rn,rc->nc", piece[:KV_RANK], w_kv, preferred_element_type=jnp.float32
        ).astype(jnp.bfloat16)
        expanded = expanded.reshape(count, head_count, NOPE + VD)
        return attend(
            state,
            expanded[:, :, :NOPE],
            expanded[:, :, NOPE:],
            piece[KV_RANK:].T,
            query_nope,
            query_rotary,
            query_pos,
        )

    peak, total, accum = lax.cond(jnp.int32(0) > last_pos, lambda state: state, compute, initial)
    heads_out = (
        (accum / total[:, :, None])
        .transpose(1, 0, 2)
        .reshape(seq_rows, head_count * VD)
        .astype(jnp.bfloat16)
    )
    w_full = lax.all_gather(w_out, "ctx", axis=0, tiled=True)
    attn_rows = lax.psum_scatter(
        jnp.dot(heads_out, w_full, preferred_element_type=jnp.float32).astype(jnp.bfloat16),
        "ep",
        scatter_dimension=0,
        tiled=True,
    ).astype(jnp.float32)
    attended = (resid.astype(jnp.float32) + attn_rows).astype(jnp.bfloat16)
    wide = attended.astype(jnp.float32)
    meansq = jnp.mean(wide * wide, axis=1, keepdims=True)
    normed = (wide * lax.rsqrt(meansq + 1e-06) * norm_gain[None, :]).astype(jnp.bfloat16)
    flat_routes = routes.reshape(-1)
    ctx_count = lax.axis_size("ctx")
    ep_count = lax.axis_size("ep")
    holder_count = ctx_count * ep_count
    expert_count = holder_count // 2
    capacity = 3 * tok_rows * TOP // (2 * expert_count)
    member = (flat_routes[:, None] == jnp.arange(expert_count, dtype=jnp.int32)[None, :]).astype(
        jnp.int32
    )
    earlier = jnp.cumsum(member, axis=0) - member
    slot_index = jnp.sum(earlier * member, axis=1)
    source_token = jnp.arange(flat_routes.shape[0], dtype=jnp.int32) // TOP
    single = (
        jnp.zeros((expert_count, capacity, width), jnp.bfloat16)
        .at[flat_routes, slot_index]
        .set(normed[source_token])
    )
    outgoing = jnp.broadcast_to(single[:, None], (expert_count, 2, capacity, width)).reshape(
        holder_count, capacity, width
    )
    returned = lax.all_to_all(
        expert_apply(
            lax.all_to_all(outgoing, ("ctx", "ep"), split_axis=0, concat_axis=0, tiled=True),
            w_gate,
            w_up,
            w_down,
        ),
        ("ctx", "ep"),
        split_axis=0,
        concat_axis=0,
        tiled=True,
    )
    halves = returned.reshape(expert_count, 2, capacity, width)
    lower = halves[flat_routes, 0, slot_index].astype(jnp.float32)
    upper = halves[flat_routes, 1, slot_index].astype(jnp.float32)
    picked = (lower + upper).astype(jnp.bfloat16).reshape(tok_rows, TOP, width)
    code_float = codes.astype(jnp.float32)
    mix = code_float / jnp.sum(code_float, axis=1, keepdims=True)
    moe = jnp.einsum("tk,tkd->td", mix, picked.astype(jnp.float32))
    layer_out = (wide + moe).astype(jnp.bfloat16)
    return (attended, layer_out)


def solution(mesh):
    placed = (
        P("ctx", "ep"),
        P(None, "ctx"),
        P(None, "ep"),
        P(("ep", "ctx"), None),
        P(("ctx", "ep"), None),
        P(),
        P(("ctx", "ep"), None),
        P(("ctx", "ep"), None),
        P(("ctx", "ep"), None, None),
        P(("ctx", "ep"), None, None),
        P(("ctx", "ep"), None, None),
    )
    return jax.shard_map(
        local,
        mesh=mesh,
        in_specs=placed,
        out_specs=(P(("ctx", "ep"), None), P(("ctx", "ep"), None)),
        check_vma=False,
    )
```

profile of v0, /device:TPU:1, one launch (start us, length us, event | category | flops | bytes accessed | tf_op | source)
XLA Modules:
  0.0 352.2 jit_solution(7851378775843418193)
XLA Ops:
  7.2 0.0 all-gather.3.cloned.1.call-start
  7.2 0.7 all-gather.3.cloned.1.call-update
  7.9 0.0 all-gather.5.cloned.1.call-start
  7.9 0.7 all-gather.5.cloned.1.call-update
  8.6 0.0 reduce-scatter.2.cloned.1.call-start
  8.7 42.7 %all-gather.3.cloned.1.call-done = bf16[576,2048]{1,0:T(8,128)(2,1)} async-done(((bf16[576,128]{1,0:T(8,128)(2,1)}), bf16[576,2048]{1,0:T(8,128)(2,1)}) %all-gather.3.cloned.1.call-update) | async-done | bytes 2359312 | tf_op jit(solution)/shard_map/all_gather | solution.py:59
  51.4 20.8 %conditional.1 = (f32[8,128]{1,0:T(8,128)S(1)}, f32[8,128,128]{1,2,0:T(8,128)S(1)}) conditional(s32[]{:T(128)} %convert_element_type.72, (s32[]{:T(128)}, s32[128]{0:T(128)S(1)}, bf16[576,2048]{1,0:T(8,128)(2,1)}, bf16[512,2048]{1,0:T(8,128)(2,1)}, bf16[128,1536]{1,0:T(8,128)(2,1)}) %tuple.19, () %tuple.20), branch_computations={%region_0.3_spmd, %region_3.4_spmd} | conditional | flops 5662571520 | bytes 92694112 | solution.py:77
  51.4 0.0 copy-start.1
  51.4 10.0 %convolution_convert_fusion = bf16[2048,2048]{0,1:T(8,128)(2,1)} fusion(bf16[512,2048]{1,0:T(8,128)(2,1)} %get-tuple-element.39, bf16[576,2048]{1,0:T(8,128)(2,1)} %get-tuple-element.28), kind=kOutput, calls=%fused_computation.8 | convolution fusion | flops 4299161600 | bytes 12582912 | tf_op jit(solution)/shard_map/cond/branch_0_fun/rn,rc->nc/dot_general | solution.py:63
  61.4 0.0 copy-done.1
  61.4 0.2 copy.26
  61.7 0.0 slice-start
  61.7 4.0 %fusion.6 = f32[8,2048,128]{2,1,0:T(8,128)S(1)} fusion(bf16[2048,8,256]{0,2,1:T(8,128)(2,1)} %bitcast.63, bf16[128,8,192]{0,2,1:T(8,128)(2,1)S(1)} %bitcast.68), kind=kOutput, calls=%fused_computation.13 | convolution fusion | flops 536870912 | bytes 12845056 | tf_op jit(solution)/shard_map/cond/branch_0_fun/qhd,nhd->hqn/dot_general | solution.py:16
  65.7 0.2 iota_compare_fusion
  65.9 0.0 slice-start.1
  65.9 2.8 select_reduce_fusion
  68.7 0.0 slice-done
  68.8 0.0 slice-done.1
  68.8 2.0 fusion.3
  70.8 1.4 fusion.2
  72.2 0.1 divide_convert_fusion
  72.3 28.4 %all-gather.5.cloned.1.call-done = bf16[1024,3584]{1,0:T(8,128)(2,1)} async-done(((bf16[64,3584]{1,0:T(8,128)(2,1)}), bf16[1024,3584]{1,0:T(8,128)(2,1)}) %all-gather.5.cloned.1.call-update) | async-done | bytes 7340048 | tf_op jit(solution)/shard_map/all_gather | solution.py:84
  100.7 0.0 copy-start.5
  100.7 0.0 copy-start.2
  100.7 0.0 copy-start.4
  100.7 5.2 %convolution_convert_fusion.2 = bf16[128,3584]{1,0:T(8,128)(2,1)} fusion(bf16[128,1024]{0,1:T(8,128)(2,1)S(1)} %bitcast.67, bf16[1024,3584]{1,0:T(8,128)(2,1)} %all-gather.5.cloned.1.call-done), kind=kOutput, calls=%fused_computation.28 | convolution fusion | flops 939982848 | bytes 8519680 | tf_op jit(solution)/shard_map/dot_general | solution.py:86
  105.9 0.0 reduce-scatter.2.cloned.1.call-update
  105.9 0.0 copy-done.5
  105.9 0.1 copy.28
  106.0 0.3 eq.15
  106.3 0.1 reshape.159
  106.4 0.1 fusion.38
  106.4 0.2 reduce_window_sum.11
  106.6 0.2 select_reduce_fusion.1
  106.8 70.1 %reduce-scatter.2.cloned.1.call-done = bf16[16,3584]{1,0:T(8,128)(2,1)} async-done(((bf16[128,3584]{1,0:T(8,128)(2,1)}), bf16[16,3584]{1,0:T(8,128)(2,1)}) %reduce-scatter.2.cloned.1.call-update) | async-done | bytes 114704 | tf_op jit(solution)/shard_map/reduce_scatter | solution.py:85
  177.0 0.0 copy-done.2
  177.0 1.1 fusion.34
  178.0 0.0 copy-start
  178.0 0.0 copy-done.4
  178.1 0.1 fusion.36
  178.2 1.1 gather_fusion
  179.3 0.1 broadcast_in_dim.37
  179.4 17.4 %scatter_fusion = bf16[64,3,3584]{2,0,1:T(8,128)(2,1)S(1)} fusion(bf16[64,3,3584]{2,0,1:T(8,128)(2,1)S(1)} %broadcast_in_dim.37, s32[128]{0:T(128)S(1)} %get-tuple-element.53, bf16[128,3584]{1,0:T(8,128)(2,1)S(1)} %gather_fusion), kind=kCustom, calls=%fused_computation.3 | custom fusion | bytes 2753536 | tf_op jit(solution)/shard_map/scatter | solution.py:110
  196.8 1.2 copy.30
  198.0 0.9 broadcast_in_dim.38
  198.9 55.0 %all_to_all.10 = bf16[128,3,3584]{2,1,0:T(4,128)(2,1)} all-to-all(bf16[128,3,3584]{2,1,0:T(4,128)(2,1)S(1)} %bitcast.62), channel_id=1, replica_groups=mesh['ctx'=16,'ep'=8] {'ctx','ep'}, dimensions={0} | all-to-all | bytes 5505024 | tf_op jit(solution)/shard_map/all_to_all | solution.py:117
  254.0 5.6 %reshape.161 = bf16[384,3584]{1,0:T(8,128)(2,1)S(1)} reshape(bf16[128,3,3584]{2,1,0:T(4,128)(2,1)} %all_to_all.10) | data formatting | bytes 5505024 | tf_op jit(solution)/shard_map/reshape | solution.py:35
  259.6 4.5 %fusion.20 = f32[384,512]{1,0:T(8,128)} fusion(bf16[384,3584]{1,0:T(8,128)(2,1)S(1)} %reshape.161, bf16[1,3584,512]{2,1,0:T(8,128)(2,1)} %param.21), kind=kOutput, calls=%fused_computation.32 | convolution fusion | flops 1409286144 | bytes 7208960 | tf_op jit(solution)/shard_map/dot_general | solution.py:36
  264.1 8.0 %convolution_convert_fusion.1 = bf16[384,3584]{1,0:T(8,128)(2,1)} fusion(bf16[1,512,3584]{2,1,0:T(8,128)(2,1)} %param.23, bf16[384,3584]{1,0:T(8,128)(2,1)S(1)} %reshape.161, bf16[1,3584,512]{2,1,0:T(8,128)(2,1)} %param.22, f32[384,512]{1,0:T(8,128)} %fusion.20), kind=kOutput, calls=%fused_computation.27 | convolution fusion | flops 2821128192 | bytes 13631488 | tf_op jit(solution)/shard_map/dot_general | solution.py:39
  272.2 6.7 %reshape.162 = bf16[128,3,3584]{2,1,0:T(4,128)(2,1)} reshape(bf16[384,3584]{1,0:T(8,128)(2,1)} %convolution_convert_fusion.1) | data formatting | bytes 5505024 | tf_op jit(solution)/shard_map/reshape | solution.py:40
  278.8 0.0 copy-start.3
  278.8 7.3 %all-to-all-start.1 = ((bf16[128,3,3584]{2,1,0:T(4,128)(2,1)}), bf16[128,3,3584]{2,1,0:T(4,128)(2,1)}, u32[]{:S(2)}, u32[]{:S(2)}) async-start(bf16[128,3,3584]{2,1,0:T(4,128)(2,1)} %reshape.162), calls=%async_computation.2 | async-start | bytes 7340032 | tf_op jit(solution)/shard_map/all_to_all | solution.py:115
  286.2 0.0 copy-done.3
  286.2 0.1 copy.35
  286.3 45.6 %all-to-all-done.1 = bf16[128,3,3584]{2,1,0:T(4,128)(2,1)} async-done(((bf16[128,3,3584]{2,1,0:T(4,128)(2,1)}), bf16[128,3,3584]{2,1,0:T(4,128)(2,1)}, u32[]{:S(2)}, u32[]{:S(2)}) %all-to-all-start.1) | async-done | bytes 2752544 | tf_op jit(solution)/shard_map/all_to_all | solution.py:115
  331.9 4.4 %copy.32 = bf16[64,2,3,3584]{3,1,2,0:T(2,128)(2,1)S(1)} copy(bf16[64,2,3,3584]{3,2,1,0:T(4,128)(2,1)} %bitcast.15) | data formatting | bytes 5505024 | tf_op jit(solution)/shard_map/reshape | solution.py:127
  336.3 3.4 gather_fusion.1
  339.7 3.4 gather_fusion.2
  343.1 1.8 fusion.29
  345.0 0.0 copy-done
  345.0 0.7 fusion.37
  (10 shorter events, 0.1 us)
Async XLA Ops:
  7.2 44.2 %all-gather.3.cloned.1.call-start = ((), (), s32[]{:S(2)}) async-start(), calls=%async_computation.3 | async-start | bytes 2506752 | tf_op jit(solution)/shard_map/all_gather | solution.py:59
  7.9 92.8 %all-gather.5.cloned.1.call-start = ((), (), s32[]{:S(2)}) async-start(), calls=%async_computation.4 | async-start | bytes 7798784 | tf_op jit(solution)/shard_map/all_gather | solution.py:84
  8.6 168.3 %reduce-scatter.2.cloned.1.call-start = ((), (), s32[]{:S(2)}) async-start(), calls=%async_computation.5 | async-start | bytes 1032192 | tf_op jit(solution)/shard_map/reduce_scatter | solution.py:85
  51.4 10.0 %copy-start.1 = (bf16[128,1536]{1,0:T(8,128)(2,1)S(1)}, bf16[128,1536]{1,0:T(8,128)(2,1)}, u32[]{:S(2)}) copy-start(bf16[128,1536]{1,0:T(8,128)(2,1)} %get-tuple-element.45) | copy-start | bytes 1179652 | tf_op jit(solution)/shard_map/cond
  61.7 7.1 %slice-start = ((s8[8388608]{0:T(1024)(128)(4,1)}), s8[4194304]{0:T(1024)(128)(4,1)S(1)}, s32[]{:S(2)}) async-start(s8[8388608]{0:T(1024)(128)(4,1)} %bitcast.64), calls=%async_computation.6 | async-start | bytes 8388608 | tf_op jit(solution)/shard_map/cond
  65.9 2.9 slice-start.1
  100.7 5.2 %copy-start.5 = (s32[16,8]{0,1:T(8,128)S(1)}, s32[16,8]{0,1:T(8,128)}, u32[]{:S(2)}) copy-start(s32[16,8]{0,1:T(8,128)} %param.19) | copy-start | bytes 1540
  100.7 76.3 %copy-start.2 = (bf16[16,3584]{1,0:T(8,128)(2,1)S(1)}, bf16[16,3584]{1,0:T(8,128)(2,1)}, u32[]{:S(2)}) copy-start(bf16[16,3584]{1,0:T(8,128)(2,1)} %param.17) | copy-start | bytes 344068
  100.7 77.4 %copy-start.4 = (f32[3584]{0:T(1024)S(1)}, f32[3584]{0:T(1024)}, u32[]{:S(2)}) copy-start(f32[3584]{0:T(1024)} %param.18) | copy-start | bytes 43012
  178.0 166.9 %copy-start = (bf16[16,3584]{1,0:T(8,128)(2,1)}, bf16[16,3584]{1,0:T(8,128)(2,1)S(1)}, u32[]{:S(2)}) copy-start(bf16[16,3584]{1,0:T(8,128)(2,1)S(1)} %get-tuple-element.48) | copy-start | bytes 344068
  278.8 7.4 %copy-start.3 = (s32[16,8]{0,1:T(8,128)S(1)}, s32[16,8]{0,1:T(8,128)}, u32[]{:S(2)}) copy-start(s32[16,8]{0,1:T(8,128)} %param.20) | copy-start | bytes 1540
  278.8 53.1 %all-to-all-start.1 = ((bf16[128,3,3584]{2,1,0:T(4,128)(2,1)}), bf16[128,3,3584]{2,1,0:T(4,128)(2,1)}, u32[]{:S(2)}, u32[]{:S(2)}) async-start(bf16[128,3,3584]{2,1,0:T(4,128)(2,1)} %reshape.162), calls=%async_computation.2 | async-start | bytes 7340032 | tf_op jit(solution)/shard_map/all_to_all | solution.py:115
Sparse Core Ops, SparseCore 0:
  9.6 41.7 all-gather.2
  53.1 47.5 all-gather.4
  106.0 70.8 reduce-scatter.1
where the time goes:
time: 353 us; the launch traced here: 352 us
  waiting for transfers between devices  188 us (53%)
  blocking collectives  55 us (16%)
  local copies, waits for them, and re-layouts  45 us (13%)
  matrix products  38.5 us (11%)
  between operations  13.9 us (4%)
  starting transfers between devices  7.46 us (2%)
  other arithmetic  3.97 us (1%)
    reduce_scatter x1, waiting for transfers between devices, local(): lax.psum_scatter(jnp.dot(heads_out, w_full, preferred_element_type=jnp.fl...  70.1 us
    all_to_all x1, blocking collectives, local(): lax.all_to_all(outgoing, ('ctx', 'ep'), split_axis=0, concat_axis=0, tile...  55 us
    all_to_all x1, waiting for transfers between devices, local(): lax.all_to_all(expert_apply(lax.all_to_all(outgoing, ('ctx', 'ep'), split...  45.6 us
    all_gather x1, waiting for transfers between devices, local(): piece = lax.all_gather(latents, 'ctx', axis=1, tiled=True)  42.7 us
    all_gather x1, waiting for transfers between devices, local(): w_full = lax.all_gather(w_out, 'ctx', axis=0, tiled=True)  28.4 us
    scatter x2, local copies, waits for them, and re-layouts, local(): single = jnp.zeros((expert_count, capacity, width), jnp.bfloat16).at[flat...  18.6 us
    dot_general x1, matrix products, compute(): jnp.einsum('rn,rc->nc', piece[:KV_RANK], w_kv, preferred_element_type=jnp...  10 us
    dot_general x1, matrix products, expert_apply(): jnp.dot(hidden, w_down[0], preferred_element_type=jnp.float32)  8.04 us
  transfers between devices with their start and end apart: 4, of which 4 were waited for; matrix products, arithmetic and copies ran while one was open for 6% of the time, Pallas kernels for 0%

commit v1 on v0

v1 whole, which is shorter than its diff:
```python
import jax
import jax.numpy as jnp
from jax import lax
from jax.sharding import Mesh, PartitionSpec as P

NOPE = 128
VD = 128
KV_RANK = 512
TOP = 8
QK = 192
CAP = 3

CTX = ("z_lo", "x", "core")
CTX_CHIPS = ("z_lo", "x")
EP = ("z_hi", "y")
CHIPS = ("z_lo", "x", "z_hi", "y")
SIZES = (2, 4, 2, 2, 4)
NAMES = ("z_lo", "x", "core", "z_hi", "y")
SWAP = ((0, 1), (1, 0))
BF = jnp.bfloat16
F32 = jnp.float32


def both_cores(mine):
    other = lax.ppermute(mine, "core", SWAP)
    first = lax.axis_index("core") == 0
    return jnp.stack([jnp.where(first, mine, other), jnp.where(first, other, mine)])


def attention(queries, lat, w_kv):
    rows = queries.shape[0]
    heads = queries.shape[1] // QK
    q = queries.reshape(rows, heads, QK)
    w = w_kv.reshape(KV_RANK, heads, NOPE + VD)
    q_lat = jnp.einsum("qhd,rhd->hqr", q[:, :, :NOPE], w[:, :, :NOPE], preferred_element_type=F32).astype(BF)
    q_all = jnp.concatenate([q_lat, q[:, :, NOPE:].transpose(1, 0, 2)], axis=2)
    scores = jnp.einsum("hqr,rn->hqn", q_all, lat, preferred_element_type=F32) * QK ** (-0.5)
    ctx = lax.axis_index(CTX)
    query_pos = ctx * rows + jnp.arange(rows, dtype=jnp.int32)
    key_pos = jnp.arange(lat.shape[1], dtype=jnp.int32)
    allowed = key_pos[None, None, :] <= query_pos[None, :, None]
    peak = jnp.max(jnp.where(allowed, scores, F32(-1e30)), axis=2, keepdims=True)
    probs = jnp.where(allowed, jnp.exp(scores - peak), F32(0.0))
    total = jnp.sum(probs, axis=2, keepdims=True)
    mixed = jnp.einsum("hqn,rn->hqr", probs.astype(BF), lat[:KV_RANK], preferred_element_type=F32)
    mixed = (mixed / total).astype(BF)
    out = jnp.einsum("hqr,rhd->qhd", mixed, w[:, :, NOPE:], preferred_element_type=F32).astype(BF)
    return out.reshape(rows, heads * VD)


def local(queries, latents, w_kv, w_out, resid, norm_gain, routes, codes, w_gate, w_up, w_down):
    tok, width = resid.shape
    chips = 64
    w_full = lax.all_gather(w_out, CTX, axis=0, tiled=True)
    parts = 16
    lat = lax.all_to_all(
        jnp.broadcast_to(latents[None], (parts,) + latents.shape), CTX, split_axis=0, concat_axis=0, tiled=True
    )
    lat = lat.transpose(1, 0, 2).reshape(latents.shape[0], -1)
    heads_out = attention(queries, lat, w_kv)
    attn = jnp.dot(heads_out, w_full, preferred_element_type=F32).astype(BF)
    attn = lax.all_to_all(attn.reshape(8, tok, width), EP, split_axis=0, concat_axis=0, tiled=True)
    attended = (resid.astype(F32) + jnp.sum(attn.astype(F32), axis=0)).astype(BF)
    wide = attended.astype(F32)
    meansq = jnp.mean(wide * wide, axis=1, keepdims=True)
    normed = (wide * lax.rsqrt(meansq + 1e-06) * norm_gain[None, :]).astype(BF)
    normed2 = both_cores(normed).reshape(2 * tok, width)

    core = lax.axis_index("core")
    code_float = codes.astype(F32)
    mix = code_float / jnp.sum(code_float, axis=1, keepdims=True)
    routes2 = both_cores(routes)
    mix2 = both_cores(mix)
    chosen = routes2[:, :, :, None] == jnp.arange(64, dtype=jnp.int32)
    weight = jnp.sum(jnp.where(chosen, mix2[..., None], F32(0.0)), axis=2)
    has = jnp.any(chosen, axis=2)

    def of_core(a):
        a = a.reshape(2, tok, 8, 2, 4)
        return jnp.where(core == 0, a[:, :, :, 0], a[:, :, :, 1]).reshape(2, tok, 32)

    weight, has = of_core(weight), of_core(has)
    count = has.astype(jnp.int32)
    slot = jnp.cumsum(count, axis=1) - count
    place = has[:, :, :, None] & (slot[:, :, :, None] == jnp.arange(CAP, dtype=jnp.int32))
    place = place.transpose(2, 3, 0, 1)[:, :, :, None, :]
    same = jnp.arange(2)[:, None, None] == jnp.arange(2)[None, :, None]
    place = (place & same).reshape(32, CAP, 2, 2 * tok)
    place = jnp.broadcast_to(place[:, None], (32, 2, CAP, 2, 2 * tok)).reshape(chips * CAP * 2, 2 * tok)
    gains = weight.transpose(2, 0, 1).reshape(32, 2 * tok)
    gains = jnp.broadcast_to(gains[:, None], (32, 2 * CAP * 2, 2 * tok)).reshape(chips * CAP * 2, 2 * tok)
    combine = jnp.where(place, gains, F32(0.0))

    outgoing = jnp.dot(place.astype(BF), normed2, preferred_element_type=F32).astype(BF)
    arrived = lax.all_to_all(
        outgoing.reshape(chips, CAP, 2, width), CHIPS, split_axis=0, concat_axis=0, tiled=True
    ).reshape(chips * CAP * 2, width)
    gate = jnp.dot(arrived, w_gate[0], preferred_element_type=F32)
    upward = jnp.dot(arrived, w_up[0], preferred_element_type=F32)
    hidden = (jax.nn.silu(gate) * upward).astype(BF)
    produced = jnp.dot(hidden, w_down[0], preferred_element_type=F32).astype(BF)
    returned = lax.all_to_all(
        produced.reshape(chips, CAP, 2, width), CHIPS, split_axis=0, concat_axis=0, tiled=True
    ).reshape(chips * CAP * 2, width)

    high = lax.reduce_precision(combine, 8, 7)
    factors = jnp.concatenate([high, combine - high], axis=1).astype(BF)
    moe = lax.dot_general(factors, returned, (((0,), (0,)), ((), ())), preferred_element_type=F32)
    moe = moe[: 2 * tok] + moe[2 * tok :]
    moe = moe.reshape(2, tok, width)
    own = jnp.where(core == 0, moe[0], moe[1])
    far = lax.ppermute(jnp.where(core == 0, moe[1], moe[0]), "core", SWAP)
    layer_out = (wide + own + far).astype(BF)
    return (attended, layer_out)


def solution(mesh):
    fine = Mesh(mesh.devices.reshape(SIZES), NAMES)
    rows = P(CTX + EP, None)
    heads = P(CTX + EP, None, None)
    placed = (
        P(CTX, EP),
        P(None, CTX),
        P(None, EP),
        P(EP + CTX, None),
        rows,
        P(),
        rows,
        rows,
        heads,
        heads,
        heads,
    )
    return jax.shard_map(local, mesh=fine, in_specs=placed, out_specs=(rows, rows), check_vma=False)
```

time: 353 us -> 249 us (0.71)
  waiting for transfers between devices: 188 us -> 83.6 us
  starting transfers between devices: 7.46 us -> 28.7 us
  blocking collectives: 55 us -> 41.6 us
  local copies, waits for them, and re-layouts: 45 us -> 35.7 us
  other arithmetic: 3.97 us -> 7.82 us
    all_gather x2 -> x1, waiting for transfers between devices: 71.1 us -> 0.02 us  [local(): w_full = lax.all_gather(w_out, CTX, axis=0, tiled=True)]
    reduce_scatter x1 -> x0, waiting for transfers between devices: 70.1 us -> none  [local(): lax.psum_scatter(jnp.dot(heads_out, w_full, preferred_element_type=jnp.fl...]
    all_to_all x1 -> x3, waiting for transfers between devices: 45.6 us -> 80.5 us  [the longest x1 35.5 us: local(): lax.all_to_all(jnp.broadcast_to(latents[None], (parts,) + latents.shape),...]
    scatter x2 -> x0, local copies, waits for them, and re-layouts: 18.6 us -> none  [local(): single = jnp.zeros((expert_count, capacity, width), jnp.bfloat16).at[flat...]
    all_to_all x1 -> x3, starting transfers between devices: 7.34 us -> 22.7 us  [the longest x1 7.93 us: local(): lax.all_to_all(attn.reshape(8, tok, width), EP, split_axis=0, concat_axis...]
    all_to_all x1, blocking collectives: 55 us -> 41.6 us  [local(): lax.all_to_all(outgoing.reshape(chips, CAP, 2, width), CHIPS, split_axis=...]
    gather x3 -> x0, local copies, waits for them, and re-layouts: 7.93 us -> none  [the longest x1 3.42 us: local(): lower = halves[flat_routes, 0, slot_index].astype(jnp.float32)]
    slice x0 -> x4, local copies, waits for them, and re-layouts: none -> 7.09 us  [the longest x3 7.08 us: attention(): lat[:KV_RANK]]
  transfers between devices with their start and end apart: 4 -> 8, of which waited for: 4 -> 6; matrix products, arithmetic and copies ran while one was open for 6% -> 19% of each run, Pallas kernels for 0% -> 0%
where the time goes in v1:
time: 249 us; the launch traced here: 247 us
  waiting for transfers between devices  83.6 us (34%)
  blocking collectives  41.6 us (17%)
  local copies, waits for them, and re-layouts  35.7 us (14%)
  matrix products  35.4 us (14%)
  starting transfers between devices  28.7 us (12%)
  between operations  14.3 us (6%)
  other arithmetic  7.82 us (3%)
    all_to_all x1, blocking collectives, local(): lax.all_to_all(outgoing.reshape(chips, CAP, 2, width), CHIPS, split_axis=...  41.6 us
    all_to_all x1, waiting for transfers between devices, local(): lax.all_to_all(jnp.broadcast_to(latents[None], (parts,) + latents.shape),...  35.5 us
    all_to_all x1, waiting for transfers between devices, local(): lax.all_to_all(produced.reshape(chips, CAP, 2, width), CHIPS, split_axis=...  30 us
    all_to_all x1, waiting for transfers between devices, local(): lax.all_to_all(attn.reshape(8, tok, width), EP, split_axis=0, concat_axis...  15.1 us
    dot_general x1, matrix products, local(): produced = jnp.dot(hidden, w_down[0], preferred_element_type=F32).astype(BF)  8.07 us
    all_to_all x1, starting transfers between devices, local(): lax.all_to_all(attn.reshape(8, tok, width), EP, split_axis=0, concat_axis...  7.93 us
    all_to_all x1, starting transfers between devices, local(): lax.all_to_all(produced.reshape(chips, CAP, 2, width), CHIPS, split_axis=...  7.46 us
    all_to_all x1, starting transfers between devices, local(): lax.all_to_all(jnp.broadcast_to(latents[None], (parts,) + latents.shape),...  7.3 us
  transfers between devices with their start and end apart: 8, of which 6 were waited for; matrix products, arithmetic and copies ran while one was open for 19% of the time, Pallas kernels for 0%

profile of v1, /device:TPU:1, one launch (start us, length us, event | category | flops | bytes accessed | tf_op | source)
XLA Modules:
  0.0 247.1 jit_solution(17089568880467493522)
XLA Ops:
  7.2 0.0 all-gather.2.cloned.1.call-start
  7.2 0.7 all-gather.2.cloned.1.call-update
  7.9 2.7 %broadcast_in_dim.42 = bf16[16,576,128]{2,1,0:T(8,128)(2,1)} broadcast(bf16[576,128]{1,0:T(8,128)(2,1)} %param.12), dimensions={1,2} | broadcast | bytes 2506752 | tf_op jit(solution)/shard_map/broadcast_in_dim | solution.py:57
  10.6 7.3 %all-to-all-start = ((bf16[16,576,128]{2,1,0:T(8,128)(2,1)}), bf16[16,576,128]{2,1,0:T(8,128)(2,1)S(1)}, u32[]{:S(2)}, u32[]{:S(2)}) async-start(bf16[16,576,128]{2,1,0:T(8,128)(2,1)} %broadcast_in_dim.42), calls=%async_computation | async-start | bytes 4718592 | tf_op jit(solution)/shard_map/all_to_all | solution.py:56
  18.0 0.2 collective-permute-start
  18.1 0.2 copy.81
  18.4 0.8 copy.103
  19.2 4.0 %copy.83 = bf16[512,2048]{0,1:T(8,128)(2,1)} copy(bf16[512,2048]{1,0:T(8,128)(2,1)} %param.13) | data formatting | bytes 4194304 | tf_op args[2]
  23.2 0.1 and.46
  23.3 0.1 and.47
  23.4 2.7 %convolution_convert_fusion.3 = bf16[8,128,512]{2,1,0:T(8,128)(2,1)} fusion(bf16[512,8,256]{0,2,1:T(8,128)(2,1)} %bitcast.61, bf16[128,8,192]{0,2,1:T(8,128)(2,1)S(1)} %bitcast.64), kind=kOutput, calls=%fused_computation.20 | convolution fusion | flops 134742016 | bytes 2359296 | tf_op jit(solution)/shard_map/qhd,rhd->hqr/dot_general | solution.py:35
  26.1 0.9 iota_compare_fusion
  27.0 35.5 %all-to-all-done = bf16[16,576,128]{2,1,0:T(8,128)(2,1)S(1)} async-done(((bf16[16,576,128]{2,1,0:T(8,128)(2,1)}), bf16[16,576,128]{2,1,0:T(8,128)(2,1)S(1)}, u32[]{:S(2)}, u32[]{:S(2)}) %all-to-all-start) | async-done | bytes 2359328 | tf_op jit(solution)/shard_map/all_to_all | solution.py:56
  62.5 0.1 slice.63
  62.7 2.9 %copy.86 = bf16[576,16,128]{2,1,0:T(8,128)(2,1)} copy(bf16[576,16,128]{2,0,1:T(8,128)(2,1)S(1)} %bitcast.60) | data formatting | bytes 4718592 | tf_op jit(solution)/shard_map/transpose | solution.py:59
  65.6 2.7 %copy.88 = bf16[512,16,128]{2,1,0:T(8,128)(2,1)} copy(bf16[512,16,128]{2,0,1:T(8,128)(2,1)S(1)} %slice.63) | data formatting | bytes 4194304 | tf_op jit(solution)/shard_map/slice | solution.py:45
  68.2 4.3 %reshape.187 = bf16[512,2048,1]{1,0,2:T(8,128)(2,1)} reshape(bf16[512,16,128]{2,1,0:T(8,128)(2,1)} %copy.88) | data formatting | bytes 4194304 | tf_op jit(solution)/shard_map/slice | solution.py:45
  72.5 2.4 reshape.186
  74.9 5.2 %fusion.17 = f32[8,128,2048]{2,1,0:T(8,128)S(1)} fusion(bf16[576,2048,1]{1,0,2:T(8,128)(2,1)} %reshape.186, bf16[8,128,64]{2,1,0:T(8,128)(2,1)} %bitcast.68, bf16[8,128,512]{2,1,0:T(8,128)(2,1)S(1)} %copy-done.4), kind=kOutput, calls=%fused_computation.21 | convolution fusion | flops 2418278400 | bytes 11927552 | tf_op jit(solution)/shard_map/hqr,rn->hqn/dot_general | solution.py:37
  80.2 5.1 %fusion.57 = (f32[8,128]{1,0:T(8,128)S(1)}, bf16[8,128,2048]{2,1,0:T(8,128)(2,1)}) fusion(f32[8,128,2048]{2,1,0:T(8,128)S(1)} %fusion.17, pred[128,2048]{1,0:T(8,128)(4,1)S(1)} %copy-done.6), kind=kOutput, calls=%fused_computation.81 | output fusion | flops 14682111 | bytes 12849152 | tf_op jit(solution)/shard_map/sub | solution.py:43
  85.3 5.5 %fusion.30 = bf16[8,128,128]{1,2,0:T(8,128)(2,1)S(1)} fusion(bf16[512,2048,1]{1,0,2:T(8,128)(2,1)} %reshape.187, bf16[8,128,2048]{2,1,0:T(8,128)(2,1)} %get-tuple-element.13, bf16[512,8,256]{0,2,1:T(8,128)(2,1)S(1)} %bitcast.62, f32[8,128]{1,0:T(8,128)S(1)} %get-tuple-element.12), kind=kOutput, calls=%fused_computation.28 | convolution fusion | flops 2282881024 | bytes 7606272 | tf_op jit(solution)/shard_map/hqr,rhd->qhd/dot_general | solution.py:47
  90.8 0.0 all-gather.2.cloned.1.call-done
  90.8 5.2 %convolution_convert_fusion.2 = bf16[128,3584]{1,0:T(8,128)(2,1)} fusion(bf16[128,1024]{0,1:T(8,128)(2,1)S(1)} %bitcast.66, bf16[1024,3584]{1,0:T(8,128)(2,1)} %all-gather.2.cloned.1.call-done), kind=kOutput, calls=%fused_computation.7 | convolution fusion | flops 939982848 | bytes 8519680 | tf_op jit(solution)/shard_map/dot_general | solution.py:61
  96.0 7.9 %all-to-all-start.1 = ((bf16[8,16,3584]{2,1,0:T(8,128)(2,1)}), bf16[8,16,3584]{2,1,0:T(8,128)(2,1)S(1)}, u32[]{:S(2)}, u32[]{:S(2)}) async-start(bf16[8,16,3584]{2,1,0:T(8,128)(2,1)} %bitcast.6), calls=%async_computation.1 | async-start | bytes 1835008 | tf_op jit(solution)/shard_map/all_to_all | solution.py:62
  103.9 0.0 collective-permute-done
  103.9 0.1 copy.89
  104.0 0.1 fusion.45
  104.1 0.1 copy.90
  104.3 0.1 copy.92
  104.4 0.1 copy.91
  104.5 15.1 %all-to-all-done.1 = bf16[8,16,3584]{2,1,0:T(8,128)(2,1)S(1)} async-done(((bf16[8,16,3584]{2,1,0:T(8,128)(2,1)}), bf16[8,16,3584]{2,1,0:T(8,128)(2,1)S(1)}, u32[]{:S(2)}, u32[]{:S(2)}) %all-to-all-start.1) | async-done | bytes 917536 | tf_op jit(solution)/shard_map/all_to_all | solution.py:62
  119.5 0.1 convert_reduce_fusion
  119.7 0.2 fusion.40
  119.9 0.1 fusion.42
  120.0 0.5 collective-permute-start.2
  120.4 0.1 bitcast_and_fusion
  120.5 0.1 copy.93
  120.7 0.1 broadcast_in_dim.72
  120.8 0.1 reshape.178
  120.9 0.5 collective-permute-done.2
  121.4 0.1 select_bitcast_fusion.1
  121.6 0.8 convolution_convert_fusion.1
  122.4 2.5 %reshape.182 = bf16[64,3,2,3584]{3,2,1,0:T(2,128)(2,1)} reshape(bf16[384,3584]{1,0:T(8,128)(2,1)S(1)} %convolution_convert_fusion.1) | data formatting | bytes 5505024 | tf_op jit(solution)/shard_map/reshape | solution.py:96
  124.9 41.6 %all_to_all.20 = bf16[64,3,2,3584]{3,2,1,0:T(2,128)(2,1)S(1)} all-to-all(bf16[64,3,2,3584]{3,2,1,0:T(2,128)(2,1)} %reshape.182), channel_id=1, replica_groups=mesh['z_lo'=2,'x'=4,'core'=2,'z_hi'=2,'y'=4] {'z_lo','x','z_hi','y'}, dimensions={0} | all-to-all | bytes 5505024 | tf_op jit(solution)/shard_map/all_to_all | solution.py:95
  166.5 2.5 %reshape.183 = bf16[384,3584]{1,0:T(8,128)(2,1)} reshape(bf16[64,3,2,3584]{3,2,1,0:T(2,128)(2,1)S(1)} %all_to_all.20) | data formatting | bytes 5505024 | tf_op jit(solution)/shard_map/reshape | solution.py:97
  169.0 5.5 %fusion.13 = f32[384,512]{1,0:T(8,128)} fusion(bf16[384,3584]{1,0:T(8,128)(2,1)} %reshape.183, bf16[1,3584,512]{2,1,0:T(8,128)(2,1)} %param.19), kind=kOutput, calls=%fused_computation.16 | convolution fusion | flops 1409286144 | bytes 7208960 | tf_op jit(solution)/shard_map/dot_general | solution.py:98
  174.5 8.1 %convolution_convert_fusion = bf16[384,3584]{1,0:T(8,128)(2,1)} fusion(bf16[1,512,3584]{2,1,0:T(8,128)(2,1)} %param.21, bf16[384,3584]{1,0:T(8,128)(2,1)S(1)} %copy-done.2, bf16[1,3584,512]{2,1,0:T(8,128)(2,1)} %param.20, f32[384,512]{1,0:T(8,128)} %fusion.13), kind=kOutput, calls=%fused_computation.5 | convolution fusion | flops 2821128192 | bytes 13631488 | tf_op jit(solution)/shard_map/dot_general | solution.py:101
  182.6 6.5 %reshape.184 = bf16[64,3,2,3584]{3,2,1,0:T(2,128)(2,1)} reshape(bf16[384,3584]{1,0:T(8,128)(2,1)} %convolution_convert_fusion) | data formatting | bytes 5505024 | tf_op jit(solution)/shard_map/reshape | solution.py:103
  189.1 7.5 %all-to-all-start.3 = ((bf16[64,3,2,3584]{3,2,1,0:T(2,128)(2,1)}), bf16[64,3,2,3584]{3,2,1,0:T(2,128)(2,1)S(1)}, u32[]{:S(2)}, u32[]{:S(2)}) async-start(bf16[64,3,2,3584]{3,2,1,0:T(2,128)(2,1)} %reshape.184), calls=%async_computation.3 | async-start | bytes 5505024 | tf_op jit(solution)/shard_map/all_to_all | solution.py:102
  196.6 1.6 collective-permute-start.1
  198.2 0.1 copy.98
  198.3 0.7 collective-permute-done.1
  199.0 0.1 copy.94
  199.1 0.1 select_reduce_fusion.1
  199.3 0.1 copy.95
  199.4 0.1 copy.96
  199.4 0.1 copy.97
  199.6 0.1 copy.99
  199.7 30.0 %all-to-all-done.3 = bf16[64,3,2,3584]{3,2,1,0:T(2,128)(2,1)S(1)} async-done(((bf16[64,3,2,3584]{3,2,1,0:T(2,128)(2,1)}), bf16[64,3,2,3584]{3,2,1,0:T(2,128)(2,1)S(1)}, u32[]{:S(2)}, u32[]{:S(2)}) %all-to-all-start.3) | async-done | bytes 2752544 | tf_op jit(solution)/shard_map/all_to_all | solution.py:102
  229.7 2.5 %reshape.185 = bf16[384,3584]{1,0:T(8,128)(2,1)} reshape(bf16[64,3,2,3584]{3,2,1,0:T(2,128)(2,1)S(1)} %all-to-all-done.3) | data formatting | bytes 5505024 | tf_op jit(solution)/shard_map/reshape | solution.py:104
  232.2 2.4 fusion.47
  234.7 3.8 %collective-permute-start.3 = (f32[16,3584]{1,0:T(8,128)S(1)}, f32[16,3584]{1,0:T(8,128)S(1)}, u32[]{:S(2)}, u32[]{:S(2)}) collective-permute-start(f32[16,3584]{1,0:T(8,128)S(1)} %slice_select_fusion), channel_id=1, source_target_pairs={{0,8},{8,0},{1,9},{9,1},{2,10},{10,2},{3,11},{11,3},{4,12},{12,4},... | collective-permute-start | bytes 688136 | tf_op jit(solution)/shard_map/ppermute | solution.py:112
  238.4 1.1 collective-permute-done.3
  239.5 0.7 fusion.44
  (44 shorter events, 0.4 us)
Async XLA Ops:
  7.2 83.6 %all-gather.2.cloned.1.call-start = ((), (), s32[]{:S(2)}) async-start(), calls=%async_computation.4 | async-start | bytes 7798784 | tf_op jit(solution)/shard_map/all_gather | solution.py:54
  10.6 7.3 %copy-start.10 = (s32[16,8]{0,1:T(8,128)S(1)}, s32[16,8]{0,1:T(8,128)}, u32[]{:S(2)}) copy-start(s32[16,8]{0,1:T(8,128)} %param.17) | copy-start | bytes 1540
  10.6 7.5 %copy-start.5 = (bf16[128,1536]{1,0:T(8,128)(2,1)S(1)}, bf16[128,1536]{1,0:T(8,128)(2,1)}, u32[]{:S(2)}) copy-start(bf16[128,1536]{1,0:T(8,128)(2,1)} %param.11) | copy-start | bytes 1179652
  10.6 51.9 %all-to-all-start = ((bf16[16,576,128]{2,1,0:T(8,128)(2,1)}), bf16[16,576,128]{2,1,0:T(8,128)(2,1)S(1)}, u32[]{:S(2)}, u32[]{:S(2)}) async-start(bf16[16,576,128]{2,1,0:T(8,128)(2,1)} %broadcast_in_dim.42), calls=%async_computation | async-start | bytes 4718592 | tf_op jit(solution)/shard_map/all_to_all | solution.py:56
  18.0 85.9 %collective-permute-start = (s32[16,8]{0,1:T(8,128)S(1)}, s32[16,8]{0,1:T(8,128)S(1)}, u32[]{:S(2)}, u32[]{:S(2)}) collective-permute-start(s32[16,8]{0,1:T(8,128)S(1)} %copy-done.10), channel_id=1, source_target_pairs={{0,8},{8,0},{1,9},{9,1},{2,10},{10,2},{3,11},{11,3},{4,12},{12,4},... | collective-permute-start | bytes 1544 | tf_op jit(solution)/shard_map/ppermute | solution.py:25
  68.2 4.3 %copy-start = (bf16[576,16,128]{2,1,0:T(8,128)(2,1)S(1)}, bf16[576,16,128]{2,1,0:T(8,128)(2,1)}, u32[]{:S(2)}) copy-start(bf16[576,16,128]{2,1,0:T(8,128)(2,1)} %copy.86) | copy-start | bytes 7077892
  72.5 2.4 copy-start.4
  74.9 5.2 %copy-start.6 = (pred[128,2048]{1,0:T(8,128)(4,1)S(1)}, pred[128,2048]{1,0:T(8,128)(4,1)}, u32[]{:S(2)}) copy-start(pred[128,2048]{1,0:T(8,128)(4,1)} %iota_compare_fusion) | copy-start | bytes 786436
  80.2 5.1 %copy-start.1 = (bf16[512,2048]{0,1:T(8,128)(2,1)S(1)}, bf16[512,2048]{0,1:T(8,128)(2,1)}, u32[]{:S(2)}) copy-start(bf16[512,2048]{0,1:T(8,128)(2,1)} %copy.83) | copy-start | bytes 6291460
  96.0 23.7 %copy-start.7 = (bf16[16,3584]{1,0:T(8,128)(2,1)S(1)}, bf16[16,3584]{1,0:T(8,128)(2,1)}, u32[]{:S(2)}) copy-start(bf16[16,3584]{1,0:T(8,128)(2,1)} %param.15) | copy-start | bytes 344068
  96.0 23.9 %copy-start.8 = (f32[3584]{0:T(1024)S(1)}, f32[3584]{0:T(1024)}, u32[]{:S(2)}) copy-start(f32[3584]{0:T(1024)} %param.16) | copy-start | bytes 43012
  96.0 23.6 %all-to-all-start.1 = ((bf16[8,16,3584]{2,1,0:T(8,128)(2,1)}), bf16[8,16,3584]{2,1,0:T(8,128)(2,1)S(1)}, u32[]{:S(2)}, u32[]{:S(2)}) async-start(bf16[8,16,3584]{2,1,0:T(8,128)(2,1)} %bitcast.6), calls=%async_computation.1 | async-start | bytes 1835008 | tf_op jit(solution)/shard_map/all_to_all | solution.py:62
  119.8 119.7 %copy-start.3 = (bf16[16,3584]{1,0:T(8,128)(2,1)}, bf16[16,3584]{1,0:T(8,128)(2,1)S(1)}, u32[]{:S(2)}) copy-start(bf16[16,3584]{1,0:T(8,128)(2,1)S(1)} %get-tuple-element.3) | copy-start | bytes 344068
  120.0 1.4 collective-permute-start.2
  169.0 5.5 %copy-start.2 = (bf16[384,3584]{1,0:T(8,128)(2,1)S(1)}, bf16[384,3584]{1,0:T(8,128)(2,1)}, u32[]{:S(2)}) copy-start(bf16[384,3584]{1,0:T(8,128)(2,1)} %reshape.183) | copy-start | bytes 8257540
  189.1 7.5 %copy-start.9 = (s32[16,8]{0,1:T(8,128)S(1)}, s32[16,8]{0,1:T(8,128)}, u32[]{:S(2)}) copy-start(s32[16,8]{0,1:T(8,128)} %param.18) | copy-start | bytes 1540
  189.1 40.6 %all-to-all-start.3 = ((bf16[64,3,2,3584]{3,2,1,0:T(2,128)(2,1)}), bf16[64,3,2,3584]{3,2,1,0:T(2,128)(2,1)S(1)}, u32[]{:S(2)}, u32[]{:S(2)}) async-start(bf16[64,3,2,3584]{3,2,1,0:T(2,128)(2,1)} %reshape.184), calls=%async_computation.3 | async-start | bytes 5505024 | tf_op jit(solution)/shard_map/all_to_all | solution.py:102
  196.6 2.4 collective-permute-start.1
  234.7 4.9 %collective-permute-start.3 = (f32[16,3584]{1,0:T(8,128)S(1)}, f32[16,3584]{1,0:T(8,128)S(1)}, u32[]{:S(2)}, u32[]{:S(2)}) collective-permute-start(f32[16,3584]{1,0:T(8,128)S(1)} %slice_select_fusion), channel_id=1, source_target_pairs={{0,8},{8,0},{1,9},{9,1},{2,10},{10,2},{3,11},{11,3},{4,12},{12,4},... | collective-permute-start | bytes 688136 | tf_op jit(solution)/shard_map/ppermute | solution.py:112
Sparse Core Ops, SparseCore 0:
  9.7 72.5 all-gather.1

commit v2 on v1

v2 whole, which is shorter than its diff:
```python
import functools

import jax
import jax.numpy as jnp
from jax import lax
from jax.experimental import pallas as pl
from jax.experimental.pallas import tpu as pltpu
from jax.sharding import Mesh, PartitionSpec as P

NOPE = 128
VD = 128
KV_RANK = 512
TOP = 8
QK = 192
CAP = 3

CTX = ("z_lo", "x", "core")
CTX_CHIPS = ("z_lo", "x")
EP = ("z_hi", "y")
CHIPS = ("z_lo", "x", "z_hi", "y")
SIZES = (2, 4, 2, 2, 4)
NAMES = ("z_lo", "x", "core", "z_hi", "y")
SWAP = ((0, 1), (1, 0))
BF = jnp.bfloat16
F32 = jnp.float32
LOG2E = 1.4426950408889634


def attend_kernel(ids_ref, q_ref, near_ref, far_ref, w_ref, out_ref, lat_ref, s_ref, p_ref, *, rows, cuts):
    heads = w_ref.shape[1] // (NOPE + VD)
    m = q_ref.shape[0]
    pairs = near_ref.shape[0]
    keys = 2 * rows * pairs

    @pl.when(pl.program_id(0) == 0)
    def _():
        for i in range(pairs):
            lat_ref[:, 2 * i * rows : (2 * i + 1) * rows] = near_ref[i]
            lat_ref[:, (2 * i + 1) * rows : (2 * i + 2) * rows] = far_ref[i]

    ctx, core = ids_ref[0], ids_ref[1]
    span = keys // cuts
    lane = lax.broadcasted_iota(jnp.int32, (m, rows), 1)
    query = lax.broadcasted_iota(jnp.int32, (m, rows), 0) % rows
    ahead = lane - query
    peak = jnp.full((m, rows), -1e30, F32)
    for j in range(cuts):
        s = jnp.dot(q_ref[...], lat_ref[:, j * span : (j + 1) * span], preferred_element_type=F32)
        for b in range(span // rows):
            block = j * (span // rows) + b
            pos = 2 * (block // 2) + (core if block % 2 == 0 else 1 - core)
            part = s[:, b * rows : (b + 1) * rows]
            part = jnp.where(ahead <= (ctx - pos) * rows, part, F32(-1e30))
            peak = jnp.maximum(peak, part)
            s_ref[:, block * rows : (block + 1) * rows] = part
    top = jnp.max(peak, axis=1, keepdims=True)
    total = jnp.zeros((m, rows), F32)
    for j in range(keys // rows):
        p = jnp.exp2((s_ref[:, j * rows : (j + 1) * rows] - top) * (QK ** (-0.5) * LOG2E))
        total = total + p
        p_ref[:, j * rows : (j + 1) * rows] = p.astype(BF)
    mixed = lax.dot_general(p_ref[...], lat_ref[:KV_RANK], (((1,), (1,)), ((), ())), preferred_element_type=F32)
    mixed = (mixed / jnp.sum(total, axis=1, keepdims=True)).astype(BF)
    for h in range(heads):
        values = w_ref[:, h * (NOPE + VD) + NOPE : (h + 1) * (NOPE + VD)]
        o = jnp.dot(mixed[h * rows : (h + 1) * rows], values, preferred_element_type=F32)
        out_ref[:, h * VD : (h + 1) * VD] = o.astype(BF)


def attend(ids, q, near, far, w_kv, group, cuts):
    pairs, depth, rows = near.shape
    heads = w_kv.shape[1] // (NOPE + VD)
    keys = 2 * rows * pairs
    m = group * rows
    return pl.pallas_call(
        functools.partial(attend_kernel, rows=rows, cuts=cuts),
        grid=(heads // group,),
        in_specs=[
            pl.BlockSpec(memory_space=pltpu.SMEM),
            pl.BlockSpec((m, depth), lambda g: (g, 0)),
            pl.BlockSpec(near.shape, lambda g: (0, 0, 0)),
            pl.BlockSpec(far.shape, lambda g: (0, 0, 0)),
            pl.BlockSpec((KV_RANK, group * (NOPE + VD)), lambda g: (0, g)),
        ],
        out_specs=pl.BlockSpec((rows, group * VD), lambda g: (0, g)),
        out_shape=jax.ShapeDtypeStruct((rows, heads * VD), BF),
        scratch_shapes=[pltpu.VMEM((depth, keys), BF), pltpu.VMEM((m, keys), F32), pltpu.VMEM((m, keys), BF)],
        compiler_params=pltpu.CompilerParams(vmem_limit_bytes=40 * 2**20),
        cost_estimate=pl.CostEstimate(
            flops=2 * heads * rows * keys * (depth + KV_RANK),
            bytes_accessed=8_000_000,
            transcendentals=heads * rows * keys,
        ),
    )(ids, q, near, far, w_kv)


def expert_kernel(x_ref, g_ref, u_ref, d_ref, out_ref, rows_ref, hid_ref, *, first):
    step = pl.program_id(0)

    @pl.when(step == 0)
    def _():
        rows_ref[...] = x_ref[...].reshape(rows_ref.shape)

    @pl.when(step < first)
    def _():
        rows = rows_ref[...]
        gate = jnp.dot(rows, g_ref[...], preferred_element_type=F32)
        upward = jnp.dot(rows, u_ref[...], preferred_element_type=F32)
        hid = (gate / (1.0 + jnp.exp(-gate)) * upward).astype(BF)
        n = g_ref.shape[1]
        for f in range(first):

            @pl.when(step == f)
            def _(f=f):
                hid_ref[:, f * n : (f + 1) * n] = hid

    @pl.when(step >= first)
    def _():
        y = jnp.dot(hid_ref[...], d_ref[...], preferred_element_type=F32).astype(BF)
        out_ref[...] = y.reshape(out_ref.shape)


def expert(x, w_gate, w_up, w_down, first, last):
    units, pair, width = x.shape
    m = units * pair
    hidden = w_gate.shape[1]
    n1, n2 = hidden // first, width // last
    return pl.pallas_call(
        functools.partial(expert_kernel, first=first),
        grid=(first + last,),
        in_specs=[
            pl.BlockSpec(x.shape, lambda i: (0, 0, 0)),
            pl.BlockSpec((width, n1), lambda i: (0, jnp.minimum(i, first - 1))),
            pl.BlockSpec((width, n1), lambda i: (0, jnp.minimum(i, first - 1))),
            pl.BlockSpec((hidden, n2), lambda i: (0, jnp.maximum(i - first, 0))),
        ],
        out_specs=pl.BlockSpec((units, pair, n2), lambda i: (0, 0, jnp.maximum(i - first, 0))),
        out_shape=jax.ShapeDtypeStruct(x.shape, BF),
        scratch_shapes=[pltpu.VMEM((m, width), BF), pltpu.VMEM((m, hidden), BF)],
        compiler_params=pltpu.CompilerParams(vmem_limit_bytes=40 * 2**20),
        cost_estimate=pl.CostEstimate(
            flops=6 * m * width * hidden, bytes_accessed=17_000_000, transcendentals=m * hidden
        ),
    )(x, w_gate, w_up, w_down)


def dispatch_kernel(place_ref, x_ref, out_ref):
    y = jnp.dot(place_ref[...], x_ref[...], preferred_element_type=F32).astype(BF)
    out_ref[...] = y.reshape(out_ref.shape)


def dispatch(place, x, cuts):
    m = place.shape[0]
    tokens, width = x.shape
    n = width // cuts
    return pl.pallas_call(
        dispatch_kernel,
        grid=(cuts,),
        in_specs=[pl.BlockSpec(place.shape, lambda i: (0, 0)), pl.BlockSpec((tokens, n), lambda i: (0, i))],
        out_specs=pl.BlockSpec((m // 2, 2, n), lambda i: (0, 0, i)),
        out_shape=jax.ShapeDtypeStruct((m // 2, 2, width), BF),
        compiler_params=pltpu.CompilerParams(vmem_limit_bytes=32 * 2**20),
        cost_estimate=pl.CostEstimate(
            flops=2 * m * tokens * width, bytes_accessed=2 * m * width + 2 * tokens * width, transcendentals=0
        ),
    )(place, x)


def combine_kernel(factors_ref, x_ref, own_ref, far_ref):
    tok = own_ref.shape[0]
    rows = x_ref[...].reshape(factors_ref.shape[1], x_ref.shape[2])
    y = jnp.dot(factors_ref[...], rows, preferred_element_type=F32)
    y = y[: 2 * tok] + y[2 * tok :]
    own_ref[...] = y[:tok]
    far_ref[...] = y[tok:]


def combine(factors, x, cuts):
    width = x.shape[2]
    n = width // cuts
    tok = factors.shape[0] // 4
    part = pl.BlockSpec((tok, n), lambda i: (0, i))
    return pl.pallas_call(
        combine_kernel,
        grid=(cuts,),
        in_specs=[
            pl.BlockSpec(factors.shape, lambda i: (0, 0)),
            pl.BlockSpec((x.shape[0], 2, n), lambda i: (0, 0, i)),
        ],
        out_specs=(part, part),
        out_shape=(jax.ShapeDtypeStruct((tok, width), F32),) * 2,
        compiler_params=pltpu.CompilerParams(vmem_limit_bytes=32 * 2**20),
        cost_estimate=pl.CostEstimate(
            flops=2 * factors.size * width, bytes_accessed=4 * x.shape[0] * width, transcendentals=0
        ),
    )(factors, x)


def both_cores(mine):
    other = lax.ppermute(mine, "core", SWAP)
    first = lax.axis_index("core") == 0
    return jnp.stack([jnp.where(first, mine, other), jnp.where(first, other, mine)])


def latent_queries(queries, w_kv):
    rows = queries.shape[0]
    heads = queries.shape[1] // QK
    q = queries.reshape(rows, heads, QK)
    keys = w_kv.reshape(KV_RANK, heads, NOPE + VD)[:, :, :NOPE]
    q_lat = jnp.einsum("qhd,rhd->hqr", q[:, :, :NOPE], keys, preferred_element_type=F32).astype(BF)
    q_all = jnp.concatenate([q_lat, q[:, :, NOPE:].transpose(1, 0, 2)], axis=2)
    return q_all.reshape(heads * rows, -1)


def routing(routes, codes):
    tok = routes.shape[0]
    core = lax.axis_index("core")
    code_float = codes.astype(F32)
    mix = code_float / jnp.sum(code_float, axis=1, keepdims=True)
    routes2, mix2 = both_cores(routes), both_cores(mix)
    chosen = routes2[:, :, :, None] == jnp.arange(64, dtype=jnp.int32)
    weight = jnp.sum(jnp.where(chosen, mix2[..., None], F32(0.0)), axis=2)
    has = jnp.any(chosen, axis=2)

    def of_core(a):
        a = a.reshape(2, tok, 8, 2, 4)
        return jnp.where(core == 0, a[:, :, :, 0], a[:, :, :, 1]).reshape(2, tok, 32)

    weight, has = of_core(weight), of_core(has)
    count = has.astype(jnp.int32)
    slot = jnp.cumsum(count, axis=1) - count
    place = has[:, :, :, None] & (slot[:, :, :, None] == jnp.arange(CAP, dtype=jnp.int32))
    place = place.transpose(2, 3, 0, 1)[:, :, :, None, :]
    same = jnp.arange(2)[:, None, None] == jnp.arange(2)[None, :, None]
    place = (place & same).reshape(32, CAP, 2, 2 * tok)
    place = jnp.broadcast_to(place[:, None], (32, 2, CAP, 2, 2 * tok)).reshape(64 * CAP * 2, 2 * tok)
    gains = weight.transpose(2, 0, 1).reshape(32, 2 * tok)
    gains = jnp.broadcast_to(gains[:, None], (32, 2 * CAP * 2, 2 * tok)).reshape(64 * CAP * 2, 2 * tok)
    factors = jnp.where(place, gains, F32(0.0)).T.reshape(2, tok, -1)
    factors = jnp.where(core == 0, factors, factors[::-1]).reshape(2 * tok, -1)
    high = lax.reduce_precision(factors, 8, 7)
    factors = jnp.concatenate([high, factors - high], axis=0).astype(BF)
    return place.astype(BF), factors


def local(queries, latents, w_kv, w_out, resid, norm_gain, routes, codes, w_gate, w_up, w_down):
    tok, width = resid.shape
    chips = 64
    w_full = lax.all_gather(w_out, CTX, axis=0, tiled=True)
    near = lax.all_to_all(
        jnp.broadcast_to(latents[None], (8,) + latents.shape), CTX_CHIPS, split_axis=0, concat_axis=0, tiled=True
    )
    far = lax.ppermute(near, "core", SWAP)
    ids = jnp.stack([lax.axis_index(CTX), lax.axis_index("core")]).astype(jnp.int32)
    heads_out = attend(ids, latent_queries(queries, w_kv), near, far, w_kv, 4, 4)
    attn = jnp.dot(heads_out, w_full, preferred_element_type=F32).astype(BF)
    attn = lax.all_to_all(attn.reshape(8, tok, width), EP, split_axis=0, concat_axis=0, tiled=True)
    attended = (resid.astype(F32) + jnp.sum(attn.astype(F32), axis=0)).astype(BF)
    wide = attended.astype(F32)
    meansq = jnp.mean(wide * wide, axis=1, keepdims=True)
    normed = (wide * lax.rsqrt(meansq + 1e-06) * norm_gain[None, :]).astype(BF)
    normed2 = both_cores(normed).reshape(2 * tok, width)

    place, factors = routing(routes, codes)
    outgoing = dispatch(place, normed2, 7)
    arrived = lax.all_to_all(
        outgoing.reshape(chips, CAP, 2, width), CHIPS, split_axis=0, concat_axis=0, tiled=True
    ).reshape(chips * CAP, 2, width)
    produced = expert(arrived, w_gate[0], w_up[0], w_down[0], 2, 7)
    returned = lax.all_to_all(
        produced.reshape(chips, CAP, 2, width), CHIPS, split_axis=0, concat_axis=0, tiled=True
    ).reshape(chips * CAP, 2, width)
    own, theirs = combine(factors, returned, 7)
    layer_out = (wide + own + lax.ppermute(theirs, "core", SWAP)).astype(BF)
    return (attended, layer_out)


def solution(mesh):
    fine = Mesh(mesh.devices.reshape(SIZES), NAMES)
    rows = P(CTX + EP, None)
    heads = P(CTX + EP, None, None)
    placed = (
        P(CTX, EP),
        P(None, CTX),
        P(None, EP),
        P(EP + CTX, None),
        rows,
        P(),
        rows,
        rows,
        heads,
        heads,
        heads,
    )
    return jax.shard_map(local, mesh=fine, in_specs=placed, out_specs=(rows, rows), check_vma=False)
```

time: 249 us -> 210 us (0.84)
  matrix products: 35.4 us -> 6.97 us
  waiting for transfers between devices: 83.6 us -> 56 us
  blocking collectives: 41.6 us -> 66.8 us
  local copies, waits for them, and re-layouts: 35.7 us -> 11 us
  Pallas kernels: 0 us -> 24.2 us
  other arithmetic: 7.82 us -> 2.02 us
    all_to_all x1 -> x0, waiting for transfers between devices: 35.5 us -> none  [local(): lax.all_to_all(jnp.broadcast_to(latents[None], (parts,) + latents.shape),...]
    dot_general x7 -> x1, matrix products: 30.2 us -> 1.82 us  [latent_queries(): jnp.einsum('qhd,rhd->hqr', q[:, :, :NOPE], keys, preferred_element_type=F32)]
    all_to_all x0 -> x1, blocking collectives: none -> 25.5 us  [local(): lax.all_to_all(jnp.broadcast_to(latents[None], (8,) + latents.shape), CTX...]
    pallas_call x0 -> x4, Pallas kernels: none -> 24.2 us  [the longest x1 10 us: expert(): pl.pallas_call(functools.partial(expert_kernel, first=first), grid=(first...]
    reshape x9 -> x2, local copies, waits for them, and re-layouts: 16.9 us -> 0.14 us  [the longest x1 0.12 us: routing(): jnp.broadcast_to(place[:, None], (32, 2, CAP, 2, 2 * tok))]
    all_gather x1, waiting for transfers between devices: 0.02 us -> 7.59 us  [local(): w_full = lax.all_gather(w_out, CTX, axis=0, tiled=True)]
    all_to_all x1 -> x0, starting transfers between devices: 7.3 us -> none  [local(): lax.all_to_all(jnp.broadcast_to(latents[None], (parts,) + latents.shape),...]
    slice x4 -> x1, local copies, waits for them, and re-layouts: 7.09 us -> 1.57 us  [latent_queries(): q_all = jnp.concatenate([q_lat, q[:, :, NOPE:].transpose(1, 0, 2)], axis=2)]
  transfers between devices with their start and end apart: 8 -> 8, of which waited for: 6 -> 6; matrix products, arithmetic and copies ran while one was open for 19% -> 8% of each run, Pallas kernels for 0% -> 5%
where the time goes in v2:
time: 210 us; the launch traced here: 208 us
  blocking collectives  66.8 us (32%)
  waiting for transfers between devices  56 us (27%)
  starting transfers between devices  26.4 us (13%)
  Pallas kernels  24.2 us (12%)
  between operations  14.4 us (7%)
  local copies, waits for them, and re-layouts  11 us (5%)
  matrix products  6.97 us (3%)
    all_to_all x1, blocking collectives, local(): lax.all_to_all(outgoing.reshape(chips, CAP, 2, width), CHIPS, split_axis=...  41.3 us
    all_to_all x1, waiting for transfers between devices, local(): lax.all_to_all(produced.reshape(chips, CAP, 2, width), CHIPS, split_axis=...  30 us
    all_to_all x1, blocking collectives, local(): lax.all_to_all(jnp.broadcast_to(latents[None], (8,) + latents.shape), CTX...  25.5 us
    all_to_all x1, waiting for transfers between devices, local(): lax.all_to_all(attn.reshape(8, tok, width), EP, split_axis=0, concat_axis...  15.4 us
    pallas_call x1, Pallas kernels, expert(): pl.pallas_call(functools.partial(expert_kernel, first=first), grid=(first...  10 us
    pallas_call x1, Pallas kernels, attend(): pl.pallas_call(functools.partial(attend_kernel, rows=rows, cuts=cuts), gr...  9.98 us
    all_gather x1, waiting for transfers between devices, local(): w_full = lax.all_gather(w_out, CTX, axis=0, tiled=True)  7.59 us
    all_to_all x1, starting transfers between devices, local(): lax.all_to_all(produced.reshape(chips, CAP, 2, width), CHIPS, split_axis=...  7.48 us
  transfers between devices with their start and end apart: 8, of which 6 were waited for; matrix products, arithmetic and copies ran while one was open for 8% of the time, Pallas kernels for 5%

profile of v2, /device:TPU:1, one launch (start us, length us, event | category | flops | bytes accessed | tf_op | source)
XLA Modules:
  0.0 207.8 jit_solution(12826245909515847933)
XLA Ops:
  7.2 0.0 copy-start.8
  7.2 0.0 copy-start.3
  7.2 0.0 all-gather.2.cloned.1.call-start
  7.2 0.7 all-gather.2.cloned.1.call-update
  7.9 1.1 broadcast_in_dim.23
  9.0 25.5 %all_to_all.20.near_ref = bf16[8,576,128]{2,1,0:T(8,128)(2,1)S(1)} all-to-all(bf16[8,576,128]{2,1,0:T(8,128)(2,1)S(1)} %broadcast_in_dim.23), channel_id=1, replica_groups=mesh['z_lo'=2,'x'=4,'core'=2,'z_hi'=2,'y'=4] {'z_lo','x'}, dimensions={0} | all-to-all | bytes 2359296 | tf_op jit(solution)/shard_map/all_to_all | solution.py:250
  34.5 5.4 %collective-permute-start = (bf16[8,576,128]{2,1,0:T(8,128)(2,1)S(1)}, bf16[8,576,128]{2,1,0:T(8,128)(2,1)}, u32[]{:S(2)}, u32[]{:S(2)}) collective-permute-start(bf16[8,576,128]{2,1,0:T(8,128)(2,1)S(1)} %all_to_all.20.near_ref), channel_id=1, source_target_pairs={{0,8},{8,0},{1,9},{9,1},{2,10},{10,2},{3,11},{11,3},{4,12},{12,4},... | collective-permute-start | bytes 3538952 | tf_op jit(solution)/shard_map/ppermute | solution.py:253
  39.9 0.0 collective-permute-start.1
  39.9 1.9 copy.33
  41.8 0.0 copy-done.3
  41.8 2.5 %copy.35 = bf16[512,2048]{0,1:T(8,128)(2,1)} copy(bf16[512,2048]{1,0:T(8,128)(2,1)S(1)} %copy-done.3) | data formatting | bytes 4194304 | tf_op args[2]
  44.3 1.6 slice.30
  45.9 1.1 copy.50
  47.0 0.1 and.46
  47.1 0.1 and.47
  47.2 0.1 pad_add_fusion.1.ids_ref
  47.2 1.8 convolution_convert_fusion.1
  49.1 0.1 pad_maximum_fusion
  49.2 0.0 collective-permute-done.far_ref
  49.2 10.0 %shard_map.122 = bf16[128,1024]{1,0:T(8,128)(2,1)S(1)} custom-call(s32[2]{0:T(128)S(1)} %pad_add_fusion.1.ids_ref, bf16[1024,576]{1,0:T(8,128)(2,1)S(1)} %bitcast.54, bf16[8,576,128]{2,1,0:T(8,128)(2,1)S(1)} %all_to_all.20.near_ref, bf16[8,576,128]{2,1,0:T(8,128)(2,1)} %collective-permute-done.far_ref, bf16[512,2048]{1,0:T(8,128)(2,1)S(1)} %copy-done.3), custom_call_target="tpu_custom_call" | custom-call | flops 4563402752 | bytes 8000000 | tf_op jit(solution)/shard_map/pallas_call | solution.py:75
  59.2 7.6 %all-gather.2.cloned.1.call-done = bf16[1024,3584]{1,0:T(8,128)(2,1)} async-done(((bf16[64,3584]{1,0:T(8,128)(2,1)}), bf16[1024,3584]{1,0:T(8,128)(2,1)}) %all-gather.2.cloned.1.call-update) | async-done | bytes 7340048 | tf_op jit(solution)/shard_map/all_gather | solution.py:249
  66.8 5.2 %convolution_convert_fusion = bf16[128,3584]{1,0:T(8,128)(2,1)} fusion(bf16[128,1024]{1,0:T(8,128)(2,1)S(1)} %shard_map.122, bf16[1024,3584]{1,0:T(8,128)(2,1)} %all-gather.2.cloned.1.call-done), kind=kOutput, calls=%fused_computation | convolution fusion | flops 939982848 | bytes 8519680 | tf_op jit(solution)/shard_map/dot_general | solution.py:256
  71.9 7.3 %all-to-all-start.1 = ((bf16[8,16,3584]{2,1,0:T(8,128)(2,1)}), bf16[8,16,3584]{2,1,0:T(8,128)(2,1)S(1)}, u32[]{:S(2)}, u32[]{:S(2)}) async-start(bf16[8,16,3584]{2,1,0:T(8,128)(2,1)} %bitcast.6), calls=%async_computation.1 | async-start | bytes 1835008 | tf_op jit(solution)/shard_map/all_to_all | solution.py:257
  79.3 0.0 collective-permute-done.1
  79.3 0.1 copy.38
  79.4 0.1 fusion.7
  79.5 0.1 copy.39
  79.7 0.1 copy.41
  79.8 0.1 copy.40
  79.9 15.4 %all-to-all-done.1 = bf16[8,16,3584]{2,1,0:T(8,128)(2,1)S(1)} async-done(((bf16[8,16,3584]{2,1,0:T(8,128)(2,1)}), bf16[8,16,3584]{2,1,0:T(8,128)(2,1)S(1)}, u32[]{:S(2)}, u32[]{:S(2)}) %all-to-all-start.1) | async-done | bytes 917536 | tf_op jit(solution)/shard_map/all_to_all | solution.py:257
  95.3 0.1 convert_reduce_fusion
  95.4 0.0 copy-done.5
  95.4 0.2 fusion.2
  95.6 0.0 copy-done.6
  95.6 0.1 fusion.4
  95.7 0.9 collective-permute-start.3
  96.6 0.1 bitcast_and_fusion
  96.7 0.1 copy.42
  96.8 0.1 broadcast_in_dim.24
  96.9 0.1 reshape.145
  97.1 0.5 collective-permute-done.3
  97.5 0.1 select_bitcast_fusion.2
  97.7 0.0 copy-start.2
  97.7 2.2 %shard_map.123 = bf16[192,2,3584]{2,1,0:T(2,128)(2,1)S(1)} custom-call(bf16[384,32]{1,0:T(8,128)(2,1)S(1)} %convert_element_type.50.place_ref, bf16[32,3584]{1,0:T(8,128)(2,1)S(1)} %bitcast.55), custom_call_target="tpu_custom_call" | custom-call | flops 88080384 | bytes 2981888 | tf_op jit(solution)/shard_map/pallas_call | solution.py:156
  100.0 0.0 copy-start.1
  100.0 41.3 %all_to_all.21 = bf16[64,3,2,3584]{3,2,1,0:T(2,128)(2,1)S(1)} all-to-all(bf16[64,3,2,3584]{3,2,1,0:T(2,128)(2,1)S(1)} %bitcast.49), channel_id=1, replica_groups=mesh['z_lo'=2,'x'=4,'core'=2,'z_hi'=2,'y'=4] {'z_lo','x','z_hi','y'}, dimensions={0} | all-to-all | bytes 5505024 | tf_op jit(solution)/shard_map/all_to_all | solution.py:266
  141.3 10.0 %shard_map.124 = bf16[192,2,3584]{2,1,0:T(2,128)(2,1)S(1)} custom-call(bf16[192,2,3584]{2,1,0:T(2,128)(2,1)S(1)} %bitcast.51, bf16[3584,512]{1,0:T(8,128)(2,1)S(1)} %bitcast.52, bf16[3584,512]{1,0:T(8,128)(2,1)S(1)} %bitcast.53, bf16[512,3584]{1,0:T(8,128)(2,1)} %bitcast.57), custom_call_target="tpu_custom_call" | custom-call | flops 4227858432 | bytes 17000000 | tf_op jit(solution)/shard_map/pallas_call | solution.py:128
  151.3 0.0 copy-start
  151.3 1.5 copy-done
  152.8 7.5 %all-to-all-start.3 = ((bf16[64,3,2,3584]{3,2,1,0:T(2,128)(2,1)}), bf16[64,3,2,3584]{3,2,1,0:T(2,128)(2,1)S(1)}, u32[]{:S(2)}, u32[]{:S(2)}) async-start(bf16[64,3,2,3584]{3,2,1,0:T(2,128)(2,1)} %bitcast.50), calls=%async_computation.3 | async-start | bytes 5505024 | tf_op jit(solution)/shard_map/all_to_all | solution.py:270
  160.3 1.6 collective-permute-start.2
  161.9 0.8 collective-permute-done.2
  162.7 0.1 copy.43
  162.8 0.1 select_reduce_fusion
  163.0 0.1 copy.44
  163.1 0.1 copy.45
  163.1 0.1 copy.46
  163.3 0.1 copy.47
  163.5 30.0 %all-to-all-done.3 = bf16[64,3,2,3584]{3,2,1,0:T(2,128)(2,1)S(1)} async-done(((bf16[64,3,2,3584]{3,2,1,0:T(2,128)(2,1)}), bf16[64,3,2,3584]{3,2,1,0:T(2,128)(2,1)S(1)}, u32[]{:S(2)}, u32[]{:S(2)}) %all-to-all-start.3) | async-done | bytes 2752544 | tf_op jit(solution)/shard_map/all_to_all | solution.py:270
  193.4 1.9 shard_map.125
  195.4 3.8 %collective-permute-start.4 = (f32[16,3584]{1,0:T(8,128)S(1)}, f32[16,3584]{1,0:T(8,128)S(1)}, u32[]{:S(2)}, u32[]{:S(2)}) collective-permute-start(f32[16,3584]{1,0:T(8,128)S(1)} %get-tuple-element.5), channel_id=1, source_target_pairs={{0,8},{8,0},{1,9},{9,1},{2,10},{10,2},{3,11},{11,3},{4,12},{12,4},... | collective-permute-start | bytes 688136 | tf_op jit(solution)/shard_map/ppermute | solution.py:274
  199.1 1.1 collective-permute-done.4
  200.3 0.0 copy-done.4
  200.3 0.7 fusion.6
  (30 shorter events, 0.3 us)
Async XLA Ops:
  7.2 32.7 %copy-start.8 = (s32[16,8]{0,1:T(8,128)S(1)}, s32[16,8]{0,1:T(8,128)}, u32[]{:S(2)}) copy-start(s32[16,8]{0,1:T(8,128)} %param.17) | copy-start | bytes 1540
  7.2 34.6 %copy-start.3 = (bf16[512,2048]{1,0:T(8,128)(2,1)S(1)}, bf16[512,2048]{1,0:T(8,128)(2,1)}, u32[]{:S(2)}) copy-start(bf16[512,2048]{1,0:T(8,128)(2,1)} %w_ref.1) | copy-start | bytes 6291460
  7.2 59.6 %all-gather.2.cloned.1.call-start = ((), (), s32[]{:S(2)}) async-start(), calls=%async_computation.4 | async-start | bytes 7798784 | tf_op jit(solution)/shard_map/all_gather | solution.py:249
  34.5 14.7 %collective-permute-start = (bf16[8,576,128]{2,1,0:T(8,128)(2,1)S(1)}, bf16[8,576,128]{2,1,0:T(8,128)(2,1)}, u32[]{:S(2)}, u32[]{:S(2)}) collective-permute-start(bf16[8,576,128]{2,1,0:T(8,128)(2,1)S(1)} %all_to_all.20.near_ref), channel_id=1, source_target_pairs={{0,8},{8,0},{1,9},{9,1},{2,10},{10,2},{3,11},{11,3},{4,12},{12,4},... | collective-permute-start | bytes 3538952 | tf_op jit(solution)/shard_map/ppermute | solution.py:253
  39.9 39.4 %collective-permute-start.1 = (s32[16,8]{0,1:T(8,128)S(1)}, s32[16,8]{0,1:T(8,128)S(1)}, u32[]{:S(2)}, u32[]{:S(2)}) collective-permute-start(s32[16,8]{0,1:T(8,128)S(1)} %copy-done.8), channel_id=1, source_target_pairs={{0,8},{8,0},{1,9},{9,1},{2,10},{10,2},{3,11},{11,3},{4,12},{12,4},... | collective-permute-start | bytes 1544 | tf_op jit(solution)/shard_map/ppermute | solution.py:200
  71.9 23.5 %copy-start.5 = (bf16[16,3584]{1,0:T(8,128)(2,1)S(1)}, bf16[16,3584]{1,0:T(8,128)(2,1)}, u32[]{:S(2)}) copy-start(bf16[16,3584]{1,0:T(8,128)(2,1)} %param.15) | copy-start | bytes 344068
  71.9 23.6 %copy-start.6 = (f32[3584]{0:T(1024)S(1)}, f32[3584]{0:T(1024)}, u32[]{:S(2)}) copy-start(f32[3584]{0:T(1024)} %param.16) | copy-start | bytes 43012
  71.9 23.3 %all-to-all-start.1 = ((bf16[8,16,3584]{2,1,0:T(8,128)(2,1)}), bf16[8,16,3584]{2,1,0:T(8,128)(2,1)S(1)}, u32[]{:S(2)}, u32[]{:S(2)}) async-start(bf16[8,16,3584]{2,1,0:T(8,128)(2,1)} %bitcast.6), calls=%async_computation.1 | async-start | bytes 1835008 | tf_op jit(solution)/shard_map/all_to_all | solution.py:257
  95.6 104.7 %copy-start.4 = (bf16[16,3584]{1,0:T(8,128)(2,1)}, bf16[16,3584]{1,0:T(8,128)(2,1)S(1)}, u32[]{:S(2)}) copy-start(bf16[16,3584]{1,0:T(8,128)(2,1)S(1)} %get-tuple-element.7) | copy-start | bytes 344068
  95.7 1.8 collective-permute-start.3
  97.7 43.6 %copy-start.2 = (bf16[1,3584,512]{2,1,0:T(8,128)(2,1)S(1)}, bf16[1,3584,512]{2,1,0:T(8,128)(2,1)}, u32[]{:S(2)}) copy-start(bf16[1,3584,512]{2,1,0:T(8,128)(2,1)} %param.20) | copy-start | bytes 11010052
  100.0 41.3 %copy-start.1 = (bf16[1,3584,512]{2,1,0:T(8,128)(2,1)S(1)}, bf16[1,3584,512]{2,1,0:T(8,128)(2,1)}, u32[]{:S(2)}) copy-start(bf16[1,3584,512]{2,1,0:T(8,128)(2,1)} %param.19) | copy-start | bytes 11010052
  151.3 1.5 copy-start
  152.8 7.5 %copy-start.7 = (s32[16,8]{0,1:T(8,128)S(1)}, s32[16,8]{0,1:T(8,128)}, u32[]{:S(2)}) copy-start(s32[16,8]{0,1:T(8,128)} %param.18) | copy-start | bytes 1540
  152.8 40.6 %all-to-all-start.3 = ((bf16[64,3,2,3584]{3,2,1,0:T(2,128)(2,1)}), bf16[64,3,2,3584]{3,2,1,0:T(2,128)(2,1)S(1)}, u32[]{:S(2)}, u32[]{:S(2)}) async-start(bf16[64,3,2,3584]{3,2,1,0:T(2,128)(2,1)} %bitcast.50), calls=%async_computation.3 | async-start | bytes 5505024 | tf_op jit(solution)/shard_map/all_to_all | solution.py:270
  160.3 2.4 %collective-permute-start.2 = (f32[16,8]{0,1:T(8,128)S(1)}, f32[16,8]{0,1:T(8,128)S(1)}, u32[]{:S(2)}, u32[]{:S(2)}) collective-permute-start(f32[16,8]{0,1:T(8,128)S(1)} %convert_divide_fusion), channel_id=1, source_target_pairs={{0,8},{8,0},{1,9},{9,1},{2,10},{10,2},{3,11},{11,3},{4,12},{12,4},... | collective-permute-start | bytes 1544 | tf_op jit(solution)/shard_map/ppermute | solution.py:200
  195.4 4.9 %collective-permute-start.4 = (f32[16,3584]{1,0:T(8,128)S(1)}, f32[16,3584]{1,0:T(8,128)S(1)}, u32[]{:S(2)}, u32[]{:S(2)}) collective-permute-start(f32[16,3584]{1,0:T(8,128)S(1)} %get-tuple-element.5), channel_id=1, source_target_pairs={{0,8},{8,0},{1,9},{9,1},{2,10},{10,2},{3,11},{11,3},{4,12},{12,4},... | collective-permute-start | bytes 688136 | tf_op jit(solution)/shard_map/ppermute | solution.py:274
Sparse Core Ops, SparseCore 0:
  9.7 57.0 all-gather.1

commit v3 on v2

--- a/solution.py
+++ b/solution.py
@@ -196,10 +196,67 @@
     )(factors, x)
 
 
-def both_cores(mine):
-    other = lax.ppermute(mine, "core", SWAP)
-    first = lax.axis_index("core") == 0
-    return jnp.stack([jnp.where(first, mine, other), jnp.where(first, other, mine)])
+def project_kernel(order_ref, own_ref, far_ref, *refs):
+    *chunk_refs, left_ref, right_ref, out_ref, x_ref, w_ref = refs
+    rows = own_ref.shape[0]
+    parts = out_ref.shape[0]
+    tok = rows // parts
+    for i in range(len(chunk_refs) + 1):
+        columns = pl.ds(pl.multiple_of(order_ref[i] * VD, VD), VD)
+        x_ref[:rows, i * VD : (i + 1) * VD] = own_ref[:, columns]
+        x_ref[rows:, i * VD : (i + 1) * VD] = far_ref[:, columns]
+    for i, ref in enumerate(chunk_refs):
+        w_ref[i * VD : (i + 1) * VD] = ref[...]
+    half = left_ref.shape[1]
+    w_ref[len(chunk_refs) * VD :, :half] = left_ref[...]
+    w_ref[len(chunk_refs) * VD :, half:] = right_ref[...]
+    n = 256
+    for c in range(0, w_ref.shape[1], n):
+        y = jnp.dot(x_ref[...], w_ref[:, c : c + n], preferred_element_type=F32).astype(BF)
+        for e in range(parts):
+            out_ref[e, 0, :, c : c + n] = y[e * tok : (e + 1) * tok]
+            out_ref[e, 1, :, c : c + n] = y[rows + e * tok : rows + (e + 1) * tok]
+
+
+def project(order, own, far, chunks, parts):
+    rows, depth = own.shape
+    width = chunks[0].shape[1]
+    whole = pl.BlockSpec(memory_space=pltpu.VMEM)
+    return pl.pallas_call(
+        project_kernel,
+        in_specs=[pl.BlockSpec(memory_space=pltpu.SMEM)] + [whole] * (2 + len(chunks)),
+        out_specs=whole,
+        out_shape=jax.ShapeDtypeStruct((parts, 2, rows // parts, width), BF),
+        scratch_shapes=[pltpu.VMEM((2 * rows, depth), BF), pltpu.VMEM((depth, width), BF)],
+        compiler_params=pltpu.CompilerParams(vmem_limit_bytes=32 * 2**20),
+        cost_estimate=pl.CostEstimate(
+            flops=4 * rows * depth * width, bytes_accessed=2 * depth * width, transcendentals=0
+        ),
+    )(order, own, far, *chunks)
+
+
+def swap(mine):
+    return lax.ppermute(mine, "core", SWAP)
+
+
+def gather_w_out(w_out):
+    core, x, z = (lax.axis_index(n) for n in ("core", "x", "z_lo"))
+    half = w_out.shape[1] // 2
+    lower, upper = w_out[:, :half], w_out[:, half:]
+    mine = jnp.where(core == 0, lower, upper)
+    other = swap(jnp.where(core == 0, upper, lower))
+    own = jnp.concatenate([jnp.where(core == 0, mine, other), jnp.where(core == 0, other, mine)], axis=0)
+    up = lambda a: lax.ppermute(a, "x", [(i, (i + 1) % 4) for i in range(4)])
+    down = lambda a: lax.ppermute(a, "x", [(i, (i + 3) % 4) for i in range(4)])
+    across = lambda a: lax.ppermute(a, "z_lo", SWAP)
+    mate, before, after = across(own), up(own), down(own)
+    mate_before, mate_after, opposite = up(mate), across(after), down(after)
+    part = half // 2
+    left, right = up(mate_before[:, :part]), down(mate_after[:, part:])
+    chunks = (own, mate, before, after, mate_before, mate_after, opposite, left, right)
+    chip = lambda zz, dx: zz * 4 + lax.rem(x + 4 + dx, 4)
+    order = (chip(z, 0), chip(1 - z, 0), chip(z, -1), chip(z, 1), chip(1 - z, -1), chip(1 - z, 1), chip(z, 2), chip(1 - z, 2))
+    return jnp.stack(order).astype(jnp.int32), chunks
 
 
 def latent_queries(queries, w_kv):
@@ -217,7 +274,7 @@
     core = lax.axis_index("core")
     code_float = codes.astype(F32)
     mix = code_float / jnp.sum(code_float, axis=1, keepdims=True)
-    routes2, mix2 = both_cores(routes), both_cores(mix)
+    routes2, mix2 = jnp.stack([routes, swap(routes)]), jnp.stack([mix, swap(mix)])
     chosen = routes2[:, :, :, None] == jnp.arange(64, dtype=jnp.int32)
     weight = jnp.sum(jnp.where(chosen, mix2[..., None], F32(0.0)), axis=2)
     has = jnp.any(chosen, axis=2)
@@ -236,8 +293,7 @@
     place = jnp.broadcast_to(place[:, None], (32, 2, CAP, 2, 2 * tok)).reshape(64 * CAP * 2, 2 * tok)
     gains = weight.transpose(2, 0, 1).reshape(32, 2 * tok)
     gains = jnp.broadcast_to(gains[:, None], (32, 2 * CAP * 2, 2 * tok)).reshape(64 * CAP * 2, 2 * tok)
-    factors = jnp.where(place, gains, F32(0.0)).T.reshape(2, tok, -1)
-    factors = jnp.where(core == 0, factors, factors[::-1]).reshape(2 * tok, -1)
+    factors = jnp.where(place, gains, F32(0.0)).T
     high = lax.reduce_precision(factors, 8, 7)
     factors = jnp.concatenate([high, factors - high], axis=0).astype(BF)
     return place.astype(BF), factors
@@ -246,20 +302,28 @@
 def local(queries, latents, w_kv, w_out, resid, norm_gain, routes, codes, w_gate, w_up, w_down):
     tok, width = resid.shape
     chips = 64
-    w_full = lax.all_gather(w_out, CTX, axis=0, tiled=True)
+    core = lax.axis_index("core")
+    order, chunks = gather_w_out(w_out)
     near = lax.all_to_all(
         jnp.broadcast_to(latents[None], (8,) + latents.shape), CTX_CHIPS, split_axis=0, concat_axis=0, tiled=True
     )
-    far = lax.ppermute(near, "core", SWAP)
-    ids = jnp.stack([lax.axis_index(CTX), lax.axis_index("core")]).astype(jnp.int32)
+    far = swap(near)
+    ids = jnp.stack([lax.axis_index(CTX), core]).astype(jnp.int32)
     heads_out = attend(ids, latent_queries(queries, w_kv), near, far, w_kv, 4, 4)
-    attn = jnp.dot(heads_out, w_full, preferred_element_type=F32).astype(BF)
-    attn = lax.all_to_all(attn.reshape(8, tok, width), EP, split_axis=0, concat_axis=0, tiled=True)
-    attended = (resid.astype(F32) + jnp.sum(attn.astype(F32), axis=0)).astype(BF)
-    wide = attended.astype(F32)
-    meansq = jnp.mean(wide * wide, axis=1, keepdims=True)
-    normed = (wide * lax.rsqrt(meansq + 1e-06) * norm_gain[None, :]).astype(BF)
-    normed2 = both_cores(normed).reshape(2 * tok, width)
+    half = width // 2
+    lower, upper = resid[:, :half], resid[:, half:]
+    resid2 = jnp.stack([jnp.where(core == 0, lower, upper), swap(jnp.where(core == 0, upper, lower))])
+    attn = project(order, heads_out, swap(heads_out), chunks, 8)
+    attn = lax.all_to_all(attn, EP, split_axis=0, concat_axis=0, tiled=True)
+    summed = (resid2.astype(F32) + jnp.sum(attn.astype(F32), axis=0)).astype(BF)
+    others = swap(summed)[::-1]
+    attended2 = jnp.concatenate(
+        [jnp.where(core == 0, summed, others), jnp.where(core == 0, others, summed)], axis=2
+    ).reshape(2 * tok, width)
+    attended = attended2[:tok]
+    wide2 = attended2.astype(F32)
+    meansq = jnp.mean(wide2 * wide2, axis=1, keepdims=True)
+    normed2 = (wide2 * lax.rsqrt(meansq + 1e-06) * norm_gain[None, :]).astype(BF)
 
     place, factors = routing(routes, codes)
     outgoing = dispatch(place, normed2, 7)
@@ -271,7 +335,7 @@
         produced.reshape(chips, CAP, 2, width), CHIPS, split_axis=0, concat_axis=0, tiled=True
     ).reshape(chips * CAP, 2, width)
     own, theirs = combine(factors, returned, 7)
-    layer_out = (wide + own + lax.ppermute(theirs, "core", SWAP)).astype(BF)
+    layer_out = (wide2[:tok] + own + swap(theirs)).astype(BF)
     return (attended, layer_out)
 
 

time: 210 us -> 199 us (0.948)
  blocking collectives: 66.8 us -> 41.5 us
  starting transfers between devices: 26.4 us -> 41.6 us
  between operations: 14.4 us -> 1 us
  waiting for transfers between devices: 56 us -> 67.5 us
  matrix products: 6.97 us -> 1.71 us
  Pallas kernels: 24.2 us -> 28.7 us
    all_to_all x1 -> x0, blocking collectives: 25.5 us -> none  [local(): lax.all_to_all(jnp.broadcast_to(latents[None], (8,) + latents.shape), CTX...]
    all_to_all x1 -> x2, waiting for transfers between devices: 15.4 us -> 27.4 us  [the longest x1 16.2 us: local(): lax.all_to_all(jnp.broadcast_to(latents[None], (8,) + latents.shape), CTX...]
    ppermute x5 -> x16, waiting for transfers between devices: 2.41 us -> 13.4 us  [the longest x3 5.51 us: gather_w_out(): down = lambda a: lax.ppermute(a, 'x', [(i, (i + 3) % 4) for i in range(4)])]
    ppermute x5 -> x16, starting transfers between devices: 11.6 us -> 20.6 us  [the longest x8 13.3 us: swap(): return lax.ppermute(mine, 'core', SWAP)]
    all_gather x1 -> x0, waiting for transfers between devices: 7.59 us -> none  [local(): w_full = lax.all_gather(w_out, CTX, axis=0, tiled=True)]
    all_to_all x1 -> x2, starting transfers between devices: 7.35 us -> 13.5 us  [the longest x1 7.21 us: local(): attn = lax.all_to_all(attn, EP, split_axis=0, concat_axis=0, tiled=True)]
    dot_general x1 -> x0, matrix products: 5.16 us -> none  [local(): attn = jnp.dot(heads_out, w_full, preferred_element_type=F32).astype(BF)]
    pallas_call x0 -> x1, Pallas kernels: none -> 3.65 us  [project(): pl.pallas_call(project_kernel, in_specs=[pl.BlockSpec(memory_space=pltpu....]
  transfers between devices with their start and end apart: 8 -> 19, of which waited for: 6 -> 10; matrix products, arithmetic and copies ran while one was open for 8% -> 6% of each run, Pallas kernels for 5% -> 6%
where the time goes in v3:
time: 199 us; the launch traced here: 197 us
  waiting for transfers between devices  67.5 us (34%)
  starting transfers between devices  41.6 us (21%)
  blocking collectives  41.5 us (21%)
  Pallas kernels  28.7 us (14%)
  local copies, waits for them, and re-layouts  11.6 us (6%)
  other arithmetic  3.64 us (2%)
    all_to_all x1, blocking collectives, local(): lax.all_to_all(outgoing.reshape(chips, CAP, 2, width), CHIPS, split_axis=...  41.5 us
    all_to_all x1, waiting for transfers between devices, local(): lax.all_to_all(produced.reshape(chips, CAP, 2, width), CHIPS, split_axis=...  26.8 us
    all_to_all x1, waiting for transfers between devices, local(): lax.all_to_all(jnp.broadcast_to(latents[None], (8,) + latents.shape), CTX...  16.2 us
    ppermute x8, starting transfers between devices, swap(): return lax.ppermute(mine, 'core', SWAP)  13.3 us
    all_to_all x1, waiting for transfers between devices, local(): attn = lax.all_to_all(attn, EP, split_axis=0, concat_axis=0, tiled=True)  11.2 us
    pallas_call x1, Pallas kernels, attend(): pl.pallas_call(functools.partial(attend_kernel, rows=rows, cuts=cuts), gr...  10.9 us
    pallas_call x1, Pallas kernels, expert(): pl.pallas_call(functools.partial(expert_kernel, first=first), grid=(first...  10 us
    all_to_all x1, starting transfers between devices, local(): lax.all_to_all(produced.reshape(chips, CAP, 2, width), CHIPS, split_axis=...  7.48 us
  transfers between devices with their start and end apart: 19, of which 10 were waited for; matrix products, arithmetic and copies ran while one was open for 6% of the time, Pallas kernels for 6%

profile of v3, /device:TPU:1, one launch (start us, length us, event | category | flops | bytes accessed | tf_op | source)
XLA Modules:
  0.0 197.3 jit_solution(15566891878581662386)
XLA Ops:
  0.6 2.2 %broadcast_in_dim.23 = bf16[8,576,128]{2,1,0:T(8,128)(2,1)} broadcast(bf16[576,128]{1,0:T(8,128)(2,1)} %param.12), dimensions={1,2} | broadcast | bytes 1327104 | tf_op jit(solution)/shard_map/broadcast_in_dim | solution.py:308
  2.8 6.3 %all-to-all-start = ((bf16[8,576,128]{2,1,0:T(8,128)(2,1)}), bf16[8,576,128]{2,1,0:T(8,128)(2,1)}, u32[]{:S(2)}, u32[]{:S(2)}) async-start(bf16[8,576,128]{2,1,0:T(8,128)(2,1)} %broadcast_in_dim.23), calls=%async_computation | async-start | bytes 2359296 | tf_op jit(solution)/shard_map/all_to_all | solution.py:307
  9.2 1.0 collective-permute-start.3
  10.2 16.2 %all-to-all-done.near_ref = bf16[8,576,128]{2,1,0:T(8,128)(2,1)} async-done(((bf16[8,576,128]{2,1,0:T(8,128)(2,1)}), bf16[8,576,128]{2,1,0:T(8,128)(2,1)}, u32[]{:S(2)}, u32[]{:S(2)}) %all-to-all-start) | async-done | bytes 1179680 | tf_op jit(solution)/shard_map/all_to_all | solution.py:307
  26.5 0.8 collective-permute-start.1
  27.3 1.0 broadcast_select_fusion.1
  28.3 0.4 collective-permute-start.4
  28.7 1.2 collective-permute-start.6
  30.0 0.2 copy.45
  30.2 0.2 copy.63
  30.4 2.5 %copy.47 = bf16[512,2048]{0,1:T(8,128)(2,1)} copy(bf16[512,2048]{1,0:T(8,128)(2,1)S(1)} %copy-done.3) | data formatting | bytes 4194304 | tf_op args[2]
  32.9 1.7 convolution_convert_fusion
  34.7 0.1 pad_maximum_fusion
  34.8 0.4 collective-permute-start.5
  35.1 5.5 %collective-permute-done.6.refs_3_ = bf16[128,1792]{1,0:T(8,128)(2,1)} collective-permute-done((bf16[128,1792]{1,0:T(8,128)(2,1)S(1)}, bf16[128,1792]{1,0:T(8,128)(2,1)}, u32[]{:S(2)}, u32[]{:S(2)}) %collective-permute-start.6) | collective-permute-done | bytes 458784 | tf_op jit(solution)/shard_map/ppermute | solution.py:250
  40.6 1.2 collective-permute-start.8
  41.8 1.5 collective-permute-start.9
  43.3 10.9 %shard_map.122.own_ref = bf16[128,1024]{1,0:T(8,128)(2,1)} custom-call(s32[2]{0:T(128)S(1)} %pad_add_fusion.1.ids_ref, bf16[1024,576]{1,0:T(8,128)(2,1)S(1)} %bitcast.67, bf16[8,576,128]{2,1,0:T(8,128)(2,1)} %all-to-all-done.near_ref, bf16[8,576,128]{2,1,0:T(8,128)(2,1)} %collective-permute-done.1.far_ref, bf16[512,2048]{1,0:T(8,128)(2,1)S(1)} %copy-done.3), custom_call_target="tpu_custom_call" | custom-call | flops 4563402752 | bytes 8000000 | tf_op jit(solution)/shard_map/pallas_call | solution.py:75
  54.2 1.9 collective-permute-start.2
  56.1 1.3 collective-permute-done.7.refs_4_
  57.5 2.7 %collective-permute-start.11 = (bf16[128,896]{1,0:T(8,128)(2,1)S(1)}, bf16[128,896]{1,0:T(8,128)(2,1)S(1)}, u32[]{:S(2)}, u32[]{:S(2)}) collective-permute-start(bf16[128,896]{1,0:T(8,128)(2,1)S(1)} %slice.72), channel_id=1, source_target_pairs={{0,48},{16,0},{32,16},{48,32},{1,49},{17,1},{33,17},{49,33},{2,50}... | collective-permute-start | bytes 688136 | tf_op jit(solution)/shard_map/ppermute | solution.py:250
  60.3 0.1 stack.74.order_ref
  60.4 4.0 %collective-permute-done.10.refs_7_ = bf16[128,896]{1,0:T(8,128)(2,1)S(1)} collective-permute-done((bf16[128,896]{1,0:T(8,128)(2,1)S(1)}, bf16[128,896]{1,0:T(8,128)(2,1)S(1)}, u32[]{:S(2)}, u32[]{:S(2)}) %collective-permute-start.10) | collective-permute-done | bytes 229408 | tf_op jit(solution)/shard_map/ppermute | solution.py:249
  64.4 3.7 %shard_map.123 = bf16[8,2,16,1792]{3,2,1,0:T(8,128)(2,1)} custom-call(s32[8]{0:T(128)S(1)} %stack.74.order_ref, bf16[128,1024]{1,0:T(8,128)(2,1)} %shard_map.122.own_ref, bf16[128,1024]{1,0:T(8,128)(2,1)S(1)} %collective-permute-done.2.far_ref, bf16[128,1792]{1,0:T(8,128)(2,1)S(1)} %pad_maximum_fusion.1.refs_0_, ...), custom_call_target="tpu_custom_call" | custom-call | flops 939524096 | bytes 3670016 | tf_op jit(solution)/shard_map/pallas_call | solution.py:225
  68.0 7.2 %all-to-all-start.1 = ((bf16[8,2,16,1792]{3,2,1,0:T(8,128)(2,1)}), bf16[8,2,16,1792]{3,2,1,0:T(8,128)(2,1)S(1)}, u32[]{:S(2)}, u32[]{:S(2)}) async-start(bf16[8,2,16,1792]{3,2,1,0:T(8,128)(2,1)} %shard_map.123), calls=%async_computation.1 | async-start | bytes 1835008 | tf_op jit(solution)/shard_map/all_to_all | solution.py:317
  75.3 2.7 %collective-permute-start = (bf16[16,1792]{1,0:T(8,128)(2,1)S(1)}, bf16[16,1792]{1,0:T(8,128)(2,1)S(1)}, u32[]{:S(2)}, u32[]{:S(2)}) collective-permute-start(bf16[16,1792]{1,0:T(8,128)(2,1)S(1)} %get-tuple-element.11), channel_id=1, source_target_pairs={{0,8},{8,0},{1,9},{9,1},{2,10},{10,2},{3,11},{11,3},{4,12},{12,4},... | collective-permute-start | bytes 172040 | tf_op jit(solution)/shard_map/ppermute | solution.py:239
  78.0 0.1 collective-permute-start.13
  78.1 0.1 and.50
  78.2 0.1 and.51
  78.3 0.9 collective-permute-done.13
  79.2 0.1 fusion.8
  79.4 0.1 copy.51
  79.5 0.1 copy.53
  79.6 0.1 copy.52
  79.7 11.2 %all-to-all-done.1 = bf16[8,2,16,1792]{3,2,1,0:T(8,128)(2,1)S(1)} async-done(((bf16[8,2,16,1792]{3,2,1,0:T(8,128)(2,1)}), bf16[8,2,16,1792]{3,2,1,0:T(8,128)(2,1)S(1)}, u32[]{:S(2)}, u32[]{:S(2)}) %all-to-all-start.1) | async-done | bytes 917536 | tf_op jit(solution)/shard_map/all_to_all | solution.py:317
  90.9 0.1 convert_reduce_fusion
  91.1 1.3 collective-permute-start.12
  92.5 0.1 bitcast_and_fusion
  92.5 0.1 copy.54
  92.7 0.1 broadcast_in_dim.24
  92.8 0.1 reshape.145
  92.9 0.5 collective-permute-done.12
  93.5 0.1 multiply_reduce_fusion
  93.6 0.1 rsqrt.12
  93.7 0.1 fusion.2.x_ref
  93.9 2.3 %shard_map.124 = bf16[192,2,3584]{2,1,0:T(2,128)(2,1)S(1)} custom-call(bf16[384,32]{1,0:T(8,128)(2,1)S(1)} %convert_element_type.50.place_ref, bf16[32,3584]{1,0:T(8,128)(2,1)S(1)} %fusion.2.x_ref), custom_call_target="tpu_custom_call" | custom-call | flops 88080384 | bytes 2981888 | tf_op jit(solution)/shard_map/pallas_call | solution.py:156
  96.2 41.5 %all_to_all.20 = bf16[64,3,2,3584]{3,2,1,0:T(2,128)(2,1)S(1)} all-to-all(bf16[64,3,2,3584]{3,2,1,0:T(2,128)(2,1)S(1)} %bitcast.62), channel_id=1, replica_groups=mesh['z_lo'=2,'x'=4,'core'=2,'z_hi'=2,'y'=4] {'z_lo','x','z_hi','y'}, dimensions={0} | all-to-all | bytes 5505024 | tf_op jit(solution)/shard_map/all_to_all | solution.py:330
  137.6 10.0 %shard_map.125 = bf16[192,2,3584]{2,1,0:T(2,128)(2,1)S(1)} custom-call(bf16[192,2,3584]{2,1,0:T(2,128)(2,1)S(1)} %bitcast.64, bf16[3584,512]{1,0:T(8,128)(2,1)S(1)} %bitcast.65, bf16[3584,512]{1,0:T(8,128)(2,1)S(1)} %bitcast.66, bf16[512,3584]{1,0:T(8,128)(2,1)} %bitcast.69), custom_call_target="tpu_custom_call" | custom-call | flops 4227858432 | bytes 17000000 | tf_op jit(solution)/shard_map/pallas_call | solution.py:128
  147.7 1.5 copy-done
  149.2 7.5 %all-to-all-start.3 = ((bf16[64,3,2,3584]{3,2,1,0:T(2,128)(2,1)}), bf16[64,3,2,3584]{3,2,1,0:T(2,128)(2,1)S(1)}, u32[]{:S(2)}, u32[]{:S(2)}) async-start(bf16[64,3,2,3584]{3,2,1,0:T(2,128)(2,1)} %bitcast.63), calls=%async_computation.3 | async-start | bytes 5505024 | tf_op jit(solution)/shard_map/all_to_all | solution.py:334
  156.7 1.6 collective-permute-start.14
  158.3 0.1 copy.59
  158.4 0.7 collective-permute-done.14
  159.2 0.1 select_reduce_fusion
  159.4 0.1 copy.56
  159.6 0.7 broadcast_in_dim.28
  160.3 1.6 reshape.147
  162.0 1.0 copy.60
  163.1 26.8 %all-to-all-done.3 = bf16[64,3,2,3584]{3,2,1,0:T(2,128)(2,1)S(1)} async-done(((bf16[64,3,2,3584]{3,2,1,0:T(2,128)(2,1)}), bf16[64,3,2,3584]{3,2,1,0:T(2,128)(2,1)S(1)}, u32[]{:S(2)}, u32[]{:S(2)}) %all-to-all-start.3) | async-done | bytes 2752544 | tf_op jit(solution)/shard_map/all_to_all | solution.py:334
  189.8 1.9 shard_map.126
  191.8 3.8 %collective-permute-start.15 = (f32[16,3584]{1,0:T(8,128)S(1)}, f32[16,3584]{1,0:T(8,128)S(1)}, u32[]{:S(2)}, u32[]{:S(2)}) collective-permute-start(f32[16,3584]{1,0:T(8,128)S(1)} %get-tuple-element.5), channel_id=1, source_target_pairs={{0,8},{8,0},{1,9},{9,1},{2,10},{10,2},{3,11},{11,3},{4,12},{12,4},... | collective-permute-start | bytes 688136 | tf_op jit(solution)/shard_map/ppermute | solution.py:239
  195.5 0.7 fusion.10
  196.2 0.5 collective-permute-done.15
  196.7 0.7 fusion.7
  (60 shorter events, 1.0 us)
Async XLA Ops:
  0.6 8.5 %copy-start.4 = (bf16[64,3584]{1,0:T(8,128)(2,1)S(1)}, bf16[64,3584]{1,0:T(8,128)(2,1)}, u32[]{:S(2)}) copy-start(bf16[64,3584]{1,0:T(8,128)(2,1)} %param.14) | copy-start | bytes 1376260
  2.8 27.2 %copy-start.5 = (bf16[128,1536]{1,0:T(8,128)(2,1)S(1)}, bf16[128,1536]{1,0:T(8,128)(2,1)}, u32[]{:S(2)}) copy-start(bf16[128,1536]{1,0:T(8,128)(2,1)} %param.11) | copy-start | bytes 1179652
  2.8 23.7 %all-to-all-start = ((bf16[8,576,128]{2,1,0:T(8,128)(2,1)}), bf16[8,576,128]{2,1,0:T(8,128)(2,1)}, u32[]{:S(2)}, u32[]{:S(2)}) async-start(bf16[8,576,128]{2,1,0:T(8,128)(2,1)} %broadcast_in_dim.23), calls=%async_computation | async-start | bytes 2359296 | tf_op jit(solution)/shard_map/all_to_all | solution.py:307
  9.2 21.2 %copy-start.3 = (bf16[512,2048]{1,0:T(8,128)(2,1)S(1)}, bf16[512,2048]{1,0:T(8,128)(2,1)}, u32[]{:S(2)}) copy-start(bf16[512,2048]{1,0:T(8,128)(2,1)} %w_ref.1) | copy-start | bytes 6291460
  9.2 18.1 %collective-permute-start.3 = (bf16[64,1792]{1,0:T(8,128)(2,1)S(1)}, bf16[64,1792]{1,0:T(8,128)(2,1)}, u32[]{:S(2)}, u32[]{:S(2)}) collective-permute-start(bf16[64,1792]{1,0:T(8,128)(2,1)S(1)} %broadcast_select_fusion.2), channel_id=1, source_target_pairs={{0,8},{8,0},{1,9},{9,1},{2,10},{10,2},{3,11},{11,3},{4,12},{12,4},... | collective-permute-start | bytes 688136 | tf_op jit(solution)/shard_map/ppermute | solution.py:239
  26.5 16.8 %collective-permute-start.1 = (bf16[8,576,128]{2,1,0:T(8,128)(2,1)}, bf16[8,576,128]{2,1,0:T(8,128)(2,1)}, u32[]{:S(2)}, u32[]{:S(2)}) collective-permute-start(bf16[8,576,128]{2,1,0:T(8,128)(2,1)} %all-to-all-done.near_ref), channel_id=1, source_target_pairs={{0,8},{8,0},{1,9},{9,1},{2,10},{10,2},{3,11},{11,3},{4,12},{12,4},... | collective-permute-start | bytes 3538952 | tf_op jit(solution)/shard_map/ppermute | solution.py:239
  28.3 15.0 %collective-permute-start.4 = (bf16[128,1792]{1,0:T(8,128)(2,1)S(1)}, bf16[128,1792]{1,0:T(8,128)(2,1)}, u32[]{:S(2)}, u32[]{:S(2)}) collective-permute-start(bf16[128,1792]{1,0:T(8,128)(2,1)S(1)} %pad_maximum_fusion.1.refs_0_), channel_id=1, source_target_pairs={{0,64},{64,0},{1,65},{65,1},{2,66},{66,2},{3,67},{67,3},{4,68},{68... | collective-permute-start | bytes 1376264 | tf_op jit(solution)/shard_map/ppermute | solution.py:251
  28.7 11.9 %collective-permute-start.6 = (bf16[128,1792]{1,0:T(8,128)(2,1)S(1)}, bf16[128,1792]{1,0:T(8,128)(2,1)}, u32[]{:S(2)}, u32[]{:S(2)}) collective-permute-start(bf16[128,1792]{1,0:T(8,128)(2,1)S(1)} %pad_maximum_fusion.1.refs_0_), channel_id=1, source_target_pairs={{0,48},{16,0},{32,16},{48,32},{1,49},{17,1},{33,17},{49,33},{2,50}... | collective-permute-start | bytes 1376264 | tf_op jit(solution)/shard_map/ppermute | solution.py:250
  34.8 25.6 %collective-permute-start.5 = (bf16[128,1792]{1,0:T(8,128)(2,1)S(1)}, bf16[128,1792]{1,0:T(8,128)(2,1)}, u32[]{:S(2)}, u32[]{:S(2)}) collective-permute-start(bf16[128,1792]{1,0:T(8,128)(2,1)S(1)} %pad_maximum_fusion.1.refs_0_), channel_id=1, source_target_pairs={{0,16},{16,32},{32,48},{48,0},{1,17},{17,33},{33,49},{49,1},{2,18}... | collective-permute-start | bytes 1376264 | tf_op jit(solution)/shard_map/ppermute | solution.py:249
  40.6 16.9 %collective-permute-start.8 = (bf16[128,1792]{1,0:T(8,128)(2,1)}, bf16[128,1792]{1,0:T(8,128)(2,1)S(1)}, u32[]{:S(2)}, u32[]{:S(2)}) collective-permute-start(bf16[128,1792]{1,0:T(8,128)(2,1)} %collective-permute-done.6.refs_3_), channel_id=1, source_target_pairs={{0,64},{64,0},{1,65},{65,1},{2,66},{66,2},{3,67},{67,3},{4,68},{68... | collective-permute-start | bytes 1376264 | tf_op jit(solution)/shard_map/ppermute | solution.py:251
  41.8 18.5 %collective-permute-start.9 = (bf16[128,1792]{1,0:T(8,128)(2,1)}, bf16[128,1792]{1,0:T(8,128)(2,1)}, u32[]{:S(2)}, u32[]{:S(2)}) collective-permute-start(bf16[128,1792]{1,0:T(8,128)(2,1)} %collective-permute-done.6.refs_3_), channel_id=1, source_target_pairs={{0,48},{16,0},{32,16},{48,32},{1,49},{17,1},{33,17},{49,33},{2,50}... | collective-permute-start | bytes 1376264 | tf_op jit(solution)/shard_map/ppermute | solution.py:250
  43.3 14.1 %collective-permute-start.7 = (bf16[128,1792]{1,0:T(8,128)(2,1)}, bf16[128,1792]{1,0:T(8,128)(2,1)S(1)}, u32[]{:S(2)}, u32[]{:S(2)}) collective-permute-start(bf16[128,1792]{1,0:T(8,128)(2,1)} %collective-permute-done.4.refs_1_), channel_id=1, source_target_pairs={{0,16},{16,32},{32,48},{48,0},{1,17},{17,33},{33,49},{49,1},{2,18}... | collective-permute-start | bytes 1376264 | tf_op jit(solution)/shard_map/ppermute | solution.py:249
  54.2 10.2 %collective-permute-start.2 = (bf16[128,1024]{1,0:T(8,128)(2,1)}, bf16[128,1024]{1,0:T(8,128)(2,1)S(1)}, u32[]{:S(2)}, u32[]{:S(2)}) collective-permute-start(bf16[128,1024]{1,0:T(8,128)(2,1)} %shard_map.122.own_ref), channel_id=1, source_target_pairs={{0,8},{8,0},{1,9},{9,1},{2,10},{10,2},{3,11},{11,3},{4,12},{12,4},... | collective-permute-start | bytes 786440 | tf_op jit(solution)/shard_map/ppermute | solution.py:239
  57.4 7.0 %collective-permute-start.10 = (bf16[128,896]{1,0:T(8,128)(2,1)S(1)}, bf16[128,896]{1,0:T(8,128)(2,1)S(1)}, u32[]{:S(2)}, u32[]{:S(2)}) collective-permute-start(bf16[128,896]{1,0:T(8,128)(2,1)S(1)} %slice.71), channel_id=1, source_target_pairs={{0,16},{16,32},{32,48},{48,0},{1,17},{17,33},{33,49},{49,1},{2,18}... | collective-permute-start | bytes 688136 | tf_op jit(solution)/shard_map/ppermute | solution.py:249
  57.5 6.8 %collective-permute-start.11 = (bf16[128,896]{1,0:T(8,128)(2,1)S(1)}, bf16[128,896]{1,0:T(8,128)(2,1)S(1)}, u32[]{:S(2)}, u32[]{:S(2)}) collective-permute-start(bf16[128,896]{1,0:T(8,128)(2,1)S(1)} %slice.72), channel_id=1, source_target_pairs={{0,48},{16,0},{32,16},{48,32},{1,49},{17,1},{33,17},{49,33},{2,50}... | collective-permute-start | bytes 688136 | tf_op jit(solution)/shard_map/ppermute | solution.py:250
  60.4 14.9 %copy-start.6 = (bf16[16,3584]{1,0:T(8,128)(2,1)S(1)}, bf16[16,3584]{1,0:T(8,128)(2,1)}, u32[]{:S(2)}) copy-start(bf16[16,3584]{1,0:T(8,128)(2,1)} %param.15) | copy-start | bytes 344068
  60.4 17.6 %copy-start.9 = (s32[16,8]{0,1:T(8,128)S(1)}, s32[16,8]{0,1:T(8,128)}, u32[]{:S(2)}) copy-start(s32[16,8]{0,1:T(8,128)} %param.17) | copy-start | bytes 1540
  68.0 22.9 %all-to-all-start.1 = ((bf16[8,2,16,1792]{3,2,1,0:T(8,128)(2,1)}), bf16[8,2,16,1792]{3,2,1,0:T(8,128)(2,1)S(1)}, u32[]{:S(2)}, u32[]{:S(2)}) async-start(bf16[8,2,16,1792]{3,2,1,0:T(8,128)(2,1)} %shard_map.123), calls=%async_computation.1 | async-start | bytes 1835008 | tf_op jit(solution)/shard_map/all_to_all | solution.py:317
  75.3 18.5 %copy-start.8 = (f32[3584]{0:T(1024)S(1)}, f32[3584]{0:T(1024)}, u32[]{:S(2)}) copy-start(f32[3584]{0:T(1024)} %param.16) | copy-start | bytes 43012
  75.3 15.8 %collective-permute-start = (bf16[16,1792]{1,0:T(8,128)(2,1)S(1)}, bf16[16,1792]{1,0:T(8,128)(2,1)S(1)}, u32[]{:S(2)}, u32[]{:S(2)}) collective-permute-start(bf16[16,1792]{1,0:T(8,128)(2,1)S(1)} %get-tuple-element.11), channel_id=1, source_target_pairs={{0,8},{8,0},{1,9},{9,1},{2,10},{10,2},{3,11},{11,3},{4,12},{12,4},... | collective-permute-start | bytes 172040 | tf_op jit(solution)/shard_map/ppermute | solution.py:239
  78.0 1.2 collective-permute-start.13
  91.1 2.3 %collective-permute-start.12 = (bf16[2,16,1792]{2,1,0:T(8,128)(2,1)S(1)}, bf16[2,16,1792]{2,1,0:T(8,128)(2,1)S(1)}, u32[]{:S(2)}, u32[]{:S(2)}) collective-permute-start(bf16[2,16,1792]{2,1,0:T(8,128)(2,1)S(1)} %add_convert_fusion), channel_id=1, source_target_pairs={{0,8},{8,0},{1,9},{9,1},{2,10},{10,2},{3,11},{11,3},{4,12},{12,4},... | collective-permute-start | bytes 344072 | tf_op jit(solution)/shard_map/ppermute | solution.py:239
  93.9 43.8 %copy-start.2 = (bf16[1,3584,512]{2,1,0:T(8,128)(2,1)S(1)}, bf16[1,3584,512]{2,1,0:T(8,128)(2,1)}, u32[]{:S(2)}) copy-start(bf16[1,3584,512]{2,1,0:T(8,128)(2,1)} %param.20) | copy-start | bytes 11010052
  96.1 41.5 %copy-start.1 = (bf16[1,3584,512]{2,1,0:T(8,128)(2,1)S(1)}, bf16[1,3584,512]{2,1,0:T(8,128)(2,1)}, u32[]{:S(2)}) copy-start(bf16[1,3584,512]{2,1,0:T(8,128)(2,1)} %param.19) | copy-start | bytes 11010052
  147.7 1.6 copy-start
  149.2 7.5 %copy-start.7 = (s32[16,8]{0,1:T(8,128)S(1)}, s32[16,8]{0,1:T(8,128)}, u32[]{:S(2)}) copy-start(s32[16,8]{0,1:T(8,128)} %param.18) | copy-start | bytes 1540
  149.2 40.6 %all-to-all-start.3 = ((bf16[64,3,2,3584]{3,2,1,0:T(2,128)(2,1)}), bf16[64,3,2,3584]{3,2,1,0:T(2,128)(2,1)S(1)}, u32[]{:S(2)}, u32[]{:S(2)}) async-start(bf16[64,3,2,3584]{3,2,1,0:T(2,128)(2,1)} %bitcast.63), calls=%async_computation.3 | async-start | bytes 5505024 | tf_op jit(solution)/shard_map/all_to_all | solution.py:334
  156.7 2.4 %collective-permute-start.14 = (f32[16,8]{0,1:T(8,128)S(1)}, f32[16,8]{0,1:T(8,128)S(1)}, u32[]{:S(2)}, u32[]{:S(2)}) collective-permute-start(f32[16,8]{0,1:T(8,128)S(1)} %convert_divide_fusion), channel_id=1, source_target_pairs={{0,8},{8,0},{1,9},{9,1},{2,10},{10,2},{3,11},{11,3},{4,12},{12,4},... | collective-permute-start | bytes 1544 | tf_op jit(solution)/shard_map/ppermute | solution.py:239
  191.8 4.9 %collective-permute-start.15 = (f32[16,3584]{1,0:T(8,128)S(1)}, f32[16,3584]{1,0:T(8,128)S(1)}, u32[]{:S(2)}, u32[]{:S(2)}) collective-permute-start(f32[16,3584]{1,0:T(8,128)S(1)} %get-tuple-element.5), channel_id=1, source_target_pairs={{0,8},{8,0},{1,9},{9,1},{2,10},{10,2},{3,11},{11,3},{4,12},{12,4},... | collective-permute-start | bytes 688136 | tf_op jit(solution)/shard_map/ppermute | solution.py:239

commit v4 on v3

--- a/solution.py
+++ b/solution.py
@@ -13,6 +13,7 @@
 TOP = 8
 QK = 192
 CAP = 3
+SLOTS = (slice(0, 2), slice(2, 3))
 
 CTX = ("z_lo", "x", "core")
 CTX_CHIPS = ("z_lo", "x")
@@ -166,34 +167,40 @@
     )(place, x)
 
 
-def combine_kernel(factors_ref, x_ref, own_ref, far_ref):
+def combine_kernel(*refs):
+    *in_refs, own_ref, far_ref = refs
     tok = own_ref.shape[0]
-    rows = x_ref[...].reshape(factors_ref.shape[1], x_ref.shape[2])
-    y = jnp.dot(factors_ref[...], rows, preferred_element_type=F32)
+    y = None
+    for factors_ref, x_ref in zip(in_refs[::2], in_refs[1::2]):
+        rows = x_ref[...].reshape(factors_ref.shape[1], x_ref.shape[2])
+        part = jnp.dot(factors_ref[...], rows, preferred_element_type=F32)
+        y = part if y is None else y + part
     y = y[: 2 * tok] + y[2 * tok :]
     own_ref[...] = y[:tok]
     far_ref[...] = y[tok:]
 
 
-def combine(factors, x, cuts):
-    width = x.shape[2]
+def combine(parts, cuts):
+    width = parts[0][1].shape[2]
     n = width // cuts
-    tok = factors.shape[0] // 4
-    part = pl.BlockSpec((tok, n), lambda i: (0, i))
+    tok = parts[0][0].shape[0] // 4
+    half = pl.BlockSpec((tok, n), lambda i: (0, i))
+    in_specs = []
+    for factors, x in parts:
+        in_specs.append(pl.BlockSpec(factors.shape, lambda i: (0, 0)))
+        in_specs.append(pl.BlockSpec((x.shape[0], 2, n), lambda i: (0, 0, i)))
+    rows = sum(2 * x.shape[0] for _, x in parts)
     return pl.pallas_call(
         combine_kernel,
         grid=(cuts,),
-        in_specs=[
-            pl.BlockSpec(factors.shape, lambda i: (0, 0)),
-            pl.BlockSpec((x.shape[0], 2, n), lambda i: (0, 0, i)),
-        ],
-        out_specs=(part, part),
+        in_specs=in_specs,
+        out_specs=(half, half),
         out_shape=(jax.ShapeDtypeStruct((tok, width), F32),) * 2,
         compiler_params=pltpu.CompilerParams(vmem_limit_bytes=32 * 2**20),
         cost_estimate=pl.CostEstimate(
-            flops=2 * factors.size * width, bytes_accessed=4 * x.shape[0] * width, transcendentals=0
-        ),
-    )(factors, x)
+            flops=8 * tok * rows * width, bytes_accessed=2 * rows * width, transcendentals=0
+        ),
+    )(*[a for part in parts for a in part])
 
 
 def project_kernel(order_ref, own_ref, far_ref, *refs):
@@ -256,7 +263,7 @@
     chunks = (own, mate, before, after, mate_before, mate_after, opposite, left, right)
     chip = lambda zz, dx: zz * 4 + lax.rem(x + 4 + dx, 4)
     order = (chip(z, 0), chip(1 - z, 0), chip(z, -1), chip(z, 1), chip(1 - z, -1), chip(1 - z, 1), chip(z, 2), chip(1 - z, 2))
-    return jnp.stack(order).astype(jnp.int32), chunks
+    return own, jnp.stack(order).astype(jnp.int32), chunks
 
 
 def latent_queries(queries, w_kv):
@@ -290,20 +297,25 @@
     place = place.transpose(2, 3, 0, 1)[:, :, :, None, :]
     same = jnp.arange(2)[:, None, None] == jnp.arange(2)[None, :, None]
     place = (place & same).reshape(32, CAP, 2, 2 * tok)
-    place = jnp.broadcast_to(place[:, None], (32, 2, CAP, 2, 2 * tok)).reshape(64 * CAP * 2, 2 * tok)
+    place = jnp.broadcast_to(place[:, None], (32, 2, CAP, 2, 2 * tok)).reshape(64, CAP, 2, 2 * tok)
     gains = weight.transpose(2, 0, 1).reshape(32, 2 * tok)
-    gains = jnp.broadcast_to(gains[:, None], (32, 2 * CAP * 2, 2 * tok)).reshape(64 * CAP * 2, 2 * tok)
-    factors = jnp.where(place, gains, F32(0.0)).T
+    gains = jnp.broadcast_to(gains[:, None], (32, 2, 2 * tok)).reshape(64, 1, 1, 2 * tok)
+    factors = jnp.where(place, gains, F32(0.0))
     high = lax.reduce_precision(factors, 8, 7)
-    factors = jnp.concatenate([high, factors - high], axis=0).astype(BF)
-    return place.astype(BF), factors
+    factors = jnp.concatenate([high, factors - high], axis=3).astype(BF)
+    place = place.astype(BF)
+    parts = []
+    for slots in SLOTS:
+        parts.append((place[:, slots].reshape(-1, 2 * tok), factors[:, slots].reshape(-1, 4 * tok).T))
+    return parts
 
 
 def local(queries, latents, w_kv, w_out, resid, norm_gain, routes, codes, w_gate, w_up, w_down):
     tok, width = resid.shape
     chips = 64
     core = lax.axis_index("core")
-    order, chunks = gather_w_out(w_out)
+    own_rows, order, chunks = gather_w_out(w_out)
+    latents, _ = lax.optimization_barrier((latents, own_rows))
     near = lax.all_to_all(
         jnp.broadcast_to(latents[None], (8,) + latents.shape), CTX_CHIPS, split_axis=0, concat_axis=0, tiled=True
     )
@@ -325,16 +337,15 @@
     meansq = jnp.mean(wide2 * wide2, axis=1, keepdims=True)
     normed2 = (wide2 * lax.rsqrt(meansq + 1e-06) * norm_gain[None, :]).astype(BF)
 
-    place, factors = routing(routes, codes)
-    outgoing = dispatch(place, normed2, 7)
-    arrived = lax.all_to_all(
-        outgoing.reshape(chips, CAP, 2, width), CHIPS, split_axis=0, concat_axis=0, tiled=True
-    ).reshape(chips * CAP, 2, width)
-    produced = expert(arrived, w_gate[0], w_up[0], w_down[0], 2, 7)
-    returned = lax.all_to_all(
-        produced.reshape(chips, CAP, 2, width), CHIPS, split_axis=0, concat_axis=0, tiled=True
-    ).reshape(chips * CAP, 2, width)
-    own, theirs = combine(factors, returned, 7)
+    def exchange(rows):
+        units = rows.reshape(chips, -1, 2, width)
+        units = lax.all_to_all(units, CHIPS, split_axis=0, concat_axis=0, tiled=True)
+        return units.reshape(rows.shape)
+
+    parts = routing(routes, codes)
+    arrived = [exchange(dispatch(place, normed2, 7)) for place, _ in parts]
+    returned = [exchange(expert(rows, w_gate[0], w_up[0], w_down[0], 2, 7)) for rows in arrived]
+    own, theirs = combine([(factors, rows) for (_, factors), rows in zip(parts, returned)], 7)
     layer_out = (wide2[:tok] + own + swap(theirs)).astype(BF)
     return (attended, layer_out)
 

time: 199 us -> 214 us (1.075)
  starting transfers between devices: 41.6 us -> 63.4 us
  blocking collectives: 41.5 us -> 22.4 us
  local copies, waits for them, and re-layouts: 11.6 us -> 22.2 us
  waiting for transfers between devices: 67.5 us -> 57 us
  Pallas kernels: 28.7 us -> 35.7 us
  other arithmetic: 3.64 us -> 9.47 us
    all_to_all x1, blocking collectives: 41.5 us -> 22.4 us  [local(): lax.all_to_all(jnp.broadcast_to(latents[None], (8,) + latents.shape), CTX...]
    all_to_all x2 -> x4, starting transfers between devices: 13.8 us -> 30.2 us  [exchange(): lax.all_to_all(units, CHIPS, split_axis=0, concat_axis=0, tiled=True)]
    unnamed x23 -> x42, local copies, waits for them, and re-layouts: 4.53 us -> 16.4 us
    all_to_all x2 -> x4, waiting for transfers between devices: 43 us -> 36 us  [exchange(): lax.all_to_all(units, CHIPS, split_axis=0, concat_axis=0, tiled=True)]
    ppermute x8, starting transfers between devices: 13.3 us -> 17.6 us  [swap(): return lax.ppermute(mine, 'core', SWAP)]
    pallas_call x1 -> x2, Pallas kernels: 10 us -> 13.9 us  [expert(): pl.pallas_call(functools.partial(expert_kernel, first=first), grid=(first...]
    pallas_call x1 -> x2, Pallas kernels: 2.26 us -> 5.29 us  [dispatch(): pl.pallas_call(dispatch_kernel, grid=(cuts,), in_specs=[pl.BlockSpec(plac...]
    slice x0 -> x5, local copies, waits for them, and re-layouts: none -> 2.58 us  [the longest x2 2.42 us: routing(): factors[:, slots].reshape(-1, 4 * tok)]
  transfers between devices with their start and end apart: 19 -> 21, of which waited for: 10 -> 11; matrix products, arithmetic and copies ran while one was open for 6% -> 8% of each run, Pallas kernels for 6% -> 13%
where the time goes in v4:
time: 214 us; the launch traced here: 213 us
  starting transfers between devices  63.4 us (30%)
  waiting for transfers between devices  57 us (27%)
  Pallas kernels  35.7 us (17%)
  blocking collectives  22.4 us (10%)
  local copies, waits for them, and re-layouts  22.2 us (10%)
  other arithmetic  9.47 us (4%)
    all_to_all x4, waiting for transfers between devices, exchange(): lax.all_to_all(units, CHIPS, split_axis=0, concat_axis=0, tiled=True)  36 us
    all_to_all x4, starting transfers between devices, exchange(): lax.all_to_all(units, CHIPS, split_axis=0, concat_axis=0, tiled=True)  30.2 us
    all_to_all x1, blocking collectives, local(): lax.all_to_all(jnp.broadcast_to(latents[None], (8,) + latents.shape), CTX...  22.4 us
    ppermute x8, starting transfers between devices, swap(): return lax.ppermute(mine, 'core', SWAP)  17.6 us
    unnamed x42, local copies, waits for them, and re-layouts  16.4 us
    pallas_call x2, Pallas kernels, expert(): pl.pallas_call(functools.partial(expert_kernel, first=first), grid=(first...  13.9 us
    pallas_call x1, Pallas kernels, attend(): pl.pallas_call(functools.partial(attend_kernel, rows=rows, cuts=cuts), gr...  10.9 us
    all_to_all x1, waiting for transfers between devices, local(): attn = lax.all_to_all(attn, EP, split_axis=0, concat_axis=0, tiled=True)  9.17 us
  transfers between devices with their start and end apart: 21, of which 11 were waited for; matrix products, arithmetic and copies ran while one was open for 8% of the time, Pallas kernels for 13%

profile of v4, /device:TPU:1, one launch (start us, length us, event | category | flops | bytes accessed | tf_op | source)
XLA Modules:
  0.0 212.8 jit_solution(13175491228662601761)
XLA Ops:
  0.6 1.1 broadcast_select_fusion.2
  1.8 1.5 collective-permute-start.1
  3.3 1.1 collective-permute-done.1
  4.4 1.1 broadcast_select_fusion.1
  5.5 0.2 broadcast_in_dim.30
  5.7 22.4 %all_to_all.30.near_ref = bf16[8,576,128]{2,1,0:T(8,128)(2,1)} all-to-all(bf16[8,576,128]{2,1,0:T(8,128)(2,1)S(1)} %broadcast_in_dim.30), channel_id=1, replica_groups=mesh['z_lo'=2,'x'=4,'core'=2,'z_hi'=2,'y'=4] {'z_lo','x'}, dimensions={0} | all-to-all | bytes 2359296 | tf_op jit(solution)/shard_map/all_to_all | solution.py:319
  28.1 1.2 collective-permute-start.2
  29.3 0.3 collective-permute-start.4
  29.6 1.2 collective-permute-start.6
  30.8 0.2 copy.89
  31.1 0.2 copy.115
  31.3 2.5 %copy.91 = bf16[512,2048]{0,1:T(8,128)(2,1)} copy(bf16[512,2048]{1,0:T(8,128)(2,1)S(1)} %copy-done.9) | data formatting | bytes 4194304 | tf_op args[2]
  33.8 1.7 convolution_convert_fusion
  35.6 0.4 collective-permute-start.5
  36.0 5.5 %collective-permute-done.6.refs_3_ = bf16[128,1792]{1,0:T(8,128)(2,1)} collective-permute-done((bf16[128,1792]{1,0:T(8,128)(2,1)S(1)}, bf16[128,1792]{1,0:T(8,128)(2,1)}, u32[]{:S(2)}, u32[]{:S(2)}) %collective-permute-start.6) | collective-permute-done | bytes 458784 | tf_op jit(solution)/shard_map/ppermute | solution.py:257
  41.5 1.2 collective-permute-start.8
  42.7 2.2 %collective-permute-start.9 = (bf16[128,1792]{1,0:T(8,128)(2,1)}, bf16[128,1792]{1,0:T(8,128)(2,1)}, u32[]{:S(2)}, u32[]{:S(2)}) collective-permute-start(bf16[128,1792]{1,0:T(8,128)(2,1)} %collective-permute-done.6.refs_3_), channel_id=1, source_target_pairs={{0,48},{16,0},{32,16},{48,32},{1,49},{17,1},{33,17},{49,33},{2,50}... | collective-permute-start | bytes 1376264 | tf_op jit(solution)/shard_map/ppermute | solution.py:257
  44.9 10.9 %shard_map.122.own_ref = bf16[128,1024]{1,0:T(8,128)(2,1)} custom-call(s32[2]{0:T(128)S(1)} %pad_add_fusion.1.ids_ref, bf16[1024,576]{1,0:T(8,128)(2,1)S(1)} %bitcast.87, bf16[8,576,128]{2,1,0:T(8,128)(2,1)} %all_to_all.30.near_ref, bf16[8,576,128]{2,1,0:T(8,128)(2,1)} %collective-permute-done.2.far_ref, bf16[512,2048]{1,0:T(8,128)(2,1)S(1)} %copy-done.9), custom_call_target="tpu_custom_call" | custom-call | flops 4563402752 | bytes 8000000 | tf_op jit(solution)/shard_map/pallas_call | solution.py:76
  55.8 1.7 collective-permute-start.3
  57.6 2.9 %collective-permute-start.11 = (bf16[128,896]{1,0:T(8,128)(2,1)S(1)}, bf16[128,896]{1,0:T(8,128)(2,1)S(1)}, u32[]{:S(2)}, u32[]{:S(2)}) collective-permute-start(bf16[128,896]{1,0:T(8,128)(2,1)S(1)} %slice.88), channel_id=1, source_target_pairs={{0,48},{16,0},{32,16},{48,32},{1,49},{17,1},{33,17},{49,33},{2,50}... | collective-permute-start | bytes 688136 | tf_op jit(solution)/shard_map/ppermute | solution.py:257
  60.7 3.2 %collective-permute-done.10.refs_7_ = bf16[128,896]{1,0:T(8,128)(2,1)S(1)} collective-permute-done((bf16[128,896]{1,0:T(8,128)(2,1)S(1)}, bf16[128,896]{1,0:T(8,128)(2,1)S(1)}, u32[]{:S(2)}, u32[]{:S(2)}) %collective-permute-start.10) | collective-permute-done | bytes 229408 | tf_op jit(solution)/shard_map/ppermute | solution.py:256
  63.9 3.7 %shard_map.123 = bf16[8,2,16,1792]{3,2,1,0:T(8,128)(2,1)} custom-call(s32[8]{0:T(128)S(1)} %stack.74.order_ref, bf16[128,1024]{1,0:T(8,128)(2,1)} %shard_map.122.own_ref, bf16[128,1024]{1,0:T(8,128)(2,1)S(1)} %collective-permute-done.3.far_ref, bf16[128,1792]{1,0:T(8,128)(2,1)S(1)} %pad_maximum_fusion.1.refs_0_, ...), custom_call_target="tpu_custom_call" | custom-call | flops 939524096 | bytes 3670016 | tf_op jit(solution)/shard_map/pallas_call | solution.py:232
  67.5 7.3 %all-to-all-start.1 = ((bf16[8,2,16,1792]{3,2,1,0:T(8,128)(2,1)}), bf16[8,2,16,1792]{3,2,1,0:T(8,128)(2,1)S(1)}, u32[]{:S(2)}, u32[]{:S(2)}) async-start(bf16[8,2,16,1792]{3,2,1,0:T(8,128)(2,1)} %shard_map.123), calls=%async_computation.1 | async-start | bytes 1835008 | tf_op jit(solution)/shard_map/all_to_all | solution.py:329
  74.9 3.5 %collective-permute-start = (bf16[16,1792]{1,0:T(8,128)(2,1)S(1)}, bf16[16,1792]{1,0:T(8,128)(2,1)S(1)}, u32[]{:S(2)}, u32[]{:S(2)}) collective-permute-start(bf16[16,1792]{1,0:T(8,128)(2,1)S(1)} %get-tuple-element.13), channel_id=1, source_target_pairs={{0,8},{8,0},{1,9},{9,1},{2,10},{10,2},{3,11},{11,3},{4,12},{12,4},... | collective-permute-start | bytes 172040 | tf_op jit(solution)/shard_map/ppermute | solution.py:246
  78.7 0.9 collective-permute-done.13
  80.3 9.2 %all-to-all-done.1 = bf16[8,2,16,1792]{3,2,1,0:T(8,128)(2,1)S(1)} async-done(((bf16[8,2,16,1792]{3,2,1,0:T(8,128)(2,1)}), bf16[8,2,16,1792]{3,2,1,0:T(8,128)(2,1)S(1)}, u32[]{:S(2)}, u32[]{:S(2)}) %all-to-all-start.1) | async-done | bytes 917536 | tf_op jit(solution)/shard_map/all_to_all | solution.py:329
  89.6 2.4 %collective-permute-start.12 = (bf16[2,16,1792]{2,1,0:T(8,128)(2,1)S(1)}, bf16[2,16,1792]{2,1,0:T(8,128)(2,1)S(1)}, u32[]{:S(2)}, u32[]{:S(2)}) collective-permute-start(bf16[2,16,1792]{2,1,0:T(8,128)(2,1)S(1)} %add_convert_fusion), channel_id=1, source_target_pairs={{0,8},{8,0},{1,9},{9,1},{2,10},{10,2},{3,11},{11,3},{4,12},{12,4},... | collective-permute-start | bytes 344072 | tf_op jit(solution)/shard_map/ppermute | solution.py:246
  92.5 0.6 collective-permute-done.12
  93.5 3.5 %shard_map.126 = bf16[64,2,3584]{2,1,0:T(2,128)(2,1)} custom-call(bf16[128,32]{1,0:T(8,128)(2,1)S(1)} %bitcast.90, bf16[32,3584]{1,0:T(8,128)(2,1)S(1)} %fusion.2.x_ref), custom_call_target="tpu_custom_call" | custom-call | flops 29360128 | bytes 1146880 | tf_op jit(solution)/shard_map/pallas_call | solution.py:157
  97.0 7.7 %all-to-all-start.4 = ((bf16[64,1,2,3584]{3,2,1,0:T(2,128)(2,1)}), bf16[64,1,2,3584]{3,2,1,0:T(2,128)(2,1)S(1)}, u32[]{:S(2)}, u32[]{:S(2)}) async-start(bf16[64,1,2,3584]{3,2,1,0:T(2,128)(2,1)} %bitcast.47), calls=%async_computation.4 | async-start | bytes 1835008 | tf_op jit(solution)/shard_map/all_to_all | solution.py:342
  104.8 1.8 shard_map.124
  106.6 1.2 copy-done.5
  107.9 12.4 %all-to-all-done.4 = bf16[64,1,2,3584]{3,2,1,0:T(2,128)(2,1)S(1)} async-done(((bf16[64,1,2,3584]{3,2,1,0:T(2,128)(2,1)}), bf16[64,1,2,3584]{3,2,1,0:T(2,128)(2,1)S(1)}, u32[]{:S(2)}, u32[]{:S(2)}) %all-to-all-start.4) | async-done | bytes 917536 | tf_op jit(solution)/shard_map/all_to_all | solution.py:342
  120.3 5.8 %all-to-all-start.2 = ((bf16[64,2,2,3584]{3,2,1,0:T(2,128)(2,1)}), bf16[64,2,2,3584]{3,2,1,0:T(2,128)(2,1)S(1)}, u32[]{:S(2)}, u32[]{:S(2)}) async-start(bf16[64,2,2,3584]{3,2,1,0:T(2,128)(2,1)} %bitcast.83), calls=%async_computation.2 | async-start | bytes 3670016 | tf_op jit(solution)/shard_map/all_to_all | solution.py:342
  126.1 2.0 copy-done
  128.2 2.0 copy-done.2
  130.2 2.0 copy-done.4
  132.2 4.3 %shard_map.127 = bf16[64,2,3584]{2,1,0:T(2,128)(2,1)S(1)} custom-call(bf16[64,2,3584]{2,1,0:T(2,128)(2,1)S(1)} %bitcast.84, bf16[3584,512]{1,0:T(8,128)(2,1)S(1)} %bitcast.75, bf16[3584,512]{1,0:T(8,128)(2,1)S(1)} %bitcast.77, bf16[512,3584]{1,0:T(8,128)(2,1)S(1)} %bitcast.80), custom_call_target="tpu_custom_call" | custom-call | flops 1409286144 | bytes 17000000 | tf_op jit(solution)/shard_map/pallas_call | solution.py:129
  136.6 0.9 copy-done.6
  137.5 12.2 %all-to-all-done.2 = bf16[64,2,2,3584]{3,2,1,0:T(2,128)(2,1)S(1)} async-done(((bf16[64,2,2,3584]{3,2,1,0:T(2,128)(2,1)}), bf16[64,2,2,3584]{3,2,1,0:T(2,128)(2,1)S(1)}, u32[]{:S(2)}, u32[]{:S(2)}) %all-to-all-start.2) | async-done | bytes 1835040 | tf_op jit(solution)/shard_map/all_to_all | solution.py:342
  149.7 7.6 %all-to-all-start.5 = ((bf16[64,1,2,3584]{3,2,1,0:T(2,128)(2,1)}), bf16[64,1,2,3584]{3,2,1,0:T(2,128)(2,1)S(1)}, u32[]{:S(2)}, u32[]{:S(2)}) async-start(bf16[64,1,2,3584]{3,2,1,0:T(2,128)(2,1)} %bitcast.85), calls=%async_computation.5 | async-start | bytes 1835008 | tf_op jit(solution)/shard_map/all_to_all | solution.py:342
  157.4 2.0 copy-done.1
  159.4 2.0 copy-done.3
  161.5 9.6 %shard_map.125 = bf16[128,2,3584]{2,1,0:T(2,128)(2,1)} custom-call(bf16[128,2,3584]{2,1,0:T(2,128)(2,1)S(1)} %bitcast.81, bf16[3584,512]{1,0:T(8,128)(2,1)S(1)} %bitcast.76, bf16[3584,512]{1,0:T(8,128)(2,1)S(1)} %bitcast.78, bf16[512,3584]{1,0:T(8,128)(2,1)} %bitcast.79), custom_call_target="tpu_custom_call" | custom-call | flops 2818572288 | bytes 17000000 | tf_op jit(solution)/shard_map/pallas_call | solution.py:129
  171.0 0.8 all-to-all-done.5
  171.8 0.9 copy-done.7
  172.7 9.0 %all-to-all-start.3 = ((bf16[64,2,2,3584]{3,2,1,0:T(2,128)(2,1)}), bf16[64,2,2,3584]{3,2,1,0:T(2,128)(2,1)S(1)}, u32[]{:S(2)}, u32[]{:S(2)}) async-start(bf16[64,2,2,3584]{3,2,1,0:T(2,128)(2,1)} %bitcast.42), calls=%async_computation.3 | async-start | bytes 3670016 | tf_op jit(solution)/shard_map/all_to_all | solution.py:342
  181.8 0.6 convert_divide_fusion
  182.4 2.4 %collective-permute-start.14 = (f32[16,8]{0,1:T(8,128)}, f32[16,8]{0,1:T(8,128)}, u32[]{:S(2)}, u32[]{:S(2)}) collective-permute-start(f32[16,8]{0,1:T(8,128)} %convert_divide_fusion), channel_id=1, source_target_pairs={{0,8},{8,0},{1,9},{9,1},{2,10},{10,2},{3,11},{11,3},{4,12},{12,4},... | collective-permute-start | bytes 1544 | tf_op jit(solution)/shard_map/ppermute | solution.py:246
  184.7 0.6 fusion.14
  185.4 0.7 copy.104
  186.1 0.7 pad_maximum_fusion.4
  187.4 0.8 fusion.11
  188.2 0.6 fusion.12
  188.8 1.6 copy.105
  190.4 0.9 copy.106
  191.3 1.3 pad_maximum_fusion.3
  192.7 0.8 copy.108
  193.6 10.7 %all-to-all-done.3 = bf16[64,2,2,3584]{3,2,1,0:T(2,128)(2,1)S(1)} async-done(((bf16[64,2,2,3584]{3,2,1,0:T(2,128)(2,1)}), bf16[64,2,2,3584]{3,2,1,0:T(2,128)(2,1)S(1)}, u32[]{:S(2)}, u32[]{:S(2)}) %all-to-all-start.3) | async-done | bytes 1835040 | tf_op jit(solution)/shard_map/all_to_all | solution.py:342
  204.3 1.9 shard_map.128
  206.2 4.8 %collective-permute-start.15 = (f32[16,3584]{1,0:T(8,128)S(1)}, f32[16,3584]{1,0:T(8,128)S(1)}, u32[]{:S(2)}, u32[]{:S(2)}) collective-permute-start(f32[16,3584]{1,0:T(8,128)S(1)} %get-tuple-element.7), channel_id=1, source_target_pairs={{0,8},{8,0},{1,9},{9,1},{2,10},{10,2},{3,11},{11,3},{4,12},{12,4},... | collective-permute-start | bytes 688136 | tf_op jit(solution)/shard_map/ppermute | solution.py:246
  211.0 0.7 fusion.10
  211.7 0.5 collective-permute-done.15
  212.1 0.7 fusion.7
  (91 shorter events, 3.3 us)
Async XLA Ops:
  0.6 4.9 %copy-start.14 = (bf16[576,128]{1,0:T(8,128)(2,1)S(1)}, bf16[576,128]{1,0:T(8,128)(2,1)}, u32[]{:S(2)}) copy-start(bf16[576,128]{1,0:T(8,128)(2,1)} %param.12) | copy-start | bytes 442372
  1.8 2.6 %collective-permute-start.1 = (bf16[64,1792]{1,0:T(8,128)(2,1)S(1)}, bf16[64,1792]{1,0:T(8,128)(2,1)S(1)}, u32[]{:S(2)}, u32[]{:S(2)}) collective-permute-start(bf16[64,1792]{1,0:T(8,128)(2,1)S(1)} %broadcast_select_fusion.2), channel_id=1, source_target_pairs={{0,8},{8,0},{1,9},{9,1},{2,10},{10,2},{3,11},{11,3},{4,12},{12,4},... | collective-permute-start | bytes 688136 | tf_op jit(solution)/shard_map/ppermute | solution.py:246
  5.5 25.3 %copy-start.11 = (bf16[128,1536]{1,0:T(8,128)(2,1)S(1)}, bf16[128,1536]{1,0:T(8,128)(2,1)}, u32[]{:S(2)}) copy-start(bf16[128,1536]{1,0:T(8,128)(2,1)} %param.11) | copy-start | bytes 1179652
  5.7 25.5 %copy-start.9 = (bf16[512,2048]{1,0:T(8,128)(2,1)S(1)}, bf16[512,2048]{1,0:T(8,128)(2,1)}, u32[]{:S(2)}) copy-start(bf16[512,2048]{1,0:T(8,128)(2,1)} %w_ref.1) | copy-start | bytes 6291460
  28.1 16.8 %collective-permute-start.2 = (bf16[8,576,128]{2,1,0:T(8,128)(2,1)}, bf16[8,576,128]{2,1,0:T(8,128)(2,1)}, u32[]{:S(2)}, u32[]{:S(2)}) collective-permute-start(bf16[8,576,128]{2,1,0:T(8,128)(2,1)} %all_to_all.30.near_ref), channel_id=1, source_target_pairs={{0,8},{8,0},{1,9},{9,1},{2,10},{10,2},{3,11},{11,3},{4,12},{12,4},... | collective-permute-start | bytes 3538952 | tf_op jit(solution)/shard_map/ppermute | solution.py:246
  29.3 15.6 %collective-permute-start.4 = (bf16[128,1792]{1,0:T(8,128)(2,1)S(1)}, bf16[128,1792]{1,0:T(8,128)(2,1)}, u32[]{:S(2)}, u32[]{:S(2)}) collective-permute-start(bf16[128,1792]{1,0:T(8,128)(2,1)S(1)} %pad_maximum_fusion.1.refs_0_), channel_id=1, source_target_pairs={{0,64},{64,0},{1,65},{65,1},{2,66},{66,2},{3,67},{67,3},{4,68},{68... | collective-permute-start | bytes 1376264 | tf_op jit(solution)/shard_map/ppermute | solution.py:258
  29.6 11.9 %collective-permute-start.6 = (bf16[128,1792]{1,0:T(8,128)(2,1)S(1)}, bf16[128,1792]{1,0:T(8,128)(2,1)}, u32[]{:S(2)}, u32[]{:S(2)}) collective-permute-start(bf16[128,1792]{1,0:T(8,128)(2,1)S(1)} %pad_maximum_fusion.1.refs_0_), channel_id=1, source_target_pairs={{0,48},{16,0},{32,16},{48,32},{1,49},{17,1},{33,17},{49,33},{2,50}... | collective-permute-start | bytes 1376264 | tf_op jit(solution)/shard_map/ppermute | solution.py:257
  35.6 25.1 %collective-permute-start.5 = (bf16[128,1792]{1,0:T(8,128)(2,1)S(1)}, bf16[128,1792]{1,0:T(8,128)(2,1)}, u32[]{:S(2)}, u32[]{:S(2)}) collective-permute-start(bf16[128,1792]{1,0:T(8,128)(2,1)S(1)} %pad_maximum_fusion.1.refs_0_), channel_id=1, source_target_pairs={{0,16},{16,32},{32,48},{48,0},{1,17},{17,33},{33,49},{49,1},{2,18}... | collective-permute-start | bytes 1376264 | tf_op jit(solution)/shard_map/ppermute | solution.py:256
  41.5 16.1 %collective-permute-start.8 = (bf16[128,1792]{1,0:T(8,128)(2,1)}, bf16[128,1792]{1,0:T(8,128)(2,1)S(1)}, u32[]{:S(2)}, u32[]{:S(2)}) collective-permute-start(bf16[128,1792]{1,0:T(8,128)(2,1)} %collective-permute-done.6.refs_3_), channel_id=1, source_target_pairs={{0,64},{64,0},{1,65},{65,1},{2,66},{66,2},{3,67},{67,3},{4,68},{68... | collective-permute-start | bytes 1376264 | tf_op jit(solution)/shard_map/ppermute | solution.py:258
  42.7 18.0 %collective-permute-start.9 = (bf16[128,1792]{1,0:T(8,128)(2,1)}, bf16[128,1792]{1,0:T(8,128)(2,1)}, u32[]{:S(2)}, u32[]{:S(2)}) collective-permute-start(bf16[128,1792]{1,0:T(8,128)(2,1)} %collective-permute-done.6.refs_3_), channel_id=1, source_target_pairs={{0,48},{16,0},{32,16},{48,32},{1,49},{17,1},{33,17},{49,33},{2,50}... | collective-permute-start | bytes 1376264 | tf_op jit(solution)/shard_map/ppermute | solution.py:257
  44.9 12.6 %collective-permute-start.7 = (bf16[128,1792]{1,0:T(8,128)(2,1)}, bf16[128,1792]{1,0:T(8,128)(2,1)S(1)}, u32[]{:S(2)}, u32[]{:S(2)}) collective-permute-start(bf16[128,1792]{1,0:T(8,128)(2,1)} %collective-permute-done.4.refs_1_), channel_id=1, source_target_pairs={{0,16},{16,32},{32,48},{48,0},{1,17},{17,33},{33,49},{49,1},{2,18}... | collective-permute-start | bytes 1376264 | tf_op jit(solution)/shard_map/ppermute | solution.py:256
  55.8 8.1 %collective-permute-start.3 = (bf16[128,1024]{1,0:T(8,128)(2,1)}, bf16[128,1024]{1,0:T(8,128)(2,1)S(1)}, u32[]{:S(2)}, u32[]{:S(2)}) collective-permute-start(bf16[128,1024]{1,0:T(8,128)(2,1)} %shard_map.122.own_ref), channel_id=1, source_target_pairs={{0,8},{8,0},{1,9},{9,1},{2,10},{10,2},{3,11},{11,3},{4,12},{12,4},... | collective-permute-start | bytes 786440 | tf_op jit(solution)/shard_map/ppermute | solution.py:246
  57.5 6.4 %collective-permute-start.10 = (bf16[128,896]{1,0:T(8,128)(2,1)S(1)}, bf16[128,896]{1,0:T(8,128)(2,1)S(1)}, u32[]{:S(2)}, u32[]{:S(2)}) collective-permute-start(bf16[128,896]{1,0:T(8,128)(2,1)S(1)} %slice.87), channel_id=1, source_target_pairs={{0,16},{16,32},{32,48},{48,0},{1,17},{17,33},{33,49},{49,1},{2,18}... | collective-permute-start | bytes 688136 | tf_op jit(solution)/shard_map/ppermute | solution.py:256
  57.6 6.2 %collective-permute-start.11 = (bf16[128,896]{1,0:T(8,128)(2,1)S(1)}, bf16[128,896]{1,0:T(8,128)(2,1)S(1)}, u32[]{:S(2)}, u32[]{:S(2)}) collective-permute-start(bf16[128,896]{1,0:T(8,128)(2,1)S(1)} %slice.88), channel_id=1, source_target_pairs={{0,48},{16,0},{32,16},{48,32},{1,49},{17,1},{33,17},{49,33},{2,50}... | collective-permute-start | bytes 688136 | tf_op jit(solution)/shard_map/ppermute | solution.py:257
  67.5 7.4 %copy-start.15 = (bf16[16,3584]{1,0:T(8,128)(2,1)S(1)}, bf16[16,3584]{1,0:T(8,128)(2,1)}, u32[]{:S(2)}) copy-start(bf16[16,3584]{1,0:T(8,128)(2,1)} %param.15) | copy-start | bytes 344068
  67.5 10.9 %copy-start.18 = (s32[16,8]{0,1:T(8,128)S(1)}, s32[16,8]{0,1:T(8,128)}, u32[]{:S(2)}) copy-start(s32[16,8]{0,1:T(8,128)} %param.17) | copy-start | bytes 1540
  67.5 21.9 %all-to-all-start.1 = ((bf16[8,2,16,1792]{3,2,1,0:T(8,128)(2,1)}), bf16[8,2,16,1792]{3,2,1,0:T(8,128)(2,1)S(1)}, u32[]{:S(2)}, u32[]{:S(2)}) async-start(bf16[8,2,16,1792]{3,2,1,0:T(8,128)(2,1)} %shard_map.123), calls=%async_computation.1 | async-start | bytes 1835008 | tf_op jit(solution)/shard_map/all_to_all | solution.py:329
  74.9 14.7 %collective-permute-start = (bf16[16,1792]{1,0:T(8,128)(2,1)S(1)}, bf16[16,1792]{1,0:T(8,128)(2,1)S(1)}, u32[]{:S(2)}, u32[]{:S(2)}) collective-permute-start(bf16[16,1792]{1,0:T(8,128)(2,1)S(1)} %get-tuple-element.13), channel_id=1, source_target_pairs={{0,8},{8,0},{1,9},{9,1},{2,10},{10,2},{3,11},{11,3},{4,12},{12,4},... | collective-permute-start | bytes 172040 | tf_op jit(solution)/shard_map/ppermute | solution.py:246
  78.4 1.2 collective-permute-start.13
  79.7 0.6 copy-start.12
  80.3 13.1 %copy-start.17 = (f32[3584]{0:T(1024)S(1)}, f32[3584]{0:T(1024)}, u32[]{:S(2)}) copy-start(f32[3584]{0:T(1024)} %param.16) | copy-start | bytes 43012
  89.6 3.4 %collective-permute-start.12 = (bf16[2,16,1792]{2,1,0:T(8,128)(2,1)S(1)}, bf16[2,16,1792]{2,1,0:T(8,128)(2,1)S(1)}, u32[]{:S(2)}, u32[]{:S(2)}) collective-permute-start(bf16[2,16,1792]{2,1,0:T(8,128)(2,1)S(1)} %add_convert_fusion), channel_id=1, source_target_pairs={{0,8},{8,0},{1,9},{9,1},{2,10},{10,2},{3,11},{11,3},{4,12},{12,4},... | collective-permute-start | bytes 344072 | tf_op jit(solution)/shard_map/ppermute | solution.py:246
  97.0 23.3 %all-to-all-start.4 = ((bf16[64,1,2,3584]{3,2,1,0:T(2,128)(2,1)}), bf16[64,1,2,3584]{3,2,1,0:T(2,128)(2,1)S(1)}, u32[]{:S(2)}, u32[]{:S(2)}) async-start(bf16[64,1,2,3584]{3,2,1,0:T(2,128)(2,1)} %bitcast.47), calls=%async_computation.4 | async-start | bytes 1835008 | tf_op jit(solution)/shard_map/all_to_all | solution.py:342
  106.6 1.3 copy-start.5
  120.3 29.5 %all-to-all-start.2 = ((bf16[64,2,2,3584]{3,2,1,0:T(2,128)(2,1)}), bf16[64,2,2,3584]{3,2,1,0:T(2,128)(2,1)S(1)}, u32[]{:S(2)}, u32[]{:S(2)}) async-start(bf16[64,2,2,3584]{3,2,1,0:T(2,128)(2,1)} %bitcast.83), calls=%async_computation.2 | async-start | bytes 3670016 | tf_op jit(solution)/shard_map/all_to_all | solution.py:342
  126.1 2.0 copy-start
  128.2 2.0 copy-start.2
  130.2 2.0 copy-start.4
  136.6 0.9 copy-start.6
  149.7 22.1 %all-to-all-start.5 = ((bf16[64,1,2,3584]{3,2,1,0:T(2,128)(2,1)}), bf16[64,1,2,3584]{3,2,1,0:T(2,128)(2,1)S(1)}, u32[]{:S(2)}, u32[]{:S(2)}) async-start(bf16[64,1,2,3584]{3,2,1,0:T(2,128)(2,1)} %bitcast.85), calls=%async_computation.5 | async-start | bytes 1835008 | tf_op jit(solution)/shard_map/all_to_all | solution.py:342
  157.4 2.0 copy-start.1
  159.4 2.0 copy-start.3
  171.8 0.9 copy-start.7
  172.7 9.0 %copy-start.16 = (s32[16,8]{0,1:T(8,128)S(1)}, s32[16,8]{0,1:T(8,128)}, u32[]{:S(2)}) copy-start(s32[16,8]{0,1:T(8,128)} %param.18) | copy-start | bytes 1540
  172.7 14.2 %copy-start.13 = (s32[2,16,8]{2,1,0:T(8,128)S(1)}, s32[2,16,8]{2,1,0:T(8,128)}, u32[]{:S(2)}) copy-start(s32[2,16,8]{2,1,0:T(8,128)} %copy-done.12) | copy-start | bytes 3076
  172.7 31.6 %copy-start.8 = (bf16[64,1,2,3584]{3,2,1,0:T(2,128)(2,1)S(1)}, bf16[64,1,2,3584]{3,2,1,0:T(2,128)(2,1)}, u32[]{:S(2)}) copy-start(bf16[64,1,2,3584]{3,2,1,0:T(2,128)(2,1)} %copy-done.7) | copy-start | bytes 2752516
  172.7 31.6 %all-to-all-start.3 = ((bf16[64,2,2,3584]{3,2,1,0:T(2,128)(2,1)}), bf16[64,2,2,3584]{3,2,1,0:T(2,128)(2,1)S(1)}, u32[]{:S(2)}, u32[]{:S(2)}) async-start(bf16[64,2,2,3584]{3,2,1,0:T(2,128)(2,1)} %bitcast.42), calls=%async_computation.3 | async-start | bytes 3670016 | tf_op jit(solution)/shard_map/all_to_all | solution.py:342
  182.4 3.8 %collective-permute-start.14 = (f32[16,8]{0,1:T(8,128)}, f32[16,8]{0,1:T(8,128)}, u32[]{:S(2)}, u32[]{:S(2)}) collective-permute-start(f32[16,8]{0,1:T(8,128)} %convert_divide_fusion), channel_id=1, source_target_pairs={{0,8},{8,0},{1,9},{9,1},{2,10},{10,2},{3,11},{11,3},{4,12},{12,4},... | collective-permute-start | bytes 1544 | tf_op jit(solution)/shard_map/ppermute | solution.py:246
  188.2 2.2 %copy-start.10 = (bf16[64,3,2,32]{0,3,2,1:T(8,128)(2,1)}, bf16[64,3,2,32]{0,3,2,1:T(8,128)(2,1)S(1)}, u32[]{:S(2)}) copy-start(bf16[64,3,2,32]{0,3,2,1:T(8,128)(2,1)S(1)} %get-tuple-element.15) | copy-start | bytes 73732
  206.2 5.9 %collective-permute-start.15 = (f32[16,3584]{1,0:T(8,128)S(1)}, f32[16,3584]{1,0:T(8,128)S(1)}, u32[]{:S(2)}, u32[]{:S(2)}) collective-permute-start(f32[16,3584]{1,0:T(8,128)S(1)} %get-tuple-element.7), channel_id=1, source_target_pairs={{0,8},{8,0},{1,9},{9,1},{2,10},{10,2},{3,11},{11,3},{4,12},{12,4},... | collective-permute-start | bytes 688136 | tf_op jit(solution)/shard_map/ppermute | solution.py:246

commit v5 on v4

--- a/solution.py
+++ b/solution.py
@@ -13,7 +13,7 @@
 TOP = 8
 QK = 192
 CAP = 3
-SLOTS = (slice(0, 2), slice(2, 3))
+SLOTS = (slice(0, 3),)
 
 CTX = ("z_lo", "x", "core")
 CTX_CHIPS = ("z_lo", "x")
@@ -27,19 +27,26 @@
 LOG2E = 1.4426950408889634
 
 
-def attend_kernel(ids_ref, q_ref, near_ref, far_ref, w_ref, out_ref, lat_ref, s_ref, p_ref, *, rows, cuts):
+def attend_kernel(order_ref, q_ref, w_ref, *refs, rows, cuts):
+    *piece_refs, out_ref, lat_ref, s_ref, p_ref = refs
     heads = w_ref.shape[1] // (NOPE + VD)
     m = q_ref.shape[0]
-    pairs = near_ref.shape[0]
-    keys = 2 * rows * pairs
+    keys = lat_ref.shape[1]
+    count = len(piece_refs) // 2
 
     @pl.when(pl.program_id(0) == 0)
     def _():
-        for i in range(pairs):
-            lat_ref[:, 2 * i * rows : (2 * i + 1) * rows] = near_ref[i]
-            lat_ref[:, (2 * i + 1) * rows : (2 * i + 2) * rows] = far_ref[i]
-
-    ctx, core = ids_ref[0], ids_ref[1]
+        for side in range(2):
+            for i in range(count - 2):
+                first = (2 * i + side) * rows
+                lat_ref[:, first : first + rows] = piece_refs[side * count + i][...]
+            first = (2 * (count - 2) + side) * rows
+            depth = piece_refs[count - 1].shape[0]
+            lat_ref[:depth, first : first + rows] = piece_refs[side * count + count - 2][...]
+            lat_ref[depth:, first : first + rows] = piece_refs[side * count + count - 1][...]
+
+    core = order_ref[count - 1]
+    ctx = 2 * order_ref[0] + core
     span = keys // cuts
     lane = lax.broadcasted_iota(jnp.int32, (m, rows), 1)
     query = lax.broadcasted_iota(jnp.int32, (m, rows), 0) % rows
@@ -49,7 +56,7 @@
         s = jnp.dot(q_ref[...], lat_ref[:, j * span : (j + 1) * span], preferred_element_type=F32)
         for b in range(span // rows):
             block = j * (span // rows) + b
-            pos = 2 * (block // 2) + (core if block % 2 == 0 else 1 - core)
+            pos = 2 * order_ref[block // 2] + (core if block % 2 == 0 else 1 - core)
             part = s[:, b * rows : (b + 1) * rows]
             part = jnp.where(ahead <= (ctx - pos) * rows, part, F32(-1e30))
             peak = jnp.maximum(peak, part)
@@ -68,21 +75,21 @@
         out_ref[:, h * VD : (h + 1) * VD] = o.astype(BF)
 
 
-def attend(ids, q, near, far, w_kv, group, cuts):
-    pairs, depth, rows = near.shape
+def attend(order, q, w_kv, near, far, group, cuts):
+    depth, rows = near[0].shape
     heads = w_kv.shape[1] // (NOPE + VD)
-    keys = 2 * rows * pairs
+    keys = 2 * rows * (len(near) - 1)
     m = group * rows
+    pieces = (*near, *far)
     return pl.pallas_call(
         functools.partial(attend_kernel, rows=rows, cuts=cuts),
         grid=(heads // group,),
         in_specs=[
             pl.BlockSpec(memory_space=pltpu.SMEM),
             pl.BlockSpec((m, depth), lambda g: (g, 0)),
-            pl.BlockSpec(near.shape, lambda g: (0, 0, 0)),
-            pl.BlockSpec(far.shape, lambda g: (0, 0, 0)),
             pl.BlockSpec((KV_RANK, group * (NOPE + VD)), lambda g: (0, g)),
-        ],
+        ]
+        + [pl.BlockSpec(a.shape, lambda g: (0, 0)) for a in pieces],
         out_specs=pl.BlockSpec((rows, group * VD), lambda g: (0, g)),
         out_shape=jax.ShapeDtypeStruct((rows, heads * VD), BF),
         scratch_shapes=[pltpu.VMEM((depth, keys), BF), pltpu.VMEM((m, keys), F32), pltpu.VMEM((m, keys), BF)],
@@ -92,7 +99,7 @@
             bytes_accessed=8_000_000,
             transcendentals=heads * rows * keys,
         ),
-    )(ids, q, near, far, w_kv)
+    )(order, q, w_kv, *pieces)
 
 
 def expert_kernel(x_ref, g_ref, u_ref, d_ref, out_ref, rows_ref, hid_ref, *, first):
@@ -246,24 +253,34 @@
     return lax.ppermute(mine, "core", SWAP)
 
 
-def gather_w_out(w_out):
-    core, x, z = (lax.axis_index(n) for n in ("core", "x", "z_lo"))
-    half = w_out.shape[1] // 2
-    lower, upper = w_out[:, :half], w_out[:, half:]
-    mine = jnp.where(core == 0, lower, upper)
-    other = swap(jnp.where(core == 0, upper, lower))
-    own = jnp.concatenate([jnp.where(core == 0, mine, other), jnp.where(core == 0, other, mine)], axis=0)
+def gather(own, axis):
     up = lambda a: lax.ppermute(a, "x", [(i, (i + 1) % 4) for i in range(4)])
     down = lambda a: lax.ppermute(a, "x", [(i, (i + 3) % 4) for i in range(4)])
     across = lambda a: lax.ppermute(a, "z_lo", SWAP)
     mate, before, after = across(own), up(own), down(own)
     mate_before, mate_after, opposite = up(mate), across(after), down(after)
-    part = half // 2
-    left, right = up(mate_before[:, :part]), down(mate_after[:, part:])
-    chunks = (own, mate, before, after, mate_before, mate_after, opposite, left, right)
+    half = own.shape[axis] // 2
+    left = up(lax.slice_in_dim(mate_before, 0, half, axis=axis))
+    right = down(lax.slice_in_dim(mate_after, half, 2 * half, axis=axis))
+    return own, mate, before, after, mate_before, mate_after, opposite, left, right
+
+
+def chip_order():
+    core, x, z = (lax.axis_index(n) for n in ("core", "x", "z_lo"))
     chip = lambda zz, dx: zz * 4 + lax.rem(x + 4 + dx, 4)
-    order = (chip(z, 0), chip(1 - z, 0), chip(z, -1), chip(z, 1), chip(1 - z, -1), chip(1 - z, 1), chip(z, 2), chip(1 - z, 2))
-    return own, jnp.stack(order).astype(jnp.int32), chunks
+    near, far = z, 1 - z
+    order = [chip(near, 0), chip(far, 0), chip(near, -1), chip(near, 1)]
+    order += [chip(far, -1), chip(far, 1), chip(near, 2), chip(far, 2), core]
+    return jnp.stack(order).astype(jnp.int32)
+
+
+def own_w_out(w_out):
+    core = lax.axis_index("core")
+    half = w_out.shape[1] // 2
+    lower, upper = w_out[:, :half], w_out[:, half:]
+    mine = jnp.where(core == 0, lower, upper)
+    other = swap(jnp.where(core == 0, upper, lower))
+    return jnp.concatenate([jnp.where(core == 0, mine, other), jnp.where(core == 0, other, mine)], axis=0)
 
 
 def latent_queries(queries, w_kv):
@@ -314,14 +331,11 @@
     tok, width = resid.shape
     chips = 64
     core = lax.axis_index("core")
-    own_rows, order, chunks = gather_w_out(w_out)
-    latents, _ = lax.optimization_barrier((latents, own_rows))
-    near = lax.all_to_all(
-        jnp.broadcast_to(latents[None], (8,) + latents.shape), CTX_CHIPS, split_axis=0, concat_axis=0, tiled=True
-    )
-    far = swap(near)
-    ids = jnp.stack([lax.axis_index(CTX), core]).astype(jnp.int32)
-    heads_out = attend(ids, latent_queries(queries, w_kv), near, far, w_kv, 4, 4)
+    order = chip_order()
+    near = gather(latents, 0)
+    far = [swap(a) for a in near]
+    chunks = gather(own_w_out(w_out), 1)
+    heads_out = attend(order, latent_queries(queries, w_kv), w_kv, near, far, 4, 4)
     half = width // 2
     lower, upper = resid[:, :half], resid[:, half:]
     resid2 = jnp.stack([jnp.where(core == 0, lower, upper), swap(jnp.where(core == 0, upper, lower))])

time: 214 us -> 211 us (0.986)
  blocking collectives: 22.4 us -> 41.3 us
  starting transfers between devices: 63.4 us -> 50.2 us
  Pallas kernels: 35.7 us -> 27 us
  local copies, waits for them, and re-layouts: 22.2 us -> 16.7 us
  waiting for transfers between devices: 57 us -> 62.4 us
  other arithmetic: 9.47 us -> 6.89 us
    all_to_all x4 -> x1, starting transfers between devices: 30.2 us -> 7.44 us  [exchange(): lax.all_to_all(units, CHIPS, split_axis=0, concat_axis=0, tiled=True)]
    all_to_all x1, blocking collectives: 22.4 us -> 41.3 us  [exchange(): lax.all_to_all(units, CHIPS, split_axis=0, concat_axis=0, tiled=True)]
    ppermute x8 -> x16, waiting for transfers between devices: 8.77 us -> 20.6 us  [the longest x6 17.8 us: gather(): up = lambda a: lax.ppermute(a, 'x', [(i, (i + 1) % 4) for i in range(4)])]
    ppermute x8 -> x16, starting transfers between devices: 8.27 us -> 18.3 us  [the longest x6 13.2 us: gather(): down = lambda a: lax.ppermute(a, 'x', [(i, (i + 3) % 4) for i in range(4)])]
    all_to_all x4 -> x1, waiting for transfers between devices: 36 us -> 27.6 us  [exchange(): lax.all_to_all(units, CHIPS, split_axis=0, concat_axis=0, tiled=True)]
    unnamed x42 -> x37, local copies, waits for them, and re-layouts: 16.4 us -> 9.14 us
    pallas_call x2 -> x1, Pallas kernels: 13.9 us -> 10 us  [expert(): pl.pallas_call(functools.partial(expert_kernel, first=first), grid=(first...]
    all_to_all x1, waiting for transfers between devices: 9.17 us -> 12.2 us  [local(): attn = lax.all_to_all(attn, EP, split_axis=0, concat_axis=0, tiled=True)]
  transfers between devices with their start and end apart: 21 -> 34, of which waited for: 11 -> 12; matrix products, arithmetic and copies ran while one was open for 8% -> 10% of each run, Pallas kernels for 13% -> 5%
where the time goes in v5:
time: 211 us; the launch traced here: 208 us
  waiting for transfers between devices  62.4 us (30%)
  starting transfers between devices  50.2 us (24%)
  blocking collectives  41.3 us (20%)
  Pallas kernels  27 us (13%)
  local copies, waits for them, and re-layouts  16.7 us (8%)
  other arithmetic  6.89 us (3%)
  matrix products  2.78 us (1%)
    all_to_all x1, blocking collectives, exchange(): lax.all_to_all(units, CHIPS, split_axis=0, concat_axis=0, tiled=True)  41.3 us
    all_to_all x1, waiting for transfers between devices, exchange(): lax.all_to_all(units, CHIPS, split_axis=0, concat_axis=0, tiled=True)  27.6 us
    ppermute x6, waiting for transfers between devices, gather(): up = lambda a: lax.ppermute(a, 'x', [(i, (i + 1) % 4) for i in range(4)])  17.8 us
    ppermute x16, starting transfers between devices, swap(): return lax.ppermute(mine, 'core', SWAP)  17.1 us
    ppermute x6, starting transfers between devices, gather(): down = lambda a: lax.ppermute(a, 'x', [(i, (i + 3) % 4) for i in range(4)])  13.2 us
    all_to_all x1, waiting for transfers between devices, local(): attn = lax.all_to_all(attn, EP, split_axis=0, concat_axis=0, tiled=True)  12.2 us
    pallas_call x1, Pallas kernels, attend(): pl.pallas_call(functools.partial(attend_kernel, rows=rows, cuts=cuts), gr...  10.1 us
    pallas_call x1, Pallas kernels, expert(): pl.pallas_call(functools.partial(expert_kernel, first=first), grid=(first...  10 us
  transfers between devices with their start and end apart: 34, of which 12 were waited for; matrix products, arithmetic and copies ran while one was open for 10% of the time, Pallas kernels for 5%

profile of v5, /device:TPU:1, one launch (start us, length us, event | category | flops | bytes accessed | tf_op | source)
XLA Modules:
  0.0 208.4 jit_solution(1566218226619067704)
XLA Ops:
  0.6 1.2 broadcast_select_fusion.2
  1.9 1.5 collective-permute-start.19
  3.4 2.6 %collective-permute-start.3 = (bf16[576,128]{1,0:T(8,128)(2,1)}, bf16[576,128]{1,0:T(8,128)(2,1)}, u32[]{:S(2)}, u32[]{:S(2)}) collective-permute-start(bf16[576,128]{1,0:T(8,128)(2,1)} %refs_0_.1), channel_id=1, source_target_pairs={{0,48},{16,0},{32,16},{48,32},{1,49},{17,1},{33,17},{49,33},{2,50}... | collective-permute-start | bytes 442376 | tf_op jit(solution)/shard_map/ppermute | solution.py:258
  6.0 1.6 collective-permute-start.1
  7.6 0.6 collective-permute-start.9
  8.2 1.2 collective-permute-done.3.refs_3_
  9.5 1.6 collective-permute-start.5
  11.1 0.6 collective-permute-done.1.refs_1_
  11.7 2.8 %collective-permute-start.6 = (bf16[576,128]{1,0:T(8,128)(2,1)}, bf16[576,128]{1,0:T(8,128)(2,1)}, u32[]{:S(2)}, u32[]{:S(2)}) collective-permute-start(bf16[576,128]{1,0:T(8,128)(2,1)} %collective-permute-done.3.refs_3_), channel_id=1, source_target_pairs={{0,48},{16,0},{32,16},{48,32},{1,49},{17,1},{33,17},{49,33},{2,50}... | collective-permute-start | bytes 442376 | tf_op jit(solution)/shard_map/ppermute | solution.py:258
  14.5 1.1 broadcast_select_fusion.1
  15.6 4.1 %collective-permute-done.4.refs_4_ = bf16[576,128]{1,0:T(8,128)(2,1)S(1)} collective-permute-done((bf16[576,128]{1,0:T(8,128)(2,1)S(1)}, bf16[576,128]{1,0:T(8,128)(2,1)S(1)}, u32[]{:S(2)}, u32[]{:S(2)}) %collective-permute-start.4) | collective-permute-done | bytes 147488 | tf_op jit(solution)/shard_map/ppermute | solution.py:257
  19.7 2.6 %collective-permute-start.10 = (bf16[576,128]{1,0:T(8,128)(2,1)S(1)}, bf16[576,128]{1,0:T(8,128)(2,1)S(1)}, u32[]{:S(2)}, u32[]{:S(2)}) collective-permute-start(bf16[576,128]{1,0:T(8,128)(2,1)S(1)} %collective-permute-done.1.refs_1_), channel_id=1, source_target_pairs={{0,8},{8,0},{1,9},{9,1},{2,10},{10,2},{3,11},{11,3},{4,12},{12,4},... | collective-permute-start | bytes 442376 | tf_op jit(solution)/shard_map/ppermute | solution.py:253
  22.3 0.6 slice.79
  23.0 0.7 copy-done.9
  23.7 0.4 collective-permute-start.11
  24.2 2.7 %collective-permute-start.22 = (bf16[128,1792]{1,0:T(8,128)(2,1)S(1)}, bf16[128,1792]{1,0:T(8,128)(2,1)S(1)}, u32[]{:S(2)}, u32[]{:S(2)}) collective-permute-start(bf16[128,1792]{1,0:T(8,128)(2,1)S(1)} %pad_maximum_fusion.1.refs_0_), channel_id=1, source_target_pairs={{0,48},{16,0},{32,16},{48,32},{1,49},{17,1},{33,17},{49,33},{2,50}... | collective-permute-start | bytes 1376264 | tf_op jit(solution)/shard_map/ppermute | solution.py:258
  26.9 0.7 copy-done.11
  27.6 1.9 copy.45
  29.5 2.5 %copy.47 = bf16[512,2048]{0,1:T(8,128)(2,1)} copy(bf16[512,2048]{1,0:T(8,128)(2,1)S(1)} %copy-done.3) | data formatting | bytes 4194304 | tf_op args[2]
  32.1 1.5 slice.80
  33.6 0.8 collective-permute-start.13
  34.5 2.8 %convolution_convert_fusion = bf16[8,128,512]{2,1,0:T(8,128)(2,1)} fusion(bf16[512,8,256]{0,2,1:T(8,128)(2,1)} %bitcast.68, bf16[128,8,192]{0,2,1:T(8,128)(2,1)} %bitcast.70), kind=kOutput, calls=%fused_computation.1 | convolution fusion | flops 134742016 | bytes 2359296 | tf_op jit(solution)/shard_map/qhd,rhd->hqr/dot_general | solution.py:291
  37.3 0.9 collective-permute-done.8.refs_8_
  38.2 1.2 collective-permute-start.15
  39.4 1.6 slice.78
  40.9 1.8 copy.63
  42.9 0.5 collective-permute-start.17
  43.4 1.4 pad_maximum_fusion
  44.9 1.6 collective-permute-start.24
  46.6 2.3 %collective-permute-start.25 = (bf16[128,1792]{1,0:T(8,128)(2,1)S(1)}, bf16[128,1792]{1,0:T(8,128)(2,1)S(1)}, u32[]{:S(2)}, u32[]{:S(2)}) collective-permute-start(bf16[128,1792]{1,0:T(8,128)(2,1)S(1)} %collective-permute-done.22.refs_3_), channel_id=1, source_target_pairs={{0,48},{16,0},{32,16},{48,32},{1,49},{17,1},{33,17},{49,33},{2,50}... | collective-permute-start | bytes 1376264 | tf_op jit(solution)/shard_map/ppermute | solution.py:258
  48.9 10.1 %shard_map.122.own_ref = bf16[128,1024]{1,0:T(8,128)(2,1)S(1)} custom-call(s32[9]{0:T(128)S(1)} %stack.69.order_ref, bf16[1024,576]{1,0:T(8,128)(2,1)S(1)} %bitcast.67, bf16[512,2048]{1,0:T(8,128)(2,1)S(1)} %copy-done.3, bf16[576,128]{1,0:T(8,128)(2,1)S(1)} %copy-done.6, bf16[576,128]{1,0:T(8,128)(2,1)S(1)} %copy-done.8, ...), custom_call_target="tpu_custom_call" | custom-call | flops 4563402752 | bytes 8000000 | tf_op jit(solution)/shard_map/pallas_call | solution.py:84
  59.1 1.0 collective-permute-start.18
  60.1 8.9 %collective-permute-done.23.refs_4_ = bf16[128,1792]{1,0:T(8,128)(2,1)S(1)} collective-permute-done((bf16[128,1792]{1,0:T(8,128)(2,1)S(1)}, bf16[128,1792]{1,0:T(8,128)(2,1)S(1)}, u32[]{:S(2)}, u32[]{:S(2)}) %collective-permute-start.23) | collective-permute-done | bytes 458784 | tf_op jit(solution)/shard_map/ppermute | solution.py:257
  69.1 2.7 %collective-permute-start.27 = (bf16[128,896]{1,0:T(8,128)(2,1)S(1)}, bf16[128,896]{1,0:T(8,128)(2,1)S(1)}, u32[]{:S(2)}, u32[]{:S(2)}) collective-permute-start(bf16[128,896]{1,0:T(8,128)(2,1)S(1)} %slice.82), channel_id=1, source_target_pairs={{0,48},{16,0},{32,16},{48,32},{1,49},{17,1},{33,17},{49,33},{2,50}... | collective-permute-start | bytes 688136 | tf_op jit(solution)/shard_map/ppermute | solution.py:258
  71.8 4.9 %collective-permute-done.26.refs_7_ = bf16[128,896]{1,0:T(8,128)(2,1)S(1)} collective-permute-done((bf16[128,896]{1,0:T(8,128)(2,1)S(1)}, bf16[128,896]{1,0:T(8,128)(2,1)S(1)}, u32[]{:S(2)}, u32[]{:S(2)}) %collective-permute-start.26) | collective-permute-done | bytes 229408 | tf_op jit(solution)/shard_map/ppermute | solution.py:257
  76.7 2.7 %shard_map.123 = bf16[8,2,16,1792]{3,2,1,0:T(8,128)(2,1)} custom-call(s32[9]{0:T(128)S(1)} %stack.69.order_ref, bf16[128,1024]{1,0:T(8,128)(2,1)S(1)} %shard_map.122.own_ref, bf16[128,1024]{1,0:T(8,128)(2,1)S(1)} %collective-permute-done.18.far_ref, bf16[128,1792]{1,0:T(8,128)(2,1)S(1)} %pad_maximum_fusion.1.refs_0_, ...), custom_call_target="tpu_custom_call" | custom-call | flops 939524096 | bytes 3670016 | tf_op jit(solution)/shard_map/pallas_call | solution.py:239
  79.4 7.3 %all-to-all-start = ((bf16[8,2,16,1792]{3,2,1,0:T(8,128)(2,1)}), bf16[8,2,16,1792]{3,2,1,0:T(8,128)(2,1)S(1)}, u32[]{:S(2)}, u32[]{:S(2)}) async-start(bf16[8,2,16,1792]{3,2,1,0:T(8,128)(2,1)} %shard_map.123), calls=%async_computation | async-start | bytes 1835008 | tf_op jit(solution)/shard_map/all_to_all | solution.py:343
  86.8 1.9 collective-permute-start
  88.9 0.9 collective-permute-done.29
  89.9 0.1 fusion.8
  90.4 12.2 %all-to-all-done = bf16[8,2,16,1792]{3,2,1,0:T(8,128)(2,1)S(1)} async-done(((bf16[8,2,16,1792]{3,2,1,0:T(8,128)(2,1)}), bf16[8,2,16,1792]{3,2,1,0:T(8,128)(2,1)S(1)}, u32[]{:S(2)}, u32[]{:S(2)}) %all-to-all-start) | async-done | bytes 917536 | tf_op jit(solution)/shard_map/all_to_all | solution.py:343
  102.6 0.1 convert_reduce_fusion
  102.8 0.9 collective-permute-start.28
  103.8 0.1 copy.54
  104.2 0.5 collective-permute-done.28
  104.8 0.1 multiply_reduce_fusion
  105.0 0.1 fusion.2.x_ref
  105.2 2.2 %shard_map.124 = bf16[192,2,3584]{2,1,0:T(2,128)(2,1)S(1)} custom-call(bf16[384,32]{1,0:T(8,128)(2,1)S(1)} %convert_element_type.52.place_ref, bf16[32,3584]{1,0:T(8,128)(2,1)S(1)} %fusion.2.x_ref), custom_call_target="tpu_custom_call" | custom-call | flops 88080384 | bytes 2981888 | tf_op jit(solution)/shard_map/pallas_call | solution.py:164
  107.4 41.3 %all_to_all.15 = bf16[64,3,2,3584]{3,2,1,0:T(2,128)(2,1)S(1)} all-to-all(bf16[64,3,2,3584]{3,2,1,0:T(2,128)(2,1)S(1)} %bitcast.62), channel_id=1, replica_groups=mesh['z_lo'=2,'x'=4,'core'=2,'z_hi'=2,'y'=4] {'z_lo','x','z_hi','y'}, dimensions={0} | all-to-all | bytes 5505024 | tf_op jit(solution)/shard_map/all_to_all | solution.py:356
  148.8 10.0 %shard_map.125 = bf16[192,2,3584]{2,1,0:T(2,128)(2,1)S(1)} custom-call(bf16[192,2,3584]{2,1,0:T(2,128)(2,1)S(1)} %bitcast.64, bf16[3584,512]{1,0:T(8,128)(2,1)S(1)} %bitcast.65, bf16[3584,512]{1,0:T(8,128)(2,1)S(1)} %bitcast.66, bf16[512,3584]{1,0:T(8,128)(2,1)} %bitcast.69), custom_call_target="tpu_custom_call" | custom-call | flops 4227858432 | bytes 17000000 | tf_op jit(solution)/shard_map/pallas_call | solution.py:136
  158.8 1.5 copy-done
  160.3 7.4 %all-to-all-start.2 = ((bf16[64,3,2,3584]{3,2,1,0:T(2,128)(2,1)}), bf16[64,3,2,3584]{3,2,1,0:T(2,128)(2,1)S(1)}, u32[]{:S(2)}, u32[]{:S(2)}) async-start(bf16[64,3,2,3584]{3,2,1,0:T(2,128)(2,1)} %bitcast.63), calls=%async_computation.2 | async-start | bytes 5505024 | tf_op jit(solution)/shard_map/all_to_all | solution.py:356
  167.8 1.6 collective-permute-start.30
  169.4 0.7 copy.59
  170.3 0.1 select_reduce_fusion
  170.8 0.7 broadcast_in_dim.58
  171.5 1.0 copy.60
  172.5 0.7 reduce-precision_convert_fusion
  173.3 27.6 %all-to-all-done.2 = bf16[64,3,2,3584]{3,2,1,0:T(2,128)(2,1)S(1)} async-done(((bf16[64,3,2,3584]{3,2,1,0:T(2,128)(2,1)}), bf16[64,3,2,3584]{3,2,1,0:T(2,128)(2,1)S(1)}, u32[]{:S(2)}, u32[]{:S(2)}) %all-to-all-start.2) | async-done | bytes 2752544 | tf_op jit(solution)/shard_map/all_to_all | solution.py:356
  200.9 1.9 shard_map.126
  202.8 3.7 %collective-permute-start.31 = (f32[16,3584]{1,0:T(8,128)S(1)}, f32[16,3584]{1,0:T(8,128)S(1)}, u32[]{:S(2)}, u32[]{:S(2)}) collective-permute-start(f32[16,3584]{1,0:T(8,128)S(1)} %get-tuple-element.5), channel_id=1, source_target_pairs={{0,8},{8,0},{1,9},{9,1},{2,10},{10,2},{3,11},{11,3},{4,12},{12,4},... | collective-permute-start | bytes 688136 | tf_op jit(solution)/shard_map/ppermute | solution.py:253
  206.6 0.7 fusion.10
  207.2 0.5 collective-permute-done.31
  207.7 0.7 fusion.7
  (104 shorter events, 2.4 us)
Async XLA Ops:
  0.6 28.9 %copy-start.3 = (bf16[512,2048]{1,0:T(8,128)(2,1)S(1)}, bf16[512,2048]{1,0:T(8,128)(2,1)}, u32[]{:S(2)}) copy-start(bf16[512,2048]{1,0:T(8,128)(2,1)} %w_ref.1) | copy-start | bytes 6291460
  1.9 12.7 %collective-permute-start.19 = (bf16[64,1792]{1,0:T(8,128)(2,1)S(1)}, bf16[64,1792]{1,0:T(8,128)(2,1)S(1)}, u32[]{:S(2)}, u32[]{:S(2)}) collective-permute-start(bf16[64,1792]{1,0:T(8,128)(2,1)S(1)} %broadcast_select_fusion.2), channel_id=1, source_target_pairs={{0,8},{8,0},{1,9},{9,1},{2,10},{10,2},{3,11},{11,3},{4,12},{12,4},... | collective-permute-start | bytes 688136 | tf_op jit(solution)/shard_map/ppermute | solution.py:253
  3.4 6.1 %collective-permute-start.3 = (bf16[576,128]{1,0:T(8,128)(2,1)}, bf16[576,128]{1,0:T(8,128)(2,1)}, u32[]{:S(2)}, u32[]{:S(2)}) collective-permute-start(bf16[576,128]{1,0:T(8,128)(2,1)} %refs_0_.1), channel_id=1, source_target_pairs={{0,48},{16,0},{32,16},{48,32},{1,49},{17,1},{33,17},{49,33},{2,50}... | collective-permute-start | bytes 442376 | tf_op jit(solution)/shard_map/ppermute | solution.py:258
  6.0 5.7 %collective-permute-start.1 = (bf16[576,128]{1,0:T(8,128)(2,1)}, bf16[576,128]{1,0:T(8,128)(2,1)S(1)}, u32[]{:S(2)}, u32[]{:S(2)}) collective-permute-start(bf16[576,128]{1,0:T(8,128)(2,1)} %refs_0_.1), channel_id=1, source_target_pairs={{0,64},{64,0},{1,65},{65,1},{2,66},{66,2},{3,67},{67,3},{4,68},{68... | collective-permute-start | bytes 442376 | tf_op jit(solution)/shard_map/ppermute | solution.py:259
  7.6 15.4 %collective-permute-start.2 = (bf16[576,128]{1,0:T(8,128)(2,1)}, bf16[576,128]{1,0:T(8,128)(2,1)}, u32[]{:S(2)}, u32[]{:S(2)}) collective-permute-start(bf16[576,128]{1,0:T(8,128)(2,1)} %refs_0_.1), channel_id=1, source_target_pairs={{0,16},{16,32},{32,48},{48,0},{1,17},{17,33},{33,49},{49,1},{2,18}... | collective-permute-start | bytes 442376 | tf_op jit(solution)/shard_map/ppermute | solution.py:257
  7.6 15.4 %collective-permute-start.9 = (bf16[576,128]{1,0:T(8,128)(2,1)}, bf16[576,128]{1,0:T(8,128)(2,1)S(1)}, u32[]{:S(2)}, u32[]{:S(2)}) collective-permute-start(bf16[576,128]{1,0:T(8,128)(2,1)} %refs_0_.1), channel_id=1, source_target_pairs={{0,8},{8,0},{1,9},{9,1},{2,10},{10,2},{3,11},{11,3},{4,12},{12,4},... | collective-permute-start | bytes 442376 | tf_op jit(solution)/shard_map/ppermute | solution.py:253
  9.5 14.7 %collective-permute-start.5 = (bf16[576,128]{1,0:T(8,128)(2,1)}, bf16[576,128]{1,0:T(8,128)(2,1)}, u32[]{:S(2)}, u32[]{:S(2)}) collective-permute-start(bf16[576,128]{1,0:T(8,128)(2,1)} %collective-permute-done.3.refs_3_), channel_id=1, source_target_pairs={{0,64},{64,0},{1,65},{65,1},{2,66},{66,2},{3,67},{67,3},{4,68},{68... | collective-permute-start | bytes 442376 | tf_op jit(solution)/shard_map/ppermute | solution.py:259
  11.7 15.2 %copy-start.7 = (bf16[576,128]{1,0:T(8,128)(2,1)}, bf16[576,128]{1,0:T(8,128)(2,1)S(1)}, u32[]{:S(2)}) copy-start(bf16[576,128]{1,0:T(8,128)(2,1)S(1)} %collective-permute-done.1.refs_1_) | copy-start | bytes 442372
  11.7 12.5 %collective-permute-start.6 = (bf16[576,128]{1,0:T(8,128)(2,1)}, bf16[576,128]{1,0:T(8,128)(2,1)}, u32[]{:S(2)}, u32[]{:S(2)}) collective-permute-start(bf16[576,128]{1,0:T(8,128)(2,1)} %collective-permute-done.3.refs_3_), channel_id=1, source_target_pairs={{0,48},{16,0},{32,16},{48,32},{1,49},{17,1},{33,17},{49,33},{2,50}... | collective-permute-start | bytes 442376 | tf_op jit(solution)/shard_map/ppermute | solution.py:258
  14.5 5.2 %collective-permute-start.4 = (bf16[576,128]{1,0:T(8,128)(2,1)S(1)}, bf16[576,128]{1,0:T(8,128)(2,1)S(1)}, u32[]{:S(2)}, u32[]{:S(2)}) collective-permute-start(bf16[576,128]{1,0:T(8,128)(2,1)S(1)} %collective-permute-done.1.refs_1_), channel_id=1, source_target_pairs={{0,16},{16,32},{32,48},{48,0},{1,17},{17,33},{33,49},{49,1},{2,18}... | collective-permute-start | bytes 442376 | tf_op jit(solution)/shard_map/ppermute | solution.py:257
  19.7 4.4 %copy-start.4 = (bf16[576,128]{1,0:T(8,128)(2,1)}, bf16[576,128]{1,0:T(8,128)(2,1)S(1)}, u32[]{:S(2)}) copy-start(bf16[576,128]{1,0:T(8,128)(2,1)S(1)} %collective-permute-done.4.refs_4_) | copy-start | bytes 442372
  19.7 7.2 %collective-permute-start.10 = (bf16[576,128]{1,0:T(8,128)(2,1)S(1)}, bf16[576,128]{1,0:T(8,128)(2,1)S(1)}, u32[]{:S(2)}, u32[]{:S(2)}) collective-permute-start(bf16[576,128]{1,0:T(8,128)(2,1)S(1)} %collective-permute-done.1.refs_1_), channel_id=1, source_target_pairs={{0,8},{8,0},{1,9},{9,1},{2,10},{10,2},{3,11},{11,3},{4,12},{12,4},... | collective-permute-start | bytes 442376 | tf_op jit(solution)/shard_map/ppermute | solution.py:253
  22.9 10.7 %collective-permute-start.12 = (bf16[576,128]{1,0:T(8,128)(2,1)}, bf16[576,128]{1,0:T(8,128)(2,1)}, u32[]{:S(2)}, u32[]{:S(2)}) collective-permute-start(bf16[576,128]{1,0:T(8,128)(2,1)} %collective-permute-done.3.refs_3_), channel_id=1, source_target_pairs={{0,8},{8,0},{1,9},{9,1},{2,10},{10,2},{3,11},{11,3},{4,12},{12,4},... | collective-permute-start | bytes 442376 | tf_op jit(solution)/shard_map/ppermute | solution.py:253
  23.0 0.7 copy-start.9
  23.7 9.9 %collective-permute-start.11 = (bf16[576,128]{1,0:T(8,128)(2,1)}, bf16[576,128]{1,0:T(8,128)(2,1)}, u32[]{:S(2)}, u32[]{:S(2)}) collective-permute-start(bf16[576,128]{1,0:T(8,128)(2,1)} %collective-permute-done.2.refs_2_), channel_id=1, source_target_pairs={{0,8},{8,0},{1,9},{9,1},{2,10},{10,2},{3,11},{11,3},{4,12},{12,4},... | collective-permute-start | bytes 442376 | tf_op jit(solution)/shard_map/ppermute | solution.py:253
  24.1 10.3 %collective-permute-start.7 = (bf16[288,128]{1,0:T(8,128)(2,1)}, bf16[288,128]{1,0:T(8,128)(2,1)S(1)}, u32[]{:S(2)}, u32[]{:S(2)}) collective-permute-start(bf16[288,128]{1,0:T(8,128)(2,1)} %slice.79), channel_id=1, source_target_pairs={{0,16},{16,32},{32,48},{48,0},{1,17},{17,33},{33,49},{49,1},{2,18}... | collective-permute-start | bytes 221192 | tf_op jit(solution)/shard_map/ppermute | solution.py:257
  24.2 20.7 %collective-permute-start.22 = (bf16[128,1792]{1,0:T(8,128)(2,1)S(1)}, bf16[128,1792]{1,0:T(8,128)(2,1)S(1)}, u32[]{:S(2)}, u32[]{:S(2)}) collective-permute-start(bf16[128,1792]{1,0:T(8,128)(2,1)S(1)} %pad_maximum_fusion.1.refs_0_), channel_id=1, source_target_pairs={{0,48},{16,0},{32,16},{48,32},{1,49},{17,1},{33,17},{49,33},{2,50}... | collective-permute-start | bytes 1376264 | tf_op jit(solution)/shard_map/ppermute | solution.py:258
  26.9 0.7 copy-start.11
  27.6 21.3 %collective-permute-start.20 = (bf16[128,1792]{1,0:T(8,128)(2,1)S(1)}, bf16[128,1792]{1,0:T(8,128)(2,1)S(1)}, u32[]{:S(2)}, u32[]{:S(2)}) collective-permute-start(bf16[128,1792]{1,0:T(8,128)(2,1)S(1)} %pad_maximum_fusion.1.refs_0_), channel_id=1, source_target_pairs={{0,64},{64,0},{1,65},{65,1},{2,66},{66,2},{3,67},{67,3},{4,68},{68... | collective-permute-start | bytes 1376264 | tf_op jit(solution)/shard_map/ppermute | solution.py:259
  33.6 4.6 %collective-permute-start.8 = (bf16[288,128]{1,0:T(8,128)(2,1)}, bf16[288,128]{1,0:T(8,128)(2,1)}, u32[]{:S(2)}, u32[]{:S(2)}) collective-permute-start(bf16[288,128]{1,0:T(8,128)(2,1)} %slice.80), channel_id=1, source_target_pairs={{0,48},{16,0},{32,16},{48,32},{1,49},{17,1},{33,17},{49,33},{2,50}... | collective-permute-start | bytes 221192 | tf_op jit(solution)/shard_map/ppermute | solution.py:258
  33.6 9.2 %collective-permute-start.13 = (bf16[576,128]{1,0:T(8,128)(2,1)}, bf16[576,128]{1,0:T(8,128)(2,1)}, u32[]{:S(2)}, u32[]{:S(2)}) collective-permute-start(bf16[576,128]{1,0:T(8,128)(2,1)} %copy-done.4), channel_id=1, source_target_pairs={{0,8},{8,0},{1,9},{9,1},{2,10},{10,2},{3,11},{11,3},{4,12},{12,4},... | collective-permute-start | bytes 442376 | tf_op jit(solution)/shard_map/ppermute | solution.py:253
  34.4 8.5 %collective-permute-start.14 = (bf16[576,128]{1,0:T(8,128)(2,1)}, bf16[576,128]{1,0:T(8,128)(2,1)}, u32[]{:S(2)}, u32[]{:S(2)}) collective-permute-start(bf16[576,128]{1,0:T(8,128)(2,1)} %collective-permute-done.5.refs_5_), channel_id=1, source_target_pairs={{0,8},{8,0},{1,9},{9,1},{2,10},{10,2},{3,11},{11,3},{4,12},{12,4},... | collective-permute-start | bytes 442376 | tf_op jit(solution)/shard_map/ppermute | solution.py:253
  38.2 6.6 %collective-permute-start.15 = (bf16[576,128]{1,0:T(8,128)(2,1)}, bf16[576,128]{1,0:T(8,128)(2,1)}, u32[]{:S(2)}, u32[]{:S(2)}) collective-permute-start(bf16[576,128]{1,0:T(8,128)(2,1)} %collective-permute-done.6.refs_6_), channel_id=1, source_target_pairs={{0,8},{8,0},{1,9},{9,1},{2,10},{10,2},{3,11},{11,3},{4,12},{12,4},... | collective-permute-start | bytes 442376 | tf_op jit(solution)/shard_map/ppermute | solution.py:253
  42.7 6.1 %copy-start.5 = (bf16[576,128]{1,0:T(8,128)(2,1)S(1)}, bf16[576,128]{1,0:T(8,128)(2,1)}, u32[]{:S(2)}) copy-start(bf16[576,128]{1,0:T(8,128)(2,1)} %copy-done.4) | copy-start | bytes 442372
  42.7 6.2 %copy-start.6 = (bf16[576,128]{1,0:T(8,128)(2,1)S(1)}, bf16[576,128]{1,0:T(8,128)(2,1)}, u32[]{:S(2)}) copy-start(bf16[576,128]{1,0:T(8,128)(2,1)} %refs_0_.1) | copy-start | bytes 442372
  42.8 6.2 %copy-start.8 = (bf16[576,128]{1,0:T(8,128)(2,1)S(1)}, bf16[576,128]{1,0:T(8,128)(2,1)}, u32[]{:S(2)}) copy-start(bf16[576,128]{1,0:T(8,128)(2,1)} %copy-done.7) | copy-start | bytes 442372
  42.8 6.2 %copy-start.10 = (bf16[576,128]{1,0:T(8,128)(2,1)S(1)}, bf16[576,128]{1,0:T(8,128)(2,1)}, u32[]{:S(2)}) copy-start(bf16[576,128]{1,0:T(8,128)(2,1)} %copy-done.9) | copy-start | bytes 442372
  42.8 6.2 %copy-start.12 = (bf16[576,128]{1,0:T(8,128)(2,1)S(1)}, bf16[576,128]{1,0:T(8,128)(2,1)}, u32[]{:S(2)}) copy-start(bf16[576,128]{1,0:T(8,128)(2,1)} %copy-done.11) | copy-start | bytes 442372
  42.8 3.8 %collective-permute-start.16 = (bf16[288,128]{1,0:T(8,128)(2,1)S(1)}, bf16[288,128]{1,0:T(8,128)(2,1)S(1)}, u32[]{:S(2)}, u32[]{:S(2)}) collective-permute-start(bf16[288,128]{1,0:T(8,128)(2,1)S(1)} %collective-permute-done.7.refs_7_), channel_id=1, source_target_pairs={{0,8},{8,0},{1,9},{9,1},{2,10},{10,2},{3,11},{11,3},{4,12},{12,4},... | collective-permute-start | bytes 221192 | tf_op jit(solution)/shard_map/ppermute | solution.py:253
  42.9 6.0 %collective-permute-start.17 = (bf16[288,128]{1,0:T(8,128)(2,1)}, bf16[288,128]{1,0:T(8,128)(2,1)S(1)}, u32[]{:S(2)}, u32[]{:S(2)}) collective-permute-start(bf16[288,128]{1,0:T(8,128)(2,1)} %collective-permute-done.8.refs_8_), channel_id=1, source_target_pairs={{0,8},{8,0},{1,9},{9,1},{2,10},{10,2},{3,11},{11,3},{4,12},{12,4},... | collective-permute-start | bytes 221192 | tf_op jit(solution)/shard_map/ppermute | solution.py:253
  44.8 27.0 %collective-permute-start.21 = (bf16[128,1792]{1,0:T(8,128)(2,1)S(1)}, bf16[128,1792]{1,0:T(8,128)(2,1)S(1)}, u32[]{:S(2)}, u32[]{:S(2)}) collective-permute-start(bf16[128,1792]{1,0:T(8,128)(2,1)S(1)} %pad_maximum_fusion.1.refs_0_), channel_id=1, source_target_pairs={{0,16},{16,32},{32,48},{48,0},{1,17},{17,33},{33,49},{49,1},{2,18}... | collective-permute-start | bytes 1376264 | tf_op jit(solution)/shard_map/ppermute | solution.py:257
  44.9 24.1 %collective-permute-start.24 = (bf16[128,1792]{1,0:T(8,128)(2,1)S(1)}, bf16[128,1792]{1,0:T(8,128)(2,1)S(1)}, u32[]{:S(2)}, u32[]{:S(2)}) collective-permute-start(bf16[128,1792]{1,0:T(8,128)(2,1)S(1)} %collective-permute-done.22.refs_3_), channel_id=1, source_target_pairs={{0,64},{64,0},{1,65},{65,1},{2,66},{66,2},{3,67},{67,3},{4,68},{68... | collective-permute-start | bytes 1376264 | tf_op jit(solution)/shard_map/ppermute | solution.py:259
  46.6 25.3 %collective-permute-start.25 = (bf16[128,1792]{1,0:T(8,128)(2,1)S(1)}, bf16[128,1792]{1,0:T(8,128)(2,1)S(1)}, u32[]{:S(2)}, u32[]{:S(2)}) collective-permute-start(bf16[128,1792]{1,0:T(8,128)(2,1)S(1)} %collective-permute-done.22.refs_3_), channel_id=1, source_target_pairs={{0,48},{16,0},{32,16},{48,32},{1,49},{17,1},{33,17},{49,33},{2,50}... | collective-permute-start | bytes 1376264 | tf_op jit(solution)/shard_map/ppermute | solution.py:258
  48.9 20.1 %collective-permute-start.23 = (bf16[128,1792]{1,0:T(8,128)(2,1)S(1)}, bf16[128,1792]{1,0:T(8,128)(2,1)S(1)}, u32[]{:S(2)}, u32[]{:S(2)}) collective-permute-start(bf16[128,1792]{1,0:T(8,128)(2,1)S(1)} %collective-permute-done.20.refs_1_), channel_id=1, source_target_pairs={{0,16},{16,32},{32,48},{48,0},{1,17},{17,33},{33,49},{49,1},{2,18}... | collective-permute-start | bytes 1376264 | tf_op jit(solution)/shard_map/ppermute | solution.py:257
  59.1 12.8 %collective-permute-start.18 = (bf16[128,1024]{1,0:T(8,128)(2,1)S(1)}, bf16[128,1024]{1,0:T(8,128)(2,1)S(1)}, u32[]{:S(2)}, u32[]{:S(2)}) collective-permute-start(bf16[128,1024]{1,0:T(8,128)(2,1)S(1)} %shard_map.122.own_ref), channel_id=1, source_target_pairs={{0,8},{8,0},{1,9},{9,1},{2,10},{10,2},{3,11},{11,3},{4,12},{12,4},... | collective-permute-start | bytes 786440 | tf_op jit(solution)/shard_map/ppermute | solution.py:253
  69.0 7.8 %collective-permute-start.26 = (bf16[128,896]{1,0:T(8,128)(2,1)S(1)}, bf16[128,896]{1,0:T(8,128)(2,1)S(1)}, u32[]{:S(2)}, u32[]{:S(2)}) collective-permute-start(bf16[128,896]{1,0:T(8,128)(2,1)S(1)} %slice.81), channel_id=1, source_target_pairs={{0,16},{16,32},{32,48},{48,0},{1,17},{17,33},{33,49},{49,1},{2,18}... | collective-permute-start | bytes 688136 | tf_op jit(solution)/shard_map/ppermute | solution.py:257
  69.1 17.6 %copy-start.13 = (bf16[16,3584]{1,0:T(8,128)(2,1)S(1)}, bf16[16,3584]{1,0:T(8,128)(2,1)}, u32[]{:S(2)}) copy-start(bf16[16,3584]{1,0:T(8,128)(2,1)} %param.15) | copy-start | bytes 344068
  69.1 19.6 %copy-start.16 = (s32[16,8]{0,1:T(8,128)S(1)}, s32[16,8]{0,1:T(8,128)}, u32[]{:S(2)}) copy-start(s32[16,8]{0,1:T(8,128)} %param.17) | copy-start | bytes 1540
  69.1 7.6 %collective-permute-start.27 = (bf16[128,896]{1,0:T(8,128)(2,1)S(1)}, bf16[128,896]{1,0:T(8,128)(2,1)S(1)}, u32[]{:S(2)}, u32[]{:S(2)}) collective-permute-start(bf16[128,896]{1,0:T(8,128)(2,1)S(1)} %slice.82), channel_id=1, source_target_pairs={{0,48},{16,0},{32,16},{48,32},{1,49},{17,1},{33,17},{49,33},{2,50}... | collective-permute-start | bytes 688136 | tf_op jit(solution)/shard_map/ppermute | solution.py:258
  79.4 25.6 %copy-start.15 = (f32[3584]{0:T(1024)S(1)}, f32[3584]{0:T(1024)}, u32[]{:S(2)}) copy-start(f32[3584]{0:T(1024)} %param.16) | copy-start | bytes 43012
  79.4 23.2 %all-to-all-start = ((bf16[8,2,16,1792]{3,2,1,0:T(8,128)(2,1)}), bf16[8,2,16,1792]{3,2,1,0:T(8,128)(2,1)S(1)}, u32[]{:S(2)}, u32[]{:S(2)}) async-start(bf16[8,2,16,1792]{3,2,1,0:T(8,128)(2,1)} %shard_map.123), calls=%async_computation | async-start | bytes 1835008 | tf_op jit(solution)/shard_map/all_to_all | solution.py:343
  86.8 16.0 %collective-permute-start = (bf16[16,1792]{1,0:T(8,128)(2,1)S(1)}, bf16[16,1792]{1,0:T(8,128)(2,1)S(1)}, u32[]{:S(2)}, u32[]{:S(2)}) collective-permute-start(bf16[16,1792]{1,0:T(8,128)(2,1)S(1)} %get-tuple-element.11), channel_id=1, source_target_pairs={{0,8},{8,0},{1,9},{9,1},{2,10},{10,2},{3,11},{11,3},{4,12},{12,4},... | collective-permute-start | bytes 172040 | tf_op jit(solution)/shard_map/ppermute | solution.py:253
  88.7 1.2 collective-permute-start.29
  102.8 1.9 collective-permute-start.28
  105.2 43.6 %copy-start.2 = (bf16[1,3584,512]{2,1,0:T(8,128)(2,1)S(1)}, bf16[1,3584,512]{2,1,0:T(8,128)(2,1)}, u32[]{:S(2)}) copy-start(bf16[1,3584,512]{2,1,0:T(8,128)(2,1)} %param.20) | copy-start | bytes 11010052
  107.4 41.3 %copy-start.1 = (bf16[1,3584,512]{2,1,0:T(8,128)(2,1)S(1)}, bf16[1,3584,512]{2,1,0:T(8,128)(2,1)}, u32[]{:S(2)}) copy-start(bf16[1,3584,512]{2,1,0:T(8,128)(2,1)} %param.19) | copy-start | bytes 11010052
  158.8 1.5 copy-start
  160.3 7.5 %copy-start.14 = (s32[16,8]{0,1:T(8,128)S(1)}, s32[16,8]{0,1:T(8,128)}, u32[]{:S(2)}) copy-start(s32[16,8]{0,1:T(8,128)} %param.18) | copy-start | bytes 1540
  160.3 40.5 %all-to-all-start.2 = ((bf16[64,3,2,3584]{3,2,1,0:T(2,128)(2,1)}), bf16[64,3,2,3584]{3,2,1,0:T(2,128)(2,1)S(1)}, u32[]{:S(2)}, u32[]{:S(2)}) async-start(bf16[64,3,2,3584]{3,2,1,0:T(2,128)(2,1)} %bitcast.63), calls=%async_computation.2 | async-start | bytes 5505024 | tf_op jit(solution)/shard_map/all_to_all | solution.py:356
  167.8 2.4 %collective-permute-start.30 = (f32[16,8]{0,1:T(8,128)S(1)}, f32[16,8]{0,1:T(8,128)S(1)}, u32[]{:S(2)}, u32[]{:S(2)}) collective-permute-start(f32[16,8]{0,1:T(8,128)S(1)} %convert_divide_fusion), channel_id=1, source_target_pairs={{0,8},{8,0},{1,9},{9,1},{2,10},{10,2},{3,11},{11,3},{4,12},{12,4},... | collective-permute-start | bytes 1544 | tf_op jit(solution)/shard_map/ppermute | solution.py:253
  202.8 4.8 %collective-permute-start.31 = (f32[16,3584]{1,0:T(8,128)S(1)}, f32[16,3584]{1,0:T(8,128)S(1)}, u32[]{:S(2)}, u32[]{:S(2)}) collective-permute-start(f32[16,3584]{1,0:T(8,128)S(1)} %get-tuple-element.5), channel_id=1, source_target_pairs={{0,8},{8,0},{1,9},{9,1},{2,10},{10,2},{3,11},{11,3},{4,12},{12,4},... | collective-permute-start | bytes 688136 | tf_op jit(solution)/shard_map/ppermute | solution.py:253

commit v6 on v4

--- a/solution.py
+++ b/solution.py
@@ -13,7 +13,7 @@
 TOP = 8
 QK = 192
 CAP = 3
-SLOTS = (slice(0, 2), slice(2, 3))
+SLOTS = (slice(0, 3),)
 
 CTX = ("z_lo", "x", "core")
 CTX_CHIPS = ("z_lo", "x")
@@ -246,24 +246,34 @@
     return lax.ppermute(mine, "core", SWAP)
 
 
-def gather_w_out(w_out):
-    core, x, z = (lax.axis_index(n) for n in ("core", "x", "z_lo"))
+def own_w_out(w_out):
+    core = lax.axis_index("core")
     half = w_out.shape[1] // 2
     lower, upper = w_out[:, :half], w_out[:, half:]
     mine = jnp.where(core == 0, lower, upper)
     other = swap(jnp.where(core == 0, upper, lower))
-    own = jnp.concatenate([jnp.where(core == 0, mine, other), jnp.where(core == 0, other, mine)], axis=0)
-    up = lambda a: lax.ppermute(a, "x", [(i, (i + 1) % 4) for i in range(4)])
-    down = lambda a: lax.ppermute(a, "x", [(i, (i + 3) % 4) for i in range(4)])
-    across = lambda a: lax.ppermute(a, "z_lo", SWAP)
-    mate, before, after = across(own), up(own), down(own)
-    mate_before, mate_after, opposite = up(mate), across(after), down(after)
-    part = half // 2
-    left, right = up(mate_before[:, :part]), down(mate_after[:, part:])
-    chunks = (own, mate, before, after, mate_before, mate_after, opposite, left, right)
+    return jnp.concatenate([jnp.where(core == 0, mine, other), jnp.where(core == 0, other, mine)], axis=0)
+
+
+def up(a):
+    return lax.ppermute(a, "x", [(i, (i + 1) % 4) for i in range(4)])
+
+
+def down(a):
+    return lax.ppermute(a, "x", [(i, (i + 3) % 4) for i in range(4)])
+
+
+def across(a):
+    return lax.ppermute(a, "z_lo", SWAP)
+
+
+def chip_order():
+    x, z = lax.axis_index("x"), lax.axis_index("z_lo")
     chip = lambda zz, dx: zz * 4 + lax.rem(x + 4 + dx, 4)
-    order = (chip(z, 0), chip(1 - z, 0), chip(z, -1), chip(z, 1), chip(1 - z, -1), chip(1 - z, 1), chip(z, 2), chip(1 - z, 2))
-    return own, jnp.stack(order).astype(jnp.int32), chunks
+    near, far = z, 1 - z
+    order = [chip(near, 0), chip(far, 0), chip(near, -1), chip(near, 1)]
+    order += [chip(far, -1), chip(far, 1), chip(near, 2), chip(far, 2)]
+    return jnp.stack(order).astype(jnp.int32)
 
 
 def latent_queries(queries, w_kv):
@@ -314,14 +324,24 @@
     tok, width = resid.shape
     chips = 64
     core = lax.axis_index("core")
-    own_rows, order, chunks = gather_w_out(w_out)
-    latents, _ = lax.optimization_barrier((latents, own_rows))
+    chunk = own_w_out(w_out)
+    mate, before, after = across(chunk), up(chunk), down(chunk)
     near = lax.all_to_all(
         jnp.broadcast_to(latents[None], (8,) + latents.shape), CTX_CHIPS, split_axis=0, concat_axis=0, tiled=True
     )
+    q = latent_queries(queries, w_kv)
+    near, q, mate, before, after = lax.optimization_barrier((near, q, mate, before, after))
     far = swap(near)
+    mate_before, mate_after, opposite = up(mate), across(after), down(after)
     ids = jnp.stack([lax.axis_index(CTX), core]).astype(jnp.int32)
-    heads_out = attend(ids, latent_queries(queries, w_kv), near, far, w_kv, 4, 4)
+    heads_out = attend(ids, q, near, far, w_kv, 4, 4)
+    heads_out, mate_before, mate_after, opposite = lax.optimization_barrier(
+        (heads_out, mate_before, mate_after, opposite)
+    )
+    part = chunk.shape[1] // 2
+    left, right = up(mate_before[:, :part]), down(mate_after[:, part:])
+    chunks = (chunk, mate, before, after, mate_before, mate_after, opposite, left, right)
+    order = chip_order()
     half = width // 2
     lower, upper = resid[:, :half], resid[:, half:]
     resid2 = jnp.stack([jnp.where(core == 0, lower, upper), swap(jnp.where(core == 0, upper, lower))])

time: 214 us -> 203 us (0.949)
  starting transfers between devices: 63.4 us -> 41.3 us
  blocking collectives: 22.4 us -> 41.3 us
  Pallas kernels: 35.7 us -> 28.4 us
  other arithmetic: 9.47 us -> 4.89 us
  waiting for transfers between devices: 57 us -> 60.9 us
    all_to_all x4 -> x1, starting transfers between devices: 30.2 us -> 7.49 us  [exchange(): lax.all_to_all(units, CHIPS, split_axis=0, concat_axis=0, tiled=True)]
    all_to_all x1, blocking collectives: 22.4 us -> 41.3 us  [exchange(): lax.all_to_all(units, CHIPS, split_axis=0, concat_axis=0, tiled=True)]
    ppermute x8, waiting for transfers between devices: 8.77 us -> 17 us  [the longest x2 9.65 us: across(): return lax.ppermute(a, 'z_lo', SWAP)]
    all_to_all x4 -> x1, waiting for transfers between devices: 36 us -> 28.4 us  [exchange(): lax.all_to_all(units, CHIPS, split_axis=0, concat_axis=0, tiled=True)]
    ppermute x8, starting transfers between devices: 17.6 us -> 11.4 us  [swap(): return lax.ppermute(mine, 'core', SWAP)]
    all_to_all x0 -> x1, starting transfers between devices: none -> 5.46 us  [local(): lax.all_to_all(jnp.broadcast_to(latents[None], (8,) + latents.shape), CTX...]
    pallas_call x2 -> x1, Pallas kernels: 13.9 us -> 10 us  [expert(): pl.pallas_call(functools.partial(expert_kernel, first=first), grid=(first...]
    all_to_all x1, waiting for transfers between devices: 9.17 us -> 13 us  [local(): attn = lax.all_to_all(attn, EP, split_axis=0, concat_axis=0, tiled=True)]
  transfers between devices with their start and end apart: 21 -> 19, of which waited for: 11 -> 11; matrix products, arithmetic and copies ran while one was open for 8% -> 9% of each run, Pallas kernels for 13% -> 5%
where the time goes in v6:
time: 203 us; the launch traced here: 200 us
  waiting for transfers between devices  60.9 us (30%)
  starting transfers between devices  41.3 us (20%)
  blocking collectives  41.3 us (20%)
  Pallas kernels  28.4 us (14%)
  local copies, waits for them, and re-layouts  20.6 us (10%)
  other arithmetic  4.89 us (2%)
    all_to_all x1, blocking collectives, exchange(): lax.all_to_all(units, CHIPS, split_axis=0, concat_axis=0, tiled=True)  41.3 us
    all_to_all x1, waiting for transfers between devices, exchange(): lax.all_to_all(units, CHIPS, split_axis=0, concat_axis=0, tiled=True)  28.4 us
    unnamed x37, local copies, waits for them, and re-layouts  13.7 us
    all_to_all x1, waiting for transfers between devices, local(): attn = lax.all_to_all(attn, EP, split_axis=0, concat_axis=0, tiled=True)  13 us
    ppermute x8, starting transfers between devices, swap(): return lax.ppermute(mine, 'core', SWAP)  11.4 us
    pallas_call x1, Pallas kernels, attend(): pl.pallas_call(functools.partial(attend_kernel, rows=rows, cuts=cuts), gr...  10.9 us
    pallas_call x1, Pallas kernels, expert(): pl.pallas_call(functools.partial(expert_kernel, first=first), grid=(first...  10 us
    ppermute x2, waiting for transfers between devices, across(): return lax.ppermute(a, 'z_lo', SWAP)  9.65 us
  transfers between devices with their start and end apart: 19, of which 11 were waited for; matrix products, arithmetic and copies ran while one was open for 9% of the time, Pallas kernels for 5%

profile of v6, /device:TPU:1, one launch (start us, length us, event | category | flops | bytes accessed | tf_op | source)
XLA Modules:
  0.0 200.2 jit_solution(6130239994848628921)
XLA Ops:
  0.6 1.1 broadcast_select_fusion.2
  1.8 1.5 collective-permute-start.1
  3.3 2.1 %broadcast_in_dim.32 = bf16[8,576,128]{2,1,0:T(8,128)(2,1)} broadcast(bf16[576,128]{1,0:T(8,128)(2,1)} %param.12), dimensions={1,2} | broadcast | bytes 1327104 | tf_op jit(solution)/shard_map/broadcast_in_dim | solution.py:330
  5.4 5.5 %all-to-all-start = ((bf16[8,576,128]{2,1,0:T(8,128)(2,1)}), bf16[8,576,128]{2,1,0:T(8,128)(2,1)}, u32[]{:S(2)}, u32[]{:S(2)}) async-start(bf16[8,576,128]{2,1,0:T(8,128)(2,1)} %broadcast_in_dim.32), calls=%async_computation | async-start | bytes 2359296 | tf_op jit(solution)/shard_map/all_to_all | solution.py:329
  11.0 1.5 collective-permute-start.2
  12.5 1.2 collective-permute-start.3
  13.7 1.5 collective-permute-start.4
  15.2 1.9 copy.45
  17.1 1.6 slice.70
  18.7 1.8 copy.63
  20.4 2.5 %copy.47 = bf16[512,2048]{0,1:T(8,128)(2,1)} copy(bf16[512,2048]{1,0:T(8,128)(2,1)S(1)} %copy-done.3) | data formatting | bytes 4194304 | tf_op args[2]
  22.9 1.8 convolution_convert_fusion
  24.8 1.2 pad_maximum_fusion
  26.0 9.6 %collective-permute-done.2.refs_1_ = bf16[128,1792]{1,0:T(8,128)(2,1)S(1)} collective-permute-done((bf16[128,1792]{1,0:T(8,128)(2,1)S(1)}, bf16[128,1792]{1,0:T(8,128)(2,1)S(1)}, u32[]{:S(2)}, u32[]{:S(2)}) %collective-permute-start.2) | collective-permute-done | bytes 458784 | tf_op jit(solution)/shard_map/ppermute | solution.py:267
  35.6 1.5 collective-permute-done.3.refs_2_
  37.1 0.8 copy-done.7
  37.9 0.8 collective-permute-start.5
  38.7 1.2 collective-permute-start.7
  39.9 1.2 collective-permute-start.8
  41.1 0.3 collective-permute-start.6
  41.5 1.3 copy-done.4
  42.8 10.9 %shard_map.122.own_ref = bf16[128,1024]{1,0:T(8,128)(2,1)} custom-call(s32[2]{0:T(128)S(1)} %pad_add_fusion.1.ids_ref, bf16[1024,576]{1,0:T(8,128)(2,1)S(1)} %bitcast.68, bf16[8,576,128]{2,1,0:T(8,128)(2,1)} %all-to-all-done.near_ref, bf16[8,576,128]{2,1,0:T(8,128)(2,1)} %collective-permute-done.5.far_ref, bf16[512,2048]{1,0:T(8,128)(2,1)S(1)} %copy-done.3), custom_call_target="tpu_custom_call" | custom-call | flops 4563402752 | bytes 8000000 | tf_op jit(solution)/shard_map/pallas_call | solution.py:76
  53.7 0.2 collective-permute-done.6.refs_4_
  54.0 0.8 copy-done.9
  54.7 1.5 collective-permute-start.9
  56.4 2.7 %collective-permute-start.11 = (bf16[128,896]{1,0:T(8,128)(2,1)S(1)}, bf16[128,896]{1,0:T(8,128)(2,1)S(1)}, u32[]{:S(2)}, u32[]{:S(2)}) collective-permute-start(bf16[128,896]{1,0:T(8,128)(2,1)S(1)} %slice.59), channel_id=1, source_target_pairs={{0,48},{16,0},{32,16},{48,32},{1,49},{17,1},{33,17},{49,33},{2,50}... | collective-permute-start | bytes 688136 | tf_op jit(solution)/shard_map/ppermute | solution.py:263
  59.1 0.1 stack.74.order_ref
  59.2 5.6 %collective-permute-done.10.refs_7_ = bf16[128,896]{1,0:T(8,128)(2,1)S(1)} collective-permute-done((bf16[128,896]{1,0:T(8,128)(2,1)S(1)}, bf16[128,896]{1,0:T(8,128)(2,1)S(1)}, u32[]{:S(2)}, u32[]{:S(2)}) %collective-permute-start.10) | collective-permute-done | bytes 229408 | tf_op jit(solution)/shard_map/ppermute | solution.py:259
  64.8 1.0 copy-done.6
  65.8 1.0 copy-done.8
  66.8 1.0 copy-done.10
  67.9 3.3 %shard_map.123 = bf16[8,2,16,1792]{3,2,1,0:T(8,128)(2,1)} custom-call(s32[8]{0:T(128)S(1)} %stack.74.order_ref, bf16[128,1024]{1,0:T(8,128)(2,1)} %shard_map.122.own_ref, bf16[128,1024]{1,0:T(8,128)(2,1)S(1)} %collective-permute-done.9.far_ref, bf16[128,1792]{1,0:T(8,128)(2,1)S(1)} %pad_maximum_fusion.1.refs_0_, bf16[128,1792]{1,0:T(8,128)(2,1)S(1)} %copy-done.6, ...), custom_call_target="tpu_custom_call" | custom-call | flops 939524096 | bytes 3670016 | tf_op jit(solution)/shard_map/pallas_call | solution.py:232
  71.1 7.2 %all-to-all-start.1 = ((bf16[8,2,16,1792]{3,2,1,0:T(8,128)(2,1)}), bf16[8,2,16,1792]{3,2,1,0:T(8,128)(2,1)S(1)}, u32[]{:S(2)}, u32[]{:S(2)}) async-start(bf16[8,2,16,1792]{3,2,1,0:T(8,128)(2,1)} %shard_map.123), calls=%async_computation.1 | async-start | bytes 1835008 | tf_op jit(solution)/shard_map/all_to_all | solution.py:349
  78.4 1.1 collective-permute-start
  79.5 0.1 collective-permute-start.13
  79.7 0.1 and.51
  79.8 0.9 collective-permute-done.13
  80.8 0.1 fusion.8
  80.9 0.1 copy.51
  81.3 13.0 %all-to-all-done.1 = bf16[8,2,16,1792]{3,2,1,0:T(8,128)(2,1)S(1)} async-done(((bf16[8,2,16,1792]{3,2,1,0:T(8,128)(2,1)}), bf16[8,2,16,1792]{3,2,1,0:T(8,128)(2,1)S(1)}, u32[]{:S(2)}, u32[]{:S(2)}) %all-to-all-start.1) | async-done | bytes 917536 | tf_op jit(solution)/shard_map/all_to_all | solution.py:349
  94.2 0.1 convert_reduce_fusion
  94.4 1.1 collective-permute-start.12
  95.6 0.1 copy.54
  95.9 0.1 reshape.153
  96.0 0.5 collective-permute-done.12
  96.6 0.1 multiply_reduce_fusion
  96.8 0.1 fusion.2.x_ref
  97.0 2.2 %shard_map.124 = bf16[192,2,3584]{2,1,0:T(2,128)(2,1)S(1)} custom-call(bf16[384,32]{1,0:T(8,128)(2,1)S(1)} %convert_element_type.52.place_ref, bf16[32,3584]{1,0:T(8,128)(2,1)S(1)} %fusion.2.x_ref), custom_call_target="tpu_custom_call" | custom-call | flops 88080384 | bytes 2981888 | tf_op jit(solution)/shard_map/pallas_call | solution.py:157
  99.2 41.3 %all_to_all.20 = bf16[64,3,2,3584]{3,2,1,0:T(2,128)(2,1)S(1)} all-to-all(bf16[64,3,2,3584]{3,2,1,0:T(2,128)(2,1)S(1)} %bitcast.63), channel_id=1, replica_groups=mesh['z_lo'=2,'x'=4,'core'=2,'z_hi'=2,'y'=4] {'z_lo','x','z_hi','y'}, dimensions={0} | all-to-all | bytes 5505024 | tf_op jit(solution)/shard_map/all_to_all | solution.py:362
  140.5 10.0 %shard_map.125 = bf16[192,2,3584]{2,1,0:T(2,128)(2,1)S(1)} custom-call(bf16[192,2,3584]{2,1,0:T(2,128)(2,1)S(1)} %bitcast.65, bf16[3584,512]{1,0:T(8,128)(2,1)S(1)} %bitcast.66, bf16[3584,512]{1,0:T(8,128)(2,1)S(1)} %bitcast.67, bf16[512,3584]{1,0:T(8,128)(2,1)} %bitcast.70), custom_call_target="tpu_custom_call" | custom-call | flops 4227858432 | bytes 17000000 | tf_op jit(solution)/shard_map/pallas_call | solution.py:129
  150.6 1.5 copy-done
  152.1 7.5 %all-to-all-start.3 = ((bf16[64,3,2,3584]{3,2,1,0:T(2,128)(2,1)}), bf16[64,3,2,3584]{3,2,1,0:T(2,128)(2,1)S(1)}, u32[]{:S(2)}, u32[]{:S(2)}) async-start(bf16[64,3,2,3584]{3,2,1,0:T(2,128)(2,1)} %bitcast.64), calls=%async_computation.3 | async-start | bytes 5505024 | tf_op jit(solution)/shard_map/all_to_all | solution.py:362
  159.6 1.6 collective-permute-start.14
  161.2 0.1 copy.59
  161.3 0.7 collective-permute-done.14
  162.1 0.1 select_reduce_fusion
  162.5 0.7 broadcast_in_dim.65
  163.2 1.0 copy.60
  164.3 28.4 %all-to-all-done.3 = bf16[64,3,2,3584]{3,2,1,0:T(2,128)(2,1)S(1)} async-done(((bf16[64,3,2,3584]{3,2,1,0:T(2,128)(2,1)}), bf16[64,3,2,3584]{3,2,1,0:T(2,128)(2,1)S(1)}, u32[]{:S(2)}, u32[]{:S(2)}) %all-to-all-start.3) | async-done | bytes 2752544 | tf_op jit(solution)/shard_map/all_to_all | solution.py:362
  192.7 1.9 shard_map.126
  194.7 3.8 %collective-permute-start.15 = (f32[16,3584]{1,0:T(8,128)S(1)}, f32[16,3584]{1,0:T(8,128)S(1)}, u32[]{:S(2)}, u32[]{:S(2)}) collective-permute-start(f32[16,3584]{1,0:T(8,128)S(1)} %get-tuple-element.23), channel_id=1, source_target_pairs={{0,8},{8,0},{1,9},{9,1},{2,10},{10,2},{3,11},{11,3},{4,12},{12,4},... | collective-permute-start | bytes 688136 | tf_op jit(solution)/shard_map/ppermute | solution.py:246
  198.4 0.7 fusion.10
  199.1 0.5 collective-permute-done.15
  199.5 0.7 fusion.7
  (74 shorter events, 1.6 us)
Async XLA Ops:
  0.6 10.2 %copy-start.11 = (bf16[64,3584]{1,0:T(8,128)(2,1)S(1)}, bf16[64,3584]{1,0:T(8,128)(2,1)}, u32[]{:S(2)}) copy-start(bf16[64,3584]{1,0:T(8,128)(2,1)} %param.14) | copy-start | bytes 1376260
  1.8 9.1 %collective-permute-start.1 = (bf16[64,1792]{1,0:T(8,128)(2,1)S(1)}, bf16[64,1792]{1,0:T(8,128)(2,1)S(1)}, u32[]{:S(2)}, u32[]{:S(2)}) collective-permute-start(bf16[64,1792]{1,0:T(8,128)(2,1)S(1)} %broadcast_select_fusion.2), channel_id=1, source_target_pairs={{0,8},{8,0},{1,9},{9,1},{2,10},{10,2},{3,11},{11,3},{4,12},{12,4},... | collective-permute-start | bytes 688136 | tf_op jit(solution)/shard_map/ppermute | solution.py:246
  5.4 32.6 %all-to-all-start = ((bf16[8,576,128]{2,1,0:T(8,128)(2,1)}), bf16[8,576,128]{2,1,0:T(8,128)(2,1)}, u32[]{:S(2)}, u32[]{:S(2)}) async-start(bf16[8,576,128]{2,1,0:T(8,128)(2,1)} %broadcast_in_dim.32), calls=%async_computation | async-start | bytes 2359296 | tf_op jit(solution)/shard_map/all_to_all | solution.py:329
  10.8 9.6 %copy-start.3 = (bf16[512,2048]{1,0:T(8,128)(2,1)S(1)}, bf16[512,2048]{1,0:T(8,128)(2,1)}, u32[]{:S(2)}) copy-start(bf16[512,2048]{1,0:T(8,128)(2,1)} %w_ref.1) | copy-start | bytes 6291460
  11.0 24.7 %collective-permute-start.2 = (bf16[128,1792]{1,0:T(8,128)(2,1)S(1)}, bf16[128,1792]{1,0:T(8,128)(2,1)S(1)}, u32[]{:S(2)}, u32[]{:S(2)}) collective-permute-start(bf16[128,1792]{1,0:T(8,128)(2,1)S(1)} %pad_maximum_fusion.1.refs_0_), channel_id=1, source_target_pairs={{0,64},{64,0},{1,65},{65,1},{2,66},{66,2},{3,67},{67,3},{4,68},{68... | collective-permute-start | bytes 1376264 | tf_op jit(solution)/shard_map/ppermute | solution.py:267
  12.5 24.6 %collective-permute-start.3 = (bf16[128,1792]{1,0:T(8,128)(2,1)S(1)}, bf16[128,1792]{1,0:T(8,128)(2,1)S(1)}, u32[]{:S(2)}, u32[]{:S(2)}) collective-permute-start(bf16[128,1792]{1,0:T(8,128)(2,1)S(1)} %pad_maximum_fusion.1.refs_0_), channel_id=1, source_target_pairs={{0,16},{16,32},{32,48},{48,0},{1,17},{17,33},{33,49},{49,1},{2,18}... | collective-permute-start | bytes 1376264 | tf_op jit(solution)/shard_map/ppermute | solution.py:259
  13.7 24.3 %collective-permute-start.4 = (bf16[128,1792]{1,0:T(8,128)(2,1)S(1)}, bf16[128,1792]{1,0:T(8,128)(2,1)}, u32[]{:S(2)}, u32[]{:S(2)}) collective-permute-start(bf16[128,1792]{1,0:T(8,128)(2,1)S(1)} %pad_maximum_fusion.1.refs_0_), channel_id=1, source_target_pairs={{0,48},{16,0},{32,16},{48,32},{1,49},{17,1},{33,17},{49,33},{2,50}... | collective-permute-start | bytes 1376264 | tf_op jit(solution)/shard_map/ppermute | solution.py:263
  22.9 1.8 copy-start.12
  35.6 3.1 %copy-start.5 = (bf16[128,1792]{1,0:T(8,128)(2,1)}, bf16[128,1792]{1,0:T(8,128)(2,1)S(1)}, u32[]{:S(2)}) copy-start(bf16[128,1792]{1,0:T(8,128)(2,1)S(1)} %collective-permute-done.2.refs_1_) | copy-start | bytes 1376260
  37.1 0.8 copy-start.7
  37.9 3.6 %collective-permute-start.5 = (bf16[8,576,128]{2,1,0:T(8,128)(2,1)}, bf16[8,576,128]{2,1,0:T(8,128)(2,1)}, u32[]{:S(2)}, u32[]{:S(2)}) collective-permute-start(bf16[8,576,128]{2,1,0:T(8,128)(2,1)} %all-to-all-done.near_ref), channel_id=1, source_target_pairs={{0,8},{8,0},{1,9},{9,1},{2,10},{10,2},{3,11},{11,3},{4,12},{12,4},... | collective-permute-start | bytes 3538952 | tf_op jit(solution)/shard_map/ppermute | solution.py:246
  38.7 15.3 %collective-permute-start.7 = (bf16[128,1792]{1,0:T(8,128)(2,1)}, bf16[128,1792]{1,0:T(8,128)(2,1)S(1)}, u32[]{:S(2)}, u32[]{:S(2)}) collective-permute-start(bf16[128,1792]{1,0:T(8,128)(2,1)} %collective-permute-done.4.refs_3_), channel_id=1, source_target_pairs={{0,64},{64,0},{1,65},{65,1},{2,66},{66,2},{3,67},{67,3},{4,68},{68... | collective-permute-start | bytes 1376264 | tf_op jit(solution)/shard_map/ppermute | solution.py:267
  39.9 14.1 %collective-permute-start.8 = (bf16[128,1792]{1,0:T(8,128)(2,1)}, bf16[128,1792]{1,0:T(8,128)(2,1)S(1)}, u32[]{:S(2)}, u32[]{:S(2)}) collective-permute-start(bf16[128,1792]{1,0:T(8,128)(2,1)} %collective-permute-done.4.refs_3_), channel_id=1, source_target_pairs={{0,48},{16,0},{32,16},{48,32},{1,49},{17,1},{33,17},{49,33},{2,50}... | collective-permute-start | bytes 1376264 | tf_op jit(solution)/shard_map/ppermute | solution.py:263
  41.1 12.8 %collective-permute-start.6 = (bf16[128,1792]{1,0:T(8,128)(2,1)}, bf16[128,1792]{1,0:T(8,128)(2,1)S(1)}, u32[]{:S(2)}, u32[]{:S(2)}) collective-permute-start(bf16[128,1792]{1,0:T(8,128)(2,1)} %copy-done.5), channel_id=1, source_target_pairs={{0,16},{16,32},{32,48},{48,0},{1,17},{17,33},{33,49},{49,1},{2,18}... | collective-permute-start | bytes 1376264 | tf_op jit(solution)/shard_map/ppermute | solution.py:259
  41.5 1.3 copy-start.4
  54.0 0.8 copy-start.9
  54.7 10.1 %collective-permute-start.9 = (bf16[128,1024]{1,0:T(8,128)(2,1)}, bf16[128,1024]{1,0:T(8,128)(2,1)S(1)}, u32[]{:S(2)}, u32[]{:S(2)}) collective-permute-start(bf16[128,1024]{1,0:T(8,128)(2,1)} %shard_map.122.own_ref), channel_id=1, source_target_pairs={{0,8},{8,0},{1,9},{9,1},{2,10},{10,2},{3,11},{11,3},{4,12},{12,4},... | collective-permute-start | bytes 786440 | tf_op jit(solution)/shard_map/ppermute | solution.py:246
  56.3 8.5 %collective-permute-start.10 = (bf16[128,896]{1,0:T(8,128)(2,1)S(1)}, bf16[128,896]{1,0:T(8,128)(2,1)S(1)}, u32[]{:S(2)}, u32[]{:S(2)}) collective-permute-start(bf16[128,896]{1,0:T(8,128)(2,1)S(1)} %slice.58), channel_id=1, source_target_pairs={{0,16},{16,32},{32,48},{48,0},{1,17},{17,33},{33,49},{49,1},{2,18}... | collective-permute-start | bytes 688136 | tf_op jit(solution)/shard_map/ppermute | solution.py:259
  56.4 8.4 %collective-permute-start.11 = (bf16[128,896]{1,0:T(8,128)(2,1)S(1)}, bf16[128,896]{1,0:T(8,128)(2,1)S(1)}, u32[]{:S(2)}, u32[]{:S(2)}) collective-permute-start(bf16[128,896]{1,0:T(8,128)(2,1)S(1)} %slice.59), channel_id=1, source_target_pairs={{0,48},{16,0},{32,16},{48,32},{1,49},{17,1},{33,17},{49,33},{2,50}... | collective-permute-start | bytes 688136 | tf_op jit(solution)/shard_map/ppermute | solution.py:263
  59.1 20.4 %copy-start.16 = (s32[16,8]{0,1:T(8,128)S(1)}, s32[16,8]{0,1:T(8,128)}, u32[]{:S(2)}) copy-start(s32[16,8]{0,1:T(8,128)} %param.17) | copy-start | bytes 1540
  64.8 1.0 copy-start.6
  65.8 1.0 copy-start.8
  66.8 1.0 copy-start.10
  67.9 10.5 %copy-start.13 = (bf16[16,3584]{1,0:T(8,128)(2,1)S(1)}, bf16[16,3584]{1,0:T(8,128)(2,1)}, u32[]{:S(2)}) copy-start(bf16[16,3584]{1,0:T(8,128)(2,1)} %param.15) | copy-start | bytes 344068
  71.1 23.1 %all-to-all-start.1 = ((bf16[8,2,16,1792]{3,2,1,0:T(8,128)(2,1)}), bf16[8,2,16,1792]{3,2,1,0:T(8,128)(2,1)S(1)}, u32[]{:S(2)}, u32[]{:S(2)}) async-start(bf16[8,2,16,1792]{3,2,1,0:T(8,128)(2,1)} %shard_map.123), calls=%async_computation.1 | async-start | bytes 1835008 | tf_op jit(solution)/shard_map/all_to_all | solution.py:349
  78.4 18.5 %copy-start.15 = (f32[3584]{0:T(1024)S(1)}, f32[3584]{0:T(1024)}, u32[]{:S(2)}) copy-start(f32[3584]{0:T(1024)} %param.16) | copy-start | bytes 43012
  78.4 16.0 %collective-permute-start = (bf16[16,1792]{1,0:T(8,128)(2,1)S(1)}, bf16[16,1792]{1,0:T(8,128)(2,1)S(1)}, u32[]{:S(2)}, u32[]{:S(2)}) collective-permute-start(bf16[16,1792]{1,0:T(8,128)(2,1)S(1)} %get-tuple-element.29), channel_id=1, source_target_pairs={{0,8},{8,0},{1,9},{9,1},{2,10},{10,2},{3,11},{11,3},{4,12},{12,4},... | collective-permute-start | bytes 172040 | tf_op jit(solution)/shard_map/ppermute | solution.py:246
  79.5 1.2 collective-permute-start.13
  94.4 2.1 %collective-permute-start.12 = (bf16[2,16,1792]{2,1,0:T(8,128)(2,1)S(1)}, bf16[2,16,1792]{2,1,0:T(8,128)(2,1)S(1)}, u32[]{:S(2)}, u32[]{:S(2)}) collective-permute-start(bf16[2,16,1792]{2,1,0:T(8,128)(2,1)S(1)} %add_convert_fusion), channel_id=1, source_target_pairs={{0,8},{8,0},{1,9},{9,1},{2,10},{10,2},{3,11},{11,3},{4,12},{12,4},... | collective-permute-start | bytes 344072 | tf_op jit(solution)/shard_map/ppermute | solution.py:246
  97.0 43.6 %copy-start.2 = (bf16[1,3584,512]{2,1,0:T(8,128)(2,1)S(1)}, bf16[1,3584,512]{2,1,0:T(8,128)(2,1)}, u32[]{:S(2)}) copy-start(bf16[1,3584,512]{2,1,0:T(8,128)(2,1)} %param.20) | copy-start | bytes 11010052
  99.2 41.3 %copy-start.1 = (bf16[1,3584,512]{2,1,0:T(8,128)(2,1)S(1)}, bf16[1,3584,512]{2,1,0:T(8,128)(2,1)}, u32[]{:S(2)}) copy-start(bf16[1,3584,512]{2,1,0:T(8,128)(2,1)} %param.19) | copy-start | bytes 11010052
  150.5 1.5 copy-start
  152.1 7.5 %copy-start.14 = (s32[16,8]{0,1:T(8,128)S(1)}, s32[16,8]{0,1:T(8,128)}, u32[]{:S(2)}) copy-start(s32[16,8]{0,1:T(8,128)} %param.18) | copy-start | bytes 1540
  152.1 40.6 %all-to-all-start.3 = ((bf16[64,3,2,3584]{3,2,1,0:T(2,128)(2,1)}), bf16[64,3,2,3584]{3,2,1,0:T(2,128)(2,1)S(1)}, u32[]{:S(2)}, u32[]{:S(2)}) async-start(bf16[64,3,2,3584]{3,2,1,0:T(2,128)(2,1)} %bitcast.64), calls=%async_computation.3 | async-start | bytes 5505024 | tf_op jit(solution)/shard_map/all_to_all | solution.py:362
  159.6 2.4 %collective-permute-start.14 = (f32[16,8]{0,1:T(8,128)S(1)}, f32[16,8]{0,1:T(8,128)S(1)}, u32[]{:S(2)}, u32[]{:S(2)}) collective-permute-start(f32[16,8]{0,1:T(8,128)S(1)} %convert_divide_fusion), channel_id=1, source_target_pairs={{0,8},{8,0},{1,9},{9,1},{2,10},{10,2},{3,11},{11,3},{4,12},{12,4},... | collective-permute-start | bytes 1544 | tf_op jit(solution)/shard_map/ppermute | solution.py:246
  194.7 4.9 %collective-permute-start.15 = (f32[16,3584]{1,0:T(8,128)S(1)}, f32[16,3584]{1,0:T(8,128)S(1)}, u32[]{:S(2)}, u32[]{:S(2)}) collective-permute-start(f32[16,3584]{1,0:T(8,128)S(1)} %get-tuple-element.23), channel_id=1, source_target_pairs={{0,8},{8,0},{1,9},{9,1},{2,10},{10,2},{3,11},{11,3},{4,12},{12,4},... | collective-permute-start | bytes 688136 | tf_op jit(solution)/shard_map/ppermute | solution.py:246

commit v7 on v6

--- a/solution.py
+++ b/solution.py
@@ -27,19 +27,26 @@
 LOG2E = 1.4426950408889634
 
 
-def attend_kernel(ids_ref, q_ref, near_ref, far_ref, w_ref, out_ref, lat_ref, s_ref, p_ref, *, rows, cuts):
+def attend_kernel(ids_ref, q_ref, w_ref, *refs, rows, cuts):
+    *piece_refs, out_ref, lat_ref, s_ref, p_ref = refs
     heads = w_ref.shape[1] // (NOPE + VD)
     m = q_ref.shape[0]
-    pairs = near_ref.shape[0]
-    keys = 2 * rows * pairs
+    keys = lat_ref.shape[1]
+    ctx, core, odd = ids_ref[0], ids_ref[1], ids_ref[2]
 
     @pl.when(pl.program_id(0) == 0)
     def _():
-        for i in range(pairs):
-            lat_ref[:, 2 * i * rows : (2 * i + 1) * rows] = near_ref[i]
-            lat_ref[:, (2 * i + 1) * rows : (2 * i + 2) * rows] = far_ref[i]
-
-    ctx, core = ids_ref[0], ids_ref[1]
+        for side in range(2):
+            whole, lower, upper = piece_refs[3 * side : 3 * side + 3]
+            pairs, depth, _ = whole.shape
+            mine = pl.ds(pl.multiple_of(odd * depth, 32), depth)
+            rest = pl.ds(pl.multiple_of((1 - odd) * depth, 32), depth)
+            for i in range(pairs):
+                first = (2 * i + side) * rows
+                lat_ref[mine, first : first + rows] = whole[i]
+                half = lower if i < pairs // 2 else upper
+                lat_ref[rest, first : first + rows] = half[i % (pairs // 2)]
+
     span = keys // cuts
     lane = lax.broadcasted_iota(jnp.int32, (m, rows), 1)
     query = lax.broadcasted_iota(jnp.int32, (m, rows), 0) % rows
@@ -68,31 +75,32 @@
         out_ref[:, h * VD : (h + 1) * VD] = o.astype(BF)
 
 
-def attend(ids, q, near, far, w_kv, group, cuts):
-    pairs, depth, rows = near.shape
+def attend(ids, q, w_kv, near, far, group, cuts):
+    pairs, half, rows = near[0].shape
+    depth = 2 * half
     heads = w_kv.shape[1] // (NOPE + VD)
     keys = 2 * rows * pairs
     m = group * rows
+    pieces = (*near, *far)
     return pl.pallas_call(
         functools.partial(attend_kernel, rows=rows, cuts=cuts),
         grid=(heads // group,),
         in_specs=[
             pl.BlockSpec(memory_space=pltpu.SMEM),
             pl.BlockSpec((m, depth), lambda g: (g, 0)),
-            pl.BlockSpec(near.shape, lambda g: (0, 0, 0)),
-            pl.BlockSpec(far.shape, lambda g: (0, 0, 0)),
             pl.BlockSpec((KV_RANK, group * (NOPE + VD)), lambda g: (0, g)),
-        ],
+        ]
+        + [pl.BlockSpec(a.shape, lambda g: (0, 0, 0)) for a in pieces],
         out_specs=pl.BlockSpec((rows, group * VD), lambda g: (0, g)),
         out_shape=jax.ShapeDtypeStruct((rows, heads * VD), BF),
         scratch_shapes=[pltpu.VMEM((depth, keys), BF), pltpu.VMEM((m, keys), F32), pltpu.VMEM((m, keys), BF)],
-        compiler_params=pltpu.CompilerParams(vmem_limit_bytes=40 * 2**20),
+        compiler_params=pltpu.CompilerParams(vmem_limit_bytes=28 * 2**20),
         cost_estimate=pl.CostEstimate(
             flops=2 * heads * rows * keys * (depth + KV_RANK),
             bytes_accessed=8_000_000,
             transcendentals=heads * rows * keys,
         ),
-    )(ids, q, near, far, w_kv)
+    )(ids, q, w_kv, *pieces)
 
 
 def expert_kernel(x_ref, g_ref, u_ref, d_ref, out_ref, rows_ref, hid_ref, *, first):
@@ -138,7 +146,7 @@
         out_specs=pl.BlockSpec((units, pair, n2), lambda i: (0, 0, jnp.maximum(i - first, 0))),
         out_shape=jax.ShapeDtypeStruct(x.shape, BF),
         scratch_shapes=[pltpu.VMEM((m, width), BF), pltpu.VMEM((m, hidden), BF)],
-        compiler_params=pltpu.CompilerParams(vmem_limit_bytes=40 * 2**20),
+        compiler_params=pltpu.CompilerParams(vmem_limit_bytes=28 * 2**20),
         cost_estimate=pl.CostEstimate(
             flops=6 * m * width * hidden, bytes_accessed=17_000_000, transcendentals=m * hidden
         ),
@@ -160,7 +168,7 @@
         in_specs=[pl.BlockSpec(place.shape, lambda i: (0, 0)), pl.BlockSpec((tokens, n), lambda i: (0, i))],
         out_specs=pl.BlockSpec((m // 2, 2, n), lambda i: (0, 0, i)),
         out_shape=jax.ShapeDtypeStruct((m // 2, 2, width), BF),
-        compiler_params=pltpu.CompilerParams(vmem_limit_bytes=32 * 2**20),
+        compiler_params=pltpu.CompilerParams(vmem_limit_bytes=16 * 2**20),
         cost_estimate=pl.CostEstimate(
             flops=2 * m * tokens * width, bytes_accessed=2 * m * width + 2 * tokens * width, transcendentals=0
         ),
@@ -196,7 +204,7 @@
         in_specs=in_specs,
         out_specs=(half, half),
         out_shape=(jax.ShapeDtypeStruct((tok, width), F32),) * 2,
-        compiler_params=pltpu.CompilerParams(vmem_limit_bytes=32 * 2**20),
+        compiler_params=pltpu.CompilerParams(vmem_limit_bytes=16 * 2**20),
         cost_estimate=pl.CostEstimate(
             flops=8 * tok * rows * width, bytes_accessed=2 * rows * width, transcendentals=0
         ),
@@ -235,7 +243,7 @@
         out_specs=whole,
         out_shape=jax.ShapeDtypeStruct((parts, 2, rows // parts, width), BF),
         scratch_shapes=[pltpu.VMEM((2 * rows, depth), BF), pltpu.VMEM((depth, width), BF)],
-        compiler_params=pltpu.CompilerParams(vmem_limit_bytes=32 * 2**20),
+        compiler_params=pltpu.CompilerParams(vmem_limit_bytes=16 * 2**20),
         cost_estimate=pl.CostEstimate(
             flops=4 * rows * depth * width, bytes_accessed=2 * depth * width, transcendentals=0
         ),
@@ -324,17 +332,23 @@
     tok, width = resid.shape
     chips = 64
     core = lax.axis_index("core")
+    odd = lax.rem(lax.axis_index("y"), 2)
+    depth = latents.shape[0] // 2
+    mine = lax.dynamic_slice_in_dim(latents, odd * depth, depth, axis=0)
+    fetched = lax.all_to_all(
+        jnp.broadcast_to(mine[None], (8,) + mine.shape), CTX_CHIPS, split_axis=0, concat_axis=0, tiled=True
+    )
     chunk = own_w_out(w_out)
+    q = latent_queries(queries, w_kv)
+    fetched, chunk, q = lax.optimization_barrier((fetched, chunk, q))
+    lower = lax.ppermute(fetched[:4], "y", [(i, (i + 1) % 4) for i in range(4)])
+    upper = lax.ppermute(fetched[4:], "y", [(i, (i + 3) % 4) for i in range(4)])
+    far = swap(fetched)
     mate, before, after = across(chunk), up(chunk), down(chunk)
-    near = lax.all_to_all(
-        jnp.broadcast_to(latents[None], (8,) + latents.shape), CTX_CHIPS, split_axis=0, concat_axis=0, tiled=True
-    )
-    q = latent_queries(queries, w_kv)
-    near, q, mate, before, after = lax.optimization_barrier((near, q, mate, before, after))
-    far = swap(near)
+    lower, upper, far, mate, before, after = lax.optimization_barrier((lower, upper, far, mate, before, after))
+    ids = jnp.stack([lax.axis_index(CTX), core, odd]).astype(jnp.int32)
     mate_before, mate_after, opposite = up(mate), across(after), down(after)
-    ids = jnp.stack([lax.axis_index(CTX), core]).astype(jnp.int32)
-    heads_out = attend(ids, q, near, far, w_kv, 4, 4)
+    heads_out = attend(ids, q, w_kv, (fetched, lower, upper), (far, swap(lower), swap(upper)), 4, 4)
     heads_out, mate_before, mate_after, opposite = lax.optimization_barrier(
         (heads_out, mate_before, mate_after, opposite)
     )

time: 203 us -> 212 us (1.044)
  other arithmetic: 4.89 us -> 10.6 us
  local copies, waits for them, and re-layouts: 20.6 us -> 26.2 us
  starting transfers between devices: 41.3 us -> 45.8 us
  Pallas kernels: 28.4 us -> 24.5 us
  waiting for transfers between devices: 60.9 us -> 57.4 us
    ppermute x0 -> x2, waiting for transfers between devices: none -> 10.4 us  [the longest x1 9 us: local(): lower = lax.ppermute(fetched[:4], 'y', [(i, (i + 1) % 4) for i in range(4)])]
    ppermute x2, waiting for transfers between devices: 9.65 us -> 0.01 us  [across(): return lax.ppermute(a, 'z_lo', SWAP)]
    unnamed x37 -> x59, local copies, waits for them, and re-layouts: 13.7 us -> 19.8 us
    ppermute x3, waiting for transfers between devices: 7.32 us -> 3.62 us  [up(): return lax.ppermute(a, 'x', [(i, (i + 1) % 4) for i in range(4)])]
    ppermute x0 -> x2, starting transfers between devices: none -> 3.67 us  [the longest x1 2.8 us: local(): upper = lax.ppermute(fetched[4:], 'y', [(i, (i + 3) % 4) for i in range(4)])]
    ppermute x3, waiting for transfers between devices: 0.01 us -> 3.18 us  [down(): return lax.ppermute(a, 'x', [(i, (i + 3) % 4) for i in range(4)])]
    ppermute x8 -> x10, starting transfers between devices: 11.4 us -> 13.8 us  [swap(): return lax.ppermute(mine, 'core', SWAP)]
    pallas_call x1, Pallas kernels: 10 us -> 7.69 us  [expert(): pl.pallas_call(functools.partial(expert_kernel, first=first), grid=(first...]
  transfers between devices with their start and end apart: 19 -> 23, of which waited for: 11 -> 10; matrix products, arithmetic and copies ran while one was open for 9% -> 10% of each run, Pallas kernels for 5% -> 6%
where the time goes in v7:
time: 212 us; the launch traced here: 208 us
  waiting for transfers between devices  57.4 us (27%)
  starting transfers between devices  45.8 us (22%)
  blocking collectives  40 us (19%)
  local copies, waits for them, and re-layouts  26.2 us (12%)
  Pallas kernels  24.5 us (12%)
  other arithmetic  10.6 us (5%)
  matrix products  2.85 us (1%)
    all_to_all x1, blocking collectives, exchange(): lax.all_to_all(units, CHIPS, split_axis=0, concat_axis=0, tiled=True)  40 us
    all_to_all x1, waiting for transfers between devices, exchange(): lax.all_to_all(units, CHIPS, split_axis=0, concat_axis=0, tiled=True)  26.3 us
    unnamed x59, local copies, waits for them, and re-layouts  19.8 us
    ppermute x10, starting transfers between devices, swap(): return lax.ppermute(mine, 'core', SWAP)  13.8 us
    all_to_all x1, waiting for transfers between devices, local(): attn = lax.all_to_all(attn, EP, split_axis=0, concat_axis=0, tiled=True)  11.9 us
    pallas_call x1, Pallas kernels, attend(): pl.pallas_call(functools.partial(attend_kernel, rows=rows, cuts=cuts), gr...  9.9 us
    ppermute x1, waiting for transfers between devices, local(): lower = lax.ppermute(fetched[:4], 'y', [(i, (i + 1) % 4) for i in range(4)])  9 us
    pallas_call x1, Pallas kernels, expert(): pl.pallas_call(functools.partial(expert_kernel, first=first), grid=(first...  7.69 us
  transfers between devices with their start and end apart: 23, of which 10 were waited for; matrix products, arithmetic and copies ran while one was open for 10% of the time, Pallas kernels for 6%

profile of v7, /device:TPU:1, one launch (start us, length us, event | category | flops | bytes accessed | tf_op | source)
XLA Modules:
  0.0 208.4 jit_solution(2582891194751636300)
XLA Ops:
  0.7 1.9 broadcast_select_fusion.2
  2.6 1.4 collective-permute-start.1
  4.0 0.9 broadcast_in_dim.32
  4.9 5.5 %all-to-all-start = ((bf16[8,288,128]{2,1,0:T(8,128)(2,1)}), bf16[8,288,128]{2,1,0:T(8,128)(2,1)S(1)}, u32[]{:S(2)}, u32[]{:S(2)}) async-start(bf16[8,288,128]{2,1,0:T(8,128)(2,1)} %broadcast_in_dim.32), calls=%async_computation | async-start | bytes 1179648 | tf_op jit(solution)/shard_map/all_to_all | solution.py:338
  10.4 0.9 copy.45
  11.3 2.5 %copy.47 = bf16[512,2048]{0,1:T(8,128)(2,1)} copy(bf16[512,2048]{1,0:T(8,128)(2,1)S(1)} %copy-done.5) | data formatting | bytes 4194304 | tf_op args[2]
  13.9 2.8 %convolution_convert_fusion = bf16[8,128,512]{2,1,0:T(8,128)(2,1)} fusion(bf16[512,8,256]{0,2,1:T(8,128)(2,1)} %bitcast.71, bf16[128,8,192]{0,2,1:T(8,128)(2,1)} %bitcast.72), kind=kOutput, calls=%fused_computation.1 | convolution fusion | flops 134742016 | bytes 2359296 | tf_op jit(solution)/shard_map/qhd,rhd->hqr/dot_general | solution.py:292
  16.7 1.6 slice.78
  18.3 1.1 copy.63
  19.4 2.4 %pad_maximum_fusion = bf16[8,128,576]{2,1,0:T(8,128)(2,1)} fusion(bf16[8,128,64]{2,1,0:T(8,128)(2,1)S(1)} %bitcast.74, bf16[8,128,512]{2,1,0:T(8,128)(2,1)} %convolution_convert_fusion), kind=kLoop, calls=%fused_computation.2 | loop fusion | flops 2359296 | bytes 2359296 | tf_op jit(solution)/shard_map/concatenate | solution.py:293
  21.8 1.0 broadcast_select_fusion.1
  22.9 2.8 %collective-permute-start.3 = (bf16[4,288,128]{2,1,0:T(8,128)(2,1)S(1)}, bf16[4,288,128]{2,1,0:T(8,128)(2,1)}, u32[]{:S(2)}, u32[]{:S(2)}) collective-permute-start(bf16[4,288,128]{2,1,0:T(8,128)(2,1)S(1)} %get-tuple-element.34), channel_id=1, source_target_pairs={{0,3},{1,0},{2,1},{3,2},{4,7},{5,4},{6,5},{7,6},{8,11},{9,8},{10,9... | collective-permute-start | bytes 884744 | tf_op jit(solution)/shard_map/ppermute | solution.py:345
  26.3 2.9 %collective-permute-start.7 = (bf16[128,1792]{1,0:T(8,128)(2,1)S(1)}, bf16[128,1792]{1,0:T(8,128)(2,1)S(1)}, u32[]{:S(2)}, u32[]{:S(2)}) collective-permute-start(bf16[128,1792]{1,0:T(8,128)(2,1)S(1)} %pad_maximum_fusion.1.refs_0_), channel_id=1, source_target_pairs={{0,48},{16,0},{32,16},{48,32},{1,49},{17,1},{33,17},{49,33},{2,50}... | collective-permute-start | bytes 1376264 | tf_op jit(solution)/shard_map/ppermute | solution.py:271
  29.2 1.2 collective-permute-start.5
  30.4 1.4 collective-permute-done.3.refs_2_
  31.8 0.9 collective-permute-start.2
  32.7 9.0 %collective-permute-done.2.refs_1_ = bf16[4,288,128]{2,1,0:T(8,128)(2,1)} collective-permute-done((bf16[4,288,128]{2,1,0:T(8,128)(2,1)S(1)}, bf16[4,288,128]{2,1,0:T(8,128)(2,1)}, u32[]{:S(2)}, u32[]{:S(2)}) %collective-permute-start.2) | collective-permute-done | bytes 294944 | tf_op jit(solution)/shard_map/ppermute | solution.py:344
  41.7 0.7 collective-permute-done.6.refs_2_
  42.4 0.8 copy-done.13
  43.2 0.9 copy-done.19
  44.0 1.2 collective-permute-start.8
  45.2 2.3 %collective-permute-start.12 = (bf16[128,1792]{1,0:T(8,128)(2,1)}, bf16[128,1792]{1,0:T(8,128)(2,1)S(1)}, u32[]{:S(2)}, u32[]{:S(2)}) collective-permute-start(bf16[128,1792]{1,0:T(8,128)(2,1)} %copy-done.11), channel_id=1, source_target_pairs={{0,48},{16,0},{32,16},{48,32},{1,49},{17,1},{33,17},{49,33},{2,50}... | collective-permute-start | bytes 1376264 | tf_op jit(solution)/shard_map/ppermute | solution.py:271
  47.6 1.2 collective-permute-start.11
  48.8 1.3 copy-done.6
  50.2 1.1 copy-done.20
  51.2 9.9 %shard_map.122.own_ref = bf16[128,1024]{1,0:T(8,128)(2,1)S(1)} custom-call(s32[3]{0:T(128)S(1)} %pad_add_fusion.1.ids_ref, bf16[1024,576]{1,0:T(8,128)(2,1)S(1)} %bitcast.70, bf16[512,2048]{1,0:T(8,128)(2,1)S(1)} %copy-done.5, bf16[8,288,128]{2,1,0:T(8,128)(2,1)S(1)} %all-to-all-done.refs_0_, bf16[4,288,128]{2,1,0:T(8,128)(2,1)} %collective-permute-done.2.refs_1_, ...), custom_call_target="tpu_custom_call" | custom-call | flops 4563402752 | bytes 8000000 | tf_op jit(solution)/shard_map/pallas_call | solution.py:85
  61.2 0.8 copy-done.17
  61.9 2.0 collective-permute-start.13
  63.9 0.8 copy-done.9
  64.7 2.1 %collective-permute-start.15 = (bf16[128,896]{1,0:T(8,128)(2,1)S(1)}, bf16[128,896]{1,0:T(8,128)(2,1)S(1)}, u32[]{:S(2)}, u32[]{:S(2)}) collective-permute-start(bf16[128,896]{1,0:T(8,128)(2,1)S(1)} %slice.67), channel_id=1, source_target_pairs={{0,48},{16,0},{32,16},{48,32},{1,49},{17,1},{33,17},{49,33},{2,50}... | collective-permute-start | bytes 688136 | tf_op jit(solution)/shard_map/ppermute | solution.py:271
  66.8 1.0 collective-permute-start.17
  68.0 3.2 %collective-permute-done.15.refs_8_ = bf16[128,896]{1,0:T(8,128)(2,1)S(1)} collective-permute-done((bf16[128,896]{1,0:T(8,128)(2,1)S(1)}, bf16[128,896]{1,0:T(8,128)(2,1)S(1)}, u32[]{:S(2)}, u32[]{:S(2)}) %collective-permute-start.15) | collective-permute-done | bytes 229408 | tf_op jit(solution)/shard_map/ppermute | solution.py:271
  71.2 3.0 %collective-permute-done.14.refs_7_ = bf16[128,896]{1,0:T(8,128)(2,1)S(1)} collective-permute-done((bf16[128,896]{1,0:T(8,128)(2,1)S(1)}, bf16[128,896]{1,0:T(8,128)(2,1)S(1)}, u32[]{:S(2)}, u32[]{:S(2)}) %collective-permute-start.14) | collective-permute-done | bytes 229408 | tf_op jit(solution)/shard_map/ppermute | solution.py:267
  74.1 1.0 copy-done.8
  75.1 1.0 copy-done.10
  76.2 1.0 copy-done.12
  77.2 1.0 copy-done.14
  78.2 1.0 copy-done.16
  79.2 1.0 copy-done.18
  80.2 2.7 %shard_map.123 = bf16[8,2,16,1792]{3,2,1,0:T(8,128)(2,1)} custom-call(s32[8]{0:T(128)S(1)} %stack.77.order_ref, bf16[128,1024]{1,0:T(8,128)(2,1)S(1)} %shard_map.122.own_ref, bf16[128,1024]{1,0:T(8,128)(2,1)S(1)} %collective-permute-done.13.far_ref, bf16[128,1792]{1,0:T(8,128)(2,1)S(1)} %pad_maximum_fusion.1.refs_0_, bf16[128,1792]{1,0:T(8,128)(2,1)S(1)} %copy-done.16, ...), custom_call_target="tpu_custom_call" | custom-call | flops 939524096 | bytes 3670016 | tf_op jit(solution)/shard_map/pallas_call | solution.py:240
  82.9 5.9 %all-to-all-start.1 = ((bf16[8,2,16,1792]{3,2,1,0:T(8,128)(2,1)}), bf16[8,2,16,1792]{3,2,1,0:T(8,128)(2,1)S(1)}, u32[]{:S(2)}, u32[]{:S(2)}) async-start(bf16[8,2,16,1792]{3,2,1,0:T(8,128)(2,1)} %shard_map.123), calls=%async_computation.1 | async-start | bytes 1835008 | tf_op jit(solution)/shard_map/all_to_all | solution.py:363
  88.8 2.5 %collective-permute-start = (bf16[16,1792]{1,0:T(8,128)(2,1)S(1)}, bf16[16,1792]{1,0:T(8,128)(2,1)S(1)}, u32[]{:S(2)}, u32[]{:S(2)}) collective-permute-start(bf16[16,1792]{1,0:T(8,128)(2,1)S(1)} %get-tuple-element.39), channel_id=1, source_target_pairs={{0,8},{8,0},{1,9},{9,1},{2,10},{10,2},{3,11},{11,3},{4,12},{12,4},... | collective-permute-start | bytes 172040 | tf_op jit(solution)/shard_map/ppermute | solution.py:254
  91.5 0.7 pad_add_fusion
  92.8 11.9 %all-to-all-done.1 = bf16[8,2,16,1792]{3,2,1,0:T(8,128)(2,1)S(1)} async-done(((bf16[8,2,16,1792]{3,2,1,0:T(8,128)(2,1)}), bf16[8,2,16,1792]{3,2,1,0:T(8,128)(2,1)S(1)}, u32[]{:S(2)}, u32[]{:S(2)}) %all-to-all-start.1) | async-done | bytes 917536 | tf_op jit(solution)/shard_map/all_to_all | solution.py:363
  104.9 0.9 collective-permute-start.16
  107.3 2.2 %shard_map.124 = bf16[192,2,3584]{2,1,0:T(2,128)(2,1)S(1)} custom-call(bf16[384,32]{1,0:T(8,128)(2,1)S(1)} %convert_element_type.52.place_ref, bf16[32,3584]{1,0:T(8,128)(2,1)S(1)} %fusion.2.x_ref), custom_call_target="tpu_custom_call" | custom-call | flops 88080384 | bytes 2981888 | tf_op jit(solution)/shard_map/pallas_call | solution.py:165
  109.5 40.0 %all_to_all.20 = bf16[64,3,2,3584]{3,2,1,0:T(2,128)(2,1)S(1)} all-to-all(bf16[64,3,2,3584]{3,2,1,0:T(2,128)(2,1)S(1)} %bitcast.64), channel_id=1, replica_groups=mesh['z_lo'=2,'x'=4,'core'=2,'z_hi'=2,'y'=4] {'z_lo','x','z_hi','y'}, dimensions={0} | all-to-all | bytes 5505024 | tf_op jit(solution)/shard_map/all_to_all | solution.py:376
  149.6 2.0 copy-done.4
  151.6 7.7 %shard_map.125 = bf16[192,2,3584]{2,1,0:T(2,128)(2,1)S(1)} custom-call(bf16[192,2,3584]{2,1,0:T(2,128)(2,1)S(1)} %bitcast.66, bf16[3584,512]{1,0:T(8,128)(2,1)S(1)} %bitcast.67, bf16[3584,512]{1,0:T(8,128)(2,1)S(1)} %bitcast.68, bf16[512,3584]{1,0:T(8,128)(2,1)S(1)} %bitcast.69), custom_call_target="tpu_custom_call" | custom-call | flops 4227858432 | bytes 17000000 | tf_op jit(solution)/shard_map/pallas_call | solution.py:137
  159.3 1.5 copy-done.1
  160.8 7.2 %all-to-all-start.3 = ((bf16[64,3,2,3584]{3,2,1,0:T(2,128)(2,1)}), bf16[64,3,2,3584]{3,2,1,0:T(2,128)(2,1)S(1)}, u32[]{:S(2)}, u32[]{:S(2)}) async-start(bf16[64,3,2,3584]{3,2,1,0:T(2,128)(2,1)} %bitcast.65), calls=%async_computation.3 | async-start | bytes 5505024 | tf_op jit(solution)/shard_map/all_to_all | solution.py:376
  168.0 0.6 convert_divide_fusion
  168.7 1.1 collective-permute-start.18
  169.9 1.0 collective-permute-done.18
  170.9 0.7 pad_maximum_fusion.3
  171.8 0.7 copy.56
  172.5 0.8 slice_select_fusion
  173.5 0.7 broadcast_in_dim.65
  174.2 1.0 copy.60
  175.3 26.3 %all-to-all-done.3 = bf16[64,3,2,3584]{3,2,1,0:T(2,128)(2,1)S(1)} async-done(((bf16[64,3,2,3584]{3,2,1,0:T(2,128)(2,1)}), bf16[64,3,2,3584]{3,2,1,0:T(2,128)(2,1)S(1)}, u32[]{:S(2)}, u32[]{:S(2)}) %all-to-all-start.3) | async-done | bytes 2752544 | tf_op jit(solution)/shard_map/all_to_all | solution.py:376
  201.6 1.9 shard_map.126
  203.5 3.1 %collective-permute-start.19 = (f32[16,3584]{1,0:T(8,128)S(1)}, f32[16,3584]{1,0:T(8,128)S(1)}, u32[]{:S(2)}, u32[]{:S(2)}) collective-permute-start(f32[16,3584]{1,0:T(8,128)S(1)} %get-tuple-element.31), channel_id=1, source_target_pairs={{0,8},{8,0},{1,9},{9,1},{2,10},{10,2},{3,11},{11,3},{4,12},{12,4},... | collective-permute-start | bytes 688136 | tf_op jit(solution)/shard_map/ppermute | solution.py:254
  206.6 0.7 fusion.10
  207.7 0.7 fusion.7
  (106 shorter events, 4.2 us)
Async XLA Ops:
  0.6 3.4 %copy-start = (bf16[576,128]{1,0:T(8,128)(2,1)S(1)}, bf16[576,128]{1,0:T(8,128)(2,1)}, u32[]{:S(2)}) copy-start(bf16[576,128]{1,0:T(8,128)(2,1)} %param.12) | copy-start | bytes 442372
  0.6 9.8 %copy-start.24 = (bf16[128,1536]{1,0:T(8,128)(2,1)S(1)}, bf16[128,1536]{1,0:T(8,128)(2,1)}, u32[]{:S(2)}) copy-start(bf16[128,1536]{1,0:T(8,128)(2,1)} %param.11) | copy-start | bytes 1179652
  0.7 10.7 %copy-start.5 = (bf16[512,2048]{1,0:T(8,128)(2,1)S(1)}, bf16[512,2048]{1,0:T(8,128)(2,1)}, u32[]{:S(2)}) copy-start(bf16[512,2048]{1,0:T(8,128)(2,1)} %w_ref.1) | copy-start | bytes 6291460
  2.6 19.2 %collective-permute-start.1 = (bf16[64,1792]{1,0:T(8,128)(2,1)}, bf16[64,1792]{1,0:T(8,128)(2,1)}, u32[]{:S(2)}, u32[]{:S(2)}) collective-permute-start(bf16[64,1792]{1,0:T(8,128)(2,1)} %broadcast_select_fusion.2), channel_id=1, source_target_pairs={{0,8},{8,0},{1,9},{9,1},{2,10},{10,2},{3,11},{11,3},{4,12},{12,4},... | collective-permute-start | bytes 688136 | tf_op jit(solution)/shard_map/ppermute | solution.py:254
  4.9 17.9 %all-to-all-start = ((bf16[8,288,128]{2,1,0:T(8,128)(2,1)}), bf16[8,288,128]{2,1,0:T(8,128)(2,1)S(1)}, u32[]{:S(2)}, u32[]{:S(2)}) async-start(bf16[8,288,128]{2,1,0:T(8,128)(2,1)} %broadcast_in_dim.32), calls=%async_computation | async-start | bytes 1179648 | tf_op jit(solution)/shard_map/all_to_all | solution.py:338
  13.9 7.9 %copy-start.21 = (bf16[64,3584]{1,0:T(8,128)(2,1)S(1)}, bf16[64,3584]{1,0:T(8,128)(2,1)}, u32[]{:S(2)}) copy-start(bf16[64,3584]{1,0:T(8,128)(2,1)} %param.14) | copy-start | bytes 1376260
  22.9 8.9 %collective-permute-start.3 = (bf16[4,288,128]{2,1,0:T(8,128)(2,1)S(1)}, bf16[4,288,128]{2,1,0:T(8,128)(2,1)}, u32[]{:S(2)}, u32[]{:S(2)}) collective-permute-start(bf16[4,288,128]{2,1,0:T(8,128)(2,1)S(1)} %get-tuple-element.34), channel_id=1, source_target_pairs={{0,3},{1,0},{2,1},{3,2},{4,7},{5,4},{6,5},{7,6},{8,11},{9,8},{10,9... | collective-permute-start | bytes 884744 | tf_op jit(solution)/shard_map/ppermute | solution.py:345
  25.7 17.4 %collective-permute-start.4 = (bf16[8,288,128]{2,1,0:T(8,128)(2,1)S(1)}, bf16[8,288,128]{2,1,0:T(8,128)(2,1)S(1)}, u32[]{:S(2)}, u32[]{:S(2)}) collective-permute-start(bf16[8,288,128]{2,1,0:T(8,128)(2,1)S(1)} %all-to-all-done.refs_0_), channel_id=1, source_target_pairs={{0,8},{8,0},{1,9},{9,1},{2,10},{10,2},{3,11},{11,3},{4,12},{12,4},... | collective-permute-start | bytes 1769480 | tf_op jit(solution)/shard_map/ppermute | solution.py:254
  26.3 15.4 %collective-permute-start.7 = (bf16[128,1792]{1,0:T(8,128)(2,1)S(1)}, bf16[128,1792]{1,0:T(8,128)(2,1)S(1)}, u32[]{:S(2)}, u32[]{:S(2)}) collective-permute-start(bf16[128,1792]{1,0:T(8,128)(2,1)S(1)} %pad_maximum_fusion.1.refs_0_), channel_id=1, source_target_pairs={{0,48},{16,0},{32,16},{48,32},{1,49},{17,1},{33,17},{49,33},{2,50}... | collective-permute-start | bytes 1376264 | tf_op jit(solution)/shard_map/ppermute | solution.py:271
  29.2 13.1 %collective-permute-start.6 = (bf16[128,1792]{1,0:T(8,128)(2,1)S(1)}, bf16[128,1792]{1,0:T(8,128)(2,1)S(1)}, u32[]{:S(2)}, u32[]{:S(2)}) collective-permute-start(bf16[128,1792]{1,0:T(8,128)(2,1)S(1)} %pad_maximum_fusion.1.refs_0_), channel_id=1, source_target_pairs={{0,16},{16,32},{32,48},{48,0},{1,17},{17,33},{33,49},{49,1},{2,18}... | collective-permute-start | bytes 1376264 | tf_op jit(solution)/shard_map/ppermute | solution.py:267
  29.2 13.9 %collective-permute-start.5 = (bf16[128,1792]{1,0:T(8,128)(2,1)S(1)}, bf16[128,1792]{1,0:T(8,128)(2,1)S(1)}, u32[]{:S(2)}, u32[]{:S(2)}) collective-permute-start(bf16[128,1792]{1,0:T(8,128)(2,1)S(1)} %pad_maximum_fusion.1.refs_0_), channel_id=1, source_target_pairs={{0,64},{64,0},{1,65},{65,1},{2,66},{66,2},{3,67},{67,3},{4,68},{68... | collective-permute-start | bytes 1376264 | tf_op jit(solution)/shard_map/ppermute | solution.py:275
  31.8 9.9 %collective-permute-start.2 = (bf16[4,288,128]{2,1,0:T(8,128)(2,1)S(1)}, bf16[4,288,128]{2,1,0:T(8,128)(2,1)}, u32[]{:S(2)}, u32[]{:S(2)}) collective-permute-start(bf16[4,288,128]{2,1,0:T(8,128)(2,1)S(1)} %get-tuple-element.35), channel_id=1, source_target_pairs={{0,1},{1,2},{2,3},{3,0},{4,5},{5,6},{6,7},{7,4},{8,9},{9,10},{10,1... | collective-permute-start | bytes 884744 | tf_op jit(solution)/shard_map/ppermute | solution.py:344
  41.7 1.5 copy-start.11
  42.4 0.8 copy-start.13
  43.1 2.1 copy-start.15
  43.2 0.9 copy-start.19
  44.0 4.8 %collective-permute-start.8 = (bf16[4,288,128]{2,1,0:T(8,128)(2,1)}, bf16[4,288,128]{2,1,0:T(8,128)(2,1)}, u32[]{:S(2)}, u32[]{:S(2)}) collective-permute-start(bf16[4,288,128]{2,1,0:T(8,128)(2,1)} %collective-permute-done.2.refs_1_), channel_id=1, source_target_pairs={{0,8},{8,0},{1,9},{9,1},{2,10},{10,2},{3,11},{11,3},{4,12},{12,4},... | collective-permute-start | bytes 884744 | tf_op jit(solution)/shard_map/ppermute | solution.py:254
  45.2 3.6 %collective-permute-start.9 = (bf16[4,288,128]{2,1,0:T(8,128)(2,1)}, bf16[4,288,128]{2,1,0:T(8,128)(2,1)}, u32[]{:S(2)}, u32[]{:S(2)}) collective-permute-start(bf16[4,288,128]{2,1,0:T(8,128)(2,1)} %collective-permute-done.3.refs_2_), channel_id=1, source_target_pairs={{0,8},{8,0},{1,9},{9,1},{2,10},{10,2},{3,11},{11,3},{4,12},{12,4},... | collective-permute-start | bytes 884744 | tf_op jit(solution)/shard_map/ppermute | solution.py:254
  45.2 15.9 %collective-permute-start.12 = (bf16[128,1792]{1,0:T(8,128)(2,1)}, bf16[128,1792]{1,0:T(8,128)(2,1)S(1)}, u32[]{:S(2)}, u32[]{:S(2)}) collective-permute-start(bf16[128,1792]{1,0:T(8,128)(2,1)} %copy-done.11), channel_id=1, source_target_pairs={{0,48},{16,0},{32,16},{48,32},{1,49},{17,1},{33,17},{49,33},{2,50}... | collective-permute-start | bytes 1376264 | tf_op jit(solution)/shard_map/ppermute | solution.py:271
  47.6 14.4 %collective-permute-start.11 = (bf16[128,1792]{1,0:T(8,128)(2,1)}, bf16[128,1792]{1,0:T(8,128)(2,1)S(1)}, u32[]{:S(2)}, u32[]{:S(2)}) collective-permute-start(bf16[128,1792]{1,0:T(8,128)(2,1)} %copy-done.11), channel_id=1, source_target_pairs={{0,64},{64,0},{1,65},{65,1},{2,66},{66,2},{3,67},{67,3},{4,68},{68... | collective-permute-start | bytes 1376264 | tf_op jit(solution)/shard_map/ppermute | solution.py:275
  48.7 12.4 %collective-permute-start.10 = (bf16[128,1792]{1,0:T(8,128)(2,1)}, bf16[128,1792]{1,0:T(8,128)(2,1)S(1)}, u32[]{:S(2)}, u32[]{:S(2)}) collective-permute-start(bf16[128,1792]{1,0:T(8,128)(2,1)} %copy-done.15), channel_id=1, source_target_pairs={{0,16},{16,32},{32,48},{48,0},{1,17},{17,33},{33,49},{49,1},{2,18}... | collective-permute-start | bytes 1376264 | tf_op jit(solution)/shard_map/ppermute | solution.py:267
  48.8 1.3 copy-start.6
  50.1 1.1 copy-start.20
  61.1 0.8 copy-start.17
  61.9 2.0 copy-start.7
  61.9 12.2 %collective-permute-start.13 = (bf16[128,1024]{1,0:T(8,128)(2,1)S(1)}, bf16[128,1024]{1,0:T(8,128)(2,1)S(1)}, u32[]{:S(2)}, u32[]{:S(2)}) collective-permute-start(bf16[128,1024]{1,0:T(8,128)(2,1)S(1)} %shard_map.122.own_ref), channel_id=1, source_target_pairs={{0,8},{8,0},{1,9},{9,1},{2,10},{10,2},{3,11},{11,3},{4,12},{12,4},... | collective-permute-start | bytes 786440 | tf_op jit(solution)/shard_map/ppermute | solution.py:254
  63.9 0.8 copy-start.9
  64.7 6.4 %collective-permute-start.15 = (bf16[128,896]{1,0:T(8,128)(2,1)S(1)}, bf16[128,896]{1,0:T(8,128)(2,1)S(1)}, u32[]{:S(2)}, u32[]{:S(2)}) collective-permute-start(bf16[128,896]{1,0:T(8,128)(2,1)S(1)} %slice.67), channel_id=1, source_target_pairs={{0,48},{16,0},{32,16},{48,32},{1,49},{17,1},{33,17},{49,33},{2,50}... | collective-permute-start | bytes 688136 | tf_op jit(solution)/shard_map/ppermute | solution.py:271
  66.8 7.3 %collective-permute-start.14 = (bf16[128,896]{1,0:T(8,128)(2,1)S(1)}, bf16[128,896]{1,0:T(8,128)(2,1)S(1)}, u32[]{:S(2)}, u32[]{:S(2)}) collective-permute-start(bf16[128,896]{1,0:T(8,128)(2,1)S(1)} %slice.66), channel_id=1, source_target_pairs={{0,16},{16,32},{32,48},{48,0},{1,17},{17,33},{33,49},{49,1},{2,18}... | collective-permute-start | bytes 688136 | tf_op jit(solution)/shard_map/ppermute | solution.py:267
  66.8 24.7 %collective-permute-start.17 = (s32[16,8]{0,1:T(8,128)}, s32[16,8]{0,1:T(8,128)S(1)}, u32[]{:S(2)}, u32[]{:S(2)}) collective-permute-start(s32[16,8]{0,1:T(8,128)} %param.17), channel_id=1, source_target_pairs={{0,8},{8,0},{1,9},{9,1},{2,10},{10,2},{3,11},{11,3},{4,12},{12,4},... | collective-permute-start | bytes 1544 | tf_op jit(solution)/shard_map/ppermute | solution.py:254
  74.1 1.0 copy-start.8
  75.1 1.0 copy-start.10
  76.1 1.0 copy-start.12
  77.2 1.0 copy-start.14
  78.2 1.0 copy-start.16
  79.2 1.0 copy-start.18
  80.2 8.6 %copy-start.25 = (bf16[16,3584]{1,0:T(8,128)(2,1)S(1)}, bf16[16,3584]{1,0:T(8,128)(2,1)}, u32[]{:S(2)}) copy-start(bf16[16,3584]{1,0:T(8,128)(2,1)} %param.15) | copy-start | bytes 344068
  82.9 24.2 %copy-start.27 = (f32[3584]{0:T(1024)S(1)}, f32[3584]{0:T(1024)}, u32[]{:S(2)}) copy-start(f32[3584]{0:T(1024)} %param.16) | copy-start | bytes 43012
  82.9 21.8 %all-to-all-start.1 = ((bf16[8,2,16,1792]{3,2,1,0:T(8,128)(2,1)}), bf16[8,2,16,1792]{3,2,1,0:T(8,128)(2,1)S(1)}, u32[]{:S(2)}, u32[]{:S(2)}) async-start(bf16[8,2,16,1792]{3,2,1,0:T(8,128)(2,1)} %shard_map.123), calls=%async_computation.1 | async-start | bytes 1835008 | tf_op jit(solution)/shard_map/all_to_all | solution.py:363
  88.8 16.0 %collective-permute-start = (bf16[16,1792]{1,0:T(8,128)(2,1)S(1)}, bf16[16,1792]{1,0:T(8,128)(2,1)S(1)}, u32[]{:S(2)}, u32[]{:S(2)}) collective-permute-start(bf16[16,1792]{1,0:T(8,128)(2,1)S(1)} %get-tuple-element.39), channel_id=1, source_target_pairs={{0,8},{8,0},{1,9},{9,1},{2,10},{10,2},{3,11},{11,3},{4,12},{12,4},... | collective-permute-start | bytes 172040 | tf_op jit(solution)/shard_map/ppermute | solution.py:254
  104.9 1.9 collective-permute-start.16
  106.8 42.7 %copy-start.22 = (bf16[2,16,1792]{2,1,0:T(8,128)(2,1)}, bf16[2,16,1792]{2,1,0:T(8,128)(2,1)S(1)}, u32[]{:S(2)}) copy-start(bf16[2,16,1792]{2,1,0:T(8,128)(2,1)S(1)} %get-tuple-element.37) | copy-start | bytes 344068
  107.2 42.3 %copy-start.3 = (bf16[1,3584,512]{2,1,0:T(8,128)(2,1)S(1)}, bf16[1,3584,512]{2,1,0:T(8,128)(2,1)}, u32[]{:S(2)}) copy-start(bf16[1,3584,512]{2,1,0:T(8,128)(2,1)} %param.20) | copy-start | bytes 11010052
  109.5 40.0 %copy-start.2 = (bf16[1,3584,512]{2,1,0:T(8,128)(2,1)S(1)}, bf16[1,3584,512]{2,1,0:T(8,128)(2,1)}, u32[]{:S(2)}) copy-start(bf16[1,3584,512]{2,1,0:T(8,128)(2,1)} %param.19) | copy-start | bytes 11010052
  149.5 2.0 copy-start.4
  159.3 1.5 copy-start.1
  160.8 7.2 %copy-start.26 = (s32[16,8]{0,1:T(8,128)S(1)}, s32[16,8]{0,1:T(8,128)}, u32[]{:S(2)}) copy-start(s32[16,8]{0,1:T(8,128)} %param.18) | copy-start | bytes 1540
  160.8 40.8 %all-to-all-start.3 = ((bf16[64,3,2,3584]{3,2,1,0:T(2,128)(2,1)}), bf16[64,3,2,3584]{3,2,1,0:T(2,128)(2,1)S(1)}, u32[]{:S(2)}, u32[]{:S(2)}) async-start(bf16[64,3,2,3584]{3,2,1,0:T(2,128)(2,1)} %bitcast.65), calls=%async_computation.3 | async-start | bytes 5505024 | tf_op jit(solution)/shard_map/all_to_all | solution.py:376
  168.7 2.2 %collective-permute-start.18 = (f32[16,8]{0,1:T(8,128)}, f32[16,8]{0,1:T(8,128)}, u32[]{:S(2)}, u32[]{:S(2)}) collective-permute-start(f32[16,8]{0,1:T(8,128)} %convert_divide_fusion), channel_id=1, source_target_pairs={{0,8},{8,0},{1,9},{9,1},{2,10},{10,2},{3,11},{11,3},{4,12},{12,4},... | collective-permute-start | bytes 1544 | tf_op jit(solution)/shard_map/ppermute | solution.py:254
  201.6 5.0 %copy-start.23 = (bf16[2,16,1792]{2,1,0:T(8,128)(2,1)S(1)}, bf16[2,16,1792]{2,1,0:T(8,128)(2,1)}, u32[]{:S(2)}) copy-start(bf16[2,16,1792]{2,1,0:T(8,128)(2,1)} %copy-done.22) | copy-start | bytes 344068
  203.5 4.2 %collective-permute-start.19 = (f32[16,3584]{1,0:T(8,128)S(1)}, f32[16,3584]{1,0:T(8,128)S(1)}, u32[]{:S(2)}, u32[]{:S(2)}) collective-permute-start(f32[16,3584]{1,0:T(8,128)S(1)} %get-tuple-element.31), channel_id=1, source_target_pairs={{0,8},{8,0},{1,9},{9,1},{2,10},{10,2},{3,11},{11,3},{4,12},{12,4},... | collective-permute-start | bytes 688136 | tf_op jit(solution)/shard_map/ppermute | solution.py:254

commit v8 on v6

--- a/solution.py
+++ b/solution.py
@@ -13,6 +13,7 @@
 TOP = 8
 QK = 192
 CAP = 3
+CARRIED = 1024
 SLOTS = (slice(0, 3),)
 
 CTX = ("z_lo", "x", "core")
@@ -203,11 +204,23 @@
     )(*[a for part in parts for a in part])
 
 
-def project_kernel(order_ref, own_ref, far_ref, *refs):
+def project_kernel(order_ref, own_ref, far_ref, gathered_ref, *refs):
     *chunk_refs, left_ref, right_ref, out_ref, x_ref, w_ref = refs
     rows = own_ref.shape[0]
     parts = out_ref.shape[0]
     tok = rows // parts
+
+    def multiply(weights_ref, first):
+        n = 256
+        for c in range(0, weights_ref.shape[1], n):
+            y = jnp.dot(x_ref[...], weights_ref[:, c : c + n], preferred_element_type=F32).astype(BF)
+            for e in range(parts):
+                out_ref[e, 0, :, first + c : first + c + n] = y[e * tok : (e + 1) * tok]
+                out_ref[e, 1, :, first + c : first + c + n] = y[rows + e * tok : rows + (e + 1) * tok]
+
+    x_ref[:rows] = own_ref[...]
+    x_ref[rows:] = far_ref[...]
+    multiply(gathered_ref, w_ref.shape[1])
     for i in range(len(chunk_refs) + 1):
         columns = pl.ds(pl.multiple_of(order_ref[i] * VD, VD), VD)
         x_ref[:rows, i * VD : (i + 1) * VD] = own_ref[:, columns]
@@ -217,29 +230,25 @@
     half = left_ref.shape[1]
     w_ref[len(chunk_refs) * VD :, :half] = left_ref[...]
     w_ref[len(chunk_refs) * VD :, half:] = right_ref[...]
-    n = 256
-    for c in range(0, w_ref.shape[1], n):
-        y = jnp.dot(x_ref[...], w_ref[:, c : c + n], preferred_element_type=F32).astype(BF)
-        for e in range(parts):
-            out_ref[e, 0, :, c : c + n] = y[e * tok : (e + 1) * tok]
-            out_ref[e, 1, :, c : c + n] = y[rows + e * tok : rows + (e + 1) * tok]
-
-
-def project(order, own, far, chunks, parts):
+    multiply(w_ref, 0)
+
+
+def project(order, own, far, gathered, chunks, parts):
     rows, depth = own.shape
-    width = chunks[0].shape[1]
+    carried = chunks[0].shape[1]
+    width = carried + gathered.shape[1]
     whole = pl.BlockSpec(memory_space=pltpu.VMEM)
     return pl.pallas_call(
         project_kernel,
-        in_specs=[pl.BlockSpec(memory_space=pltpu.SMEM)] + [whole] * (2 + len(chunks)),
+        in_specs=[pl.BlockSpec(memory_space=pltpu.SMEM)] + [whole] * (3 + len(chunks)),
         out_specs=whole,
         out_shape=jax.ShapeDtypeStruct((parts, 2, rows // parts, width), BF),
-        scratch_shapes=[pltpu.VMEM((2 * rows, depth), BF), pltpu.VMEM((depth, width), BF)],
+        scratch_shapes=[pltpu.VMEM((2 * rows, depth), BF), pltpu.VMEM((depth, carried), BF)],
         compiler_params=pltpu.CompilerParams(vmem_limit_bytes=32 * 2**20),
         cost_estimate=pl.CostEstimate(
             flops=4 * rows * depth * width, bytes_accessed=2 * depth * width, transcendentals=0
         ),
-    )(order, own, far, *chunks)
+    )(order, own, far, gathered, *chunks)
 
 
 def swap(mine):
@@ -325,6 +334,8 @@
     chips = 64
     core = lax.axis_index("core")
     chunk = own_w_out(w_out)
+    gathered = lax.all_gather(chunk[:, CARRIED:], CTX_CHIPS, axis=0, tiled=True)
+    chunk = chunk[:, :CARRIED]
     mate, before, after = across(chunk), up(chunk), down(chunk)
     near = lax.all_to_all(
         jnp.broadcast_to(latents[None], (8,) + latents.shape), CTX_CHIPS, split_axis=0, concat_axis=0, tiled=True
@@ -345,7 +356,7 @@
     half = width // 2
     lower, upper = resid[:, :half], resid[:, half:]
     resid2 = jnp.stack([jnp.where(core == 0, lower, upper), swap(jnp.where(core == 0, upper, lower))])
-    attn = project(order, heads_out, swap(heads_out), chunks, 8)
+    attn = project(order, heads_out, swap(heads_out), gathered, chunks, 8)
     attn = lax.all_to_all(attn, EP, split_axis=0, concat_axis=0, tiled=True)
     summed = (resid2.astype(F32) + jnp.sum(attn.astype(F32), axis=0)).astype(BF)
     others = swap(summed)[::-1]

time: 203 us -> 218 us (1.074)
  between operations: 0.98 us -> 14.4 us
  local copies, waits for them, and re-layouts: 20.6 us -> 16.2 us
  other arithmetic: 4.89 us -> 7.44 us
    unnamed x37, local copies, waits for them, and re-layouts: 13.7 us -> 10.8 us
    ppermute x2, waiting for transfers between devices: 9.65 us -> 12.1 us  [across(): return lax.ppermute(a, 'z_lo', SWAP)]
  transfers between devices with their start and end apart: 19 -> 20, of which waited for: 11 -> 10; matrix products, arithmetic and copies ran while one was open for 9% -> 8% of each run, Pallas kernels for 5% -> 5%
where the time goes in v8:
time: 218 us; the launch traced here: 216 us
  waiting for transfers between devices  62.9 us (29%)
  starting transfers between devices  42.5 us (19%)
  blocking collectives  41.3 us (19%)
  Pallas kernels  28.4 us (13%)
  local copies, waits for them, and re-layouts  16.2 us (7%)
  between operations  14.4 us (7%)
  other arithmetic  7.44 us (3%)
  matrix products  2.71 us (1%)
    all_to_all x1, blocking collectives, exchange(): lax.all_to_all(units, CHIPS, split_axis=0, concat_axis=0, tiled=True)  41.3 us
    all_to_all x1, waiting for transfers between devices, exchange(): lax.all_to_all(units, CHIPS, split_axis=0, concat_axis=0, tiled=True)  28.4 us
    all_to_all x1, waiting for transfers between devices, local(): attn = lax.all_to_all(attn, EP, split_axis=0, concat_axis=0, tiled=True)  13 us
    ppermute x2, waiting for transfers between devices, across(): return lax.ppermute(a, 'z_lo', SWAP)  12.1 us
    ppermute x8, starting transfers between devices, swap(): return lax.ppermute(mine, 'core', SWAP)  11.6 us
    pallas_call x1, Pallas kernels, attend(): pl.pallas_call(functools.partial(attend_kernel, rows=rows, cuts=cuts), gr...  10.9 us
    unnamed x37, local copies, waits for them, and re-layouts  10.8 us
    pallas_call x1, Pallas kernels, expert(): pl.pallas_call(functools.partial(expert_kernel, first=first), grid=(first...  10 us
  transfers between devices with their start and end apart: 20, of which 10 were waited for; matrix products, arithmetic and copies ran while one was open for 8% of the time, Pallas kernels for 5%

profile of v8, /device:TPU:1, one launch (start us, length us, event | category | flops | bytes accessed | tf_op | source)
XLA Modules:
  0.0 215.8 jit_solution(12591018054195618033)
XLA Ops:
  7.2 1.1 broadcast_select_fusion.2
  8.3 1.5 collective-permute-start.1
  9.8 2.1 broadcast_in_dim.32
  11.9 5.6 %all-to-all-start = ((bf16[8,576,128]{2,1,0:T(8,128)(2,1)}), bf16[8,576,128]{2,1,0:T(8,128)(2,1)}, u32[]{:S(2)}, u32[]{:S(2)}) async-start(bf16[8,576,128]{2,1,0:T(8,128)(2,1)} %broadcast_in_dim.32), calls=%async_computation | async-start | bytes 2359296 | tf_op jit(solution)/shard_map/all_to_all | solution.py:340
  17.6 1.0 broadcast_select_fusion
  18.6 0.7 pad_maximum_fusion.2
  19.3 0.2 copy.45
  19.5 2.5 %copy.47 = bf16[512,2048]{0,1:T(8,128)(2,1)} copy(bf16[512,2048]{1,0:T(8,128)(2,1)S(1)} %copy-done.3) | data formatting | bytes 4194304 | tf_op args[2]
  22.1 0.7 fusion.3.refs_0_
  22.8 1.4 collective-permute-start.2
  24.2 1.2 collective-permute-start.3
  25.4 1.5 collective-permute-start.4
  26.9 2.7 %convolution_convert_fusion = bf16[8,128,512]{2,1,0:T(8,128)(2,1)} fusion(bf16[512,8,256]{0,2,1:T(8,128)(2,1)} %bitcast.69, bf16[128,8,192]{0,2,1:T(8,128)(2,1)S(1)} %bitcast.71), kind=kOutput, calls=%fused_computation.1 | convolution fusion | flops 134742016 | bytes 2359296 | tf_op jit(solution)/shard_map/qhd,rhd->hqr/dot_general | solution.py:293
  29.6 0.8 copy.63
  30.4 1.4 pad_maximum_fusion
  31.9 12.1 %collective-permute-done.2.refs_1_ = bf16[128,1024]{1,0:T(8,128)(2,1)} collective-permute-done((bf16[128,1024]{1,0:T(8,128)(2,1)}, bf16[128,1024]{1,0:T(8,128)(2,1)}, u32[]{:S(2)}, u32[]{:S(2)}) %collective-permute-start.2) | collective-permute-done | bytes 262176 | tf_op jit(solution)/shard_map/ppermute | solution.py:276
  44.0 0.8 collective-permute-done.3.refs_2_
  44.8 1.4 collective-permute-start.5
  46.3 1.1 collective-permute-start.7
  47.5 2.4 %collective-permute-start.8 = (bf16[128,1024]{1,0:T(8,128)(2,1)}, bf16[128,1024]{1,0:T(8,128)(2,1)S(1)}, u32[]{:S(2)}, u32[]{:S(2)}) collective-permute-start(bf16[128,1024]{1,0:T(8,128)(2,1)} %collective-permute-done.4.refs_3_), channel_id=1, source_target_pairs={{0,48},{16,0},{32,16},{48,32},{1,49},{17,1},{33,17},{49,33},{2,50}... | collective-permute-start | bytes 786440 | tf_op jit(solution)/shard_map/ppermute | solution.py:272
  49.9 10.9 %shard_map.122.own_ref = bf16[128,1024]{1,0:T(8,128)(2,1)} custom-call(s32[2]{0:T(128)S(1)} %pad_add_fusion.1.ids_ref, bf16[1024,576]{1,0:T(8,128)(2,1)S(1)} %bitcast.68, bf16[8,576,128]{2,1,0:T(8,128)(2,1)} %all-to-all-done.near_ref, bf16[8,576,128]{2,1,0:T(8,128)(2,1)} %collective-permute-done.5.far_ref, bf16[512,2048]{1,0:T(8,128)(2,1)S(1)} %copy-done.3), custom_call_target="tpu_custom_call" | custom-call | flops 4563402752 | bytes 8000000 | tf_op jit(solution)/shard_map/pallas_call | solution.py:77
  60.8 2.5 %collective-permute-done.6.refs_4_ = bf16[128,1024]{1,0:T(8,128)(2,1)S(1)} collective-permute-done((bf16[128,1024]{1,0:T(8,128)(2,1)}, bf16[128,1024]{1,0:T(8,128)(2,1)S(1)}, u32[]{:S(2)}, u32[]{:S(2)}) %collective-permute-start.6) | collective-permute-done | bytes 262176 | tf_op jit(solution)/shard_map/ppermute | solution.py:268
  63.3 0.7 copy-done.9
  64.0 1.0 collective-permute-start.9
  65.1 0.7 copy-done.7
  65.8 2.7 %collective-permute-start.11 = (bf16[128,512]{1,0:T(8,128)(2,1)S(1)}, bf16[128,512]{1,0:T(8,128)(2,1)S(1)}, u32[]{:S(2)}, u32[]{:S(2)}) collective-permute-start(bf16[128,512]{1,0:T(8,128)(2,1)S(1)} %slice.67), channel_id=1, source_target_pairs={{0,48},{16,0},{32,16},{48,32},{1,49},{17,1},{33,17},{49,33},{2,50}... | collective-permute-start | bytes 393224 | tf_op jit(solution)/shard_map/ppermute | solution.py:272
  68.6 3.5 %collective-permute-done.10.refs_7_ = bf16[128,512]{1,0:T(8,128)(2,1)S(1)} collective-permute-done((bf16[128,512]{1,0:T(8,128)(2,1)S(1)}, bf16[128,512]{1,0:T(8,128)(2,1)S(1)}, u32[]{:S(2)}, u32[]{:S(2)}) %collective-permute-start.10) | collective-permute-done | bytes 131104 | tf_op jit(solution)/shard_map/ppermute | solution.py:268
  72.1 1.4 copy-done.4
  73.5 0.9 copy-done.6
  74.5 0.9 copy-done.8
  75.4 0.9 copy-done.10
  76.4 3.4 %shard_map.123 = bf16[8,2,16,1792]{3,2,1,0:T(8,128)(2,1)} custom-call(s32[8]{0:T(128)S(1)} %stack.74.order_ref, bf16[128,1024]{1,0:T(8,128)(2,1)} %shard_map.122.own_ref, bf16[128,1024]{1,0:T(8,128)(2,1)S(1)} %collective-permute-done.9.far_ref, bf16[1024,768]{1,0:T(8,128)(2,1)S(1)} %copy-done.4, bf16[128,1024]{1,0:T(8,128)(2,1)} %fusion.3.refs_0_, ...), custom_call_target="tpu_custom_call" | custom-call | flops 939524096 | bytes 3670016 | tf_op jit(solution)/shard_map/pallas_call | solution.py:241
  79.8 7.4 %all-to-all-start.1 = ((bf16[8,2,16,1792]{3,2,1,0:T(8,128)(2,1)}), bf16[8,2,16,1792]{3,2,1,0:T(8,128)(2,1)S(1)}, u32[]{:S(2)}, u32[]{:S(2)}) async-start(bf16[8,2,16,1792]{3,2,1,0:T(8,128)(2,1)} %shard_map.123), calls=%async_computation.1 | async-start | bytes 1835008 | tf_op jit(solution)/shard_map/all_to_all | solution.py:360
  87.2 1.1 collective-permute-start
  88.3 0.1 collective-permute-start.13
  88.5 0.1 and.51
  88.6 0.9 collective-permute-done.13
  89.5 0.1 fusion.9
  89.7 0.1 copy.51
  90.0 13.0 %all-to-all-done.1 = bf16[8,2,16,1792]{3,2,1,0:T(8,128)(2,1)S(1)} async-done(((bf16[8,2,16,1792]{3,2,1,0:T(8,128)(2,1)}), bf16[8,2,16,1792]{3,2,1,0:T(8,128)(2,1)S(1)}, u32[]{:S(2)}, u32[]{:S(2)}) %all-to-all-start.1) | async-done | bytes 917536 | tf_op jit(solution)/shard_map/all_to_all | solution.py:360
  103.0 0.1 convert_reduce_fusion
  103.2 1.1 collective-permute-start.12
  104.4 0.1 copy.54
  104.6 0.1 reshape.153
  104.8 0.5 collective-permute-done.12
  105.4 0.1 multiply_reduce_fusion
  105.6 0.1 fusion.2.x_ref
  105.7 2.2 %shard_map.124 = bf16[192,2,3584]{2,1,0:T(2,128)(2,1)S(1)} custom-call(bf16[384,32]{1,0:T(8,128)(2,1)S(1)} %convert_element_type.52.place_ref, bf16[32,3584]{1,0:T(8,128)(2,1)S(1)} %fusion.2.x_ref), custom_call_target="tpu_custom_call" | custom-call | flops 88080384 | bytes 2981888 | tf_op jit(solution)/shard_map/pallas_call | solution.py:158
  108.0 41.3 %all_to_all.20 = bf16[64,3,2,3584]{3,2,1,0:T(2,128)(2,1)S(1)} all-to-all(bf16[64,3,2,3584]{3,2,1,0:T(2,128)(2,1)S(1)} %bitcast.63), channel_id=1, replica_groups=mesh['z_lo'=2,'x'=4,'core'=2,'z_hi'=2,'y'=4] {'z_lo','x','z_hi','y'}, dimensions={0} | all-to-all | bytes 5505024 | tf_op jit(solution)/shard_map/all_to_all | solution.py:373
  149.3 10.0 %shard_map.125 = bf16[192,2,3584]{2,1,0:T(2,128)(2,1)S(1)} custom-call(bf16[192,2,3584]{2,1,0:T(2,128)(2,1)S(1)} %bitcast.65, bf16[3584,512]{1,0:T(8,128)(2,1)S(1)} %bitcast.66, bf16[3584,512]{1,0:T(8,128)(2,1)S(1)} %bitcast.67, bf16[512,3584]{1,0:T(8,128)(2,1)} %bitcast.70), custom_call_target="tpu_custom_call" | custom-call | flops 4227858432 | bytes 17000000 | tf_op jit(solution)/shard_map/pallas_call | solution.py:130
  159.3 1.5 copy-done
  160.8 7.5 %all-to-all-start.3 = ((bf16[64,3,2,3584]{3,2,1,0:T(2,128)(2,1)}), bf16[64,3,2,3584]{3,2,1,0:T(2,128)(2,1)S(1)}, u32[]{:S(2)}, u32[]{:S(2)}) async-start(bf16[64,3,2,3584]{3,2,1,0:T(2,128)(2,1)} %bitcast.64), calls=%async_computation.3 | async-start | bytes 5505024 | tf_op jit(solution)/shard_map/all_to_all | solution.py:373
  168.4 1.6 collective-permute-start.14
  169.9 0.1 copy.59
  170.1 0.7 collective-permute-done.14
  170.8 0.1 select_reduce_fusion
  171.3 0.7 broadcast_in_dim.65
  172.0 1.0 copy.60
  173.1 28.4 %all-to-all-done.3 = bf16[64,3,2,3584]{3,2,1,0:T(2,128)(2,1)S(1)} async-done(((bf16[64,3,2,3584]{3,2,1,0:T(2,128)(2,1)}), bf16[64,3,2,3584]{3,2,1,0:T(2,128)(2,1)S(1)}, u32[]{:S(2)}, u32[]{:S(2)}) %all-to-all-start.3) | async-done | bytes 2752544 | tf_op jit(solution)/shard_map/all_to_all | solution.py:373
  201.5 1.9 shard_map.126
  203.4 3.8 %collective-permute-start.15 = (f32[16,3584]{1,0:T(8,128)S(1)}, f32[16,3584]{1,0:T(8,128)S(1)}, u32[]{:S(2)}, u32[]{:S(2)}) collective-permute-start(f32[16,3584]{1,0:T(8,128)S(1)} %get-tuple-element.23), channel_id=1, source_target_pairs={{0,8},{8,0},{1,9},{9,1},{2,10},{10,2},{3,11},{11,3},{4,12},{12,4},... | collective-permute-start | bytes 688136 | tf_op jit(solution)/shard_map/ppermute | solution.py:255
  207.2 0.7 fusion.11
  207.8 0.5 collective-permute-done.15
  208.3 0.7 fusion.8
  (78 shorter events, 1.5 us)
Async XLA Ops:
  7.2 10.4 %copy-start.11 = (bf16[64,3584]{1,0:T(8,128)(2,1)S(1)}, bf16[64,3584]{1,0:T(8,128)(2,1)}, u32[]{:S(2)}) copy-start(bf16[64,3584]{1,0:T(8,128)(2,1)} %param.14) | copy-start | bytes 1376260
  8.3 9.2 %collective-permute-start.1 = (bf16[64,1792]{1,0:T(8,128)(2,1)S(1)}, bf16[64,1792]{1,0:T(8,128)(2,1)}, u32[]{:S(2)}, u32[]{:S(2)}) collective-permute-start(bf16[64,1792]{1,0:T(8,128)(2,1)S(1)} %broadcast_select_fusion.2), channel_id=1, source_target_pairs={{0,8},{8,0},{1,9},{9,1},{2,10},{10,2},{3,11},{11,3},{4,12},{12,4},... | collective-permute-start | bytes 688136 | tf_op jit(solution)/shard_map/ppermute | solution.py:255
  11.9 7.4 %copy-start.12 = (bf16[128,1536]{1,0:T(8,128)(2,1)S(1)}, bf16[128,1536]{1,0:T(8,128)(2,1)}, u32[]{:S(2)}) copy-start(bf16[128,1536]{1,0:T(8,128)(2,1)} %param.11) | copy-start | bytes 1179652
  11.9 7.6 %copy-start.3 = (bf16[512,2048]{1,0:T(8,128)(2,1)S(1)}, bf16[512,2048]{1,0:T(8,128)(2,1)}, u32[]{:S(2)}) copy-start(bf16[512,2048]{1,0:T(8,128)(2,1)} %w_ref.1) | copy-start | bytes 6291460
  11.9 32.9 %all-to-all-start = ((bf16[8,576,128]{2,1,0:T(8,128)(2,1)}), bf16[8,576,128]{2,1,0:T(8,128)(2,1)}, u32[]{:S(2)}, u32[]{:S(2)}) async-start(bf16[8,576,128]{2,1,0:T(8,128)(2,1)} %broadcast_in_dim.32), calls=%async_computation | async-start | bytes 2359296 | tf_op jit(solution)/shard_map/all_to_all | solution.py:340
  17.5 54.6 %all-gather.2.cloned.1.call-start = ((), (), s32[]{:S(2)}) async-start(), calls=%async_computation.4 | async-start | bytes 1769472 | tf_op jit(solution)/shard_map/all_gather | solution.py:337
  22.8 21.2 %collective-permute-start.2 = (bf16[128,1024]{1,0:T(8,128)(2,1)}, bf16[128,1024]{1,0:T(8,128)(2,1)}, u32[]{:S(2)}, u32[]{:S(2)}) collective-permute-start(bf16[128,1024]{1,0:T(8,128)(2,1)} %fusion.3.refs_0_), channel_id=1, source_target_pairs={{0,64},{64,0},{1,65},{65,1},{2,66},{66,2},{3,67},{67,3},{4,68},{68... | collective-permute-start | bytes 786440 | tf_op jit(solution)/shard_map/ppermute | solution.py:276
  24.2 20.6 %collective-permute-start.3 = (bf16[128,1024]{1,0:T(8,128)(2,1)}, bf16[128,1024]{1,0:T(8,128)(2,1)}, u32[]{:S(2)}, u32[]{:S(2)}) collective-permute-start(bf16[128,1024]{1,0:T(8,128)(2,1)} %fusion.3.refs_0_), channel_id=1, source_target_pairs={{0,16},{16,32},{32,48},{48,0},{1,17},{17,33},{33,49},{49,1},{2,18}... | collective-permute-start | bytes 786440 | tf_op jit(solution)/shard_map/ppermute | solution.py:268
  25.4 19.5 %collective-permute-start.4 = (bf16[128,1024]{1,0:T(8,128)(2,1)}, bf16[128,1024]{1,0:T(8,128)(2,1)}, u32[]{:S(2)}, u32[]{:S(2)}) collective-permute-start(bf16[128,1024]{1,0:T(8,128)(2,1)} %fusion.3.refs_0_), channel_id=1, source_target_pairs={{0,48},{16,0},{32,16},{48,32},{1,49},{17,1},{33,17},{49,33},{2,50}... | collective-permute-start | bytes 786440 | tf_op jit(solution)/shard_map/ppermute | solution.py:272
  44.8 5.1 %collective-permute-start.5 = (bf16[8,576,128]{2,1,0:T(8,128)(2,1)}, bf16[8,576,128]{2,1,0:T(8,128)(2,1)}, u32[]{:S(2)}, u32[]{:S(2)}) collective-permute-start(bf16[8,576,128]{2,1,0:T(8,128)(2,1)} %all-to-all-done.near_ref), channel_id=1, source_target_pairs={{0,8},{8,0},{1,9},{9,1},{2,10},{10,2},{3,11},{11,3},{4,12},{12,4},... | collective-permute-start | bytes 3538952 | tf_op jit(solution)/shard_map/ppermute | solution.py:255
  46.3 17.0 %collective-permute-start.7 = (bf16[128,1024]{1,0:T(8,128)(2,1)}, bf16[128,1024]{1,0:T(8,128)(2,1)S(1)}, u32[]{:S(2)}, u32[]{:S(2)}) collective-permute-start(bf16[128,1024]{1,0:T(8,128)(2,1)} %collective-permute-done.4.refs_3_), channel_id=1, source_target_pairs={{0,64},{64,0},{1,65},{65,1},{2,66},{66,2},{3,67},{67,3},{4,68},{68... | collective-permute-start | bytes 786440 | tf_op jit(solution)/shard_map/ppermute | solution.py:276
  47.5 15.8 %collective-permute-start.8 = (bf16[128,1024]{1,0:T(8,128)(2,1)}, bf16[128,1024]{1,0:T(8,128)(2,1)S(1)}, u32[]{:S(2)}, u32[]{:S(2)}) collective-permute-start(bf16[128,1024]{1,0:T(8,128)(2,1)} %collective-permute-done.4.refs_3_), channel_id=1, source_target_pairs={{0,48},{16,0},{32,16},{48,32},{1,49},{17,1},{33,17},{49,33},{2,50}... | collective-permute-start | bytes 786440 | tf_op jit(solution)/shard_map/ppermute | solution.py:272
  49.9 13.4 %collective-permute-start.6 = (bf16[128,1024]{1,0:T(8,128)(2,1)}, bf16[128,1024]{1,0:T(8,128)(2,1)S(1)}, u32[]{:S(2)}, u32[]{:S(2)}) collective-permute-start(bf16[128,1024]{1,0:T(8,128)(2,1)} %collective-permute-done.2.refs_1_), channel_id=1, source_target_pairs={{0,16},{16,32},{32,48},{48,0},{1,17},{17,33},{33,49},{49,1},{2,18}... | collective-permute-start | bytes 786440 | tf_op jit(solution)/shard_map/ppermute | solution.py:268
  63.3 2.4 %copy-start.5 = (bf16[128,1024]{1,0:T(8,128)(2,1)}, bf16[128,1024]{1,0:T(8,128)(2,1)S(1)}, u32[]{:S(2)}) copy-start(bf16[128,1024]{1,0:T(8,128)(2,1)S(1)} %collective-permute-done.7.refs_5_) | copy-start | bytes 786436
  63.3 0.7 copy-start.9
  64.0 8.1 %collective-permute-start.9 = (bf16[128,1024]{1,0:T(8,128)(2,1)}, bf16[128,1024]{1,0:T(8,128)(2,1)S(1)}, u32[]{:S(2)}, u32[]{:S(2)}) collective-permute-start(bf16[128,1024]{1,0:T(8,128)(2,1)} %shard_map.122.own_ref), channel_id=1, source_target_pairs={{0,8},{8,0},{1,9},{9,1},{2,10},{10,2},{3,11},{11,3},{4,12},{12,4},... | collective-permute-start | bytes 786440 | tf_op jit(solution)/shard_map/ppermute | solution.py:255
  65.0 0.7 copy-start.7
  65.7 6.3 %collective-permute-start.10 = (bf16[128,512]{1,0:T(8,128)(2,1)S(1)}, bf16[128,512]{1,0:T(8,128)(2,1)S(1)}, u32[]{:S(2)}, u32[]{:S(2)}) collective-permute-start(bf16[128,512]{1,0:T(8,128)(2,1)S(1)} %slice.66), channel_id=1, source_target_pairs={{0,16},{16,32},{32,48},{48,0},{1,17},{17,33},{33,49},{49,1},{2,18}... | collective-permute-start | bytes 393224 | tf_op jit(solution)/shard_map/ppermute | solution.py:268
  65.8 6.3 %collective-permute-start.11 = (bf16[128,512]{1,0:T(8,128)(2,1)S(1)}, bf16[128,512]{1,0:T(8,128)(2,1)S(1)}, u32[]{:S(2)}, u32[]{:S(2)}) collective-permute-start(bf16[128,512]{1,0:T(8,128)(2,1)S(1)} %slice.67), channel_id=1, source_target_pairs={{0,48},{16,0},{32,16},{48,32},{1,49},{17,1},{33,17},{49,33},{2,50}... | collective-permute-start | bytes 393224 | tf_op jit(solution)/shard_map/ppermute | solution.py:272
  68.5 19.8 %copy-start.16 = (s32[16,8]{0,1:T(8,128)S(1)}, s32[16,8]{0,1:T(8,128)}, u32[]{:S(2)}) copy-start(s32[16,8]{0,1:T(8,128)} %param.17) | copy-start | bytes 1540
  72.1 1.4 copy-start.4
  73.5 0.9 copy-start.6
  74.5 0.9 copy-start.8
  75.4 0.9 copy-start.10
  76.4 10.7 %copy-start.13 = (bf16[16,3584]{1,0:T(8,128)(2,1)S(1)}, bf16[16,3584]{1,0:T(8,128)(2,1)}, u32[]{:S(2)}) copy-start(bf16[16,3584]{1,0:T(8,128)(2,1)} %param.15) | copy-start | bytes 344068
  79.8 23.3 %all-to-all-start.1 = ((bf16[8,2,16,1792]{3,2,1,0:T(8,128)(2,1)}), bf16[8,2,16,1792]{3,2,1,0:T(8,128)(2,1)S(1)}, u32[]{:S(2)}, u32[]{:S(2)}) async-start(bf16[8,2,16,1792]{3,2,1,0:T(8,128)(2,1)} %shard_map.123), calls=%async_computation.1 | async-start | bytes 1835008 | tf_op jit(solution)/shard_map/all_to_all | solution.py:360
  87.1 18.5 %copy-start.15 = (f32[3584]{0:T(1024)S(1)}, f32[3584]{0:T(1024)}, u32[]{:S(2)}) copy-start(f32[3584]{0:T(1024)} %param.16) | copy-start | bytes 43012
  87.2 16.0 %collective-permute-start = (bf16[16,1792]{1,0:T(8,128)(2,1)S(1)}, bf16[16,1792]{1,0:T(8,128)(2,1)S(1)}, u32[]{:S(2)}, u32[]{:S(2)}) collective-permute-start(bf16[16,1792]{1,0:T(8,128)(2,1)S(1)} %get-tuple-element.29), channel_id=1, source_target_pairs={{0,8},{8,0},{1,9},{9,1},{2,10},{10,2},{3,11},{11,3},{4,12},{12,4},... | collective-permute-start | bytes 172040 | tf_op jit(solution)/shard_map/ppermute | solution.py:255
  88.3 1.2 collective-permute-start.13
  103.2 2.1 collective-permute-start.12
  105.7 43.6 %copy-start.2 = (bf16[1,3584,512]{2,1,0:T(8,128)(2,1)S(1)}, bf16[1,3584,512]{2,1,0:T(8,128)(2,1)}, u32[]{:S(2)}) copy-start(bf16[1,3584,512]{2,1,0:T(8,128)(2,1)} %param.20) | copy-start | bytes 11010052
  108.0 41.3 %copy-start.1 = (bf16[1,3584,512]{2,1,0:T(8,128)(2,1)S(1)}, bf16[1,3584,512]{2,1,0:T(8,128)(2,1)}, u32[]{:S(2)}) copy-start(bf16[1,3584,512]{2,1,0:T(8,128)(2,1)} %param.19) | copy-start | bytes 11010052
  159.3 1.5 copy-start
  160.8 7.5 %copy-start.14 = (s32[16,8]{0,1:T(8,128)S(1)}, s32[16,8]{0,1:T(8,128)}, u32[]{:S(2)}) copy-start(s32[16,8]{0,1:T(8,128)} %param.18) | copy-start | bytes 1540
  160.8 40.6 %all-to-all-start.3 = ((bf16[64,3,2,3584]{3,2,1,0:T(2,128)(2,1)}), bf16[64,3,2,3584]{3,2,1,0:T(2,128)(2,1)S(1)}, u32[]{:S(2)}, u32[]{:S(2)}) async-start(bf16[64,3,2,3584]{3,2,1,0:T(2,128)(2,1)} %bitcast.64), calls=%async_computation.3 | async-start | bytes 5505024 | tf_op jit(solution)/shard_map/all_to_all | solution.py:373
  168.4 2.4 %collective-permute-start.14 = (f32[16,8]{0,1:T(8,128)S(1)}, f32[16,8]{0,1:T(8,128)S(1)}, u32[]{:S(2)}, u32[]{:S(2)}) collective-permute-start(f32[16,8]{0,1:T(8,128)S(1)} %convert_divide_fusion), channel_id=1, source_target_pairs={{0,8},{8,0},{1,9},{9,1},{2,10},{10,2},{3,11},{11,3},{4,12},{12,4},... | collective-permute-start | bytes 1544 | tf_op jit(solution)/shard_map/ppermute | solution.py:255
  203.4 4.9 %collective-permute-start.15 = (f32[16,3584]{1,0:T(8,128)S(1)}, f32[16,3584]{1,0:T(8,128)S(1)}, u32[]{:S(2)}, u32[]{:S(2)}) collective-permute-start(f32[16,3584]{1,0:T(8,128)S(1)} %get-tuple-element.23), channel_id=1, source_target_pairs={{0,8},{8,0},{1,9},{9,1},{2,10},{10,2},{3,11},{11,3},{4,12},{12,4},... | collective-permute-start | bytes 688136 | tf_op jit(solution)/shard_map/ppermute | solution.py:255
Sparse Core Ops, SparseCore 0:
  20.0 42.4 all-gather.1

commit v9 on v6

--- a/solution.py
+++ b/solution.py
@@ -203,20 +203,39 @@
     )(*[a for part in parts for a in part])
 
 
-def project_kernel(order_ref, own_ref, far_ref, *refs):
-    *chunk_refs, left_ref, right_ref, out_ref, x_ref, w_ref = refs
-    rows = own_ref.shape[0]
+def project_kernel(order_ref, *refs):
+    *head_refs, chunk_refs, (left_ref, right_ref), out_ref, x_ref, w_ref, sems = refs
     parts = out_ref.shape[0]
+    rows = head_refs[0].shape[0]
     tok = rows // parts
-    for i in range(len(chunk_refs) + 1):
-        columns = pl.ds(pl.multiple_of(order_ref[i] * VD, VD), VD)
-        x_ref[:rows, i * VD : (i + 1) * VD] = own_ref[:, columns]
-        x_ref[rows:, i * VD : (i + 1) * VD] = far_ref[:, columns]
-    for i, ref in enumerate(chunk_refs):
-        w_ref[i * VD : (i + 1) * VD] = ref[...]
+    whole = len(chunk_refs)
     half = left_ref.shape[1]
-    w_ref[len(chunk_refs) * VD :, :half] = left_ref[...]
-    w_ref[len(chunk_refs) * VD :, half:] = right_ref[...]
+    copies = [
+        pltpu.make_async_copy(ref, w_ref.at[i * VD : (i + 1) * VD], sems.at[i]) for i, ref in enumerate(chunk_refs)
+    ]
+    copies.append(pltpu.make_async_copy(left_ref, w_ref.at[whole * VD :, :half], sems.at[whole]))
+    copies.append(pltpu.make_async_copy(right_ref, w_ref.at[whole * VD :, half:], sems.at[whole + 1]))
+    for copy in copies:
+        copy.start()
+    lower, upper, far_lower, far_upper = head_refs
+    count = lower.shape[1] // VD
+    for i in range(whole + 1):
+        chip = order_ref[i]
+        columns = pl.ds(pl.multiple_of(lax.rem(chip, count) * VD, VD), VD)
+        here = slice(i * VD, (i + 1) * VD)
+
+        @pl.when(chip < count)
+        def _():
+            x_ref[:rows, here] = lower[:, columns]
+            x_ref[rows:, here] = far_lower[:, columns]
+
+        @pl.when(chip >= count)
+        def _():
+            x_ref[:rows, here] = upper[:, columns]
+            x_ref[rows:, here] = far_upper[:, columns]
+
+    for copy in copies:
+        copy.wait()
     n = 256
     for c in range(0, w_ref.shape[1], n):
         y = jnp.dot(x_ref[...], w_ref[:, c : c + n], preferred_element_type=F32).astype(BF)
@@ -225,21 +244,35 @@
             out_ref[e, 1, :, c : c + n] = y[rows + e * tok : rows + (e + 1) * tok]
 
 
-def project(order, own, far, chunks, parts):
-    rows, depth = own.shape
-    width = chunks[0].shape[1]
-    whole = pl.BlockSpec(memory_space=pltpu.VMEM)
+def project(order, heads, chunks, parts):
+    *whole, left, right = chunks
+    rows = heads[0].shape[0]
+    width = whole[0].shape[1]
+    depth = VD * (len(whole) + 1)
+    vmem = pl.BlockSpec(memory_space=pltpu.VMEM)
+    hbm = pl.BlockSpec(memory_space=pl.ANY)
+
+    def kernel(*refs):
+        order_ref, *refs = refs
+        head_refs, refs = refs[: len(heads)], refs[len(heads) :]
+        chunk_refs, refs = refs[: len(whole)], refs[len(whole) :]
+        project_kernel(order_ref, *head_refs, chunk_refs, refs[:2], *refs[2:])
+
     return pl.pallas_call(
-        project_kernel,
-        in_specs=[pl.BlockSpec(memory_space=pltpu.SMEM)] + [whole] * (2 + len(chunks)),
-        out_specs=whole,
+        kernel,
+        in_specs=[pl.BlockSpec(memory_space=pltpu.SMEM)] + [vmem] * len(heads) + [hbm] * len(chunks),
+        out_specs=vmem,
         out_shape=jax.ShapeDtypeStruct((parts, 2, rows // parts, width), BF),
-        scratch_shapes=[pltpu.VMEM((2 * rows, depth), BF), pltpu.VMEM((depth, width), BF)],
+        scratch_shapes=[
+            pltpu.VMEM((2 * rows, depth), BF),
+            pltpu.VMEM((depth, width), BF),
+            pltpu.SemaphoreType.DMA((len(chunks),)),
+        ],
         compiler_params=pltpu.CompilerParams(vmem_limit_bytes=32 * 2**20),
         cost_estimate=pl.CostEstimate(
             flops=4 * rows * depth * width, bytes_accessed=2 * depth * width, transcendentals=0
         ),
-    )(order, own, far, *chunks)
+    )(order, *heads, *chunks)
 
 
 def swap(mine):
@@ -334,18 +367,20 @@
     far = swap(near)
     mate_before, mate_after, opposite = up(mate), across(after), down(after)
     ids = jnp.stack([lax.axis_index(CTX), core]).astype(jnp.int32)
-    heads_out = attend(ids, q, near, far, w_kv, 4, 4)
-    heads_out, mate_before, mate_after, opposite = lax.optimization_barrier(
-        (heads_out, mate_before, mate_after, opposite)
+    wide_half, tall_half = w_kv.shape[1] // 2, q.shape[0] // 2
+    heads_lower = attend(ids, q[:tall_half], near, far, w_kv[:, :wide_half], 4, 4)
+    heads_lower, q_upper, mate_before, mate_after, opposite = lax.optimization_barrier(
+        (heads_lower, q[tall_half:], mate_before, mate_after, opposite)
     )
     part = chunk.shape[1] // 2
     left, right = up(mate_before[:, :part]), down(mate_after[:, part:])
+    heads_upper = attend(ids, q_upper, near, far, w_kv[:, wide_half:], 4, 4)
     chunks = (chunk, mate, before, after, mate_before, mate_after, opposite, left, right)
     order = chip_order()
     half = width // 2
     lower, upper = resid[:, :half], resid[:, half:]
     resid2 = jnp.stack([jnp.where(core == 0, lower, upper), swap(jnp.where(core == 0, upper, lower))])
-    attn = project(order, heads_out, swap(heads_out), chunks, 8)
+    attn = project(order, (heads_lower, heads_upper, swap(heads_lower), swap(heads_upper)), chunks, 8)
     attn = lax.all_to_all(attn, EP, split_axis=0, concat_axis=0, tiled=True)
     summed = (resid2.astype(F32) + jnp.sum(attn.astype(F32), axis=0)).astype(BF)
     others = swap(summed)[::-1]
@@ -363,9 +398,9 @@
         return units.reshape(rows.shape)
 
     parts = routing(routes, codes)
-    arrived = [exchange(dispatch(place, normed2, 7)) for place, _ in parts]
+    arrived = [exchange(dispatch(place, normed2, 2)) for place, _ in parts]
     returned = [exchange(expert(rows, w_gate[0], w_up[0], w_down[0], 2, 7)) for rows in arrived]
-    own, theirs = combine([(factors, rows) for (_, factors), rows in zip(parts, returned)], 7)
+    own, theirs = combine([(factors, rows) for (_, factors), rows in zip(parts, returned)], 4)
     layer_out = (wide2[:tok] + own + swap(theirs)).astype(BF)
     return (attended, layer_out)
 

time: 203 us -> 204 us (level)
  waiting for transfers between devices: 60.9 us -> 67.3 us
  local copies, waits for them, and re-layouts: 20.6 us -> 15.6 us
  Pallas kernels: 28.4 us -> 30.8 us
    unnamed x37 -> x27, local copies, waits for them, and re-layouts: 13.7 us -> 6.93 us
    ppermute x2, waiting for transfers between devices: 9.65 us -> 13.2 us  [across(): return lax.ppermute(a, 'z_lo', SWAP)]
    pallas_call x1, Pallas kernels: 3.28 us -> 5.91 us  [project(): pl.pallas_call(kernel, in_specs=[pl.BlockSpec(memory_space=pltpu.SMEM)] +...]
    pallas_call x1 -> x2, Pallas kernels: 10.9 us -> 12.1 us  [attend(): pl.pallas_call(functools.partial(attend_kernel, rows=rows, cuts=cuts), gr...]
    ppermute x8 -> x9, starting transfers between devices: 11.4 us -> 10.3 us  [swap(): return lax.ppermute(mine, 'core', SWAP)]
  transfers between devices with their start and end apart: 19 -> 20, of which waited for: 11 -> 10; matrix products, arithmetic and copies ran while one was open for 9% -> 9% of each run, Pallas kernels for 5% -> 6%
where the time goes in v9:
time: 204 us; the launch traced here: 201 us
  waiting for transfers between devices  67.3 us (33%)
  starting transfers between devices  40 us (20%)
  blocking collectives  40 us (20%)
  Pallas kernels  30.8 us (15%)
  local copies, waits for them, and re-layouts  15.6 us (8%)
  other arithmetic  4.88 us (2%)
    all_to_all x1, blocking collectives, exchange(): lax.all_to_all(units, CHIPS, split_axis=0, concat_axis=0, tiled=True)  40 us
    all_to_all x1, waiting for transfers between devices, exchange(): lax.all_to_all(units, CHIPS, split_axis=0, concat_axis=0, tiled=True)  29.2 us
    all_to_all x1, waiting for transfers between devices, local(): attn = lax.all_to_all(attn, EP, split_axis=0, concat_axis=0, tiled=True)  13.5 us
    ppermute x2, waiting for transfers between devices, across(): return lax.ppermute(a, 'z_lo', SWAP)  13.2 us
    pallas_call x2, Pallas kernels, attend(): pl.pallas_call(functools.partial(attend_kernel, rows=rows, cuts=cuts), gr...  12.1 us
    ppermute x9, starting transfers between devices, swap(): return lax.ppermute(mine, 'core', SWAP)  10.3 us
    pallas_call x1, Pallas kernels, expert(): pl.pallas_call(functools.partial(expert_kernel, first=first), grid=(first...  10 us
    ppermute x3, waiting for transfers between devices, up(): return lax.ppermute(a, 'x', [(i, (i + 1) % 4) for i in range(4)])  7.77 us
  transfers between devices with their start and end apart: 20, of which 10 were waited for; matrix products, arithmetic and copies ran while one was open for 9% of the time, Pallas kernels for 6%

profile of v9, /device:TPU:1, one launch (start us, length us, event | category | flops | bytes accessed | tf_op | source)
XLA Modules:
  0.0 201.2 jit_solution(17053854159290219139)
XLA Ops:
  0.6 1.1 broadcast_select_fusion.2
  1.8 1.5 collective-permute-start.1
  3.3 2.1 %broadcast_in_dim.32 = bf16[8,576,128]{2,1,0:T(8,128)(2,1)} broadcast(bf16[576,128]{1,0:T(8,128)(2,1)} %param.12), dimensions={1,2} | broadcast | bytes 1327104 | tf_op jit(solution)/shard_map/broadcast_in_dim | solution.py:363
  5.4 5.6 %all-to-all-start = ((bf16[8,576,128]{2,1,0:T(8,128)(2,1)}), bf16[8,576,128]{2,1,0:T(8,128)(2,1)S(1)}, u32[]{:S(2)}, u32[]{:S(2)}) async-start(bf16[8,576,128]{2,1,0:T(8,128)(2,1)} %broadcast_in_dim.32), calls=%async_computation | async-start | bytes 2359296 | tf_op jit(solution)/shard_map/all_to_all | solution.py:362
  11.1 1.5 collective-permute-start.2
  12.6 1.2 collective-permute-start.3
  13.8 1.5 collective-permute-start.4
  15.3 0.2 copy.45
  15.5 0.2 copy.63
  15.7 3.9 %copy.47 = bf16[512,2048]{0,1:T(8,128)(2,1)} copy(bf16[512,2048]{1,0:T(8,128)(2,1)} %param.13) | data formatting | bytes 4194304 | tf_op args[2]
  19.6 1.7 convolution_convert_fusion
  21.4 1.2 pad_maximum_fusion
  22.5 13.2 %collective-permute-done.2.refs_6_ = bf16[128,1792]{1,0:T(8,128)(2,1)S(1)} collective-permute-done((bf16[128,1792]{1,0:T(8,128)(2,1)S(1)}, bf16[128,1792]{1,0:T(8,128)(2,1)S(1)}, u32[]{:S(2)}, u32[]{:S(2)}) %collective-permute-start.2) | collective-permute-done | bytes 458784 | tf_op jit(solution)/shard_map/ppermute | solution.py:300
  35.7 1.5 collective-permute-done.3.refs_7_
  37.3 0.8 collective-permute-start.5
  38.1 1.8 fusion.13
  39.9 1.3 collective-permute-start.7
  41.2 1.2 collective-permute-start.8
  42.4 0.3 collective-permute-start.6
  42.6 0.1 fusion.14
  42.8 6.1 %shard_map.122.refs_1_ = bf16[128,512]{1,0:T(8,128)(2,1)} custom-call(s32[2]{0:T(128)S(1)} %pad_add_fusion.1.ids_ref, bf16[512,576]{1,0:T(8,128)(2,1)S(1)} %get-tuple-element.29.q_ref, bf16[8,576,128]{2,1,0:T(8,128)(2,1)S(1)} %all-to-all-done.near_ref, bf16[8,576,128]{2,1,0:T(8,128)(2,1)} %collective-permute-done.5.far_ref, ...), custom_call_target="tpu_custom_call" | custom-call | flops 2281701376 | bytes 8000000 | tf_op jit(solution)/shard_map/pallas_call | solution.py:76
  48.8 6.3 %collective-permute-done.6.refs_9_ = bf16[128,1792]{1,0:T(8,128)(2,1)S(1)} collective-permute-done((bf16[128,1792]{1,0:T(8,128)(2,1)S(1)}, bf16[128,1792]{1,0:T(8,128)(2,1)S(1)}, u32[]{:S(2)}, u32[]{:S(2)}) %collective-permute-start.6) | collective-permute-done | bytes 458784 | tf_op jit(solution)/shard_map/ppermute | solution.py:292
  55.1 1.5 collective-permute-start.9
  56.6 0.7 slice.74
  57.3 0.7 slice.75
  58.0 2.7 %collective-permute-start.12 = (bf16[128,896]{1,0:T(8,128)(2,1)}, bf16[128,896]{1,0:T(8,128)(2,1)}, u32[]{:S(2)}, u32[]{:S(2)}) collective-permute-start(bf16[128,896]{1,0:T(8,128)(2,1)} %slice.75), channel_id=1, source_target_pairs={{0,48},{16,0},{32,16},{48,32},{1,49},{17,1},{33,17},{49,33},{2,50}... | collective-permute-start | bytes 688136 | tf_op jit(solution)/shard_map/ppermute | solution.py:296
  60.7 6.0 %shard_map.123.refs_2_ = bf16[128,512]{1,0:T(8,128)(2,1)} custom-call(s32[2]{0:T(128)S(1)} %pad_add_fusion.1.ids_ref, bf16[512,576]{1,0:T(8,128)(2,1)S(1)} %get-tuple-element.19.q_ref, bf16[8,576,128]{2,1,0:T(8,128)(2,1)S(1)} %all-to-all-done.near_ref, bf16[8,576,128]{2,1,0:T(8,128)(2,1)} %collective-permute-done.5.far_ref, ...), custom_call_target="tpu_custom_call" | custom-call | flops 2281701376 | bytes 8000000 | tf_op jit(solution)/shard_map/pallas_call | solution.py:76
  66.7 0.6 collective-permute-start.10
  67.4 0.1 stack.74.refs_0_
  67.5 1.1 collective-permute-done.10.refs_4_
  68.6 1.0 copy-done.4
  69.6 5.9 %shard_map.124 = bf16[8,2,16,1792]{3,2,1,0:T(8,128)(2,1)} custom-call(s32[8]{0:T(128)S(1)} %stack.74.refs_0_, bf16[128,512]{1,0:T(8,128)(2,1)} %shard_map.122.refs_1_, bf16[128,512]{1,0:T(8,128)(2,1)} %shard_map.123.refs_2_, bf16[128,512]{1,0:T(8,128)(2,1)} %collective-permute-done.9.refs_3_, bf16[128,512]{1,0:T(8,128)(2,1)S(1)} %collective-permute-done.10.refs_4_, ...), custom_call_target="tpu_custom_call" | custom-call | flops 939524096 | bytes 3670016 | tf_op jit(solution)/shard_map/pallas_call | solution.py:261
  75.5 7.2 %all-to-all-start.1 = ((bf16[8,2,16,1792]{3,2,1,0:T(8,128)(2,1)}), bf16[8,2,16,1792]{3,2,1,0:T(8,128)(2,1)S(1)}, u32[]{:S(2)}, u32[]{:S(2)}) async-start(bf16[8,2,16,1792]{3,2,1,0:T(8,128)(2,1)} %shard_map.124), calls=%async_computation.1 | async-start | bytes 1835008 | tf_op jit(solution)/shard_map/all_to_all | solution.py:384
  82.8 0.7 collective-permute-start
  83.5 0.1 collective-permute-start.14
  83.7 0.1 and.51
  83.8 0.9 collective-permute-done.14
  84.8 0.1 fusion.8
  84.9 0.1 copy.51
  85.2 13.5 %all-to-all-done.1 = bf16[8,2,16,1792]{3,2,1,0:T(8,128)(2,1)S(1)} async-done(((bf16[8,2,16,1792]{3,2,1,0:T(8,128)(2,1)}), bf16[8,2,16,1792]{3,2,1,0:T(8,128)(2,1)S(1)}, u32[]{:S(2)}, u32[]{:S(2)}) %all-to-all-start.1) | async-done | bytes 917536 | tf_op jit(solution)/shard_map/all_to_all | solution.py:384
  98.7 0.1 convert_reduce_fusion
  98.9 0.9 collective-permute-start.13
  99.9 0.1 copy.54
  100.1 0.1 reshape.153
  100.2 0.5 collective-permute-done.13
  100.8 0.1 multiply_reduce_fusion
  101.0 0.1 fusion.2.x_ref
  101.2 1.4 shard_map.125
  102.6 40.0 %all_to_all.20 = bf16[64,3,2,3584]{3,2,1,0:T(2,128)(2,1)S(1)} all-to-all(bf16[64,3,2,3584]{3,2,1,0:T(2,128)(2,1)S(1)} %bitcast.63), channel_id=1, replica_groups=mesh['z_lo'=2,'x'=4,'core'=2,'z_hi'=2,'y'=4] {'z_lo','x','z_hi','y'}, dimensions={0} | all-to-all | bytes 5505024 | tf_op jit(solution)/shard_map/all_to_all | solution.py:397
  142.6 10.0 %shard_map.126 = bf16[192,2,3584]{2,1,0:T(2,128)(2,1)S(1)} custom-call(bf16[192,2,3584]{2,1,0:T(2,128)(2,1)S(1)} %bitcast.65, bf16[3584,512]{1,0:T(8,128)(2,1)S(1)} %bitcast.66, bf16[3584,512]{1,0:T(8,128)(2,1)S(1)} %bitcast.67, bf16[512,3584]{1,0:T(8,128)(2,1)} %bitcast.70), custom_call_target="tpu_custom_call" | custom-call | flops 4227858432 | bytes 17000000 | tf_op jit(solution)/shard_map/pallas_call | solution.py:129
  152.6 1.5 copy-done
  154.1 7.2 %all-to-all-start.3 = ((bf16[64,3,2,3584]{3,2,1,0:T(2,128)(2,1)}), bf16[64,3,2,3584]{3,2,1,0:T(2,128)(2,1)S(1)}, u32[]{:S(2)}, u32[]{:S(2)}) async-start(bf16[64,3,2,3584]{3,2,1,0:T(2,128)(2,1)} %bitcast.64), calls=%async_computation.3 | async-start | bytes 5505024 | tf_op jit(solution)/shard_map/all_to_all | solution.py:397
  161.4 1.2 collective-permute-start.15
  162.6 0.1 copy.59
  162.7 0.7 collective-permute-done.15
  163.5 0.1 select_reduce_fusion
  163.9 0.8 broadcast_in_dim.65
  164.6 1.0 copy.60
  165.7 29.2 %all-to-all-done.3 = bf16[64,3,2,3584]{3,2,1,0:T(2,128)(2,1)S(1)} async-done(((bf16[64,3,2,3584]{3,2,1,0:T(2,128)(2,1)}), bf16[64,3,2,3584]{3,2,1,0:T(2,128)(2,1)S(1)}, u32[]{:S(2)}, u32[]{:S(2)}) %all-to-all-start.3) | async-done | bytes 2752544 | tf_op jit(solution)/shard_map/all_to_all | solution.py:397
  194.9 1.4 shard_map.127
  196.3 3.1 %collective-permute-start.16 = (f32[16,3584]{1,0:T(8,128)S(1)}, f32[16,3584]{1,0:T(8,128)S(1)}, u32[]{:S(2)}, u32[]{:S(2)}) collective-permute-start(f32[16,3584]{1,0:T(8,128)S(1)} %get-tuple-element.25), channel_id=1, source_target_pairs={{0,8},{8,0},{1,9},{9,1},{2,10},{10,2},{3,11},{11,3},{4,12},{12,4},... | collective-permute-start | bytes 688136 | tf_op jit(solution)/shard_map/ppermute | solution.py:279
  199.4 0.7 fusion.10
  200.1 0.5 collective-permute-done.16
  200.5 0.7 fusion.7
  (69 shorter events, 1.4 us)
Async XLA Ops:
  0.6 10.3 %copy-start.6 = (bf16[64,3584]{1,0:T(8,128)(2,1)S(1)}, bf16[64,3584]{1,0:T(8,128)(2,1)}, u32[]{:S(2)}) copy-start(bf16[64,3584]{1,0:T(8,128)(2,1)} %param.14) | copy-start | bytes 1376260
  1.8 9.2 %collective-permute-start.1 = (bf16[64,1792]{1,0:T(8,128)(2,1)S(1)}, bf16[64,1792]{1,0:T(8,128)(2,1)S(1)}, u32[]{:S(2)}, u32[]{:S(2)}) collective-permute-start(bf16[64,1792]{1,0:T(8,128)(2,1)S(1)} %broadcast_select_fusion.2), channel_id=1, source_target_pairs={{0,8},{8,0},{1,9},{9,1},{2,10},{10,2},{3,11},{11,3},{4,12},{12,4},... | collective-permute-start | bytes 688136 | tf_op jit(solution)/shard_map/ppermute | solution.py:279
  5.4 9.9 %copy-start.7 = (bf16[128,1536]{1,0:T(8,128)(2,1)S(1)}, bf16[128,1536]{1,0:T(8,128)(2,1)}, u32[]{:S(2)}) copy-start(bf16[128,1536]{1,0:T(8,128)(2,1)} %param.11) | copy-start | bytes 1179652
  5.4 31.9 %all-to-all-start = ((bf16[8,576,128]{2,1,0:T(8,128)(2,1)}), bf16[8,576,128]{2,1,0:T(8,128)(2,1)S(1)}, u32[]{:S(2)}, u32[]{:S(2)}) async-start(bf16[8,576,128]{2,1,0:T(8,128)(2,1)} %broadcast_in_dim.32), calls=%async_computation | async-start | bytes 2359296 | tf_op jit(solution)/shard_map/all_to_all | solution.py:362
  11.1 24.7 %collective-permute-start.2 = (bf16[128,1792]{1,0:T(8,128)(2,1)S(1)}, bf16[128,1792]{1,0:T(8,128)(2,1)S(1)}, u32[]{:S(2)}, u32[]{:S(2)}) collective-permute-start(bf16[128,1792]{1,0:T(8,128)(2,1)S(1)} %pad_maximum_fusion.1.refs_5_), channel_id=1, source_target_pairs={{0,64},{64,0},{1,65},{65,1},{2,66},{66,2},{3,67},{67,3},{4,68},{68... | collective-permute-start | bytes 1376264 | tf_op jit(solution)/shard_map/ppermute | solution.py:300
  12.6 24.6 %collective-permute-start.3 = (bf16[128,1792]{1,0:T(8,128)(2,1)S(1)}, bf16[128,1792]{1,0:T(8,128)(2,1)S(1)}, u32[]{:S(2)}, u32[]{:S(2)}) collective-permute-start(bf16[128,1792]{1,0:T(8,128)(2,1)S(1)} %pad_maximum_fusion.1.refs_5_), channel_id=1, source_target_pairs={{0,16},{16,32},{32,48},{48,0},{1,17},{17,33},{33,49},{49,1},{2,18}... | collective-permute-start | bytes 1376264 | tf_op jit(solution)/shard_map/ppermute | solution.py:292
  13.8 23.5 %collective-permute-start.4 = (bf16[128,1792]{1,0:T(8,128)(2,1)S(1)}, bf16[128,1792]{1,0:T(8,128)(2,1)}, u32[]{:S(2)}, u32[]{:S(2)}) collective-permute-start(bf16[128,1792]{1,0:T(8,128)(2,1)S(1)} %pad_maximum_fusion.1.refs_5_), channel_id=1, source_target_pairs={{0,48},{16,0},{32,16},{48,32},{1,49},{17,1},{33,17},{49,33},{2,50}... | collective-permute-start | bytes 1376264 | tf_op jit(solution)/shard_map/ppermute | solution.py:296
  37.3 5.5 %collective-permute-start.5 = (bf16[8,576,128]{2,1,0:T(8,128)(2,1)S(1)}, bf16[8,576,128]{2,1,0:T(8,128)(2,1)}, u32[]{:S(2)}, u32[]{:S(2)}) collective-permute-start(bf16[8,576,128]{2,1,0:T(8,128)(2,1)S(1)} %all-to-all-done.near_ref), channel_id=1, source_target_pairs={{0,8},{8,0},{1,9},{9,1},{2,10},{10,2},{3,11},{11,3},{4,12},{12,4},... | collective-permute-start | bytes 3538952 | tf_op jit(solution)/shard_map/ppermute | solution.py:279
  38.1 4.6 %copy-start.5 = (bf16[8,128,576]{2,1,0:T(8,128)(2,1)S(1)}, bf16[8,128,576]{2,1,0:T(8,128)(2,1)}, u32[]{:S(2)}) copy-start(bf16[8,128,576]{2,1,0:T(8,128)(2,1)} %pad_maximum_fusion) | copy-start | bytes 3538948
  39.9 15.2 %collective-permute-start.7 = (bf16[128,1792]{1,0:T(8,128)(2,1)}, bf16[128,1792]{1,0:T(8,128)(2,1)S(1)}, u32[]{:S(2)}, u32[]{:S(2)}) collective-permute-start(bf16[128,1792]{1,0:T(8,128)(2,1)} %collective-permute-done.4.refs_8_), channel_id=1, source_target_pairs={{0,64},{64,0},{1,65},{65,1},{2,66},{66,2},{3,67},{67,3},{4,68},{68... | collective-permute-start | bytes 1376264 | tf_op jit(solution)/shard_map/ppermute | solution.py:300
  41.2 13.9 %collective-permute-start.8 = (bf16[128,1792]{1,0:T(8,128)(2,1)}, bf16[128,1792]{1,0:T(8,128)(2,1)S(1)}, u32[]{:S(2)}, u32[]{:S(2)}) collective-permute-start(bf16[128,1792]{1,0:T(8,128)(2,1)} %collective-permute-done.4.refs_8_), channel_id=1, source_target_pairs={{0,48},{16,0},{32,16},{48,32},{1,49},{17,1},{33,17},{49,33},{2,50}... | collective-permute-start | bytes 1376264 | tf_op jit(solution)/shard_map/ppermute | solution.py:296
  42.4 12.7 %collective-permute-start.6 = (bf16[128,1792]{1,0:T(8,128)(2,1)S(1)}, bf16[128,1792]{1,0:T(8,128)(2,1)S(1)}, u32[]{:S(2)}, u32[]{:S(2)}) collective-permute-start(bf16[128,1792]{1,0:T(8,128)(2,1)S(1)} %collective-permute-done.2.refs_6_), channel_id=1, source_target_pairs={{0,16},{16,32},{32,48},{48,0},{1,17},{17,33},{33,49},{49,1},{2,18}... | collective-permute-start | bytes 1376264 | tf_op jit(solution)/shard_map/ppermute | solution.py:292
  55.1 11.7 %copy-start.3 = (bf16[128,1792]{1,0:T(8,128)(2,1)}, bf16[128,1792]{1,0:T(8,128)(2,1)S(1)}, u32[]{:S(2)}) copy-start(bf16[128,1792]{1,0:T(8,128)(2,1)S(1)} %collective-permute-done.8.refs_11_) | copy-start | bytes 1376260
  55.1 12.4 %collective-permute-start.9 = (bf16[128,512]{1,0:T(8,128)(2,1)}, bf16[128,512]{1,0:T(8,128)(2,1)}, u32[]{:S(2)}, u32[]{:S(2)}) collective-permute-start(bf16[128,512]{1,0:T(8,128)(2,1)} %shard_map.122.refs_1_), channel_id=1, source_target_pairs={{0,8},{8,0},{1,9},{9,1},{2,10},{10,2},{3,11},{11,3},{4,12},{12,4},... | collective-permute-start | bytes 393224 | tf_op jit(solution)/shard_map/ppermute | solution.py:279
  57.3 11.3 %collective-permute-start.11 = (bf16[128,896]{1,0:T(8,128)(2,1)}, bf16[128,896]{1,0:T(8,128)(2,1)}, u32[]{:S(2)}, u32[]{:S(2)}) collective-permute-start(bf16[128,896]{1,0:T(8,128)(2,1)} %slice.74), channel_id=1, source_target_pairs={{0,16},{16,32},{32,48},{48,0},{1,17},{17,33},{33,49},{49,1},{2,18}... | collective-permute-start | bytes 688136 | tf_op jit(solution)/shard_map/ppermute | solution.py:292
  58.0 10.6 %collective-permute-start.12 = (bf16[128,896]{1,0:T(8,128)(2,1)}, bf16[128,896]{1,0:T(8,128)(2,1)}, u32[]{:S(2)}, u32[]{:S(2)}) collective-permute-start(bf16[128,896]{1,0:T(8,128)(2,1)} %slice.75), channel_id=1, source_target_pairs={{0,48},{16,0},{32,16},{48,32},{1,49},{17,1},{33,17},{49,33},{2,50}... | collective-permute-start | bytes 688136 | tf_op jit(solution)/shard_map/ppermute | solution.py:296
  66.7 1.8 collective-permute-start.10
  67.4 16.1 %copy-start.11 = (s32[16,8]{0,1:T(8,128)S(1)}, s32[16,8]{0,1:T(8,128)}, u32[]{:S(2)}) copy-start(s32[16,8]{0,1:T(8,128)} %param.17) | copy-start | bytes 1540
  68.6 1.0 copy-start.4
  69.6 13.2 %copy-start.8 = (bf16[16,3584]{1,0:T(8,128)(2,1)S(1)}, bf16[16,3584]{1,0:T(8,128)(2,1)}, u32[]{:S(2)}) copy-start(bf16[16,3584]{1,0:T(8,128)(2,1)} %param.15) | copy-start | bytes 344068
  75.5 23.2 %all-to-all-start.1 = ((bf16[8,2,16,1792]{3,2,1,0:T(8,128)(2,1)}), bf16[8,2,16,1792]{3,2,1,0:T(8,128)(2,1)S(1)}, u32[]{:S(2)}, u32[]{:S(2)}) async-start(bf16[8,2,16,1792]{3,2,1,0:T(8,128)(2,1)} %shard_map.124), calls=%async_computation.1 | async-start | bytes 1835008 | tf_op jit(solution)/shard_map/all_to_all | solution.py:384
  82.7 18.3 %copy-start.10 = (f32[3584]{0:T(1024)S(1)}, f32[3584]{0:T(1024)}, u32[]{:S(2)}) copy-start(f32[3584]{0:T(1024)} %param.16) | copy-start | bytes 43012
  82.8 16.1 %collective-permute-start = (bf16[16,1792]{1,0:T(8,128)(2,1)S(1)}, bf16[16,1792]{1,0:T(8,128)(2,1)S(1)}, u32[]{:S(2)}, u32[]{:S(2)}) collective-permute-start(bf16[16,1792]{1,0:T(8,128)(2,1)S(1)} %get-tuple-element.35), channel_id=1, source_target_pairs={{0,8},{8,0},{1,9},{9,1},{2,10},{10,2},{3,11},{11,3},{4,12},{12,4},... | collective-permute-start | bytes 172040 | tf_op jit(solution)/shard_map/ppermute | solution.py:279
  83.5 1.2 collective-permute-start.14
  98.9 1.8 collective-permute-start.13
  101.2 41.4 %copy-start.2 = (bf16[1,3584,512]{2,1,0:T(8,128)(2,1)S(1)}, bf16[1,3584,512]{2,1,0:T(8,128)(2,1)}, u32[]{:S(2)}) copy-start(bf16[1,3584,512]{2,1,0:T(8,128)(2,1)} %param.20) | copy-start | bytes 11010052
  102.6 40.0 %copy-start.1 = (bf16[1,3584,512]{2,1,0:T(8,128)(2,1)S(1)}, bf16[1,3584,512]{2,1,0:T(8,128)(2,1)}, u32[]{:S(2)}) copy-start(bf16[1,3584,512]{2,1,0:T(8,128)(2,1)} %param.19) | copy-start | bytes 11010052
  152.6 1.5 copy-start
  154.1 7.2 %copy-start.9 = (s32[16,8]{0,1:T(8,128)S(1)}, s32[16,8]{0,1:T(8,128)}, u32[]{:S(2)}) copy-start(s32[16,8]{0,1:T(8,128)} %param.18) | copy-start | bytes 1540
  154.1 40.8 %all-to-all-start.3 = ((bf16[64,3,2,3584]{3,2,1,0:T(2,128)(2,1)}), bf16[64,3,2,3584]{3,2,1,0:T(2,128)(2,1)S(1)}, u32[]{:S(2)}, u32[]{:S(2)}) async-start(bf16[64,3,2,3584]{3,2,1,0:T(2,128)(2,1)} %bitcast.64), calls=%async_computation.3 | async-start | bytes 5505024 | tf_op jit(solution)/shard_map/all_to_all | solution.py:397
  161.4 2.0 collective-permute-start.15
  196.3 4.2 %collective-permute-start.16 = (f32[16,3584]{1,0:T(8,128)S(1)}, f32[16,3584]{1,0:T(8,128)S(1)}, u32[]{:S(2)}, u32[]{:S(2)}) collective-permute-start(f32[16,3584]{1,0:T(8,128)S(1)} %get-tuple-element.25), channel_id=1, source_target_pairs={{0,8},{8,0},{1,9},{9,1},{2,10},{10,2},{3,11},{11,3},{4,12},{12,4},... | collective-permute-start | bytes 688136 | tf_op jit(solution)/shard_map/ppermute | solution.py:279

commit v10 on v4

--- a/solution.py
+++ b/solution.py
@@ -13,7 +13,7 @@
 TOP = 8
 QK = 192
 CAP = 3
-SLOTS = (slice(0, 2), slice(2, 3))
+SLOTS = (slice(0, 3),)
 
 CTX = ("z_lo", "x", "core")
 CTX_CHIPS = ("z_lo", "x")
@@ -69,7 +69,8 @@
 
 
 def attend(ids, q, near, far, w_kv, group, cuts):
-    pairs, depth, rows = near.shape
+    pairs, _, rows = near.shape
+    depth = q.shape[1]
     heads = w_kv.shape[1] // (NOPE + VD)
     keys = 2 * rows * pairs
     m = group * rows
@@ -79,8 +80,8 @@
         in_specs=[
             pl.BlockSpec(memory_space=pltpu.SMEM),
             pl.BlockSpec((m, depth), lambda g: (g, 0)),
-            pl.BlockSpec(near.shape, lambda g: (0, 0, 0)),
-            pl.BlockSpec(far.shape, lambda g: (0, 0, 0)),
+            pl.BlockSpec((pairs, depth, rows), lambda g: (0, 0, 0)),
+            pl.BlockSpec((pairs, depth, rows), lambda g: (0, 0, 0)),
             pl.BlockSpec((KV_RANK, group * (NOPE + VD)), lambda g: (0, g)),
         ],
         out_specs=pl.BlockSpec((rows, group * VD), lambda g: (0, g)),
@@ -203,67 +204,60 @@
     )(*[a for part in parts for a in part])
 
 
-def project_kernel(order_ref, own_ref, far_ref, *refs):
-    *chunk_refs, left_ref, right_ref, out_ref, x_ref, w_ref = refs
+def project_kernel(ids_ref, own_ref, before_ref, after_ref, left_ref, right_ref, near_ref, far_ref, out_ref, x_ref, w_ref):
     rows = own_ref.shape[0]
-    parts = out_ref.shape[0]
-    tok = rows // parts
-    for i in range(len(chunk_refs) + 1):
-        columns = pl.ds(pl.multiple_of(order_ref[i] * VD, VD), VD)
-        x_ref[:rows, i * VD : (i + 1) * VD] = own_ref[:, columns]
-        x_ref[rows:, i * VD : (i + 1) * VD] = far_ref[:, columns]
-    for i, ref in enumerate(chunk_refs):
-        w_ref[i * VD : (i + 1) * VD] = ref[...]
+    group, tok = 4, out_ref.shape[1]
+    parts = out_ref.shape[0] // group
+    core, x = ids_ref[1], ids_ref[2]
     half = left_ref.shape[1]
-    w_ref[len(chunk_refs) * VD :, :half] = left_ref[...]
-    w_ref[len(chunk_refs) * VD :, half:] = right_ref[...]
-    n = 256
-    for c in range(0, w_ref.shape[1], n):
-        y = jnp.dot(x_ref[...], w_ref[:, c : c + n], preferred_element_type=F32).astype(BF)
+    x_ref[:rows] = own_ref[...]
+    x_ref[rows : 2 * rows] = after_ref[...]
+    x_ref[2 * rows : 3 * rows, :half] = left_ref[...]
+    x_ref[2 * rows : 3 * rows, half:] = right_ref[...]
+    x_ref[3 * rows :] = before_ref[...]
+    deep = VD // 2
+    blocks = w_ref.shape[1] // 128
+    first = near_ref.shape[1] - blocks * deep
+    for side, ref in enumerate((near_ref, far_ref)):
+        offset = (core if side == 0 else 1 - core) * deep
+        for j in range(ref.shape[0]):
+            here = pl.ds(pl.multiple_of(j * VD + offset, deep), deep)
+            for b in range(blocks):
+                w_ref[here, b * 128 : (b + 1) * 128] = ref[j, first + b * deep : first + (b + 1) * deep]
+    for d in range(group):
+        y = jnp.dot(x_ref[d * rows : (d + 1) * rows], w_ref[...], preferred_element_type=F32).astype(BF)
+        target = lax.rem(x + d, group)
         for e in range(parts):
-            out_ref[e, 0, :, c : c + n] = y[e * tok : (e + 1) * tok]
-            out_ref[e, 1, :, c : c + n] = y[rows + e * tok : rows + (e + 1) * tok]
-
-
-def project(order, own, far, chunks, parts):
-    rows, depth = own.shape
-    width = chunks[0].shape[1]
+            out_ref[e * group + target] = y[e * tok : (e + 1) * tok]
+
+
+def project(ids, pieces, near, far, parts, width):
+    rows, depth = pieces[0].shape
     whole = pl.BlockSpec(memory_space=pltpu.VMEM)
+    group = 4
     return pl.pallas_call(
         project_kernel,
-        in_specs=[pl.BlockSpec(memory_space=pltpu.SMEM)] + [whole] * (2 + len(chunks)),
+        in_specs=[pl.BlockSpec(memory_space=pltpu.SMEM)] + [whole] * (len(pieces) + 2),
         out_specs=whole,
-        out_shape=jax.ShapeDtypeStruct((parts, 2, rows // parts, width), BF),
-        scratch_shapes=[pltpu.VMEM((2 * rows, depth), BF), pltpu.VMEM((depth, width), BF)],
+        out_shape=jax.ShapeDtypeStruct((parts * group, rows // parts, width), BF),
+        scratch_shapes=[pltpu.VMEM((group * rows, depth), BF), pltpu.VMEM((depth, width), BF)],
         compiler_params=pltpu.CompilerParams(vmem_limit_bytes=32 * 2**20),
         cost_estimate=pl.CostEstimate(
-            flops=4 * rows * depth * width, bytes_accessed=2 * depth * width, transcendentals=0
-        ),
-    )(order, own, far, *chunks)
+            flops=2 * group * rows * depth * width, bytes_accessed=2 * depth * width, transcendentals=0
+        ),
+    )(ids, *pieces, near, far)
 
 
 def swap(mine):
     return lax.ppermute(mine, "core", SWAP)
 
 
-def gather_w_out(w_out):
-    core, x, z = (lax.axis_index(n) for n in ("core", "x", "z_lo"))
-    half = w_out.shape[1] // 2
-    lower, upper = w_out[:, :half], w_out[:, half:]
-    mine = jnp.where(core == 0, lower, upper)
-    other = swap(jnp.where(core == 0, upper, lower))
-    own = jnp.concatenate([jnp.where(core == 0, mine, other), jnp.where(core == 0, other, mine)], axis=0)
-    up = lambda a: lax.ppermute(a, "x", [(i, (i + 1) % 4) for i in range(4)])
-    down = lambda a: lax.ppermute(a, "x", [(i, (i + 3) % 4) for i in range(4)])
-    across = lambda a: lax.ppermute(a, "z_lo", SWAP)
-    mate, before, after = across(own), up(own), down(own)
-    mate_before, mate_after, opposite = up(mate), across(after), down(after)
-    part = half // 2
-    left, right = up(mate_before[:, :part]), down(mate_after[:, part:])
-    chunks = (own, mate, before, after, mate_before, mate_after, opposite, left, right)
-    chip = lambda zz, dx: zz * 4 + lax.rem(x + 4 + dx, 4)
-    order = (chip(z, 0), chip(1 - z, 0), chip(z, -1), chip(z, 1), chip(1 - z, -1), chip(1 - z, 1), chip(z, 2), chip(1 - z, 2))
-    return own, jnp.stack(order).astype(jnp.int32), chunks
+def up(a):
+    return lax.ppermute(a, "x", [(i, (i + 1) % 4) for i in range(4)])
+
+
+def down(a):
+    return lax.ppermute(a, "x", [(i, (i + 3) % 4) for i in range(4)])
 
 
 def latent_queries(queries, w_kv):
@@ -314,28 +308,30 @@
     tok, width = resid.shape
     chips = 64
     core = lax.axis_index("core")
-    own_rows, order, chunks = gather_w_out(w_out)
-    latents, _ = lax.optimization_barrier((latents, own_rows))
+    group = 4
+    columns = width // group
+    w_blocks = w_out.reshape(-1, group, columns // 128, 128).transpose(1, 2, 0, 3).reshape(group, -1, 128)
+    payload = jnp.concatenate(
+        [jnp.broadcast_to(latents[None], (group,) + latents.shape), w_blocks], axis=1
+    )
     near = lax.all_to_all(
-        jnp.broadcast_to(latents[None], (8,) + latents.shape), CTX_CHIPS, split_axis=0, concat_axis=0, tiled=True
+        jnp.concatenate([payload, payload], axis=0), CTX_CHIPS, split_axis=0, concat_axis=0, tiled=True
     )
     far = swap(near)
-    ids = jnp.stack([lax.axis_index(CTX), core]).astype(jnp.int32)
-    heads_out = attend(ids, latent_queries(queries, w_kv), near, far, w_kv, 4, 4)
-    half = width // 2
-    lower, upper = resid[:, :half], resid[:, half:]
-    resid2 = jnp.stack([jnp.where(core == 0, lower, upper), swap(jnp.where(core == 0, upper, lower))])
-    attn = project(order, heads_out, swap(heads_out), chunks, 8)
-    attn = lax.all_to_all(attn, EP, split_axis=0, concat_axis=0, tiled=True)
-    summed = (resid2.astype(F32) + jnp.sum(attn.astype(F32), axis=0)).astype(BF)
-    others = swap(summed)[::-1]
-    attended2 = jnp.concatenate(
-        [jnp.where(core == 0, summed, others), jnp.where(core == 0, others, summed)], axis=2
-    ).reshape(2 * tok, width)
-    attended = attended2[:tok]
-    wide2 = attended2.astype(F32)
-    meansq = jnp.mean(wide2 * wide2, axis=1, keepdims=True)
-    normed2 = (wide2 * lax.rsqrt(meansq + 1e-06) * norm_gain[None, :]).astype(BF)
+    ids = jnp.stack([lax.axis_index(CTX), core, lax.axis_index("x")]).astype(jnp.int32)
+    own = attend(ids, latent_queries(queries, w_kv), near, far, w_kv, 4, 4)
+    before, after = up(own), down(own)
+    half = own.shape[1] // 2
+    left, right = up(before[:, :half]), down(after[:, half:])
+    attn = project(ids, (own, before, after, left, right), near, far, 8, columns)
+    attn = lax.all_to_all(attn, EP + ("x",), split_axis=0, concat_axis=0, tiled=True)
+    attn = jnp.sum(attn.reshape(8, group, tok, columns).astype(F32), axis=0)
+    attn = attn.transpose(1, 0, 2).reshape(tok, width)
+    attended = (resid.astype(F32) + attn).astype(BF)
+    wide = attended.astype(F32)
+    meansq = jnp.mean(wide * wide, axis=1, keepdims=True)
+    normed = (wide * lax.rsqrt(meansq + 1e-06) * norm_gain[None, :]).astype(BF)
+    normed2 = jnp.concatenate([normed, swap(normed)], axis=0)
 
     def exchange(rows):
         units = rows.reshape(chips, -1, 2, width)
@@ -343,10 +339,10 @@
         return units.reshape(rows.shape)
 
     parts = routing(routes, codes)
-    arrived = [exchange(dispatch(place, normed2, 7)) for place, _ in parts]
+    arrived = [exchange(dispatch(place, normed2, 2)) for place, _ in parts]
     returned = [exchange(expert(rows, w_gate[0], w_up[0], w_down[0], 2, 7)) for rows in arrived]
-    own, theirs = combine([(factors, rows) for (_, factors), rows in zip(parts, returned)], 7)
-    layer_out = (wide2[:tok] + own + swap(theirs)).astype(BF)
+    mine, theirs = combine([(factors, rows) for (_, factors), rows in zip(parts, returned)], 4)
+    layer_out = (wide + mine + swap(theirs)).astype(BF)
     return (attended, layer_out)
 
 

time: 214 us -> 205 us (0.958)
  blocking collectives: 22.4 us -> 73 us
  starting transfers between devices: 63.4 us -> 36.3 us
  local copies, waits for them, and re-layouts: 22.2 us -> 10.1 us
  Pallas kernels: 35.7 us -> 26.9 us
  other arithmetic: 9.47 us -> 2.1 us
  waiting for transfers between devices: 57 us -> 52.1 us
    all_to_all x1 -> x2, blocking collectives: 22.4 us -> 73 us  [the longest x1 40.8 us: exchange(): lax.all_to_all(units, CHIPS, split_axis=0, concat_axis=0, tiled=True)]
    all_to_all x4 -> x1, starting transfers between devices: 30.2 us -> 7.46 us  [exchange(): lax.all_to_all(units, CHIPS, split_axis=0, concat_axis=0, tiled=True)]
    unnamed x42 -> x23, local copies, waits for them, and re-layouts: 16.4 us -> 5.89 us
    all_to_all x4 -> x1, waiting for transfers between devices: 36 us -> 29.9 us  [exchange(): lax.all_to_all(units, CHIPS, split_axis=0, concat_axis=0, tiled=True)]
    ppermute x8 -> x5, starting transfers between devices: 17.6 us -> 13.4 us  [swap(): return lax.ppermute(mine, 'core', SWAP)]
    pallas_call x2 -> x1, Pallas kernels: 5.29 us -> 1.35 us  [dispatch(): pl.pallas_call(dispatch_kernel, grid=(cuts,), in_specs=[pl.BlockSpec(plac...]
    pallas_call x2 -> x1, Pallas kernels: 13.9 us -> 10 us  [expert(): pl.pallas_call(functools.partial(expert_kernel, first=first), grid=(first...]
    ppermute x8 -> x4, starting transfers between devices: 8.27 us -> 5.54 us  [the longest x2 4.55 us: down(): return lax.ppermute(a, 'x', [(i, (i + 3) % 4) for i in range(4)])]
  transfers between devices with their start and end apart: 21 -> 11, of which waited for: 11 -> 8; matrix products, arithmetic and copies ran while one was open for 8% -> 4% of each run, Pallas kernels for 13% -> 0%
where the time goes in v10:
time: 205 us; the launch traced here: 203 us
  blocking collectives  73 us (36%)
  waiting for transfers between devices  52.1 us (25%)
  starting transfers between devices  36.3 us (18%)
  Pallas kernels  26.9 us (13%)
  local copies, waits for them, and re-layouts  10.1 us (5%)
  other arithmetic  2.1 us (1%)
    all_to_all x1, blocking collectives, exchange(): lax.all_to_all(units, CHIPS, split_axis=0, concat_axis=0, tiled=True)  40.8 us
    all_to_all x1, blocking collectives, local(): lax.all_to_all(jnp.concatenate([payload, payload], axis=0), CTX_CHIPS, sp...  32.2 us
    all_to_all x1, waiting for transfers between devices, exchange(): lax.all_to_all(units, CHIPS, split_axis=0, concat_axis=0, tiled=True)  29.9 us
    ppermute x5, starting transfers between devices, swap(): return lax.ppermute(mine, 'core', SWAP)  13.4 us
    all_to_all x1, waiting for transfers between devices, local(): lax.all_to_all(attn, EP + ('x',), split_axis=0, concat_axis=0, tiled=True)  10.1 us
    pallas_call x1, Pallas kernels, attend(): pl.pallas_call(functools.partial(attend_kernel, rows=rows, cuts=cuts), gr...  10 us
    pallas_call x1, Pallas kernels, expert(): pl.pallas_call(functools.partial(expert_kernel, first=first), grid=(first...  10 us
    all_to_all x1, starting transfers between devices, local(): lax.all_to_all(attn, EP + ('x',), split_axis=0, concat_axis=0, tiled=True)  9.81 us
  transfers between devices with their start and end apart: 11, of which 8 were waited for; matrix products, arithmetic and copies ran while one was open for 4% of the time, Pallas kernels for 0%

profile of v10, /device:TPU:1, one launch (start us, length us, event | category | flops | bytes accessed | tf_op | source)
XLA Modules:
  0.0 203.3 jit_solution(7129986558068028967)
XLA Ops:
  0.6 1.6 reshape.151
  2.2 0.2 copy.69
  2.4 1.0 broadcast_in_dim.32
  3.4 0.3 maximum_maximum_fusion
  3.7 0.0 copy-start.5
  3.7 32.2 %all_to_all.20.near_ref = bf16[8,1024,128]{2,1,0:T(8,128)(2,1)S(1)} all-to-all(bf16[8,1024,128]{2,1,0:T(8,128)(2,1)S(1)} %maximum_maximum_fusion), channel_id=1, replica_groups=mesh['z_lo'=2,'x'=4,'core'=2,'z_hi'=2,'y'=4] {'z_lo','x'}, dimensions={0} | all-to-all | bytes 4194304 | tf_op jit(solution)/shard_map/all_to_all | solution.py:317
  35.9 1.8 collective-permute-start
  37.7 0.2 copy.64
  38.0 0.2 copy.84
  38.2 3.9 %copy.66 = bf16[512,2048]{0,1:T(8,128)(2,1)} copy(bf16[512,2048]{1,0:T(8,128)(2,1)} %w_ref.1) | data formatting | bytes 4194304 | tf_op args[2]
  42.1 0.1 pad_add_fusion.1.ids_ref
  42.2 1.9 convolution_convert_fusion
  44.0 0.1 pad_maximum_fusion
  44.2 10.0 %shard_map.122.own_ref = bf16[128,1024]{1,0:T(8,128)(2,1)S(1)} custom-call(s32[3]{0:T(128)S(1)} %pad_add_fusion.1.ids_ref, bf16[1024,576]{1,0:T(8,128)(2,1)S(1)} %bitcast.49, bf16[8,1024,128]{2,1,0:T(8,128)(2,1)S(1)} %all_to_all.20.near_ref, bf16[8,1024,128]{2,1,0:T(8,128)(2,1)} %collective-permute-done.far_ref, bf16[512,2048]{1,0:T(8,128)(2,1)S(1)} %copy-done.3), custom_call_target="tpu_custom_call" | custom-call | flops 4563402752 | bytes 8000000 | tf_op jit(solution)/shard_map/pallas_call | solution.py:77
  54.2 0.9 collective-permute-start.1
  55.1 1.8 collective-permute-start.2
  56.9 6.5 %collective-permute-done.1.before_ref = bf16[128,1024]{1,0:T(8,128)(2,1)S(1)} collective-permute-done((bf16[128,1024]{1,0:T(8,128)(2,1)S(1)}, bf16[128,1024]{1,0:T(8,128)(2,1)S(1)}, u32[]{:S(2)}, u32[]{:S(2)}) %collective-permute-start.1) | collective-permute-done | bytes 262176 | tf_op jit(solution)/shard_map/ppermute | solution.py:256
  63.4 0.1 collective-permute-start.3
  63.5 0.0 copy-start.9
  63.5 2.7 %collective-permute-start.4 = (bf16[128,512]{1,0:T(8,128)(2,1)S(1)}, bf16[128,512]{1,0:T(8,128)(2,1)S(1)}, u32[]{:S(2)}, u32[]{:S(2)}) collective-permute-start(bf16[128,512]{1,0:T(8,128)(2,1)S(1)} %slice.40), channel_id=1, source_target_pairs={{0,48},{16,0},{32,16},{48,32},{1,49},{17,1},{33,17},{49,33},{2,50}... | collective-permute-start | bytes 393224 | tf_op jit(solution)/shard_map/ppermute | solution.py:260
  66.3 2.7 %collective-permute-done.3.left_ref = bf16[128,512]{1,0:T(8,128)(2,1)S(1)} collective-permute-done((bf16[128,512]{1,0:T(8,128)(2,1)S(1)}, bf16[128,512]{1,0:T(8,128)(2,1)S(1)}, u32[]{:S(2)}, u32[]{:S(2)}) %collective-permute-start.3) | collective-permute-done | bytes 131104 | tf_op jit(solution)/shard_map/ppermute | solution.py:256
  68.9 4.1 %shard_map.123 = bf16[32,16,896]{2,1,0:T(8,128)(2,1)} custom-call(s32[3]{0:T(128)S(1)} %pad_add_fusion.1.ids_ref, bf16[128,1024]{1,0:T(8,128)(2,1)S(1)} %shard_map.122.own_ref, bf16[128,1024]{1,0:T(8,128)(2,1)S(1)} %collective-permute-done.1.before_ref, bf16[128,1024]{1,0:T(8,128)(2,1)S(1)} %collective-permute-done.2.after_ref, ...), custom_call_target="tpu_custom_call" | custom-call | flops 939524096 | bytes 1835008 | tf_op jit(solution)/shard_map/pallas_call | solution.py:238
  73.1 9.8 %all-to-all-start.1 = ((bf16[32,16,896]{2,1,0:T(8,128)(2,1)}), bf16[32,16,896]{2,1,0:T(8,128)(2,1)S(1)}, u32[]{:S(2)}, u32[]{:S(2)}) async-start(bf16[32,16,896]{2,1,0:T(8,128)(2,1)} %shard_map.123), calls=%async_computation.1 | async-start | bytes 1835008 | tf_op jit(solution)/shard_map/all_to_all | solution.py:327
  82.9 2.6 %collective-permute-start.5 = (s32[16,8]{0,1:T(8,128)S(1)}, s32[16,8]{0,1:T(8,128)S(1)}, u32[]{:S(2)}, u32[]{:S(2)}) collective-permute-start(s32[16,8]{0,1:T(8,128)S(1)} %copy-done.9), channel_id=1, source_target_pairs={{0,8},{8,0},{1,9},{9,1},{2,10},{10,2},{3,11},{11,3},{4,12},{12,4},... | collective-permute-start | bytes 1544 | tf_op jit(solution)/shard_map/ppermute | solution.py:252
  85.5 0.1 and.46
  85.6 0.1 and.47
  85.6 0.7 collective-permute-done.5
  86.3 0.1 copy.71
  86.4 0.1 fusion.7
  86.5 0.1 copy.72
  86.6 0.1 copy.74
  86.8 0.1 copy.73
  86.9 10.1 %all-to-all-done.1 = bf16[32,16,896]{2,1,0:T(8,128)(2,1)S(1)} async-done(((bf16[32,16,896]{2,1,0:T(8,128)(2,1)}), bf16[32,16,896]{2,1,0:T(8,128)(2,1)S(1)}, u32[]{:S(2)}, u32[]{:S(2)}) %all-to-all-start.1) | async-done | bytes 917536 | tf_op jit(solution)/shard_map/all_to_all | solution.py:327
  96.9 0.1 convert_reduce_fusion
  97.1 0.2 fusion.2
  97.3 0.1 fusion.4
  97.4 3.7 %collective-permute-start.7 = (bf16[16,3584]{1,0:T(8,128)(2,1)S(1)}, bf16[16,3584]{1,0:T(8,128)(2,1)S(1)}, u32[]{:S(2)}, u32[]{:S(2)}) collective-permute-start(bf16[16,3584]{1,0:T(8,128)(2,1)S(1)} %fusion.4), channel_id=1, source_target_pairs={{0,8},{8,0},{1,9},{9,1},{2,10},{10,2},{3,11},{11,3},{4,12},{12,4},... | collective-permute-start | bytes 344072 | tf_op jit(solution)/shard_map/ppermute | solution.py:252
  101.1 0.1 bitcast_and_fusion
  101.2 0.1 copy.75
  101.3 0.1 broadcast_in_dim.33
  101.4 0.1 reshape.155
  101.6 0.5 collective-permute-done.7
  102.1 0.0 copy-start.2
  102.1 1.4 shard_map.124
  103.4 0.0 copy-start.1
  103.4 40.8 %all_to_all.21 = bf16[64,3,2,3584]{3,2,1,0:T(2,128)(2,1)S(1)} all-to-all(bf16[64,3,2,3584]{3,2,1,0:T(2,128)(2,1)S(1)} %bitcast.44), channel_id=1, replica_groups=mesh['z_lo'=2,'x'=4,'core'=2,'z_hi'=2,'y'=4] {'z_lo','x','z_hi','y'}, dimensions={0} | all-to-all | bytes 5505024 | tf_op jit(solution)/shard_map/all_to_all | solution.py:338
  144.2 10.0 %shard_map.125 = bf16[192,2,3584]{2,1,0:T(2,128)(2,1)S(1)} custom-call(bf16[192,2,3584]{2,1,0:T(2,128)(2,1)S(1)} %bitcast.46, bf16[3584,512]{1,0:T(8,128)(2,1)S(1)} %bitcast.47, bf16[3584,512]{1,0:T(8,128)(2,1)S(1)} %bitcast.48, bf16[512,3584]{1,0:T(8,128)(2,1)} %bitcast.52), custom_call_target="tpu_custom_call" | custom-call | flops 4227858432 | bytes 17000000 | tf_op jit(solution)/shard_map/pallas_call | solution.py:130
  154.3 1.5 copy-done
  155.8 7.5 %all-to-all-start.3 = ((bf16[64,3,2,3584]{3,2,1,0:T(2,128)(2,1)}), bf16[64,3,2,3584]{3,2,1,0:T(2,128)(2,1)S(1)}, u32[]{:S(2)}, u32[]{:S(2)}) async-start(bf16[64,3,2,3584]{3,2,1,0:T(2,128)(2,1)} %bitcast.45), calls=%async_computation.3 | async-start | bytes 5505024 | tf_op jit(solution)/shard_map/all_to_all | solution.py:338
  163.3 1.6 collective-permute-start.6
  164.9 0.1 copy.80
  165.0 0.7 collective-permute-done.6
  165.7 0.1 copy.76
  165.8 0.1 select_reduce_fusion
  165.9 0.1 copy.77
  166.0 0.1 copy.78
  166.1 0.1 copy.79
  166.2 0.1 broadcast_in_dim.65
  166.3 0.1 copy.81
  166.4 29.9 %all-to-all-done.3 = bf16[64,3,2,3584]{3,2,1,0:T(2,128)(2,1)S(1)} async-done(((bf16[64,3,2,3584]{3,2,1,0:T(2,128)(2,1)}), bf16[64,3,2,3584]{3,2,1,0:T(2,128)(2,1)S(1)}, u32[]{:S(2)}, u32[]{:S(2)}) %all-to-all-start.3) | async-done | bytes 2752544 | tf_op jit(solution)/shard_map/all_to_all | solution.py:338
  196.3 1.4 shard_map.126
  197.7 3.8 %collective-permute-start.8 = (f32[16,3584]{1,0:T(8,128)S(1)}, f32[16,3584]{1,0:T(8,128)S(1)}, u32[]{:S(2)}, u32[]{:S(2)}) collective-permute-start(f32[16,3584]{1,0:T(8,128)S(1)} %get-tuple-element.5), channel_id=1, source_target_pairs={{0,8},{8,0},{1,9},{9,1},{2,10},{10,2},{3,11},{11,3},{4,12},{12,4},... | collective-permute-start | bytes 688136 | tf_op jit(solution)/shard_map/ppermute | solution.py:252
  201.5 1.1 collective-permute-done.8
  202.6 0.7 fusion.6
  (40 shorter events, 0.3 us)
Async XLA Ops:
  3.7 34.0 %copy-start.5 = (bf16[128,1536]{1,0:T(8,128)(2,1)S(1)}, bf16[128,1536]{1,0:T(8,128)(2,1)}, u32[]{:S(2)}) copy-start(bf16[128,1536]{1,0:T(8,128)(2,1)} %param.11) | copy-start | bytes 1179652
  35.9 8.2 %collective-permute-start = (bf16[8,1024,128]{2,1,0:T(8,128)(2,1)S(1)}, bf16[8,1024,128]{2,1,0:T(8,128)(2,1)}, u32[]{:S(2)}, u32[]{:S(2)}) collective-permute-start(bf16[8,1024,128]{2,1,0:T(8,128)(2,1)S(1)} %all_to_all.20.near_ref), channel_id=1, source_target_pairs={{0,8},{8,0},{1,9},{9,1},{2,10},{10,2},{3,11},{11,3},{4,12},{12,4},... | collective-permute-start | bytes 6291464 | tf_op jit(solution)/shard_map/ppermute | solution.py:252
  42.2 2.0 copy-start.3
  54.2 9.2 %collective-permute-start.1 = (bf16[128,1024]{1,0:T(8,128)(2,1)S(1)}, bf16[128,1024]{1,0:T(8,128)(2,1)S(1)}, u32[]{:S(2)}, u32[]{:S(2)}) collective-permute-start(bf16[128,1024]{1,0:T(8,128)(2,1)S(1)} %shard_map.122.own_ref), channel_id=1, source_target_pairs={{0,16},{16,32},{32,48},{48,0},{1,17},{17,33},{33,49},{49,1},{2,18}... | collective-permute-start | bytes 786440 | tf_op jit(solution)/shard_map/ppermute | solution.py:256
  55.1 8.4 %collective-permute-start.2 = (bf16[128,1024]{1,0:T(8,128)(2,1)S(1)}, bf16[128,1024]{1,0:T(8,128)(2,1)S(1)}, u32[]{:S(2)}, u32[]{:S(2)}) collective-permute-start(bf16[128,1024]{1,0:T(8,128)(2,1)S(1)} %shard_map.122.own_ref), channel_id=1, source_target_pairs={{0,48},{16,0},{32,16},{48,32},{1,49},{17,1},{33,17},{49,33},{2,50}... | collective-permute-start | bytes 786440 | tf_op jit(solution)/shard_map/ppermute | solution.py:260
  63.4 5.5 %collective-permute-start.3 = (bf16[128,512]{1,0:T(8,128)(2,1)S(1)}, bf16[128,512]{1,0:T(8,128)(2,1)S(1)}, u32[]{:S(2)}, u32[]{:S(2)}) collective-permute-start(bf16[128,512]{1,0:T(8,128)(2,1)S(1)} %slice.39), channel_id=1, source_target_pairs={{0,16},{16,32},{32,48},{48,0},{1,17},{17,33},{33,49},{49,1},{2,18}... | collective-permute-start | bytes 393224 | tf_op jit(solution)/shard_map/ppermute | solution.py:256
  63.5 19.4 %copy-start.9 = (s32[16,8]{0,1:T(8,128)S(1)}, s32[16,8]{0,1:T(8,128)}, u32[]{:S(2)}) copy-start(s32[16,8]{0,1:T(8,128)} %param.17) | copy-start | bytes 1540
  63.5 5.4 %collective-permute-start.4 = (bf16[128,512]{1,0:T(8,128)(2,1)S(1)}, bf16[128,512]{1,0:T(8,128)(2,1)S(1)}, u32[]{:S(2)}, u32[]{:S(2)}) collective-permute-start(bf16[128,512]{1,0:T(8,128)(2,1)S(1)} %slice.40), channel_id=1, source_target_pairs={{0,48},{16,0},{32,16},{48,32},{1,49},{17,1},{33,17},{49,33},{2,50}... | collective-permute-start | bytes 393224 | tf_op jit(solution)/shard_map/ppermute | solution.py:260
  73.1 24.0 %copy-start.6 = (bf16[16,3584]{1,0:T(8,128)(2,1)S(1)}, bf16[16,3584]{1,0:T(8,128)(2,1)}, u32[]{:S(2)}) copy-start(bf16[16,3584]{1,0:T(8,128)(2,1)} %param.15) | copy-start | bytes 344068
  73.1 24.2 %copy-start.8 = (f32[3584]{0:T(1024)S(1)}, f32[3584]{0:T(1024)}, u32[]{:S(2)}) copy-start(f32[3584]{0:T(1024)} %param.16) | copy-start | bytes 43012
  73.1 23.9 %all-to-all-start.1 = ((bf16[32,16,896]{2,1,0:T(8,128)(2,1)}), bf16[32,16,896]{2,1,0:T(8,128)(2,1)S(1)}, u32[]{:S(2)}, u32[]{:S(2)}) async-start(bf16[32,16,896]{2,1,0:T(8,128)(2,1)} %shard_map.123), calls=%async_computation.1 | async-start | bytes 1835008 | tf_op jit(solution)/shard_map/all_to_all | solution.py:327
  82.9 3.4 %collective-permute-start.5 = (s32[16,8]{0,1:T(8,128)S(1)}, s32[16,8]{0,1:T(8,128)S(1)}, u32[]{:S(2)}, u32[]{:S(2)}) collective-permute-start(s32[16,8]{0,1:T(8,128)S(1)} %copy-done.9), channel_id=1, source_target_pairs={{0,8},{8,0},{1,9},{9,1},{2,10},{10,2},{3,11},{11,3},{4,12},{12,4},... | collective-permute-start | bytes 1544 | tf_op jit(solution)/shard_map/ppermute | solution.py:252
  97.2 105.4 %copy-start.4 = (bf16[16,3584]{1,0:T(8,128)(2,1)}, bf16[16,3584]{1,0:T(8,128)(2,1)S(1)}, u32[]{:S(2)}) copy-start(bf16[16,3584]{1,0:T(8,128)(2,1)S(1)} %get-tuple-element.7) | copy-start | bytes 344068
  97.4 4.7 %collective-permute-start.7 = (bf16[16,3584]{1,0:T(8,128)(2,1)S(1)}, bf16[16,3584]{1,0:T(8,128)(2,1)S(1)}, u32[]{:S(2)}, u32[]{:S(2)}) collective-permute-start(bf16[16,3584]{1,0:T(8,128)(2,1)S(1)} %fusion.4), channel_id=1, source_target_pairs={{0,8},{8,0},{1,9},{9,1},{2,10},{10,2},{3,11},{11,3},{4,12},{12,4},... | collective-permute-start | bytes 344072 | tf_op jit(solution)/shard_map/ppermute | solution.py:252
  102.1 42.2 %copy-start.2 = (bf16[1,3584,512]{2,1,0:T(8,128)(2,1)S(1)}, bf16[1,3584,512]{2,1,0:T(8,128)(2,1)}, u32[]{:S(2)}) copy-start(bf16[1,3584,512]{2,1,0:T(8,128)(2,1)} %param.20) | copy-start | bytes 11010052
  103.4 40.8 %copy-start.1 = (bf16[1,3584,512]{2,1,0:T(8,128)(2,1)S(1)}, bf16[1,3584,512]{2,1,0:T(8,128)(2,1)}, u32[]{:S(2)}) copy-start(bf16[1,3584,512]{2,1,0:T(8,128)(2,1)} %param.19) | copy-start | bytes 11010052
  154.2 1.5 copy-start
  155.8 7.5 %copy-start.7 = (s32[16,8]{0,1:T(8,128)S(1)}, s32[16,8]{0,1:T(8,128)}, u32[]{:S(2)}) copy-start(s32[16,8]{0,1:T(8,128)} %param.18) | copy-start | bytes 1540
  155.8 40.6 %all-to-all-start.3 = ((bf16[64,3,2,3584]{3,2,1,0:T(2,128)(2,1)}), bf16[64,3,2,3584]{3,2,1,0:T(2,128)(2,1)S(1)}, u32[]{:S(2)}, u32[]{:S(2)}) async-start(bf16[64,3,2,3584]{3,2,1,0:T(2,128)(2,1)} %bitcast.45), calls=%async_computation.3 | async-start | bytes 5505024 | tf_op jit(solution)/shard_map/all_to_all | solution.py:338
  163.3 2.4 %collective-permute-start.6 = (f32[16,8]{0,1:T(8,128)S(1)}, f32[16,8]{0,1:T(8,128)S(1)}, u32[]{:S(2)}, u32[]{:S(2)}) collective-permute-start(f32[16,8]{0,1:T(8,128)S(1)} %convert_divide_fusion), channel_id=1, source_target_pairs={{0,8},{8,0},{1,9},{9,1},{2,10},{10,2},{3,11},{11,3},{4,12},{12,4},... | collective-permute-start | bytes 1544 | tf_op jit(solution)/shard_map/ppermute | solution.py:252
  197.7 4.9 %collective-permute-start.8 = (f32[16,3584]{1,0:T(8,128)S(1)}, f32[16,3584]{1,0:T(8,128)S(1)}, u32[]{:S(2)}, u32[]{:S(2)}) collective-permute-start(f32[16,3584]{1,0:T(8,128)S(1)} %get-tuple-element.5), channel_id=1, source_target_pairs={{0,8},{8,0},{1,9},{9,1},{2,10},{10,2},{3,11},{11,3},{4,12},{12,4},... | collective-permute-start | bytes 688136 | tf_op jit(solution)/shard_map/ppermute | solution.py:252

commit v11 on v10

--- a/solution.py
+++ b/solution.py
@@ -27,18 +27,22 @@
 LOG2E = 1.4426950408889634
 
 
-def attend_kernel(ids_ref, q_ref, near_ref, far_ref, w_ref, out_ref, lat_ref, s_ref, p_ref, *, rows, cuts):
+def attend_kernel(ids_ref, q_ref, w_ref, near_ref, far_ref, out_ref, lat_ref, s_ref, latq_ref, mixed_ref, *, cuts):
     heads = w_ref.shape[1] // (NOPE + VD)
-    m = q_ref.shape[0]
+    rows = q_ref.shape[0]
+    m = heads * rows
     pairs = near_ref.shape[0]
     keys = 2 * rows * pairs
-
-    @pl.when(pl.program_id(0) == 0)
-    def _():
-        for i in range(pairs):
-            lat_ref[:, 2 * i * rows : (2 * i + 1) * rows] = near_ref[i]
-            lat_ref[:, (2 * i + 1) * rows : (2 * i + 2) * rows] = far_ref[i]
-
+    for i in range(pairs):
+        lat_ref[:, 2 * i * rows : (2 * i + 1) * rows] = near_ref[i]
+        lat_ref[:, (2 * i + 1) * rows : (2 * i + 2) * rows] = far_ref[i]
+    for h in range(heads):
+        here = slice(h * rows, (h + 1) * rows)
+        key_weights = w_ref[:, h * (NOPE + VD) : h * (NOPE + VD) + NOPE]
+        plain = q_ref[:, h * QK : h * QK + NOPE]
+        latq = lax.dot_general(plain, key_weights, (((1,), (1,)), ((), ())), preferred_element_type=F32)
+        latq_ref[here, :KV_RANK] = latq.astype(BF)
+        latq_ref[here, KV_RANK:] = q_ref[:, h * QK + NOPE : (h + 1) * QK]
     ctx, core = ids_ref[0], ids_ref[1]
     span = keys // cuts
     lane = lax.broadcasted_iota(jnp.int32, (m, rows), 1)
@@ -46,7 +50,7 @@
     ahead = lane - query
     peak = jnp.full((m, rows), -1e30, F32)
     for j in range(cuts):
-        s = jnp.dot(q_ref[...], lat_ref[:, j * span : (j + 1) * span], preferred_element_type=F32)
+        s = jnp.dot(latq_ref[...], lat_ref[:, j * span : (j + 1) * span], preferred_element_type=F32)
         for b in range(span // rows):
             block = j * (span // rows) + b
             pos = 2 * (block // 2) + (core if block % 2 == 0 else 1 - core)
@@ -56,90 +60,103 @@
             s_ref[:, block * rows : (block + 1) * rows] = part
     top = jnp.max(peak, axis=1, keepdims=True)
     total = jnp.zeros((m, rows), F32)
-    for j in range(keys // rows):
-        p = jnp.exp2((s_ref[:, j * rows : (j + 1) * rows] - top) * (QK ** (-0.5) * LOG2E))
-        total = total + p
-        p_ref[:, j * rows : (j + 1) * rows] = p.astype(BF)
-    mixed = lax.dot_general(p_ref[...], lat_ref[:KV_RANK], (((1,), (1,)), ((), ())), preferred_element_type=F32)
-    mixed = (mixed / jnp.sum(total, axis=1, keepdims=True)).astype(BF)
+    for j in range(cuts):
+        probs = []
+        for b in range(span // rows):
+            first = j * span + b * rows
+            p = jnp.exp2((s_ref[:, first : first + rows] - top) * (QK ** (-0.5) * LOG2E))
+            total = total + p
+            probs.append(p.astype(BF))
+        part = lax.dot_general(
+            jnp.concatenate(probs, axis=1),
+            lat_ref[:KV_RANK, j * span : (j + 1) * span],
+            (((1,), (1,)), ((), ())),
+            preferred_element_type=F32,
+        )
+        mixed_ref[...] = part if j == 0 else mixed_ref[...] + part
+    mixed = (mixed_ref[...] / jnp.sum(total, axis=1, keepdims=True)).astype(BF)
     for h in range(heads):
         values = w_ref[:, h * (NOPE + VD) + NOPE : (h + 1) * (NOPE + VD)]
         o = jnp.dot(mixed[h * rows : (h + 1) * rows], values, preferred_element_type=F32)
         out_ref[:, h * VD : (h + 1) * VD] = o.astype(BF)
 
 
-def attend(ids, q, near, far, w_kv, group, cuts):
-    pairs, _, rows = near.shape
-    depth = q.shape[1]
+def attend(ids, q, w_kv, near, far, cuts):
+    pairs, depth, rows = near.shape
     heads = w_kv.shape[1] // (NOPE + VD)
     keys = 2 * rows * pairs
-    m = group * rows
-    return pl.pallas_call(
-        functools.partial(attend_kernel, rows=rows, cuts=cuts),
-        grid=(heads // group,),
-        in_specs=[
-            pl.BlockSpec(memory_space=pltpu.SMEM),
-            pl.BlockSpec((m, depth), lambda g: (g, 0)),
-            pl.BlockSpec((pairs, depth, rows), lambda g: (0, 0, 0)),
-            pl.BlockSpec((pairs, depth, rows), lambda g: (0, 0, 0)),
-            pl.BlockSpec((KV_RANK, group * (NOPE + VD)), lambda g: (0, g)),
+    m = heads * rows
+    whole = pl.BlockSpec(memory_space=pltpu.VMEM)
+    return pl.pallas_call(
+        functools.partial(attend_kernel, cuts=cuts),
+        in_specs=[pl.BlockSpec(memory_space=pltpu.SMEM)] + [whole] * 4,
+        out_specs=whole,
+        out_shape=jax.ShapeDtypeStruct((rows, heads * VD), BF),
+        scratch_shapes=[
+            pltpu.VMEM((depth, keys), BF),
+            pltpu.VMEM((m, keys), F32),
+            pltpu.VMEM((m, depth), BF),
+            pltpu.VMEM((m, KV_RANK), F32),
         ],
-        out_specs=pl.BlockSpec((rows, group * VD), lambda g: (0, g)),
-        out_shape=jax.ShapeDtypeStruct((rows, heads * VD), BF),
-        scratch_shapes=[pltpu.VMEM((depth, keys), BF), pltpu.VMEM((m, keys), F32), pltpu.VMEM((m, keys), BF)],
-        compiler_params=pltpu.CompilerParams(vmem_limit_bytes=40 * 2**20),
-        cost_estimate=pl.CostEstimate(
-            flops=2 * heads * rows * keys * (depth + KV_RANK),
-            bytes_accessed=8_000_000,
-            transcendentals=heads * rows * keys,
-        ),
-    )(ids, q, near, far, w_kv)
-
-
-def expert_kernel(x_ref, g_ref, u_ref, d_ref, out_ref, rows_ref, hid_ref, *, first):
-    step = pl.program_id(0)
-
-    @pl.when(step == 0)
-    def _():
-        rows_ref[...] = x_ref[...].reshape(rows_ref.shape)
-
-    @pl.when(step < first)
-    def _():
-        rows = rows_ref[...]
-        gate = jnp.dot(rows, g_ref[...], preferred_element_type=F32)
-        upward = jnp.dot(rows, u_ref[...], preferred_element_type=F32)
-        hid = (gate / (1.0 + jnp.exp(-gate)) * upward).astype(BF)
-        n = g_ref.shape[1]
-        for f in range(first):
-
-            @pl.when(step == f)
-            def _(f=f):
-                hid_ref[:, f * n : (f + 1) * n] = hid
-
-    @pl.when(step >= first)
-    def _():
-        y = jnp.dot(hid_ref[...], d_ref[...], preferred_element_type=F32).astype(BF)
-        out_ref[...] = y.reshape(out_ref.shape)
+        compiler_params=pltpu.CompilerParams(vmem_limit_bytes=36 * 2**20),
+        cost_estimate=pl.CostEstimate(
+            flops=2 * m * keys * (depth + KV_RANK), bytes_accessed=8_000_000, transcendentals=m * keys
+        ),
+    )(ids, q, w_kv, near, far)
+
+
+def expert_kernel(x_hbm, g_ref, u_ref, d_ref, out_hbm, x_ref, hid_ref, gate_ref, up_ref, y_ref, sem_in, sem_out):
+    units, pair, width = x_ref.shape
+    m = units * pair
+    first, last = sem_in.shape[0], sem_out.shape[0]
+    depth, wide = width // first, width // last
+    arrivals = []
+    for k in range(first):
+        part = slice(k * depth, (k + 1) * depth)
+        arrivals.append(pltpu.make_async_copy(x_hbm.at[:, :, part], x_ref.at[:, :, part], sem_in.at[k]))
+        arrivals[-1].start()
+    for k in range(first):
+        part = slice(k * depth, (k + 1) * depth)
+        arrivals[k].wait()
+        rows = x_ref[:, :, part].reshape(m, depth)
+        gate = jnp.dot(rows, g_ref[part], preferred_element_type=F32)
+        upward = jnp.dot(rows, u_ref[part], preferred_element_type=F32)
+        gate_ref[...] = gate if k == 0 else gate_ref[...] + gate
+        up_ref[...] = upward if k == 0 else up_ref[...] + upward
+    gate = gate_ref[...]
+    hid_ref[...] = (gate / (1.0 + jnp.exp(-gate)) * up_ref[...]).astype(BF)
+    departures = []
+    for n in range(last):
+        part = slice(n * wide, (n + 1) * wide)
+        y = jnp.dot(hid_ref[...], d_ref[:, part], preferred_element_type=F32).astype(BF)
+        y_ref[:, :, part] = y.reshape(units, pair, wide)
+        departures.append(pltpu.make_async_copy(y_ref.at[:, :, part], out_hbm.at[:, :, part], sem_out.at[n]))
+        departures[-1].start()
+    for copy in departures:
+        copy.wait()
 
 
 def expert(x, w_gate, w_up, w_down, first, last):
     units, pair, width = x.shape
     m = units * pair
     hidden = w_gate.shape[1]
-    n1, n2 = hidden // first, width // last
-    return pl.pallas_call(
-        functools.partial(expert_kernel, first=first),
-        grid=(first + last,),
-        in_specs=[
-            pl.BlockSpec(x.shape, lambda i: (0, 0, 0)),
-            pl.BlockSpec((width, n1), lambda i: (0, jnp.minimum(i, first - 1))),
-            pl.BlockSpec((width, n1), lambda i: (0, jnp.minimum(i, first - 1))),
-            pl.BlockSpec((hidden, n2), lambda i: (0, jnp.maximum(i - first, 0))),
+    whole = pl.BlockSpec(memory_space=pltpu.VMEM)
+    far = pl.BlockSpec(memory_space=pltpu.HBM)
+    return pl.pallas_call(
+        expert_kernel,
+        in_specs=[far, whole, whole, whole],
+        out_specs=far,
+        out_shape=jax.ShapeDtypeStruct(x.shape, BF),
+        scratch_shapes=[
+            pltpu.VMEM(x.shape, BF),
+            pltpu.VMEM((m, hidden), BF),
+            pltpu.VMEM((m, hidden), F32),
+            pltpu.VMEM((m, hidden), F32),
+            pltpu.VMEM(x.shape, BF),
+            pltpu.SemaphoreType.DMA((first,)),
+            pltpu.SemaphoreType.DMA((last,)),
         ],
-        out_specs=pl.BlockSpec((units, pair, n2), lambda i: (0, 0, jnp.maximum(i - first, 0))),
-        out_shape=jax.ShapeDtypeStruct(x.shape, BF),
-        scratch_shapes=[pltpu.VMEM((m, width), BF), pltpu.VMEM((m, hidden), BF)],
-        compiler_params=pltpu.CompilerParams(vmem_limit_bytes=40 * 2**20),
+        compiler_params=pltpu.CompilerParams(vmem_limit_bytes=32 * 2**20),
         cost_estimate=pl.CostEstimate(
             flops=6 * m * width * hidden, bytes_accessed=17_000_000, transcendentals=m * hidden
         ),
@@ -217,13 +234,12 @@
     x_ref[3 * rows :] = before_ref[...]
     deep = VD // 2
     blocks = w_ref.shape[1] // 128
-    first = near_ref.shape[1] - blocks * deep
     for side, ref in enumerate((near_ref, far_ref)):
         offset = (core if side == 0 else 1 - core) * deep
         for j in range(ref.shape[0]):
             here = pl.ds(pl.multiple_of(j * VD + offset, deep), deep)
             for b in range(blocks):
-                w_ref[here, b * 128 : (b + 1) * 128] = ref[j, first + b * deep : first + (b + 1) * deep]
+                w_ref[here, b * 128 : (b + 1) * 128] = ref[j, b * deep : (b + 1) * deep]
     for d in range(group):
         y = jnp.dot(x_ref[d * rows : (d + 1) * rows], w_ref[...], preferred_element_type=F32).astype(BF)
         target = lax.rem(x + d, group)
@@ -258,16 +274,6 @@
 
 def down(a):
     return lax.ppermute(a, "x", [(i, (i + 3) % 4) for i in range(4)])
-
-
-def latent_queries(queries, w_kv):
-    rows = queries.shape[0]
-    heads = queries.shape[1] // QK
-    q = queries.reshape(rows, heads, QK)
-    keys = w_kv.reshape(KV_RANK, heads, NOPE + VD)[:, :, :NOPE]
-    q_lat = jnp.einsum("qhd,rhd->hqr", q[:, :, :NOPE], keys, preferred_element_type=F32).astype(BF)
-    q_all = jnp.concatenate([q_lat, q[:, :, NOPE:].transpose(1, 0, 2)], axis=2)
-    return q_all.reshape(heads * rows, -1)
 
 
 def routing(routes, codes):
@@ -310,20 +316,22 @@
     core = lax.axis_index("core")
     group = 4
     columns = width // group
-    w_blocks = w_out.reshape(-1, group, columns // 128, 128).transpose(1, 2, 0, 3).reshape(group, -1, 128)
-    payload = jnp.concatenate(
-        [jnp.broadcast_to(latents[None], (group,) + latents.shape), w_blocks], axis=1
-    )
     near = lax.all_to_all(
-        jnp.concatenate([payload, payload], axis=0), CTX_CHIPS, split_axis=0, concat_axis=0, tiled=True
+        jnp.broadcast_to(latents[None], (8,) + latents.shape), CTX_CHIPS, split_axis=0, concat_axis=0, tiled=True
     )
     far = swap(near)
+    w_blocks = w_out.reshape(-1, group, columns // 128, 128).transpose(1, 2, 0, 3).reshape(group, -1, 128)
+    w_blocks, _ = lax.optimization_barrier((w_blocks, near[0, :8]))
+    w_near = lax.all_to_all(
+        jnp.concatenate([w_blocks, w_blocks], axis=0), CTX_CHIPS, split_axis=0, concat_axis=0, tiled=True
+    )
+    w_far = swap(w_near)
     ids = jnp.stack([lax.axis_index(CTX), core, lax.axis_index("x")]).astype(jnp.int32)
-    own = attend(ids, latent_queries(queries, w_kv), near, far, w_kv, 4, 4)
+    own = attend(ids, queries, w_kv, near, far, 4)
     before, after = up(own), down(own)
     half = own.shape[1] // 2
     left, right = up(before[:, :half]), down(after[:, half:])
-    attn = project(ids, (own, before, after, left, right), near, far, 8, columns)
+    attn = project(ids, (own, before, after, left, right), w_near, w_far, 8, columns)
     attn = lax.all_to_all(attn, EP + ("x",), split_axis=0, concat_axis=0, tiled=True)
     attn = jnp.sum(attn.reshape(8, group, tok, columns).astype(F32), axis=0)
     attn = attn.transpose(1, 0, 2).reshape(tok, width)

time: 205 us -> 205 us (level)
  waiting for transfers between devices: 52.1 us -> 68.8 us
  blocking collectives: 73 us -> 63 us
  Pallas kernels: 26.9 us -> 20.6 us
    all_to_all x0 -> x1, waiting for transfers between devices: none -> 14.5 us  [local(): lax.all_to_all(jnp.concatenate([w_blocks, w_blocks], axis=0), CTX_CHIPS,...]
    all_to_all x1, blocking collectives: 32.2 us -> 22.4 us  [local(): lax.all_to_all(jnp.broadcast_to(latents[None], (8,) + latents.shape), CTX...]
    ppermute x2, waiting for transfers between devices: 0.01 us -> 8.86 us  [down(): return lax.ppermute(a, 'x', [(i, (i + 3) % 4) for i in range(4)])]
    ppermute x2, waiting for transfers between devices: 9.13 us -> 2.62 us  [up(): return lax.ppermute(a, 'x', [(i, (i + 1) % 4) for i in range(4)])]
    pallas_call x2, Pallas kernels: 20 us -> 14.8 us  [the longest x1 8.37 us: attend(): pl.pallas_call(functools.partial(attend_kernel, cuts=cuts), in_specs=[pl....]
    all_to_all x0 -> x1, starting transfers between devices: none -> 3.55 us  [local(): lax.all_to_all(jnp.concatenate([w_blocks, w_blocks], axis=0), CTX_CHIPS,...]
    ppermute x2, starting transfers between devices: 4.55 us -> 2.38 us  [down(): return lax.ppermute(a, 'x', [(i, (i + 3) % 4) for i in range(4)])]
    ppermute x5 -> x6, starting transfers between devices: 13.4 us -> 14.2 us  [swap(): return lax.ppermute(mine, 'core', SWAP)]
  transfers between devices with their start and end apart: 11 -> 13, of which waited for: 8 -> 10; matrix products, arithmetic and copies ran while one was open for 4% -> 2% of each run, Pallas kernels for 0% -> 4%
where the time goes in v11:
time: 205 us; the launch traced here: 203 us
  waiting for transfers between devices  68.8 us (34%)
  blocking collectives  63 us (31%)
  starting transfers between devices  36.4 us (18%)
  Pallas kernels  20.6 us (10%)
  local copies, waits for them, and re-layouts  10.5 us (5%)
  other arithmetic  2.71 us (1%)
    all_to_all x1, blocking collectives, exchange(): lax.all_to_all(units, CHIPS, split_axis=0, concat_axis=0, tiled=True)  40.6 us
    all_to_all x1, waiting for transfers between devices, exchange(): lax.all_to_all(units, CHIPS, split_axis=0, concat_axis=0, tiled=True)  30 us
    all_to_all x1, blocking collectives, local(): lax.all_to_all(jnp.broadcast_to(latents[None], (8,) + latents.shape), CTX...  22.4 us
    all_to_all x1, waiting for transfers between devices, local(): lax.all_to_all(jnp.concatenate([w_blocks, w_blocks], axis=0), CTX_CHIPS,...  14.5 us
    ppermute x6, starting transfers between devices, swap(): return lax.ppermute(mine, 'core', SWAP)  14.2 us
    all_to_all x1, waiting for transfers between devices, local(): lax.all_to_all(attn, EP + ('x',), split_axis=0, concat_axis=0, tiled=True)  9.92 us
    ppermute x2, waiting for transfers between devices, down(): return lax.ppermute(a, 'x', [(i, (i + 3) % 4) for i in range(4)])  8.86 us
    pallas_call x1, Pallas kernels, attend(): pl.pallas_call(functools.partial(attend_kernel, cuts=cuts), in_specs=[pl....  8.37 us
  transfers between devices with their start and end apart: 13, of which 10 were waited for; matrix products, arithmetic and copies ran while one was open for 2% of the time, Pallas kernels for 4%

profile of v11, /device:TPU:1, one launch (start us, length us, event | category | flops | bytes accessed | tf_op | source)
XLA Modules:
  0.0 202.9 jit_solution(14174610874354469756)
XLA Ops:
  0.6 1.1 broadcast_in_dim.32
  1.7 22.4 %all_to_all.25.near_ref = bf16[8,576,128]{2,1,0:T(8,128)(2,1)S(1)} all-to-all(bf16[8,576,128]{2,1,0:T(8,128)(2,1)S(1)} %broadcast_in_dim.32), channel_id=1, replica_groups=mesh['z_lo'=2,'x'=4,'core'=2,'z_hi'=2,'y'=4] {'z_lo','x'}, dimensions={0} | all-to-all | bytes 2359296 | tf_op jit(solution)/shard_map/all_to_all | solution.py:319
  24.1 1.7 collective-permute-start
  25.8 1.6 reshape.139
  27.4 0.2 copy.49
  27.6 1.0 pad_maximum_fusion
  28.6 3.6 %all-to-all-start.1 = ((bf16[8,448,128]{2,1,0:T(8,128)(2,1)}), bf16[8,448,128]{2,1,0:T(8,128)(2,1)S(1)}, u32[]{:S(2)}, u32[]{:S(2)}) async-start(bf16[8,448,128]{2,1,0:T(8,128)(2,1)} %pad_maximum_fusion), calls=%async_computation.1 | async-start | bytes 1835008 | tf_op jit(solution)/shard_map/all_to_all | solution.py:325
  32.2 14.5 %all-to-all-done.1.near_ref = bf16[8,448,128]{2,1,0:T(8,128)(2,1)S(1)} async-done(((bf16[8,448,128]{2,1,0:T(8,128)(2,1)}), bf16[8,448,128]{2,1,0:T(8,128)(2,1)S(1)}, u32[]{:S(2)}, u32[]{:S(2)}) %all-to-all-start.1) | async-done | bytes 917536 | tf_op jit(solution)/shard_map/all_to_all | solution.py:325
  46.6 0.7 collective-permute-start.5
  47.3 0.1 pad_add_fusion.1.ids_ref
  47.4 1.6 copy-done.4
  49.0 1.0 copy-done.5
  50.0 8.4 %shard_map.122.own_ref = bf16[128,1024]{1,0:T(8,128)(2,1)S(1)} custom-call(s32[3]{0:T(128)S(1)} %pad_add_fusion.1.ids_ref, bf16[128,1536]{1,0:T(8,128)(2,1)S(1)} %copy-done.5, bf16[512,2048]{1,0:T(8,128)(2,1)S(1)} %copy-done.4, bf16[8,576,128]{2,1,0:T(8,128)(2,1)S(1)} %all_to_all.25.near_ref, bf16[8,576,128]{2,1,0:T(8,128)(2,1)S(1)} %collective-permute-done.far_ref), custom_call_target="tpu_custom_call" | custom-call | flops 4563402752 | bytes 8000000 | tf_op jit(solution)/shard_map/pallas_call | solution.py:90
  58.4 0.6 collective-permute-start.2
  59.0 1.0 collective-permute-start.1
  59.9 6.5 %collective-permute-done.2.after_ref = bf16[128,1024]{1,0:T(8,128)(2,1)S(1)} collective-permute-done((bf16[128,1024]{1,0:T(8,128)(2,1)S(1)}, bf16[128,1024]{1,0:T(8,128)(2,1)S(1)}, u32[]{:S(2)}, u32[]{:S(2)}) %collective-permute-start.2) | collective-permute-done | bytes 262176 | tf_op jit(solution)/shard_map/ppermute | solution.py:276
  66.4 1.8 collective-permute-start.4
  68.2 0.0 copy-start.10
  68.2 0.1 collective-permute-start.3
  68.3 2.4 %collective-permute-done.4.right_ref = bf16[128,512]{1,0:T(8,128)(2,1)S(1)} collective-permute-done((bf16[128,512]{1,0:T(8,128)(2,1)S(1)}, bf16[128,512]{1,0:T(8,128)(2,1)S(1)}, u32[]{:S(2)}, u32[]{:S(2)}) %collective-permute-start.4) | collective-permute-done | bytes 131104 | tf_op jit(solution)/shard_map/ppermute | solution.py:276
  70.7 2.6 %collective-permute-done.3.left_ref = bf16[128,512]{1,0:T(8,128)(2,1)S(1)} collective-permute-done((bf16[128,512]{1,0:T(8,128)(2,1)S(1)}, bf16[128,512]{1,0:T(8,128)(2,1)S(1)}, u32[]{:S(2)}, u32[]{:S(2)}) %collective-permute-start.3) | collective-permute-done | bytes 131104 | tf_op jit(solution)/shard_map/ppermute | solution.py:272
  73.3 3.0 %shard_map.123 = bf16[32,16,896]{2,1,0:T(8,128)(2,1)} custom-call(s32[3]{0:T(128)S(1)} %pad_add_fusion.1.ids_ref, bf16[128,1024]{1,0:T(8,128)(2,1)S(1)} %shard_map.122.own_ref, bf16[128,1024]{1,0:T(8,128)(2,1)S(1)} %collective-permute-done.1.before_ref, bf16[128,1024]{1,0:T(8,128)(2,1)S(1)} %collective-permute-done.2.after_ref, ...), custom_call_target="tpu_custom_call" | custom-call | flops 939524096 | bytes 1835008 | tf_op jit(solution)/shard_map/pallas_call | solution.py:254
  76.4 7.8 %all-to-all-start.2 = ((bf16[32,16,896]{2,1,0:T(8,128)(2,1)}), bf16[32,16,896]{2,1,0:T(8,128)(2,1)S(1)}, u32[]{:S(2)}, u32[]{:S(2)}) async-start(bf16[32,16,896]{2,1,0:T(8,128)(2,1)} %shard_map.123), calls=%async_computation.2 | async-start | bytes 1835008 | tf_op jit(solution)/shard_map/all_to_all | solution.py:335
  84.2 2.7 %collective-permute-start.6 = (s32[16,8]{0,1:T(8,128)S(1)}, s32[16,8]{0,1:T(8,128)S(1)}, u32[]{:S(2)}, u32[]{:S(2)}) collective-permute-start(s32[16,8]{0,1:T(8,128)S(1)} %copy-done.10), channel_id=1, source_target_pairs={{0,8},{8,0},{1,9},{9,1},{2,10},{10,2},{3,11},{11,3},{4,12},{12,4},... | collective-permute-start | bytes 1544 | tf_op jit(solution)/shard_map/ppermute | solution.py:268
  86.9 0.1 and.46
  87.0 0.1 and.47
  87.0 0.7 collective-permute-done.6
  87.7 0.1 copy.51
  87.8 0.1 fusion.5
  87.9 0.1 copy.52
  88.0 0.1 copy.54
  88.1 0.1 copy.53
  88.3 9.9 %all-to-all-done.2 = bf16[32,16,896]{2,1,0:T(8,128)(2,1)S(1)} async-done(((bf16[32,16,896]{2,1,0:T(8,128)(2,1)}), bf16[32,16,896]{2,1,0:T(8,128)(2,1)S(1)}, u32[]{:S(2)}, u32[]{:S(2)}) %all-to-all-start.2) | async-done | bytes 917536 | tf_op jit(solution)/shard_map/all_to_all | solution.py:335
  98.2 0.1 convert_reduce_fusion
  98.3 0.2 fusion
  98.5 0.1 fusion.2
  98.6 3.7 %collective-permute-start.8 = (bf16[16,3584]{1,0:T(8,128)(2,1)S(1)}, bf16[16,3584]{1,0:T(8,128)(2,1)S(1)}, u32[]{:S(2)}, u32[]{:S(2)}) collective-permute-start(bf16[16,3584]{1,0:T(8,128)(2,1)S(1)} %fusion.2), channel_id=1, source_target_pairs={{0,8},{8,0},{1,9},{9,1},{2,10},{10,2},{3,11},{11,3},{4,12},{12,4},... | collective-permute-start | bytes 344072 | tf_op jit(solution)/shard_map/ppermute | solution.py:268
  102.4 0.1 bitcast_and_fusion
  102.4 0.1 copy.55
  102.6 0.1 broadcast_in_dim.33
  102.7 0.1 reshape.143
  102.8 0.5 collective-permute-done.8
  103.3 0.0 copy-start.2
  103.3 1.4 shard_map.124
  104.7 40.6 %all_to_all.26 = bf16[64,3,2,3584]{3,2,1,0:T(2,128)(2,1)S(1)} all-to-all(bf16[64,3,2,3584]{3,2,1,0:T(2,128)(2,1)S(1)} %bitcast.40), channel_id=1, replica_groups=mesh['z_lo'=2,'x'=4,'core'=2,'z_hi'=2,'y'=4] {'z_lo','x','z_hi','y'}, dimensions={0} | all-to-all | bytes 5505024 | tf_op jit(solution)/shard_map/all_to_all | solution.py:346
  145.3 2.0 %copy-done.3 = bf16[1,512,3584]{2,1,0:T(8,128)(2,1)S(1)} copy-done((bf16[1,512,3584]{2,1,0:T(8,128)(2,1)S(1)}, bf16[1,512,3584]{2,1,0:T(8,128)(2,1)}, u32[]{:S(2)}) %copy-start.3) | copy-done | bytes 3670040
  147.4 6.4 %shard_map.125 = bf16[192,2,3584]{2,1,0:T(2,128)(2,1)S(1)} custom-call(bf16[192,2,3584]{2,1,0:T(2,128)(2,1)S(1)} %bitcast.42, bf16[3584,512]{1,0:T(8,128)(2,1)S(1)} %bitcast.43, bf16[3584,512]{1,0:T(8,128)(2,1)S(1)} %bitcast.44, bf16[512,3584]{1,0:T(8,128)(2,1)S(1)} %bitcast.45), custom_call_target="tpu_custom_call" | custom-call | flops 4227858432 | bytes 17000000 | tf_op jit(solution)/shard_map/pallas_call | solution.py:145
  153.8 1.5 copy-done
  155.4 7.5 %all-to-all-start.4 = ((bf16[64,3,2,3584]{3,2,1,0:T(2,128)(2,1)}), bf16[64,3,2,3584]{3,2,1,0:T(2,128)(2,1)S(1)}, u32[]{:S(2)}, u32[]{:S(2)}) async-start(bf16[64,3,2,3584]{3,2,1,0:T(2,128)(2,1)} %bitcast.41), calls=%async_computation.4 | async-start | bytes 5505024 | tf_op jit(solution)/shard_map/all_to_all | solution.py:346
  162.9 1.6 collective-permute-start.7
  164.4 0.1 copy.60
  164.6 0.7 collective-permute-done.7
  165.3 0.1 copy.56
  165.3 0.1 select_reduce_fusion
  165.5 0.1 copy.57
  165.6 0.1 copy.58
  165.7 0.1 copy.59
  165.8 0.1 broadcast_in_dim.65
  165.8 0.1 copy.61
  166.0 30.0 %all-to-all-done.4 = bf16[64,3,2,3584]{3,2,1,0:T(2,128)(2,1)S(1)} async-done(((bf16[64,3,2,3584]{3,2,1,0:T(2,128)(2,1)}), bf16[64,3,2,3584]{3,2,1,0:T(2,128)(2,1)S(1)}, u32[]{:S(2)}, u32[]{:S(2)}) %all-to-all-start.4) | async-done | bytes 2752544 | tf_op jit(solution)/shard_map/all_to_all | solution.py:346
  195.9 1.4 shard_map.126
  197.3 3.8 %collective-permute-start.9 = (f32[16,3584]{1,0:T(8,128)S(1)}, f32[16,3584]{1,0:T(8,128)S(1)}, u32[]{:S(2)}, u32[]{:S(2)}) collective-permute-start(f32[16,3584]{1,0:T(8,128)S(1)} %get-tuple-element.5), channel_id=1, source_target_pairs={{0,8},{8,0},{1,9},{9,1},{2,10},{10,2},{3,11},{11,3},{4,12},{12,4},... | collective-permute-start | bytes 688136 | tf_op jit(solution)/shard_map/ppermute | solution.py:268
  201.1 1.1 collective-permute-done.9
  202.2 0.7 fusion.4
  (40 shorter events, 0.3 us)
Async XLA Ops:
  24.1 23.3 %collective-permute-start = (bf16[8,576,128]{2,1,0:T(8,128)(2,1)S(1)}, bf16[8,576,128]{2,1,0:T(8,128)(2,1)S(1)}, u32[]{:S(2)}, u32[]{:S(2)}) collective-permute-start(bf16[8,576,128]{2,1,0:T(8,128)(2,1)S(1)} %all_to_all.25.near_ref), channel_id=1, source_target_pairs={{0,8},{8,0},{1,9},{9,1},{2,10},{10,2},{3,11},{11,3},{4,12},{12,4},... | collective-permute-start | bytes 3538952 | tf_op jit(solution)/shard_map/ppermute | solution.py:268
  28.6 18.0 %all-to-all-start.1 = ((bf16[8,448,128]{2,1,0:T(8,128)(2,1)}), bf16[8,448,128]{2,1,0:T(8,128)(2,1)S(1)}, u32[]{:S(2)}, u32[]{:S(2)}) async-start(bf16[8,448,128]{2,1,0:T(8,128)(2,1)} %pad_maximum_fusion), calls=%async_computation.1 | async-start | bytes 1835008 | tf_op jit(solution)/shard_map/all_to_all | solution.py:325
  46.6 21.7 %collective-permute-start.5 = (bf16[8,448,128]{2,1,0:T(8,128)(2,1)S(1)}, bf16[8,448,128]{2,1,0:T(8,128)(2,1)S(1)}, u32[]{:S(2)}, u32[]{:S(2)}) collective-permute-start(bf16[8,448,128]{2,1,0:T(8,128)(2,1)S(1)} %all-to-all-done.1.near_ref), channel_id=1, source_target_pairs={{0,8},{8,0},{1,9},{9,1},{2,10},{10,2},{3,11},{11,3},{4,12},{12,4},... | collective-permute-start | bytes 2752520 | tf_op jit(solution)/shard_map/ppermute | solution.py:268
  47.4 1.6 copy-start.4
  49.0 1.0 copy-start.5
  58.4 8.0 %collective-permute-start.2 = (bf16[128,1024]{1,0:T(8,128)(2,1)S(1)}, bf16[128,1024]{1,0:T(8,128)(2,1)S(1)}, u32[]{:S(2)}, u32[]{:S(2)}) collective-permute-start(bf16[128,1024]{1,0:T(8,128)(2,1)S(1)} %shard_map.122.own_ref), channel_id=1, source_target_pairs={{0,48},{16,0},{32,16},{48,32},{1,49},{17,1},{33,17},{49,33},{2,50}... | collective-permute-start | bytes 786440 | tf_op jit(solution)/shard_map/ppermute | solution.py:276
  59.0 9.2 %collective-permute-start.1 = (bf16[128,1024]{1,0:T(8,128)(2,1)S(1)}, bf16[128,1024]{1,0:T(8,128)(2,1)S(1)}, u32[]{:S(2)}, u32[]{:S(2)}) collective-permute-start(bf16[128,1024]{1,0:T(8,128)(2,1)S(1)} %shard_map.122.own_ref), channel_id=1, source_target_pairs={{0,16},{16,32},{32,48},{48,0},{1,17},{17,33},{33,49},{49,1},{2,18}... | collective-permute-start | bytes 786440 | tf_op jit(solution)/shard_map/ppermute | solution.py:272
  66.4 4.3 %collective-permute-start.4 = (bf16[128,512]{1,0:T(8,128)(2,1)S(1)}, bf16[128,512]{1,0:T(8,128)(2,1)S(1)}, u32[]{:S(2)}, u32[]{:S(2)}) collective-permute-start(bf16[128,512]{1,0:T(8,128)(2,1)S(1)} %slice.26), channel_id=1, source_target_pairs={{0,48},{16,0},{32,16},{48,32},{1,49},{17,1},{33,17},{49,33},{2,50}... | collective-permute-start | bytes 393224 | tf_op jit(solution)/shard_map/ppermute | solution.py:276
  68.2 15.9 %copy-start.10 = (s32[16,8]{0,1:T(8,128)S(1)}, s32[16,8]{0,1:T(8,128)}, u32[]{:S(2)}) copy-start(s32[16,8]{0,1:T(8,128)} %param.17) | copy-start | bytes 1540
  68.2 5.1 %collective-permute-start.3 = (bf16[128,512]{1,0:T(8,128)(2,1)S(1)}, bf16[128,512]{1,0:T(8,128)(2,1)S(1)}, u32[]{:S(2)}, u32[]{:S(2)}) collective-permute-start(bf16[128,512]{1,0:T(8,128)(2,1)S(1)} %slice.25), channel_id=1, source_target_pairs={{0,16},{16,32},{32,48},{48,0},{1,17},{17,33},{33,49},{49,1},{2,18}... | collective-permute-start | bytes 393224 | tf_op jit(solution)/shard_map/ppermute | solution.py:272
  76.4 22.0 %copy-start.7 = (bf16[16,3584]{1,0:T(8,128)(2,1)S(1)}, bf16[16,3584]{1,0:T(8,128)(2,1)}, u32[]{:S(2)}) copy-start(bf16[16,3584]{1,0:T(8,128)(2,1)} %param.15) | copy-start | bytes 344068
  76.4 22.1 %copy-start.9 = (f32[3584]{0:T(1024)S(1)}, f32[3584]{0:T(1024)}, u32[]{:S(2)}) copy-start(f32[3584]{0:T(1024)} %param.16) | copy-start | bytes 43012
  76.4 21.8 %all-to-all-start.2 = ((bf16[32,16,896]{2,1,0:T(8,128)(2,1)}), bf16[32,16,896]{2,1,0:T(8,128)(2,1)S(1)}, u32[]{:S(2)}, u32[]{:S(2)}) async-start(bf16[32,16,896]{2,1,0:T(8,128)(2,1)} %shard_map.123), calls=%async_computation.2 | async-start | bytes 1835008 | tf_op jit(solution)/shard_map/all_to_all | solution.py:335
  84.2 3.5 %collective-permute-start.6 = (s32[16,8]{0,1:T(8,128)S(1)}, s32[16,8]{0,1:T(8,128)S(1)}, u32[]{:S(2)}, u32[]{:S(2)}) collective-permute-start(s32[16,8]{0,1:T(8,128)S(1)} %copy-done.10), channel_id=1, source_target_pairs={{0,8},{8,0},{1,9},{9,1},{2,10},{10,2},{3,11},{11,3},{4,12},{12,4},... | collective-permute-start | bytes 1544 | tf_op jit(solution)/shard_map/ppermute | solution.py:268
  98.5 103.7 %copy-start.6 = (bf16[16,3584]{1,0:T(8,128)(2,1)}, bf16[16,3584]{1,0:T(8,128)(2,1)S(1)}, u32[]{:S(2)}) copy-start(bf16[16,3584]{1,0:T(8,128)(2,1)S(1)} %get-tuple-element.7) | copy-start | bytes 344068
  98.6 4.7 %collective-permute-start.8 = (bf16[16,3584]{1,0:T(8,128)(2,1)S(1)}, bf16[16,3584]{1,0:T(8,128)(2,1)S(1)}, u32[]{:S(2)}, u32[]{:S(2)}) collective-permute-start(bf16[16,3584]{1,0:T(8,128)(2,1)S(1)} %fusion.2), channel_id=1, source_target_pairs={{0,8},{8,0},{1,9},{9,1},{2,10},{10,2},{3,11},{11,3},{4,12},{12,4},... | collective-permute-start | bytes 344072 | tf_op jit(solution)/shard_map/ppermute | solution.py:268
  103.3 42.0 %copy-start.2 = (bf16[1,3584,512]{2,1,0:T(8,128)(2,1)S(1)}, bf16[1,3584,512]{2,1,0:T(8,128)(2,1)}, u32[]{:S(2)}) copy-start(bf16[1,3584,512]{2,1,0:T(8,128)(2,1)} %param.20) | copy-start | bytes 11010052
  104.7 40.6 %copy-start.1 = (bf16[1,3584,512]{2,1,0:T(8,128)(2,1)S(1)}, bf16[1,3584,512]{2,1,0:T(8,128)(2,1)}, u32[]{:S(2)}) copy-start(bf16[1,3584,512]{2,1,0:T(8,128)(2,1)} %param.19) | copy-start | bytes 11010052
  145.3 2.0 %copy-start.3 = (bf16[1,512,3584]{2,1,0:T(8,128)(2,1)S(1)}, bf16[1,512,3584]{2,1,0:T(8,128)(2,1)}, u32[]{:S(2)}) copy-start(bf16[1,512,3584]{2,1,0:T(8,128)(2,1)} %param.21) | copy-start | bytes 11010052
  153.8 1.5 copy-start
  155.4 7.5 %copy-start.8 = (s32[16,8]{0,1:T(8,128)S(1)}, s32[16,8]{0,1:T(8,128)}, u32[]{:S(2)}) copy-start(s32[16,8]{0,1:T(8,128)} %param.18) | copy-start | bytes 1540
  155.4 40.6 %all-to-all-start.4 = ((bf16[64,3,2,3584]{3,2,1,0:T(2,128)(2,1)}), bf16[64,3,2,3584]{3,2,1,0:T(2,128)(2,1)S(1)}, u32[]{:S(2)}, u32[]{:S(2)}) async-start(bf16[64,3,2,3584]{3,2,1,0:T(2,128)(2,1)} %bitcast.41), calls=%async_computation.4 | async-start | bytes 5505024 | tf_op jit(solution)/shard_map/all_to_all | solution.py:346
  162.9 2.4 %collective-permute-start.7 = (f32[16,8]{0,1:T(8,128)S(1)}, f32[16,8]{0,1:T(8,128)S(1)}, u32[]{:S(2)}, u32[]{:S(2)}) collective-permute-start(f32[16,8]{0,1:T(8,128)S(1)} %convert_divide_fusion), channel_id=1, source_target_pairs={{0,8},{8,0},{1,9},{9,1},{2,10},{10,2},{3,11},{11,3},{4,12},{12,4},... | collective-permute-start | bytes 1544 | tf_op jit(solution)/shard_map/ppermute | solution.py:268
  197.3 4.9 %collective-permute-start.9 = (f32[16,3584]{1,0:T(8,128)S(1)}, f32[16,3584]{1,0:T(8,128)S(1)}, u32[]{:S(2)}, u32[]{:S(2)}) collective-permute-start(f32[16,3584]{1,0:T(8,128)S(1)} %get-tuple-element.5), channel_id=1, source_target_pairs={{0,8},{8,0},{1,9},{9,1},{2,10},{10,2},{3,11},{11,3},{4,12},{12,4},... | collective-permute-start | bytes 688136 | tf_op jit(solution)/shard_map/ppermute | solution.py:268

commit v12 on v11

--- a/solution.py
+++ b/solution.py
@@ -98,7 +98,7 @@
             pltpu.VMEM((m, depth), BF),
             pltpu.VMEM((m, KV_RANK), F32),
         ],
-        compiler_params=pltpu.CompilerParams(vmem_limit_bytes=36 * 2**20),
+        compiler_params=pltpu.CompilerParams(vmem_limit_bytes=24 * 2**20),
         cost_estimate=pl.CostEstimate(
             flops=2 * m * keys * (depth + KV_RANK), bytes_accessed=8_000_000, transcendentals=m * keys
         ),
@@ -156,7 +156,7 @@
             pltpu.SemaphoreType.DMA((first,)),
             pltpu.SemaphoreType.DMA((last,)),
         ],
-        compiler_params=pltpu.CompilerParams(vmem_limit_bytes=32 * 2**20),
+        compiler_params=pltpu.CompilerParams(vmem_limit_bytes=20 * 2**20),
         cost_estimate=pl.CostEstimate(
             flops=6 * m * width * hidden, bytes_accessed=17_000_000, transcendentals=m * hidden
         ),
@@ -321,13 +321,12 @@
     )
     far = swap(near)
     w_blocks = w_out.reshape(-1, group, columns // 128, 128).transpose(1, 2, 0, 3).reshape(group, -1, 128)
-    w_blocks, _ = lax.optimization_barrier((w_blocks, near[0, :8]))
-    w_near = lax.all_to_all(
-        jnp.concatenate([w_blocks, w_blocks], axis=0), CTX_CHIPS, split_axis=0, concat_axis=0, tiled=True
-    )
-    w_far = swap(w_near)
+    w_blocks, _ = lax.optimization_barrier((jnp.concatenate([w_blocks, w_blocks], axis=0), near[0, :8]))
+    w_near = lax.all_to_all(w_blocks, CTX_CHIPS, split_axis=0, concat_axis=0, tiled=True)
     ids = jnp.stack([lax.axis_index(CTX), core, lax.axis_index("x")]).astype(jnp.int32)
     own = attend(ids, queries, w_kv, near, far, 4)
+    own, w_near = lax.optimization_barrier((own, w_near))
+    w_far = swap(w_near)
     before, after = up(own), down(own)
     half = own.shape[1] // 2
     left, right = up(before[:, :half]), down(after[:, half:])

time: 205 us -> 194 us (0.946)
  waiting for transfers between devices: 68.8 us -> 57.7 us
    all_to_all x1, waiting for transfers between devices: 14.5 us -> 3.47 us  [local(): lax.all_to_all(w_blocks, CTX_CHIPS, split_axis=0, concat_axis=0, tiled=True)]
  transfers between devices with their start and end apart: 13 -> 13, of which waited for: 10 -> 10; matrix products, arithmetic and copies ran while one was open for 2% -> 3% of each run, Pallas kernels for 4% -> 4%
where the time goes in v12:
time: 194 us; the launch traced here: 192 us
  blocking collectives  63 us (32%)
  waiting for transfers between devices  57.7 us (30%)
  starting transfers between devices  36.3 us (19%)
  Pallas kernels  20.5 us (11%)
  local copies, waits for them, and re-layouts  10.5 us (5%)
  other arithmetic  2.71 us (1%)
    all_to_all x1, blocking collectives, exchange(): lax.all_to_all(units, CHIPS, split_axis=0, concat_axis=0, tiled=True)  40.7 us
    all_to_all x1, waiting for transfers between devices, exchange(): lax.all_to_all(units, CHIPS, split_axis=0, concat_axis=0, tiled=True)  29.9 us
    all_to_all x1, blocking collectives, local(): lax.all_to_all(jnp.broadcast_to(latents[None], (8,) + latents.shape), CTX...  22.4 us
    ppermute x6, starting transfers between devices, swap(): return lax.ppermute(mine, 'core', SWAP)  14.2 us
    all_to_all x1, waiting for transfers between devices, local(): lax.all_to_all(attn, EP + ('x',), split_axis=0, concat_axis=0, tiled=True)  9.91 us
    ppermute x2, waiting for transfers between devices, down(): return lax.ppermute(a, 'x', [(i, (i + 3) % 4) for i in range(4)])  8.88 us
    pallas_call x1, Pallas kernels, attend(): pl.pallas_call(functools.partial(attend_kernel, cuts=cuts), in_specs=[pl....  8.32 us
    all_to_all x1, starting transfers between devices, local(): lax.all_to_all(attn, EP + ('x',), split_axis=0, concat_axis=0, tiled=True)  7.77 us
  transfers between devices with their start and end apart: 13, of which 10 were waited for; matrix products, arithmetic and copies ran while one was open for 3% of the time, Pallas kernels for 4%

profile of v12, /device:TPU:1, one launch (start us, length us, event | category | flops | bytes accessed | tf_op | source)
XLA Modules:
  0.0 191.8 jit_solution(16936096676884951679)
XLA Ops:
  0.6 1.1 broadcast_in_dim.32
  1.7 22.4 %all_to_all.25.near_ref = bf16[8,576,128]{2,1,0:T(8,128)(2,1)S(1)} all-to-all(bf16[8,576,128]{2,1,0:T(8,128)(2,1)S(1)} %broadcast_in_dim.32), channel_id=1, replica_groups=mesh['z_lo'=2,'x'=4,'core'=2,'z_hi'=2,'y'=4] {'z_lo','x'}, dimensions={0} | all-to-all | bytes 2359296 | tf_op jit(solution)/shard_map/all_to_all | solution.py:319
  24.1 1.7 collective-permute-start
  25.8 1.6 reshape.139
  27.4 0.2 copy.49
  27.6 1.0 pad_maximum_fusion
  28.6 3.6 %all-to-all-start.1 = ((bf16[8,448,128]{2,1,0:T(8,128)(2,1)}), bf16[8,448,128]{2,1,0:T(8,128)(2,1)S(1)}, u32[]{:S(2)}, u32[]{:S(2)}) async-start(bf16[8,448,128]{2,1,0:T(8,128)(2,1)} %pad_maximum_fusion), calls=%async_computation.1 | async-start | bytes 1835008 | tf_op jit(solution)/shard_map/all_to_all | solution.py:325
  32.2 0.1 pad_add_fusion.1.ids_ref
  32.2 1.6 copy-done.4
  33.8 1.0 copy-done.5
  34.8 8.3 %shard_map.122.own_ref = bf16[128,1024]{1,0:T(8,128)(2,1)S(1)} custom-call(s32[3]{0:T(128)S(1)} %pad_add_fusion.1.ids_ref, bf16[128,1536]{1,0:T(8,128)(2,1)S(1)} %copy-done.5, bf16[512,2048]{1,0:T(8,128)(2,1)S(1)} %copy-done.4, bf16[8,576,128]{2,1,0:T(8,128)(2,1)S(1)} %all_to_all.25.near_ref, bf16[8,576,128]{2,1,0:T(8,128)(2,1)S(1)} %collective-permute-done.far_ref), custom_call_target="tpu_custom_call" | custom-call | flops 4563402752 | bytes 8000000 | tf_op jit(solution)/shard_map/pallas_call | solution.py:90
  43.2 3.5 %all-to-all-done.1.near_ref = bf16[8,448,128]{2,1,0:T(8,128)(2,1)S(1)} async-done(((bf16[8,448,128]{2,1,0:T(8,128)(2,1)}), bf16[8,448,128]{2,1,0:T(8,128)(2,1)S(1)}, u32[]{:S(2)}, u32[]{:S(2)}) %all-to-all-start.1) | async-done | bytes 917536 | tf_op jit(solution)/shard_map/all_to_all | solution.py:325
  46.6 0.7 collective-permute-start.5
  47.3 0.5 collective-permute-start.2
  47.8 1.0 collective-permute-start.1
  48.8 6.5 %collective-permute-done.2.after_ref = bf16[128,1024]{1,0:T(8,128)(2,1)S(1)} collective-permute-done((bf16[128,1024]{1,0:T(8,128)(2,1)S(1)}, bf16[128,1024]{1,0:T(8,128)(2,1)S(1)}, u32[]{:S(2)}, u32[]{:S(2)}) %collective-permute-start.2) | collective-permute-done | bytes 262176 | tf_op jit(solution)/shard_map/ppermute | solution.py:276
  55.3 1.8 collective-permute-start.4
  57.1 0.0 copy-start.10
  57.1 0.1 collective-permute-start.3
  57.2 2.4 %collective-permute-done.4.right_ref = bf16[128,512]{1,0:T(8,128)(2,1)S(1)} collective-permute-done((bf16[128,512]{1,0:T(8,128)(2,1)S(1)}, bf16[128,512]{1,0:T(8,128)(2,1)S(1)}, u32[]{:S(2)}, u32[]{:S(2)}) %collective-permute-start.4) | collective-permute-done | bytes 131104 | tf_op jit(solution)/shard_map/ppermute | solution.py:276
  59.6 2.6 %collective-permute-done.3.left_ref = bf16[128,512]{1,0:T(8,128)(2,1)S(1)} collective-permute-done((bf16[128,512]{1,0:T(8,128)(2,1)S(1)}, bf16[128,512]{1,0:T(8,128)(2,1)S(1)}, u32[]{:S(2)}, u32[]{:S(2)}) %collective-permute-start.3) | collective-permute-done | bytes 131104 | tf_op jit(solution)/shard_map/ppermute | solution.py:272
  62.2 3.0 %shard_map.123 = bf16[32,16,896]{2,1,0:T(8,128)(2,1)} custom-call(s32[3]{0:T(128)S(1)} %pad_add_fusion.1.ids_ref, bf16[128,1024]{1,0:T(8,128)(2,1)S(1)} %shard_map.122.own_ref, bf16[128,1024]{1,0:T(8,128)(2,1)S(1)} %collective-permute-done.1.before_ref, bf16[128,1024]{1,0:T(8,128)(2,1)S(1)} %collective-permute-done.2.after_ref, ...), custom_call_target="tpu_custom_call" | custom-call | flops 939524096 | bytes 1835008 | tf_op jit(solution)/shard_map/pallas_call | solution.py:254
  65.3 7.8 %all-to-all-start.2 = ((bf16[32,16,896]{2,1,0:T(8,128)(2,1)}), bf16[32,16,896]{2,1,0:T(8,128)(2,1)S(1)}, u32[]{:S(2)}, u32[]{:S(2)}) async-start(bf16[32,16,896]{2,1,0:T(8,128)(2,1)} %shard_map.123), calls=%async_computation.2 | async-start | bytes 1835008 | tf_op jit(solution)/shard_map/all_to_all | solution.py:334
  73.0 2.7 %collective-permute-start.6 = (s32[16,8]{0,1:T(8,128)S(1)}, s32[16,8]{0,1:T(8,128)S(1)}, u32[]{:S(2)}, u32[]{:S(2)}) collective-permute-start(s32[16,8]{0,1:T(8,128)S(1)} %copy-done.10), channel_id=1, source_target_pairs={{0,8},{8,0},{1,9},{9,1},{2,10},{10,2},{3,11},{11,3},{4,12},{12,4},... | collective-permute-start | bytes 1544 | tf_op jit(solution)/shard_map/ppermute | solution.py:268
  75.8 0.1 and.46
  75.8 0.1 and.47
  75.9 0.7 collective-permute-done.6
  76.6 0.1 copy.51
  76.7 0.1 fusion.5
  76.8 0.1 copy.52
  76.9 0.1 copy.54
  77.0 0.1 copy.53
  77.1 9.9 %all-to-all-done.2 = bf16[32,16,896]{2,1,0:T(8,128)(2,1)S(1)} async-done(((bf16[32,16,896]{2,1,0:T(8,128)(2,1)}), bf16[32,16,896]{2,1,0:T(8,128)(2,1)S(1)}, u32[]{:S(2)}, u32[]{:S(2)}) %all-to-all-start.2) | async-done | bytes 917536 | tf_op jit(solution)/shard_map/all_to_all | solution.py:334
  87.1 0.1 convert_reduce_fusion
  87.2 0.2 fusion
  87.4 0.1 fusion.2
  87.5 3.7 %collective-permute-start.8 = (bf16[16,3584]{1,0:T(8,128)(2,1)S(1)}, bf16[16,3584]{1,0:T(8,128)(2,1)S(1)}, u32[]{:S(2)}, u32[]{:S(2)}) collective-permute-start(bf16[16,3584]{1,0:T(8,128)(2,1)S(1)} %fusion.2), channel_id=1, source_target_pairs={{0,8},{8,0},{1,9},{9,1},{2,10},{10,2},{3,11},{11,3},{4,12},{12,4},... | collective-permute-start | bytes 344072 | tf_op jit(solution)/shard_map/ppermute | solution.py:268
  91.2 0.1 bitcast_and_fusion
  91.3 0.1 copy.55
  91.5 0.1 broadcast_in_dim.33
  91.6 0.1 reshape.143
  91.7 0.5 collective-permute-done.8
  92.2 0.0 copy-start.2
  92.2 1.3 shard_map.124
  93.6 40.7 %all_to_all.26 = bf16[64,3,2,3584]{3,2,1,0:T(2,128)(2,1)S(1)} all-to-all(bf16[64,3,2,3584]{3,2,1,0:T(2,128)(2,1)S(1)} %bitcast.40), channel_id=1, replica_groups=mesh['z_lo'=2,'x'=4,'core'=2,'z_hi'=2,'y'=4] {'z_lo','x','z_hi','y'}, dimensions={0} | all-to-all | bytes 5505024 | tf_op jit(solution)/shard_map/all_to_all | solution.py:345
  134.3 2.0 %copy-done.3 = bf16[1,512,3584]{2,1,0:T(8,128)(2,1)S(1)} copy-done((bf16[1,512,3584]{2,1,0:T(8,128)(2,1)S(1)}, bf16[1,512,3584]{2,1,0:T(8,128)(2,1)}, u32[]{:S(2)}) %copy-start.3) | copy-done | bytes 3670040
  136.3 6.4 %shard_map.125 = bf16[192,2,3584]{2,1,0:T(2,128)(2,1)S(1)} custom-call(bf16[192,2,3584]{2,1,0:T(2,128)(2,1)S(1)} %bitcast.42, bf16[3584,512]{1,0:T(8,128)(2,1)S(1)} %bitcast.43, bf16[3584,512]{1,0:T(8,128)(2,1)S(1)} %bitcast.44, bf16[512,3584]{1,0:T(8,128)(2,1)S(1)} %bitcast.45), custom_call_target="tpu_custom_call" | custom-call | flops 4227858432 | bytes 17000000 | tf_op jit(solution)/shard_map/pallas_call | solution.py:145
  142.7 1.5 copy-done
  144.3 7.5 %all-to-all-start.4 = ((bf16[64,3,2,3584]{3,2,1,0:T(2,128)(2,1)}), bf16[64,3,2,3584]{3,2,1,0:T(2,128)(2,1)S(1)}, u32[]{:S(2)}, u32[]{:S(2)}) async-start(bf16[64,3,2,3584]{3,2,1,0:T(2,128)(2,1)} %bitcast.41), calls=%async_computation.4 | async-start | bytes 5505024 | tf_op jit(solution)/shard_map/all_to_all | solution.py:345
  151.8 1.6 collective-permute-start.7
  153.4 0.1 copy.60
  153.5 0.7 collective-permute-done.7
  154.2 0.1 copy.56
  154.3 0.1 select_reduce_fusion
  154.4 0.1 copy.57
  154.5 0.1 copy.58
  154.6 0.1 copy.59
  154.7 0.1 broadcast_in_dim.65
  154.8 0.1 copy.61
  154.9 29.9 %all-to-all-done.4 = bf16[64,3,2,3584]{3,2,1,0:T(2,128)(2,1)S(1)} async-done(((bf16[64,3,2,3584]{3,2,1,0:T(2,128)(2,1)}), bf16[64,3,2,3584]{3,2,1,0:T(2,128)(2,1)S(1)}, u32[]{:S(2)}, u32[]{:S(2)}) %all-to-all-start.4) | async-done | bytes 2752544 | tf_op jit(solution)/shard_map/all_to_all | solution.py:345
  184.8 1.4 shard_map.126
  186.2 3.8 %collective-permute-start.9 = (f32[16,3584]{1,0:T(8,128)S(1)}, f32[16,3584]{1,0:T(8,128)S(1)}, u32[]{:S(2)}, u32[]{:S(2)}) collective-permute-start(f32[16,3584]{1,0:T(8,128)S(1)} %get-tuple-element.9), channel_id=1, source_target_pairs={{0,8},{8,0},{1,9},{9,1},{2,10},{10,2},{3,11},{11,3},{4,12},{12,4},... | collective-permute-start | bytes 688136 | tf_op jit(solution)/shard_map/ppermute | solution.py:268
  190.0 1.1 collective-permute-done.9
  191.1 0.7 fusion.4
  (40 shorter events, 0.3 us)
Async XLA Ops:
  24.1 8.2 %collective-permute-start = (bf16[8,576,128]{2,1,0:T(8,128)(2,1)S(1)}, bf16[8,576,128]{2,1,0:T(8,128)(2,1)S(1)}, u32[]{:S(2)}, u32[]{:S(2)}) collective-permute-start(bf16[8,576,128]{2,1,0:T(8,128)(2,1)S(1)} %all_to_all.25.near_ref), channel_id=1, source_target_pairs={{0,8},{8,0},{1,9},{9,1},{2,10},{10,2},{3,11},{11,3},{4,12},{12,4},... | collective-permute-start | bytes 3538952 | tf_op jit(solution)/shard_map/ppermute | solution.py:268
  28.6 18.0 %all-to-all-start.1 = ((bf16[8,448,128]{2,1,0:T(8,128)(2,1)}), bf16[8,448,128]{2,1,0:T(8,128)(2,1)S(1)}, u32[]{:S(2)}, u32[]{:S(2)}) async-start(bf16[8,448,128]{2,1,0:T(8,128)(2,1)} %pad_maximum_fusion), calls=%async_computation.1 | async-start | bytes 1835008 | tf_op jit(solution)/shard_map/all_to_all | solution.py:325
  32.2 1.6 copy-start.4
  33.8 1.0 copy-start.5
  46.6 15.6 %collective-permute-start.5 = (bf16[8,448,128]{2,1,0:T(8,128)(2,1)S(1)}, bf16[8,448,128]{2,1,0:T(8,128)(2,1)S(1)}, u32[]{:S(2)}, u32[]{:S(2)}) collective-permute-start(bf16[8,448,128]{2,1,0:T(8,128)(2,1)S(1)} %all-to-all-done.1.near_ref), channel_id=1, source_target_pairs={{0,8},{8,0},{1,9},{9,1},{2,10},{10,2},{3,11},{11,3},{4,12},{12,4},... | collective-permute-start | bytes 2752520 | tf_op jit(solution)/shard_map/ppermute | solution.py:268
  47.3 7.9 %collective-permute-start.2 = (bf16[128,1024]{1,0:T(8,128)(2,1)S(1)}, bf16[128,1024]{1,0:T(8,128)(2,1)S(1)}, u32[]{:S(2)}, u32[]{:S(2)}) collective-permute-start(bf16[128,1024]{1,0:T(8,128)(2,1)S(1)} %shard_map.122.own_ref), channel_id=1, source_target_pairs={{0,48},{16,0},{32,16},{48,32},{1,49},{17,1},{33,17},{49,33},{2,50}... | collective-permute-start | bytes 786440 | tf_op jit(solution)/shard_map/ppermute | solution.py:276
  47.8 9.2 %collective-permute-start.1 = (bf16[128,1024]{1,0:T(8,128)(2,1)S(1)}, bf16[128,1024]{1,0:T(8,128)(2,1)S(1)}, u32[]{:S(2)}, u32[]{:S(2)}) collective-permute-start(bf16[128,1024]{1,0:T(8,128)(2,1)S(1)} %shard_map.122.own_ref), channel_id=1, source_target_pairs={{0,16},{16,32},{32,48},{48,0},{1,17},{17,33},{33,49},{49,1},{2,18}... | collective-permute-start | bytes 786440 | tf_op jit(solution)/shard_map/ppermute | solution.py:272
  55.3 4.3 %collective-permute-start.4 = (bf16[128,512]{1,0:T(8,128)(2,1)S(1)}, bf16[128,512]{1,0:T(8,128)(2,1)S(1)}, u32[]{:S(2)}, u32[]{:S(2)}) collective-permute-start(bf16[128,512]{1,0:T(8,128)(2,1)S(1)} %slice.26), channel_id=1, source_target_pairs={{0,48},{16,0},{32,16},{48,32},{1,49},{17,1},{33,17},{49,33},{2,50}... | collective-permute-start | bytes 393224 | tf_op jit(solution)/shard_map/ppermute | solution.py:276
  57.1 15.9 %copy-start.10 = (s32[16,8]{0,1:T(8,128)S(1)}, s32[16,8]{0,1:T(8,128)}, u32[]{:S(2)}) copy-start(s32[16,8]{0,1:T(8,128)} %param.17) | copy-start | bytes 1540
  57.1 5.1 %collective-permute-start.3 = (bf16[128,512]{1,0:T(8,128)(2,1)S(1)}, bf16[128,512]{1,0:T(8,128)(2,1)S(1)}, u32[]{:S(2)}, u32[]{:S(2)}) collective-permute-start(bf16[128,512]{1,0:T(8,128)(2,1)S(1)} %slice.25), channel_id=1, source_target_pairs={{0,16},{16,32},{32,48},{48,0},{1,17},{17,33},{33,49},{49,1},{2,18}... | collective-permute-start | bytes 393224 | tf_op jit(solution)/shard_map/ppermute | solution.py:272
  65.2 22.0 %copy-start.7 = (bf16[16,3584]{1,0:T(8,128)(2,1)S(1)}, bf16[16,3584]{1,0:T(8,128)(2,1)}, u32[]{:S(2)}) copy-start(bf16[16,3584]{1,0:T(8,128)(2,1)} %param.15) | copy-start | bytes 344068
  65.3 22.1 %copy-start.9 = (f32[3584]{0:T(1024)S(1)}, f32[3584]{0:T(1024)}, u32[]{:S(2)}) copy-start(f32[3584]{0:T(1024)} %param.16) | copy-start | bytes 43012
  65.3 21.8 %all-to-all-start.2 = ((bf16[32,16,896]{2,1,0:T(8,128)(2,1)}), bf16[32,16,896]{2,1,0:T(8,128)(2,1)S(1)}, u32[]{:S(2)}, u32[]{:S(2)}) async-start(bf16[32,16,896]{2,1,0:T(8,128)(2,1)} %shard_map.123), calls=%async_computation.2 | async-start | bytes 1835008 | tf_op jit(solution)/shard_map/all_to_all | solution.py:334
  73.0 3.5 %collective-permute-start.6 = (s32[16,8]{0,1:T(8,128)S(1)}, s32[16,8]{0,1:T(8,128)S(1)}, u32[]{:S(2)}, u32[]{:S(2)}) collective-permute-start(s32[16,8]{0,1:T(8,128)S(1)} %copy-done.10), channel_id=1, source_target_pairs={{0,8},{8,0},{1,9},{9,1},{2,10},{10,2},{3,11},{11,3},{4,12},{12,4},... | collective-permute-start | bytes 1544 | tf_op jit(solution)/shard_map/ppermute | solution.py:268
  87.4 103.7 %copy-start.6 = (bf16[16,3584]{1,0:T(8,128)(2,1)}, bf16[16,3584]{1,0:T(8,128)(2,1)S(1)}, u32[]{:S(2)}) copy-start(bf16[16,3584]{1,0:T(8,128)(2,1)S(1)} %get-tuple-element.11) | copy-start | bytes 344068
  87.5 4.7 %collective-permute-start.8 = (bf16[16,3584]{1,0:T(8,128)(2,1)S(1)}, bf16[16,3584]{1,0:T(8,128)(2,1)S(1)}, u32[]{:S(2)}, u32[]{:S(2)}) collective-permute-start(bf16[16,3584]{1,0:T(8,128)(2,1)S(1)} %fusion.2), channel_id=1, source_target_pairs={{0,8},{8,0},{1,9},{9,1},{2,10},{10,2},{3,11},{11,3},{4,12},{12,4},... | collective-permute-start | bytes 344072 | tf_op jit(solution)/shard_map/ppermute | solution.py:268
  92.2 42.0 %copy-start.2 = (bf16[1,3584,512]{2,1,0:T(8,128)(2,1)S(1)}, bf16[1,3584,512]{2,1,0:T(8,128)(2,1)}, u32[]{:S(2)}) copy-start(bf16[1,3584,512]{2,1,0:T(8,128)(2,1)} %param.20) | copy-start | bytes 11010052
  93.6 40.7 %copy-start.1 = (bf16[1,3584,512]{2,1,0:T(8,128)(2,1)S(1)}, bf16[1,3584,512]{2,1,0:T(8,128)(2,1)}, u32[]{:S(2)}) copy-start(bf16[1,3584,512]{2,1,0:T(8,128)(2,1)} %param.19) | copy-start | bytes 11010052
  134.3 2.0 %copy-start.3 = (bf16[1,512,3584]{2,1,0:T(8,128)(2,1)S(1)}, bf16[1,512,3584]{2,1,0:T(8,128)(2,1)}, u32[]{:S(2)}) copy-start(bf16[1,512,3584]{2,1,0:T(8,128)(2,1)} %param.21) | copy-start | bytes 11010052
  142.7 1.5 copy-start
  144.3 7.5 %copy-start.8 = (s32[16,8]{0,1:T(8,128)S(1)}, s32[16,8]{0,1:T(8,128)}, u32[]{:S(2)}) copy-start(s32[16,8]{0,1:T(8,128)} %param.18) | copy-start | bytes 1540
  144.3 40.6 %all-to-all-start.4 = ((bf16[64,3,2,3584]{3,2,1,0:T(2,128)(2,1)}), bf16[64,3,2,3584]{3,2,1,0:T(2,128)(2,1)S(1)}, u32[]{:S(2)}, u32[]{:S(2)}) async-start(bf16[64,3,2,3584]{3,2,1,0:T(2,128)(2,1)} %bitcast.41), calls=%async_computation.4 | async-start | bytes 5505024 | tf_op jit(solution)/shard_map/all_to_all | solution.py:345
  151.8 2.4 %collective-permute-start.7 = (f32[16,8]{0,1:T(8,128)S(1)}, f32[16,8]{0,1:T(8,128)S(1)}, u32[]{:S(2)}, u32[]{:S(2)}) collective-permute-start(f32[16,8]{0,1:T(8,128)S(1)} %convert_divide_fusion), channel_id=1, source_target_pairs={{0,8},{8,0},{1,9},{9,1},{2,10},{10,2},{3,11},{11,3},{4,12},{12,4},... | collective-permute-start | bytes 1544 | tf_op jit(solution)/shard_map/ppermute | solution.py:268
  186.2 4.9 %collective-permute-start.9 = (f32[16,3584]{1,0:T(8,128)S(1)}, f32[16,3584]{1,0:T(8,128)S(1)}, u32[]{:S(2)}, u32[]{:S(2)}) collective-permute-start(f32[16,3584]{1,0:T(8,128)S(1)} %get-tuple-element.9), channel_id=1, source_target_pairs={{0,8},{8,0},{1,9},{9,1},{2,10},{10,2},{3,11},{11,3},{4,12},{12,4},... | collective-permute-start | bytes 688136 | tf_op jit(solution)/shard_map/ppermute | solution.py:268

commit v13 on v12

--- a/solution.py
+++ b/solution.py
@@ -27,15 +27,27 @@
 LOG2E = 1.4426950408889634
 
 
-def attend_kernel(ids_ref, q_ref, w_ref, near_ref, far_ref, out_ref, lat_ref, s_ref, latq_ref, mixed_ref, *, cuts):
+def in_hbm(a):
+    return pltpu.with_memory_space_constraint(a, pltpu.HBM)
+
+
+def attend_kernel(
+    ids_ref, q_hbm, w_hbm, near_ref, far_ref, out_ref, q_ref, w_ref, lat_ref, s_ref, latq_ref, mixed_ref, sems, *, cuts
+):
     heads = w_ref.shape[1] // (NOPE + VD)
     rows = q_ref.shape[0]
     m = heads * rows
     pairs = near_ref.shape[0]
     keys = 2 * rows * pairs
+    q_copy = pltpu.make_async_copy(q_hbm, q_ref, sems.at[0])
+    w_copy = pltpu.make_async_copy(w_hbm, w_ref, sems.at[1])
+    q_copy.start()
+    w_copy.start()
     for i in range(pairs):
         lat_ref[:, 2 * i * rows : (2 * i + 1) * rows] = near_ref[i]
         lat_ref[:, (2 * i + 1) * rows : (2 * i + 2) * rows] = far_ref[i]
+    q_copy.wait()
+    w_copy.wait()
     for h in range(heads):
         here = slice(h * rows, (h + 1) * rows)
         key_weights = w_ref[:, h * (NOPE + VD) : h * (NOPE + VD) + NOPE]
@@ -87,25 +99,29 @@
     keys = 2 * rows * pairs
     m = heads * rows
     whole = pl.BlockSpec(memory_space=pltpu.VMEM)
+    hbm = pl.BlockSpec(memory_space=pltpu.HBM)
     return pl.pallas_call(
         functools.partial(attend_kernel, cuts=cuts),
-        in_specs=[pl.BlockSpec(memory_space=pltpu.SMEM)] + [whole] * 4,
+        in_specs=[pl.BlockSpec(memory_space=pltpu.SMEM), hbm, hbm, whole, whole],
         out_specs=whole,
         out_shape=jax.ShapeDtypeStruct((rows, heads * VD), BF),
         scratch_shapes=[
+            pltpu.VMEM(q.shape, BF),
+            pltpu.VMEM(w_kv.shape, BF),
             pltpu.VMEM((depth, keys), BF),
             pltpu.VMEM((m, keys), F32),
             pltpu.VMEM((m, depth), BF),
             pltpu.VMEM((m, KV_RANK), F32),
+            pltpu.SemaphoreType.DMA((2,)),
         ],
-        compiler_params=pltpu.CompilerParams(vmem_limit_bytes=24 * 2**20),
+        compiler_params=pltpu.CompilerParams(vmem_limit_bytes=28 * 2**20),
         cost_estimate=pl.CostEstimate(
             flops=2 * m * keys * (depth + KV_RANK), bytes_accessed=8_000_000, transcendentals=m * keys
         ),
-    )(ids, q, w_kv, near, far)
-
-
-def expert_kernel(x_hbm, g_ref, u_ref, d_ref, out_hbm, x_ref, hid_ref, gate_ref, up_ref, y_ref, sem_in, sem_out):
+    )(ids, in_hbm(q), in_hbm(w_kv), near, far)
+
+
+def expert_kernel(x_hbm, g_ref, u_ref, d_hbm, out_hbm, d_ref, x_ref, hid_ref, gate_ref, up_ref, y_ref, sem_d, sem_in, sem_out):
     units, pair, width = x_ref.shape
     m = units * pair
     first, last = sem_in.shape[0], sem_out.shape[0]
@@ -115,6 +131,8 @@
         part = slice(k * depth, (k + 1) * depth)
         arrivals.append(pltpu.make_async_copy(x_hbm.at[:, :, part], x_ref.at[:, :, part], sem_in.at[k]))
         arrivals[-1].start()
+    d_copy = pltpu.make_async_copy(d_hbm, d_ref, sem_d.at[0])
+    d_copy.start()
     for k in range(first):
         part = slice(k * depth, (k + 1) * depth)
         arrivals[k].wait()
@@ -125,6 +143,7 @@
         up_ref[...] = upward if k == 0 else up_ref[...] + upward
     gate = gate_ref[...]
     hid_ref[...] = (gate / (1.0 + jnp.exp(-gate)) * up_ref[...]).astype(BF)
+    d_copy.wait()
     departures = []
     for n in range(last):
         part = slice(n * wide, (n + 1) * wide)
@@ -144,23 +163,25 @@
     far = pl.BlockSpec(memory_space=pltpu.HBM)
     return pl.pallas_call(
         expert_kernel,
-        in_specs=[far, whole, whole, whole],
+        in_specs=[far, whole, whole, far],
         out_specs=far,
-        out_shape=jax.ShapeDtypeStruct(x.shape, BF),
+        out_shape=pltpu.HBM(x.shape, BF),
         scratch_shapes=[
+            pltpu.VMEM(w_down.shape, BF),
             pltpu.VMEM(x.shape, BF),
             pltpu.VMEM((m, hidden), BF),
             pltpu.VMEM((m, hidden), F32),
             pltpu.VMEM((m, hidden), F32),
             pltpu.VMEM(x.shape, BF),
+            pltpu.SemaphoreType.DMA((1,)),
             pltpu.SemaphoreType.DMA((first,)),
             pltpu.SemaphoreType.DMA((last,)),
         ],
-        compiler_params=pltpu.CompilerParams(vmem_limit_bytes=20 * 2**20),
+        compiler_params=pltpu.CompilerParams(vmem_limit_bytes=24 * 2**20),
         cost_estimate=pl.CostEstimate(
             flops=6 * m * width * hidden, bytes_accessed=17_000_000, transcendentals=m * hidden
         ),
-    )(x, w_gate, w_up, w_down)
+    )(x, w_gate, w_up, in_hbm(w_down))
 
 
 def dispatch_kernel(place_ref, x_ref, out_ref):
@@ -233,13 +254,10 @@
     x_ref[2 * rows : 3 * rows, half:] = right_ref[...]
     x_ref[3 * rows :] = before_ref[...]
     deep = VD // 2
-    blocks = w_ref.shape[1] // 128
     for side, ref in enumerate((near_ref, far_ref)):
         offset = (core if side == 0 else 1 - core) * deep
         for j in range(ref.shape[0]):
-            here = pl.ds(pl.multiple_of(j * VD + offset, deep), deep)
-            for b in range(blocks):
-                w_ref[here, b * 128 : (b + 1) * 128] = ref[j, b * deep : (b + 1) * deep]
+            w_ref[pl.ds(pl.multiple_of(j * VD + offset, deep), deep)] = ref[j]
     for d in range(group):
         y = jnp.dot(x_ref[d * rows : (d + 1) * rows], w_ref[...], preferred_element_type=F32).astype(BF)
         target = lax.rem(x + d, group)
@@ -320,8 +338,8 @@
         jnp.broadcast_to(latents[None], (8,) + latents.shape), CTX_CHIPS, split_axis=0, concat_axis=0, tiled=True
     )
     far = swap(near)
-    w_blocks = w_out.reshape(-1, group, columns // 128, 128).transpose(1, 2, 0, 3).reshape(group, -1, 128)
-    w_blocks, _ = lax.optimization_barrier((jnp.concatenate([w_blocks, w_blocks], axis=0), near[0, :8]))
+    w_blocks = jnp.stack([w_out[:, i * columns : (i + 1) * columns] for i in range(group)] * 2)
+    w_blocks, _ = lax.optimization_barrier((w_blocks, near[0, :8]))
     w_near = lax.all_to_all(w_blocks, CTX_CHIPS, split_axis=0, concat_axis=0, tiled=True)
     ids = jnp.stack([lax.axis_index(CTX), core, lax.axis_index("x")]).astype(jnp.int32)
     own = attend(ids, queries, w_kv, near, far, 4)

time: 194 us -> 190 us (0.979)
  blocking collectives: 63 us -> 40.7 us
  waiting for transfers between devices: 57.7 us -> 73.4 us
  starting transfers between devices: 36.3 us -> 41.5 us
    all_to_all x1 -> x0, blocking collectives: 22.4 us -> none  [local(): lax.all_to_all(jnp.broadcast_to(latents[None], (8,) + latents.shape), CTX...]
    all_to_all x0 -> x1, waiting for transfers between devices: none -> 14.6 us  [local(): lax.all_to_all(jnp.broadcast_to(latents[None], (8,) + latents.shape), CTX...]
    all_to_all x0 -> x1, starting transfers between devices: none -> 6.2 us  [local(): lax.all_to_all(jnp.broadcast_to(latents[None], (8,) + latents.shape), CTX...]
    unnamed x22 -> x23, local copies, waits for them, and re-layouts: 6.19 us -> 4.62 us
  transfers between devices with their start and end apart: 13 -> 14, of which waited for: 10 -> 11; matrix products, arithmetic and copies ran while one was open for 3% -> 4% of each run, Pallas kernels for 4% -> 5%
where the time goes in v13:
time: 190 us; the launch traced here: 188 us
  waiting for transfers between devices  73.4 us (39%)
  starting transfers between devices  41.5 us (22%)
  blocking collectives  40.7 us (21%)
  Pallas kernels  21.3 us (11%)
  local copies, waits for them, and re-layouts  8.87 us (5%)
    all_to_all x1, blocking collectives, exchange(): lax.all_to_all(units, CHIPS, split_axis=0, concat_axis=0, tiled=True)  40.7 us
    all_to_all x1, waiting for transfers between devices, exchange(): lax.all_to_all(units, CHIPS, split_axis=0, concat_axis=0, tiled=True)  29.9 us
    all_to_all x1, waiting for transfers between devices, local(): lax.all_to_all(jnp.broadcast_to(latents[None], (8,) + latents.shape), CTX...  14.6 us
    ppermute x6, starting transfers between devices, swap(): return lax.ppermute(mine, 'core', SWAP)  13.3 us
    all_to_all x1, waiting for transfers between devices, local(): lax.all_to_all(attn, EP + ('x',), split_axis=0, concat_axis=0, tiled=True)  9.91 us
    pallas_call x1, Pallas kernels, attend(): pl.pallas_call(functools.partial(attend_kernel, cuts=cuts), in_specs=[pl....  9.82 us
    ppermute x2, waiting for transfers between devices, down(): return lax.ppermute(a, 'x', [(i, (i + 3) % 4) for i in range(4)])  8.88 us
    all_to_all x1, starting transfers between devices, local(): lax.all_to_all(attn, EP + ('x',), split_axis=0, concat_axis=0, tiled=True)  7.77 us
  transfers between devices with their start and end apart: 14, of which 11 were waited for; matrix products, arithmetic and copies ran while one was open for 4% of the time, Pallas kernels for 5%

profile of v13, /device:TPU:1, one launch (start us, length us, event | category | flops | bytes accessed | tf_op | source)
XLA Modules:
  0.0 188.5 jit_solution(10060478507124306706)
XLA Ops:
  0.6 2.1 %broadcast_in_dim.32 = bf16[8,576,128]{2,1,0:T(8,128)(2,1)} broadcast(bf16[576,128]{1,0:T(8,128)(2,1)} %param.12), dimensions={1,2} | broadcast | bytes 1327104 | tf_op jit(solution)/shard_map/broadcast_in_dim | solution.py:338
  2.8 6.2 %all-to-all-start = ((bf16[8,576,128]{2,1,0:T(8,128)(2,1)}), bf16[8,576,128]{2,1,0:T(8,128)(2,1)S(1)}, u32[]{:S(2)}, u32[]{:S(2)}) async-start(bf16[8,576,128]{2,1,0:T(8,128)(2,1)} %broadcast_in_dim.32), calls=%async_computation | async-start | bytes 2359296 | tf_op jit(solution)/shard_map/all_to_all | solution.py:337
  9.0 0.7 bitcast_dynamic-update-slice_fusion.6
  9.6 0.6 bitcast_dynamic-update-slice_fusion.4
  10.3 0.6 bitcast_dynamic-update-slice_fusion.2
  10.9 0.7 bitcast_dynamic-update-slice_fusion
  11.6 14.6 %all-to-all-done.near_ref = bf16[8,576,128]{2,1,0:T(8,128)(2,1)S(1)} async-done(((bf16[8,576,128]{2,1,0:T(8,128)(2,1)}), bf16[8,576,128]{2,1,0:T(8,128)(2,1)S(1)}, u32[]{:S(2)}, u32[]{:S(2)}) %all-to-all-start) | async-done | bytes 1179680 | tf_op jit(solution)/shard_map/all_to_all | solution.py:337
  26.2 0.8 collective-permute-start
  27.0 0.6 bitcast_dynamic-update-slice_fusion.7
  27.7 0.7 bitcast_dynamic-update-slice_fusion.5
  28.3 0.7 bitcast_dynamic-update-slice_fusion.3
  29.0 0.6 bitcast_dynamic-update-slice_fusion.1
  29.7 3.6 %all-to-all-start.1 = ((bf16[8,64,896]{2,1,0:T(8,128)(2,1)}), bf16[8,64,896]{2,1,0:T(8,128)(2,1)S(1)}, u32[]{:S(2)}, u32[]{:S(2)}) async-start(bf16[8,64,896]{2,1,0:T(8,128)(2,1)} %bitcast_dynamic-update-slice_fusion.1), calls=%async_computation.1 | async-start | bytes 1835008 | tf_op jit(solution)/shard_map/all_to_all | solution.py:343
  33.2 0.1 pad_add_fusion.1.ids_ref
  33.3 9.8 %shard_map.122.own_ref = bf16[128,1024]{1,0:T(8,128)(2,1)S(1)} custom-call(s32[3]{0:T(128)S(1)} %pad_add_fusion.1.ids_ref, bf16[128,1536]{1,0:T(8,128)(2,1)} %q_hbm.1, bf16[512,2048]{1,0:T(8,128)(2,1)} %w_hbm.1, bf16[8,576,128]{2,1,0:T(8,128)(2,1)S(1)} %all-to-all-done.near_ref, bf16[8,576,128]{2,1,0:T(8,128)(2,1)S(1)} %collective-permute-done.far_ref), custom_call_target="tpu_custom_call" | custom-call | flops 4563402752 | bytes 8000000 | tf_op jit(solution)/shard_map/pallas_call | solution.py:103
  43.1 4.6 %all-to-all-done.1.near_ref = bf16[8,64,896]{2,1,0:T(8,128)(2,1)S(1)} async-done(((bf16[8,64,896]{2,1,0:T(8,128)(2,1)}), bf16[8,64,896]{2,1,0:T(8,128)(2,1)S(1)}, u32[]{:S(2)}, u32[]{:S(2)}) %all-to-all-start.1) | async-done | bytes 917536 | tf_op jit(solution)/shard_map/all_to_all | solution.py:343
  47.7 0.7 collective-permute-start.5
  48.4 0.5 collective-permute-start.2
  48.9 1.0 collective-permute-start.1
  49.9 6.5 %collective-permute-done.2.after_ref = bf16[128,1024]{1,0:T(8,128)(2,1)S(1)} collective-permute-done((bf16[128,1024]{1,0:T(8,128)(2,1)S(1)}, bf16[128,1024]{1,0:T(8,128)(2,1)S(1)}, u32[]{:S(2)}, u32[]{:S(2)}) %collective-permute-start.2) | collective-permute-done | bytes 262176 | tf_op jit(solution)/shard_map/ppermute | solution.py:294
  56.4 1.8 collective-permute-start.4
  58.2 0.1 collective-permute-start.3
  58.2 2.4 %collective-permute-done.4.right_ref = bf16[128,512]{1,0:T(8,128)(2,1)S(1)} collective-permute-done((bf16[128,512]{1,0:T(8,128)(2,1)S(1)}, bf16[128,512]{1,0:T(8,128)(2,1)S(1)}, u32[]{:S(2)}, u32[]{:S(2)}) %collective-permute-start.4) | collective-permute-done | bytes 131104 | tf_op jit(solution)/shard_map/ppermute | solution.py:294
  60.7 2.6 %collective-permute-done.3.left_ref = bf16[128,512]{1,0:T(8,128)(2,1)S(1)} collective-permute-done((bf16[128,512]{1,0:T(8,128)(2,1)S(1)}, bf16[128,512]{1,0:T(8,128)(2,1)S(1)}, u32[]{:S(2)}, u32[]{:S(2)}) %collective-permute-start.3) | collective-permute-done | bytes 131104 | tf_op jit(solution)/shard_map/ppermute | solution.py:290
  63.3 2.9 %shard_map.123 = bf16[32,16,896]{2,1,0:T(8,128)(2,1)} custom-call(s32[3]{0:T(128)S(1)} %pad_add_fusion.1.ids_ref, bf16[128,1024]{1,0:T(8,128)(2,1)S(1)} %shard_map.122.own_ref, bf16[128,1024]{1,0:T(8,128)(2,1)S(1)} %collective-permute-done.1.before_ref, bf16[128,1024]{1,0:T(8,128)(2,1)S(1)} %collective-permute-done.2.after_ref, ...), custom_call_target="tpu_custom_call" | custom-call | flops 939524096 | bytes 1835008 | tf_op jit(solution)/shard_map/pallas_call | solution.py:272
  66.1 7.8 %all-to-all-start.2 = ((bf16[32,16,896]{2,1,0:T(8,128)(2,1)}), bf16[32,16,896]{2,1,0:T(8,128)(2,1)S(1)}, u32[]{:S(2)}, u32[]{:S(2)}) async-start(bf16[32,16,896]{2,1,0:T(8,128)(2,1)} %shard_map.123), calls=%async_computation.2 | async-start | bytes 1835008 | tf_op jit(solution)/shard_map/all_to_all | solution.py:352
  73.9 2.7 %collective-permute-start.6 = (s32[16,8]{0,1:T(8,128)S(1)}, s32[16,8]{0,1:T(8,128)S(1)}, u32[]{:S(2)}, u32[]{:S(2)}) collective-permute-start(s32[16,8]{0,1:T(8,128)S(1)} %copy-done.7), channel_id=1, source_target_pairs={{0,8},{8,0},{1,9},{9,1},{2,10},{10,2},{3,11},{11,3},{4,12},{12,4},... | collective-permute-start | bytes 1544 | tf_op jit(solution)/shard_map/ppermute | solution.py:286
  76.7 0.1 and.46
  76.7 0.1 and.47
  76.8 0.7 collective-permute-done.6
  77.5 0.1 copy.46
  77.6 0.1 fusion.5
  77.7 0.1 copy.47
  77.8 0.1 copy.49
  77.9 0.1 copy.48
  78.0 9.9 %all-to-all-done.2 = bf16[32,16,896]{2,1,0:T(8,128)(2,1)S(1)} async-done(((bf16[32,16,896]{2,1,0:T(8,128)(2,1)}), bf16[32,16,896]{2,1,0:T(8,128)(2,1)S(1)}, u32[]{:S(2)}, u32[]{:S(2)}) %all-to-all-start.2) | async-done | bytes 917536 | tf_op jit(solution)/shard_map/all_to_all | solution.py:352
  88.0 0.1 convert_reduce_fusion
  88.1 0.2 fusion
  88.3 0.1 fusion.2
  88.4 3.7 %collective-permute-start.8 = (bf16[16,3584]{1,0:T(8,128)(2,1)S(1)}, bf16[16,3584]{1,0:T(8,128)(2,1)S(1)}, u32[]{:S(2)}, u32[]{:S(2)}) collective-permute-start(bf16[16,3584]{1,0:T(8,128)(2,1)S(1)} %fusion.2), channel_id=1, source_target_pairs={{0,8},{8,0},{1,9},{9,1},{2,10},{10,2},{3,11},{11,3},{4,12},{12,4},... | collective-permute-start | bytes 344072 | tf_op jit(solution)/shard_map/ppermute | solution.py:286
  92.1 0.1 bitcast_and_fusion
  92.2 0.1 copy.50
  92.4 0.1 broadcast_in_dim.33
  92.5 0.1 reshape.135
  92.6 0.5 collective-permute-done.8
  93.1 1.4 shard_map.124
  94.5 40.7 %all_to_all.25 = bf16[64,3,2,3584]{3,2,1,0:T(2,128)(2,1)S(1)} all-to-all(bf16[64,3,2,3584]{3,2,1,0:T(2,128)(2,1)S(1)} %bitcast.50), channel_id=1, replica_groups=mesh['z_lo'=2,'x'=4,'core'=2,'z_hi'=2,'y'=4] {'z_lo','x','z_hi','y'}, dimensions={0} | all-to-all | bytes 5505024 | tf_op jit(solution)/shard_map/all_to_all | solution.py:363
  135.1 5.9 %shard_map.125 = bf16[192,2,3584]{2,1,0:T(2,128)(2,1)} custom-call(bf16[192,2,3584]{2,1,0:T(2,128)(2,1)S(1)} %bitcast.51, bf16[3584,512]{1,0:T(8,128)(2,1)S(1)} %bitcast.52, bf16[3584,512]{1,0:T(8,128)(2,1)S(1)} %bitcast.53, bf16[512,3584]{1,0:T(8,128)(2,1)} %bitcast.56), custom_call_target="tpu_custom_call" | custom-call | flops 4227858432 | bytes 17000000 | tf_op jit(solution)/shard_map/pallas_call | solution.py:164
  141.0 7.3 %all-to-all-start.4 = ((bf16[64,3,2,3584]{3,2,1,0:T(2,128)(2,1)}), bf16[64,3,2,3584]{3,2,1,0:T(2,128)(2,1)S(1)}, u32[]{:S(2)}, u32[]{:S(2)}) async-start(bf16[64,3,2,3584]{3,2,1,0:T(2,128)(2,1)} %bitcast.54), calls=%async_computation.4 | async-start | bytes 5505024 | tf_op jit(solution)/shard_map/all_to_all | solution.py:363
  148.4 1.6 collective-permute-start.7
  150.0 0.1 copy.55
  150.1 0.7 collective-permute-done.7
  150.8 0.1 copy.51
  150.9 0.1 select_reduce_fusion
  151.1 0.1 copy.52
  151.2 0.1 copy.53
  151.2 0.1 copy.54
  151.3 0.1 broadcast_in_dim.65
  151.4 0.1 copy.56
  151.5 29.9 %all-to-all-done.4 = bf16[64,3,2,3584]{3,2,1,0:T(2,128)(2,1)S(1)} async-done(((bf16[64,3,2,3584]{3,2,1,0:T(2,128)(2,1)}), bf16[64,3,2,3584]{3,2,1,0:T(2,128)(2,1)S(1)}, u32[]{:S(2)}, u32[]{:S(2)}) %all-to-all-start.4) | async-done | bytes 2752544 | tf_op jit(solution)/shard_map/all_to_all | solution.py:363
  181.5 1.4 shard_map.126
  182.9 3.8 %collective-permute-start.9 = (f32[16,3584]{1,0:T(8,128)S(1)}, f32[16,3584]{1,0:T(8,128)S(1)}, u32[]{:S(2)}, u32[]{:S(2)}) collective-permute-start(f32[16,3584]{1,0:T(8,128)S(1)} %get-tuple-element.9), channel_id=1, source_target_pairs={{0,8},{8,0},{1,9},{9,1},{2,10},{10,2},{3,11},{11,3},{4,12},{12,4},... | collective-permute-start | bytes 688136 | tf_op jit(solution)/shard_map/ppermute | solution.py:286
  186.7 1.1 collective-permute-done.9
  187.8 0.7 fusion.4
  (40 shorter events, 0.3 us)
Async XLA Ops:
  0.6 8.3 %copy-start.2 = (bf16[64,3584]{1,0:T(8,128)(2,1)S(1)}, bf16[64,3584]{1,0:T(8,128)(2,1)}, u32[]{:S(2)}) copy-start(bf16[64,3584]{1,0:T(8,128)(2,1)} %param.14) | copy-start | bytes 1376260
  2.8 23.4 %all-to-all-start = ((bf16[8,576,128]{2,1,0:T(8,128)(2,1)}), bf16[8,576,128]{2,1,0:T(8,128)(2,1)S(1)}, u32[]{:S(2)}, u32[]{:S(2)}) async-start(bf16[8,576,128]{2,1,0:T(8,128)(2,1)} %broadcast_in_dim.32), calls=%async_computation | async-start | bytes 2359296 | tf_op jit(solution)/shard_map/all_to_all | solution.py:337
  26.2 7.1 %collective-permute-start = (bf16[8,576,128]{2,1,0:T(8,128)(2,1)S(1)}, bf16[8,576,128]{2,1,0:T(8,128)(2,1)S(1)}, u32[]{:S(2)}, u32[]{:S(2)}) collective-permute-start(bf16[8,576,128]{2,1,0:T(8,128)(2,1)S(1)} %all-to-all-done.near_ref), channel_id=1, source_target_pairs={{0,8},{8,0},{1,9},{9,1},{2,10},{10,2},{3,11},{11,3},{4,12},{12,4},... | collective-permute-start | bytes 3538952 | tf_op jit(solution)/shard_map/ppermute | solution.py:286
  29.7 18.0 %all-to-all-start.1 = ((bf16[8,64,896]{2,1,0:T(8,128)(2,1)}), bf16[8,64,896]{2,1,0:T(8,128)(2,1)S(1)}, u32[]{:S(2)}, u32[]{:S(2)}) async-start(bf16[8,64,896]{2,1,0:T(8,128)(2,1)} %bitcast_dynamic-update-slice_fusion.1), calls=%async_computation.1 | async-start | bytes 1835008 | tf_op jit(solution)/shard_map/all_to_all | solution.py:343
  47.7 15.6 %collective-permute-start.5 = (bf16[8,64,896]{2,1,0:T(8,128)(2,1)S(1)}, bf16[8,64,896]{2,1,0:T(8,128)(2,1)S(1)}, u32[]{:S(2)}, u32[]{:S(2)}) collective-permute-start(bf16[8,64,896]{2,1,0:T(8,128)(2,1)S(1)} %all-to-all-done.1.near_ref), channel_id=1, source_target_pairs={{0,8},{8,0},{1,9},{9,1},{2,10},{10,2},{3,11},{11,3},{4,12},{12,4},... | collective-permute-start | bytes 2752520 | tf_op jit(solution)/shard_map/ppermute | solution.py:286
  48.4 7.9 %collective-permute-start.2 = (bf16[128,1024]{1,0:T(8,128)(2,1)S(1)}, bf16[128,1024]{1,0:T(8,128)(2,1)S(1)}, u32[]{:S(2)}, u32[]{:S(2)}) collective-permute-start(bf16[128,1024]{1,0:T(8,128)(2,1)S(1)} %shard_map.122.own_ref), channel_id=1, source_target_pairs={{0,48},{16,0},{32,16},{48,32},{1,49},{17,1},{33,17},{49,33},{2,50}... | collective-permute-start | bytes 786440 | tf_op jit(solution)/shard_map/ppermute | solution.py:294
  48.9 9.2 %collective-permute-start.1 = (bf16[128,1024]{1,0:T(8,128)(2,1)S(1)}, bf16[128,1024]{1,0:T(8,128)(2,1)S(1)}, u32[]{:S(2)}, u32[]{:S(2)}) collective-permute-start(bf16[128,1024]{1,0:T(8,128)(2,1)S(1)} %shard_map.122.own_ref), channel_id=1, source_target_pairs={{0,16},{16,32},{32,48},{48,0},{1,17},{17,33},{33,49},{49,1},{2,18}... | collective-permute-start | bytes 786440 | tf_op jit(solution)/shard_map/ppermute | solution.py:290
  56.4 4.3 %collective-permute-start.4 = (bf16[128,512]{1,0:T(8,128)(2,1)S(1)}, bf16[128,512]{1,0:T(8,128)(2,1)S(1)}, u32[]{:S(2)}, u32[]{:S(2)}) collective-permute-start(bf16[128,512]{1,0:T(8,128)(2,1)S(1)} %slice.42), channel_id=1, source_target_pairs={{0,48},{16,0},{32,16},{48,32},{1,49},{17,1},{33,17},{49,33},{2,50}... | collective-permute-start | bytes 393224 | tf_op jit(solution)/shard_map/ppermute | solution.py:294
  58.2 15.8 %copy-start.7 = (s32[16,8]{0,1:T(8,128)S(1)}, s32[16,8]{0,1:T(8,128)}, u32[]{:S(2)}) copy-start(s32[16,8]{0,1:T(8,128)} %param.17) | copy-start | bytes 1540
  58.2 5.1 %collective-permute-start.3 = (bf16[128,512]{1,0:T(8,128)(2,1)S(1)}, bf16[128,512]{1,0:T(8,128)(2,1)S(1)}, u32[]{:S(2)}, u32[]{:S(2)}) collective-permute-start(bf16[128,512]{1,0:T(8,128)(2,1)S(1)} %slice.41), channel_id=1, source_target_pairs={{0,16},{16,32},{32,48},{48,0},{1,17},{17,33},{33,49},{49,1},{2,18}... | collective-permute-start | bytes 393224 | tf_op jit(solution)/shard_map/ppermute | solution.py:290
  66.1 22.0 %copy-start.4 = (bf16[16,3584]{1,0:T(8,128)(2,1)S(1)}, bf16[16,3584]{1,0:T(8,128)(2,1)}, u32[]{:S(2)}) copy-start(bf16[16,3584]{1,0:T(8,128)(2,1)} %param.15) | copy-start | bytes 344068
  66.1 22.1 %copy-start.6 = (f32[3584]{0:T(1024)S(1)}, f32[3584]{0:T(1024)}, u32[]{:S(2)}) copy-start(f32[3584]{0:T(1024)} %param.16) | copy-start | bytes 43012
  66.1 21.8 %all-to-all-start.2 = ((bf16[32,16,896]{2,1,0:T(8,128)(2,1)}), bf16[32,16,896]{2,1,0:T(8,128)(2,1)S(1)}, u32[]{:S(2)}, u32[]{:S(2)}) async-start(bf16[32,16,896]{2,1,0:T(8,128)(2,1)} %shard_map.123), calls=%async_computation.2 | async-start | bytes 1835008 | tf_op jit(solution)/shard_map/all_to_all | solution.py:352
  73.9 3.5 %collective-permute-start.6 = (s32[16,8]{0,1:T(8,128)S(1)}, s32[16,8]{0,1:T(8,128)S(1)}, u32[]{:S(2)}, u32[]{:S(2)}) collective-permute-start(s32[16,8]{0,1:T(8,128)S(1)} %copy-done.7), channel_id=1, source_target_pairs={{0,8},{8,0},{1,9},{9,1},{2,10},{10,2},{3,11},{11,3},{4,12},{12,4},... | collective-permute-start | bytes 1544 | tf_op jit(solution)/shard_map/ppermute | solution.py:286
  88.3 99.5 %copy-start.3 = (bf16[16,3584]{1,0:T(8,128)(2,1)}, bf16[16,3584]{1,0:T(8,128)(2,1)S(1)}, u32[]{:S(2)}) copy-start(bf16[16,3584]{1,0:T(8,128)(2,1)S(1)} %get-tuple-element.11) | copy-start | bytes 344068
  88.4 4.7 %collective-permute-start.8 = (bf16[16,3584]{1,0:T(8,128)(2,1)S(1)}, bf16[16,3584]{1,0:T(8,128)(2,1)S(1)}, u32[]{:S(2)}, u32[]{:S(2)}) collective-permute-start(bf16[16,3584]{1,0:T(8,128)(2,1)S(1)} %fusion.2), channel_id=1, source_target_pairs={{0,8},{8,0},{1,9},{9,1},{2,10},{10,2},{3,11},{11,3},{4,12},{12,4},... | collective-permute-start | bytes 344072 | tf_op jit(solution)/shard_map/ppermute | solution.py:286
  93.1 42.0 %copy-start.1 = (bf16[1,3584,512]{2,1,0:T(8,128)(2,1)S(1)}, bf16[1,3584,512]{2,1,0:T(8,128)(2,1)}, u32[]{:S(2)}) copy-start(bf16[1,3584,512]{2,1,0:T(8,128)(2,1)} %param.20) | copy-start | bytes 11010052
  94.5 40.7 %copy-start = (bf16[1,3584,512]{2,1,0:T(8,128)(2,1)S(1)}, bf16[1,3584,512]{2,1,0:T(8,128)(2,1)}, u32[]{:S(2)}) copy-start(bf16[1,3584,512]{2,1,0:T(8,128)(2,1)} %param.19) | copy-start | bytes 11010052
  141.0 7.4 %copy-start.5 = (s32[16,8]{0,1:T(8,128)S(1)}, s32[16,8]{0,1:T(8,128)}, u32[]{:S(2)}) copy-start(s32[16,8]{0,1:T(8,128)} %param.18) | copy-start | bytes 1540
  141.0 40.5 %all-to-all-start.4 = ((bf16[64,3,2,3584]{3,2,1,0:T(2,128)(2,1)}), bf16[64,3,2,3584]{3,2,1,0:T(2,128)(2,1)S(1)}, u32[]{:S(2)}, u32[]{:S(2)}) async-start(bf16[64,3,2,3584]{3,2,1,0:T(2,128)(2,1)} %bitcast.54), calls=%async_computation.4 | async-start | bytes 5505024 | tf_op jit(solution)/shard_map/all_to_all | solution.py:363
  148.4 2.4 %collective-permute-start.7 = (f32[16,8]{0,1:T(8,128)S(1)}, f32[16,8]{0,1:T(8,128)S(1)}, u32[]{:S(2)}, u32[]{:S(2)}) collective-permute-start(f32[16,8]{0,1:T(8,128)S(1)} %convert_divide_fusion), channel_id=1, source_target_pairs={{0,8},{8,0},{1,9},{9,1},{2,10},{10,2},{3,11},{11,3},{4,12},{12,4},... | collective-permute-start | bytes 1544 | tf_op jit(solution)/shard_map/ppermute | solution.py:286
  182.9 4.9 %collective-permute-start.9 = (f32[16,3584]{1,0:T(8,128)S(1)}, f32[16,3584]{1,0:T(8,128)S(1)}, u32[]{:S(2)}, u32[]{:S(2)}) collective-permute-start(f32[16,3584]{1,0:T(8,128)S(1)} %get-tuple-element.9), channel_id=1, source_target_pairs={{0,8},{8,0},{1,9},{9,1},{2,10},{10,2},{3,11},{11,3},{4,12},{12,4},... | collective-permute-start | bytes 688136 | tf_op jit(solution)/shard_map/ppermute | solution.py:286

commit v14 on v13

--- a/solution.py
+++ b/solution.py
@@ -32,15 +32,17 @@
 
 
 def attend_kernel(
-    ids_ref, q_hbm, w_hbm, near_ref, far_ref, out_ref, q_ref, w_ref, lat_ref, s_ref, latq_ref, mixed_ref, sems, *, cuts
+    ids_ref, q_hbm, w_hbm, near_ref, far_ref, out_ref, q_ref, w_ref, lat_ref, s_ref, latq_ref, mixed_ref, sems, *, turn, cuts
 ):
     heads = w_ref.shape[1] // (NOPE + VD)
     rows = q_ref.shape[0]
     m = heads * rows
     pairs = near_ref.shape[0]
     keys = 2 * rows * pairs
-    q_copy = pltpu.make_async_copy(q_hbm, q_ref, sems.at[0])
-    w_copy = pltpu.make_async_copy(w_hbm, w_ref, sems.at[1])
+    q_part = q_hbm.at[:, turn * q_ref.shape[1] : (turn + 1) * q_ref.shape[1]]
+    w_part = w_hbm.at[:, turn * w_ref.shape[1] : (turn + 1) * w_ref.shape[1]]
+    q_copy = pltpu.make_async_copy(q_part, q_ref, sems.at[0])
+    w_copy = pltpu.make_async_copy(w_part, w_ref, sems.at[1])
     q_copy.start()
     w_copy.start()
     for i in range(pairs):
@@ -93,21 +95,21 @@
         out_ref[:, h * VD : (h + 1) * VD] = o.astype(BF)
 
 
-def attend(ids, q, w_kv, near, far, cuts):
+def attend(ids, q, w_kv, near, far, turn, turns, cuts):
     pairs, depth, rows = near.shape
-    heads = w_kv.shape[1] // (NOPE + VD)
+    heads = w_kv.shape[1] // (NOPE + VD) // turns
     keys = 2 * rows * pairs
     m = heads * rows
     whole = pl.BlockSpec(memory_space=pltpu.VMEM)
     hbm = pl.BlockSpec(memory_space=pltpu.HBM)
     return pl.pallas_call(
-        functools.partial(attend_kernel, cuts=cuts),
+        functools.partial(attend_kernel, turn=turn, cuts=cuts),
         in_specs=[pl.BlockSpec(memory_space=pltpu.SMEM), hbm, hbm, whole, whole],
         out_specs=whole,
         out_shape=jax.ShapeDtypeStruct((rows, heads * VD), BF),
         scratch_shapes=[
-            pltpu.VMEM(q.shape, BF),
-            pltpu.VMEM(w_kv.shape, BF),
+            pltpu.VMEM((rows, heads * QK), BF),
+            pltpu.VMEM((KV_RANK, heads * (NOPE + VD)), BF),
             pltpu.VMEM((depth, keys), BF),
             pltpu.VMEM((m, keys), F32),
             pltpu.VMEM((m, depth), BF),
@@ -242,17 +244,14 @@
     )(*[a for part in parts for a in part])
 
 
-def project_kernel(ids_ref, own_ref, before_ref, after_ref, left_ref, right_ref, near_ref, far_ref, out_ref, x_ref, w_ref):
-    rows = own_ref.shape[0]
+def project_kernel(ids_ref, *refs):
+    *piece_refs, near_ref, far_ref, out_ref, x_ref, w_ref = refs
+    rows, half = piece_refs[0].shape
     group, tok = 4, out_ref.shape[1]
     parts = out_ref.shape[0] // group
     core, x = ids_ref[1], ids_ref[2]
-    half = left_ref.shape[1]
-    x_ref[:rows] = own_ref[...]
-    x_ref[rows : 2 * rows] = after_ref[...]
-    x_ref[2 * rows : 3 * rows, :half] = left_ref[...]
-    x_ref[2 * rows : 3 * rows, half:] = right_ref[...]
-    x_ref[3 * rows :] = before_ref[...]
+    for i, ref in enumerate(piece_refs):
+        x_ref[i // 2 * rows : (i // 2 + 1) * rows, i % 2 * half : (i % 2 + 1) * half] = ref[...]
     deep = VD // 2
     for side, ref in enumerate((near_ref, far_ref)):
         offset = (core if side == 0 else 1 - core) * deep
@@ -266,7 +265,7 @@
 
 
 def project(ids, pieces, near, far, parts, width):
-    rows, depth = pieces[0].shape
+    rows, depth = pieces[0].shape[0], 2 * pieces[0].shape[1]
     whole = pl.BlockSpec(memory_space=pltpu.VMEM)
     group = 4
     return pl.pallas_call(
@@ -280,6 +279,31 @@
             flops=2 * group * rows * depth * width, bytes_accessed=2 * depth * width, transcendentals=0
         ),
     )(ids, *pieces, near, far)
+
+
+def blocks_kernel(w_ref, out_ref, sems):
+    wide = out_ref.shape[2]
+    group = w_ref.shape[1] // wide
+    copies = []
+    for i in range(out_ref.shape[0]):
+        first = i % group * wide
+        copies.append(pltpu.make_async_copy(w_ref.at[:, first : first + wide], out_ref.at[i], sems.at[i]))
+        copies[-1].start()
+    for copy in copies:
+        copy.wait()
+
+
+def column_blocks(w, group, count):
+    shape = (count, w.shape[0], w.shape[1] // group)
+    hbm = pl.BlockSpec(memory_space=pltpu.HBM)
+    return pl.pallas_call(
+        blocks_kernel,
+        in_specs=[hbm],
+        out_specs=hbm,
+        out_shape=pltpu.HBM(shape, w.dtype),
+        scratch_shapes=[pltpu.SemaphoreType.DMA((count,))],
+        cost_estimate=pl.CostEstimate(flops=0, bytes_accessed=6 * w.size, transcendentals=0),
+    )(in_hbm(w))
 
 
 def swap(mine):
@@ -338,17 +362,19 @@
         jnp.broadcast_to(latents[None], (8,) + latents.shape), CTX_CHIPS, split_axis=0, concat_axis=0, tiled=True
     )
     far = swap(near)
-    w_blocks = jnp.stack([w_out[:, i * columns : (i + 1) * columns] for i in range(group)] * 2)
-    w_blocks, _ = lax.optimization_barrier((w_blocks, near[0, :8]))
+    w_blocks, _ = lax.optimization_barrier((column_blocks(w_out, group, 8), near[0, :8]))
     w_near = lax.all_to_all(w_blocks, CTX_CHIPS, split_axis=0, concat_axis=0, tiled=True)
     ids = jnp.stack([lax.axis_index(CTX), core, lax.axis_index("x")]).astype(jnp.int32)
-    own = attend(ids, queries, w_kv, near, far, 4)
-    own, w_near = lax.optimization_barrier((own, w_near))
+    lower = attend(ids, queries, w_kv, near, far, 0, 2, 4)
+    before_lower, after_lower = up(lower), down(lower)
+    ids, _ = lax.optimization_barrier((ids, lower[:8, :128]))
+    upper = attend(ids, queries, w_kv, near, far, 1, 2, 4)
+    before_upper, after_upper = up(upper), down(upper)
+    left, right = up(before_lower), down(after_upper)
+    w_near, _ = lax.optimization_barrier((w_near, upper[:8, :128]))
     w_far = swap(w_near)
-    before, after = up(own), down(own)
-    half = own.shape[1] // 2
-    left, right = up(before[:, :half]), down(after[:, half:])
-    attn = project(ids, (own, before, after, left, right), w_near, w_far, 8, columns)
+    pieces = (lower, upper, after_lower, after_upper, left, right, before_lower, before_upper)
+    attn = project(ids, pieces, w_near, w_far, 8, columns)
     attn = lax.all_to_all(attn, EP + ("x",), split_axis=0, concat_axis=0, tiled=True)
     attn = jnp.sum(attn.reshape(8, group, tok, columns).astype(F32), axis=0)
     attn = attn.transpose(1, 0, 2).reshape(tok, width)

time: 190 us -> 227 us (1.19)
  blocking collectives: 40.7 us -> 80.6 us
  Pallas kernels: 21.3 us -> 53.5 us
  waiting for transfers between devices: 73.4 us -> 45.3 us
  local copies, waits for them, and re-layouts: 8.87 us -> 2.55 us
    all_to_all x0 -> x2, blocking collectives: none -> 40 us  [the longest x1 22.4 us: local(): lax.all_to_all(jnp.broadcast_to(latents[None], (8,) + latents.shape), CTX...]
    pallas_call x1 -> x3, Pallas kernels: 9.82 us -> 41.9 us  [the longest x1 29 us: column_blocks(): pl.pallas_call(blocks_kernel, in_specs=[hbm], out_specs=hbm, out_shape=pl...]
    all_to_all x2 -> x0, waiting for transfers between devices: 19.2 us -> none  [the longest x1 14.6 us: local(): lax.all_to_all(jnp.broadcast_to(latents[None], (8,) + latents.shape), CTX...]
    all_to_all x2 -> x0, starting transfers between devices: 9.75 us -> none  [the longest x1 6.2 us: local(): lax.all_to_all(jnp.broadcast_to(latents[None], (8,) + latents.shape), CTX...]
    ppermute x2 -> x3, waiting for transfers between devices: 8.88 us -> 1.22 us  [down(): return lax.ppermute(a, 'x', [(i, (i + 3) % 4) for i in range(4)])]
    unnamed x23 -> x14, local copies, waits for them, and re-layouts: 4.62 us -> 0.04 us
    ppermute x2 -> x3, starting transfers between devices: 2.3 us -> 5.56 us  [down(): return lax.ppermute(a, 'x', [(i, (i + 3) % 4) for i in range(4)])]
    ppermute x6, starting transfers between devices: 13.3 us -> 16 us  [swap(): return lax.ppermute(mine, 'core', SWAP)]
  transfers between devices with their start and end apart: 14 -> 14, of which waited for: 11 -> 8; matrix products, arithmetic and copies ran while one was open for 4% -> 1% of each run, Pallas kernels for 5% -> 19%
where the time goes in v14:
time: 227 us; the launch traced here: 225 us
  blocking collectives  80.6 us (36%)
  Pallas kernels  53.5 us (24%)
  waiting for transfers between devices  45.3 us (20%)
  starting transfers between devices  40.8 us (18%)
  local copies, waits for them, and re-layouts  2.55 us (1%)
    all_to_all x1, blocking collectives, exchange(): lax.all_to_all(units, CHIPS, split_axis=0, concat_axis=0, tiled=True)  40.6 us
    all_to_all x1, waiting for transfers between devices, exchange(): lax.all_to_all(units, CHIPS, split_axis=0, concat_axis=0, tiled=True)  30 us
    pallas_call x1, Pallas kernels, column_blocks(): pl.pallas_call(blocks_kernel, in_specs=[hbm], out_specs=hbm, out_shape=pl...  29 us
    all_to_all x1, blocking collectives, local(): lax.all_to_all(jnp.broadcast_to(latents[None], (8,) + latents.shape), CTX...  22.4 us
    all_to_all x1, blocking collectives, local(): lax.all_to_all(w_blocks, CTX_CHIPS, split_axis=0, concat_axis=0, tiled=True)  17.6 us
    ppermute x6, starting transfers between devices, swap(): return lax.ppermute(mine, 'core', SWAP)  16 us
    pallas_call x2, Pallas kernels, attend(): pl.pallas_call(functools.partial(attend_kernel, turn=turn, cuts=cuts), in...  13 us
    all_to_all x1, starting transfers between devices, local(): lax.all_to_all(attn, EP + ('x',), split_axis=0, concat_axis=0, tiled=True)  9.9 us
  transfers between devices with their start and end apart: 14, of which 8 were waited for; matrix products, arithmetic and copies ran while one was open for 1% of the time, Pallas kernels for 19%

profile of v14, /device:TPU:1, one launch (start us, length us, event | category | flops | bytes accessed | tf_op | source)
XLA Modules:
  0.0 225.4 jit_solution(17452688890480679471)
XLA Ops:
  0.6 1.1 broadcast_in_dim.32
  1.7 22.4 %all_to_all.25.near_ref = bf16[8,576,128]{2,1,0:T(8,128)(2,1)S(1)} all-to-all(bf16[8,576,128]{2,1,0:T(8,128)(2,1)S(1)} %broadcast_in_dim.32), channel_id=1, replica_groups=mesh['z_lo'=2,'x'=4,'core'=2,'z_hi'=2,'y'=4] {'z_lo','x'}, dimensions={0} | all-to-all | bytes 2359296 | tf_op jit(solution)/shard_map/all_to_all | solution.py:361
  24.1 1.7 collective-permute-start
  25.8 29.0 %shard_map.124 = bf16[8,64,896]{2,1,0:T(8,128)(2,1)} custom-call(bf16[64,3584]{1,0:T(8,128)(2,1)} %w_ref.1), custom_call_target="tpu_custom_call" | custom-call | bytes 1376256 | tf_op jit(solution)/shard_map/pallas_call | solution.py:299
  54.8 17.6 %all_to_all.26.refs_8_ = bf16[8,64,896]{2,1,0:T(8,128)(2,1)S(1)} all-to-all(bf16[8,64,896]{2,1,0:T(8,128)(2,1)} %shard_map.124), channel_id=1, replica_groups=mesh['z_lo'=2,'x'=4,'core'=2,'z_hi'=2,'y'=4] {'z_lo','x'}, dimensions={0} | all-to-all | bytes 1835008 | tf_op jit(solution)/shard_map/all_to_all | solution.py:366
  72.3 1.1 collective-permute-start.7
  73.5 0.1 pad_add_fusion.1.ids_ref
  73.6 0.0 collective-permute-done.far_ref
  73.6 6.5 %shard_map.122.refs_0_ = bf16[128,512]{1,0:T(8,128)(2,1)S(1)} custom-call(s32[3]{0:T(128)S(1)} %pad_add_fusion.1.ids_ref, bf16[128,1536]{1,0:T(8,128)(2,1)} %q_hbm.3, bf16[512,2048]{1,0:T(8,128)(2,1)} %w_hbm.3, bf16[8,576,128]{2,1,0:T(8,128)(2,1)S(1)} %all_to_all.25.near_ref, bf16[8,576,128]{2,1,0:T(8,128)(2,1)} %collective-permute-done.far_ref), custom_call_target="tpu_custom_call" | custom-call | flops 2281701376 | bytes 8000000 | tf_op jit(solution)/shard_map/pallas_call | solution.py:105
  80.1 0.6 collective-permute-start.3
  80.7 6.5 %shard_map.123.refs_1_ = bf16[128,512]{1,0:T(8,128)(2,1)S(1)} custom-call(s32[3]{0:T(128)S(1)} %pad_add_fusion.1.ids_ref, bf16[128,1536]{1,0:T(8,128)(2,1)} %q_hbm.3, bf16[512,2048]{1,0:T(8,128)(2,1)} %w_hbm.3, bf16[8,576,128]{2,1,0:T(8,128)(2,1)S(1)} %all_to_all.25.near_ref, bf16[8,576,128]{2,1,0:T(8,128)(2,1)} %collective-permute-done.far_ref), custom_call_target="tpu_custom_call" | custom-call | flops 2281701376 | bytes 8000000 | tf_op jit(solution)/shard_map/pallas_call | solution.py:105
  87.2 0.0 copy-start.6
  87.2 2.2 collective-permute-start.2
  89.4 0.1 collective-permute-start.1
  89.5 1.4 collective-permute-start.6
  90.8 0.0 collective-permute-done.3.refs_6_
  90.9 0.0 collective-permute-start.4
  90.9 1.2 collective-permute-done.2.refs_3_
  92.1 3.3 %collective-permute-start.5 = (bf16[128,512]{1,0:T(8,128)(2,1)S(1)}, bf16[128,512]{1,0:T(8,128)(2,1)S(1)}, u32[]{:S(2)}, u32[]{:S(2)}) collective-permute-start(bf16[128,512]{1,0:T(8,128)(2,1)S(1)} %collective-permute-done.2.refs_3_), channel_id=1, source_target_pairs={{0,48},{16,0},{32,16},{48,32},{1,49},{17,1},{33,17},{49,33},{2,50}... | collective-permute-start | bytes 393224 | tf_op jit(solution)/shard_map/ppermute | solution.py:318
  95.4 0.0 collective-permute-done.7.refs_9_
  95.4 2.6 %collective-permute-done.4.refs_4_ = bf16[128,512]{1,0:T(8,128)(2,1)S(1)} collective-permute-done((bf16[128,512]{1,0:T(8,128)(2,1)S(1)}, bf16[128,512]{1,0:T(8,128)(2,1)S(1)}, u32[]{:S(2)}, u32[]{:S(2)}) %collective-permute-start.4) | collective-permute-done | bytes 131104 | tf_op jit(solution)/shard_map/ppermute | solution.py:314
  98.0 3.0 %shard_map.125 = bf16[32,16,896]{2,1,0:T(8,128)(2,1)} custom-call(s32[3]{0:T(128)S(1)} %pad_add_fusion.1.ids_ref, bf16[128,512]{1,0:T(8,128)(2,1)S(1)} %shard_map.122.refs_0_, bf16[128,512]{1,0:T(8,128)(2,1)S(1)} %shard_map.123.refs_1_, bf16[128,512]{1,0:T(8,128)(2,1)S(1)} %collective-permute-done.1.refs_2_, ...), custom_call_target="tpu_custom_call" | custom-call | flops 939524096 | bytes 1835008 | tf_op jit(solution)/shard_map/pallas_call | solution.py:271
  101.0 9.9 %all-to-all-start.2 = ((bf16[32,16,896]{2,1,0:T(8,128)(2,1)}), bf16[32,16,896]{2,1,0:T(8,128)(2,1)S(1)}, u32[]{:S(2)}, u32[]{:S(2)}) async-start(bf16[32,16,896]{2,1,0:T(8,128)(2,1)} %shard_map.125), calls=%async_computation.2 | async-start | bytes 1835008 | tf_op jit(solution)/shard_map/all_to_all | solution.py:378
  110.9 3.3 %collective-permute-start.8 = (s32[16,8]{0,1:T(8,128)S(1)}, s32[16,8]{0,1:T(8,128)S(1)}, u32[]{:S(2)}, u32[]{:S(2)}) collective-permute-start(s32[16,8]{0,1:T(8,128)S(1)} %copy-done.6), channel_id=1, source_target_pairs={{0,8},{8,0},{1,9},{9,1},{2,10},{10,2},{3,11},{11,3},{4,12},{12,4},... | collective-permute-start | bytes 1544 | tf_op jit(solution)/shard_map/ppermute | solution.py:310
  114.2 0.1 and.46
  114.3 0.1 and.47
  114.4 0.7 collective-permute-done.8
  115.0 0.1 copy.46
  115.1 0.1 fusion.5
  115.2 0.1 copy.47
  115.4 0.1 copy.49
  115.5 0.1 copy.48
  115.6 8.6 %all-to-all-done.2 = bf16[32,16,896]{2,1,0:T(8,128)(2,1)S(1)} async-done(((bf16[32,16,896]{2,1,0:T(8,128)(2,1)}), bf16[32,16,896]{2,1,0:T(8,128)(2,1)S(1)}, u32[]{:S(2)}, u32[]{:S(2)}) %all-to-all-start.2) | async-done | bytes 917536 | tf_op jit(solution)/shard_map/all_to_all | solution.py:378
  124.1 0.1 convert_reduce_fusion
  124.3 0.2 fusion
  124.5 0.1 fusion.2
  124.6 4.5 %collective-permute-start.10 = (bf16[16,3584]{1,0:T(8,128)(2,1)S(1)}, bf16[16,3584]{1,0:T(8,128)(2,1)S(1)}, u32[]{:S(2)}, u32[]{:S(2)}) collective-permute-start(bf16[16,3584]{1,0:T(8,128)(2,1)S(1)} %fusion.2), channel_id=1, source_target_pairs={{0,8},{8,0},{1,9},{9,1},{2,10},{10,2},{3,11},{11,3},{4,12},{12,4},... | collective-permute-start | bytes 344072 | tf_op jit(solution)/shard_map/ppermute | solution.py:310
  129.1 0.1 bitcast_and_fusion
  129.2 0.1 copy.50
  129.3 0.1 broadcast_in_dim.33
  129.4 0.1 reshape.135
  129.6 0.5 collective-permute-done.10
  130.1 0.0 copy-start.1
  130.1 1.4 shard_map.126
  131.4 0.0 copy-start
  131.4 40.6 %all_to_all.27 = bf16[64,3,2,3584]{3,2,1,0:T(2,128)(2,1)S(1)} all-to-all(bf16[64,3,2,3584]{3,2,1,0:T(2,128)(2,1)S(1)} %bitcast.38), channel_id=1, replica_groups=mesh['z_lo'=2,'x'=4,'core'=2,'z_hi'=2,'y'=4] {'z_lo','x','z_hi','y'}, dimensions={0} | all-to-all | bytes 5505024 | tf_op jit(solution)/shard_map/all_to_all | solution.py:389
  172.1 5.9 %shard_map.127 = bf16[192,2,3584]{2,1,0:T(2,128)(2,1)} custom-call(bf16[192,2,3584]{2,1,0:T(2,128)(2,1)S(1)} %bitcast.39, bf16[3584,512]{1,0:T(8,128)(2,1)S(1)} %bitcast.40, bf16[3584,512]{1,0:T(8,128)(2,1)S(1)} %bitcast.41, bf16[512,3584]{1,0:T(8,128)(2,1)} %bitcast.44), custom_call_target="tpu_custom_call" | custom-call | flops 4227858432 | bytes 17000000 | tf_op jit(solution)/shard_map/pallas_call | solution.py:166
  177.9 0.0 copy-start.4
  177.9 7.4 %all-to-all-start.4 = ((bf16[64,3,2,3584]{3,2,1,0:T(2,128)(2,1)}), bf16[64,3,2,3584]{3,2,1,0:T(2,128)(2,1)S(1)}, u32[]{:S(2)}, u32[]{:S(2)}) async-start(bf16[64,3,2,3584]{3,2,1,0:T(2,128)(2,1)} %bitcast.42), calls=%async_computation.4 | async-start | bytes 5505024 | tf_op jit(solution)/shard_map/all_to_all | solution.py:389
  185.3 1.6 collective-permute-start.9
  186.9 0.1 copy.55
  187.0 0.7 collective-permute-done.9
  187.7 0.1 copy.51
  187.8 0.1 select_reduce_fusion
  188.0 0.1 copy.52
  188.1 0.1 copy.53
  188.1 0.1 copy.54
  188.2 0.1 broadcast_in_dim.65
  188.3 0.1 copy.56
  188.4 30.0 %all-to-all-done.4 = bf16[64,3,2,3584]{3,2,1,0:T(2,128)(2,1)S(1)} async-done(((bf16[64,3,2,3584]{3,2,1,0:T(2,128)(2,1)}), bf16[64,3,2,3584]{3,2,1,0:T(2,128)(2,1)S(1)}, u32[]{:S(2)}, u32[]{:S(2)}) %all-to-all-start.4) | async-done | bytes 2752544 | tf_op jit(solution)/shard_map/all_to_all | solution.py:389
  218.4 1.4 shard_map.128
  219.8 3.8 %collective-permute-start.11 = (f32[16,3584]{1,0:T(8,128)S(1)}, f32[16,3584]{1,0:T(8,128)S(1)}, u32[]{:S(2)}, u32[]{:S(2)}) collective-permute-start(f32[16,3584]{1,0:T(8,128)S(1)} %get-tuple-element.5), channel_id=1, source_target_pairs={{0,8},{8,0},{1,9},{9,1},{2,10},{10,2},{3,11},{11,3},{4,12},{12,4},... | collective-permute-start | bytes 688136 | tf_op jit(solution)/shard_map/ppermute | solution.py:310
  223.6 1.1 collective-permute-done.11
  224.7 0.7 fusion.4
  (32 shorter events, 0.3 us)
Async XLA Ops:
  24.1 49.5 %collective-permute-start = (bf16[8,576,128]{2,1,0:T(8,128)(2,1)S(1)}, bf16[8,576,128]{2,1,0:T(8,128)(2,1)}, u32[]{:S(2)}, u32[]{:S(2)}) collective-permute-start(bf16[8,576,128]{2,1,0:T(8,128)(2,1)S(1)} %all_to_all.25.near_ref), channel_id=1, source_target_pairs={{0,8},{8,0},{1,9},{9,1},{2,10},{10,2},{3,11},{11,3},{4,12},{12,4},... | collective-permute-start | bytes 3538952 | tf_op jit(solution)/shard_map/ppermute | solution.py:310
  72.3 23.1 %collective-permute-start.7 = (bf16[8,64,896]{2,1,0:T(8,128)(2,1)S(1)}, bf16[8,64,896]{2,1,0:T(8,128)(2,1)S(1)}, u32[]{:S(2)}, u32[]{:S(2)}) collective-permute-start(bf16[8,64,896]{2,1,0:T(8,128)(2,1)S(1)} %all_to_all.26.refs_8_), channel_id=1, source_target_pairs={{0,8},{8,0},{1,9},{9,1},{2,10},{10,2},{3,11},{11,3},{4,12},{12,4},... | collective-permute-start | bytes 2752520 | tf_op jit(solution)/shard_map/ppermute | solution.py:310
  80.1 10.8 %collective-permute-start.3 = (bf16[128,512]{1,0:T(8,128)(2,1)S(1)}, bf16[128,512]{1,0:T(8,128)(2,1)S(1)}, u32[]{:S(2)}, u32[]{:S(2)}) collective-permute-start(bf16[128,512]{1,0:T(8,128)(2,1)S(1)} %shard_map.122.refs_0_), channel_id=1, source_target_pairs={{0,16},{16,32},{32,48},{48,0},{1,17},{17,33},{33,49},{49,1},{2,18}... | collective-permute-start | bytes 393224 | tf_op jit(solution)/shard_map/ppermute | solution.py:314
  87.2 23.7 %copy-start.6 = (s32[16,8]{0,1:T(8,128)S(1)}, s32[16,8]{0,1:T(8,128)}, u32[]{:S(2)}) copy-start(s32[16,8]{0,1:T(8,128)} %param.17) | copy-start | bytes 1540
  87.2 4.9 %collective-permute-start.2 = (bf16[128,512]{1,0:T(8,128)(2,1)S(1)}, bf16[128,512]{1,0:T(8,128)(2,1)S(1)}, u32[]{:S(2)}, u32[]{:S(2)}) collective-permute-start(bf16[128,512]{1,0:T(8,128)(2,1)S(1)} %shard_map.123.refs_1_), channel_id=1, source_target_pairs={{0,48},{16,0},{32,16},{48,32},{1,49},{17,1},{33,17},{49,33},{2,50}... | collective-permute-start | bytes 393224 | tf_op jit(solution)/shard_map/ppermute | solution.py:318
  89.4 6.0 %collective-permute-start.1 = (bf16[128,512]{1,0:T(8,128)(2,1)S(1)}, bf16[128,512]{1,0:T(8,128)(2,1)S(1)}, u32[]{:S(2)}, u32[]{:S(2)}) collective-permute-start(bf16[128,512]{1,0:T(8,128)(2,1)S(1)} %shard_map.122.refs_0_), channel_id=1, source_target_pairs={{0,48},{16,0},{32,16},{48,32},{1,49},{17,1},{33,17},{49,33},{2,50}... | collective-permute-start | bytes 393224 | tf_op jit(solution)/shard_map/ppermute | solution.py:318
  89.5 6.0 %collective-permute-start.6 = (bf16[128,512]{1,0:T(8,128)(2,1)S(1)}, bf16[128,512]{1,0:T(8,128)(2,1)S(1)}, u32[]{:S(2)}, u32[]{:S(2)}) collective-permute-start(bf16[128,512]{1,0:T(8,128)(2,1)S(1)} %shard_map.123.refs_1_), channel_id=1, source_target_pairs={{0,16},{16,32},{32,48},{48,0},{1,17},{17,33},{33,49},{49,1},{2,18}... | collective-permute-start | bytes 393224 | tf_op jit(solution)/shard_map/ppermute | solution.py:314
  90.9 7.1 %collective-permute-start.4 = (bf16[128,512]{1,0:T(8,128)(2,1)S(1)}, bf16[128,512]{1,0:T(8,128)(2,1)S(1)}, u32[]{:S(2)}, u32[]{:S(2)}) collective-permute-start(bf16[128,512]{1,0:T(8,128)(2,1)S(1)} %collective-permute-done.3.refs_6_), channel_id=1, source_target_pairs={{0,16},{16,32},{32,48},{48,0},{1,17},{17,33},{33,49},{49,1},{2,18}... | collective-permute-start | bytes 393224 | tf_op jit(solution)/shard_map/ppermute | solution.py:314
  92.1 5.9 %collective-permute-start.5 = (bf16[128,512]{1,0:T(8,128)(2,1)S(1)}, bf16[128,512]{1,0:T(8,128)(2,1)S(1)}, u32[]{:S(2)}, u32[]{:S(2)}) collective-permute-start(bf16[128,512]{1,0:T(8,128)(2,1)S(1)} %collective-permute-done.2.refs_3_), channel_id=1, source_target_pairs={{0,48},{16,0},{32,16},{48,32},{1,49},{17,1},{33,17},{49,33},{2,50}... | collective-permute-start | bytes 393224 | tf_op jit(solution)/shard_map/ppermute | solution.py:318
  101.0 23.3 %copy-start.3 = (bf16[16,3584]{1,0:T(8,128)(2,1)S(1)}, bf16[16,3584]{1,0:T(8,128)(2,1)}, u32[]{:S(2)}) copy-start(bf16[16,3584]{1,0:T(8,128)(2,1)} %param.15) | copy-start | bytes 344068
  101.0 23.5 %copy-start.5 = (f32[3584]{0:T(1024)S(1)}, f32[3584]{0:T(1024)}, u32[]{:S(2)}) copy-start(f32[3584]{0:T(1024)} %param.16) | copy-start | bytes 43012
  101.0 23.2 %all-to-all-start.2 = ((bf16[32,16,896]{2,1,0:T(8,128)(2,1)}), bf16[32,16,896]{2,1,0:T(8,128)(2,1)S(1)}, u32[]{:S(2)}, u32[]{:S(2)}) async-start(bf16[32,16,896]{2,1,0:T(8,128)(2,1)} %shard_map.125), calls=%async_computation.2 | async-start | bytes 1835008 | tf_op jit(solution)/shard_map/all_to_all | solution.py:378
  110.9 4.1 %collective-permute-start.8 = (s32[16,8]{0,1:T(8,128)S(1)}, s32[16,8]{0,1:T(8,128)S(1)}, u32[]{:S(2)}, u32[]{:S(2)}) collective-permute-start(s32[16,8]{0,1:T(8,128)S(1)} %copy-done.6), channel_id=1, source_target_pairs={{0,8},{8,0},{1,9},{9,1},{2,10},{10,2},{3,11},{11,3},{4,12},{12,4},... | collective-permute-start | bytes 1544 | tf_op jit(solution)/shard_map/ppermute | solution.py:310
  124.5 100.2 %copy-start.2 = (bf16[16,3584]{1,0:T(8,128)(2,1)}, bf16[16,3584]{1,0:T(8,128)(2,1)S(1)}, u32[]{:S(2)}) copy-start(bf16[16,3584]{1,0:T(8,128)(2,1)S(1)} %get-tuple-element.7) | copy-start | bytes 344068
  124.6 5.5 %collective-permute-start.10 = (bf16[16,3584]{1,0:T(8,128)(2,1)S(1)}, bf16[16,3584]{1,0:T(8,128)(2,1)S(1)}, u32[]{:S(2)}, u32[]{:S(2)}) collective-permute-start(bf16[16,3584]{1,0:T(8,128)(2,1)S(1)} %fusion.2), channel_id=1, source_target_pairs={{0,8},{8,0},{1,9},{9,1},{2,10},{10,2},{3,11},{11,3},{4,12},{12,4},... | collective-permute-start | bytes 344072 | tf_op jit(solution)/shard_map/ppermute | solution.py:310
  130.1 42.0 %copy-start.1 = (bf16[1,3584,512]{2,1,0:T(8,128)(2,1)S(1)}, bf16[1,3584,512]{2,1,0:T(8,128)(2,1)}, u32[]{:S(2)}) copy-start(bf16[1,3584,512]{2,1,0:T(8,128)(2,1)} %param.20) | copy-start | bytes 11010052
  131.4 40.6 %copy-start = (bf16[1,3584,512]{2,1,0:T(8,128)(2,1)S(1)}, bf16[1,3584,512]{2,1,0:T(8,128)(2,1)}, u32[]{:S(2)}) copy-start(bf16[1,3584,512]{2,1,0:T(8,128)(2,1)} %param.19) | copy-start | bytes 11010052
  177.9 7.4 %copy-start.4 = (s32[16,8]{0,1:T(8,128)S(1)}, s32[16,8]{0,1:T(8,128)}, u32[]{:S(2)}) copy-start(s32[16,8]{0,1:T(8,128)} %param.18) | copy-start | bytes 1540
  177.9 40.5 %all-to-all-start.4 = ((bf16[64,3,2,3584]{3,2,1,0:T(2,128)(2,1)}), bf16[64,3,2,3584]{3,2,1,0:T(2,128)(2,1)S(1)}, u32[]{:S(2)}, u32[]{:S(2)}) async-start(bf16[64,3,2,3584]{3,2,1,0:T(2,128)(2,1)} %bitcast.42), calls=%async_computation.4 | async-start | bytes 5505024 | tf_op jit(solution)/shard_map/all_to_all | solution.py:389
  185.3 2.4 %collective-permute-start.9 = (f32[16,8]{0,1:T(8,128)S(1)}, f32[16,8]{0,1:T(8,128)S(1)}, u32[]{:S(2)}, u32[]{:S(2)}) collective-permute-start(f32[16,8]{0,1:T(8,128)S(1)} %convert_divide_fusion), channel_id=1, source_target_pairs={{0,8},{8,0},{1,9},{9,1},{2,10},{10,2},{3,11},{11,3},{4,12},{12,4},... | collective-permute-start | bytes 1544 | tf_op jit(solution)/shard_map/ppermute | solution.py:310
  219.8 4.9 %collective-permute-start.11 = (f32[16,3584]{1,0:T(8,128)S(1)}, f32[16,3584]{1,0:T(8,128)S(1)}, u32[]{:S(2)}, u32[]{:S(2)}) collective-permute-start(f32[16,3584]{1,0:T(8,128)S(1)} %get-tuple-element.5), channel_id=1, source_target_pairs={{0,8},{8,0},{1,9},{9,1},{2,10},{10,2},{3,11},{11,3},{4,12},{12,4},... | collective-permute-start | bytes 688136 | tf_op jit(solution)/shard_map/ppermute | solution.py:310

commit v15 on v13

--- a/solution.py
+++ b/solution.py
@@ -282,6 +282,30 @@
     )(ids, *pieces, near, far)
 
 
+def blocks_kernel(w_ref, out_ref, sems):
+    wide = out_ref.shape[2]
+    group = w_ref.shape[1] // wide
+    copies = []
+    for i in range(out_ref.shape[0]):
+        first = i % group * wide
+        copies.append(pltpu.make_async_copy(w_ref.at[:, first : first + wide], out_ref.at[i], sems.at[i]))
+        copies[-1].start()
+    for copy in copies:
+        copy.wait()
+
+
+def column_blocks(w, group, count):
+    shape = (count, w.shape[0], w.shape[1] // group)
+    return pl.pallas_call(
+        blocks_kernel,
+        in_specs=[pl.BlockSpec(memory_space=pltpu.VMEM)],
+        out_specs=pl.BlockSpec(memory_space=pltpu.HBM),
+        out_shape=pltpu.HBM(shape, w.dtype),
+        scratch_shapes=[pltpu.SemaphoreType.DMA((count,))],
+        cost_estimate=pl.CostEstimate(flops=0, bytes_accessed=6 * w.size, transcendentals=0),
+    )(w)
+
+
 def swap(mine):
     return lax.ppermute(mine, "core", SWAP)
 
@@ -338,14 +362,12 @@
         jnp.broadcast_to(latents[None], (8,) + latents.shape), CTX_CHIPS, split_axis=0, concat_axis=0, tiled=True
     )
     far = swap(near)
-    w_blocks = jnp.stack([w_out[:, i * columns : (i + 1) * columns] for i in range(group)] * 2)
-    w_blocks, _ = lax.optimization_barrier((w_blocks, near[0, :8]))
+    w_blocks, _ = lax.optimization_barrier((column_blocks(w_out, group, 8), near[0, :8]))
     w_near = lax.all_to_all(w_blocks, CTX_CHIPS, split_axis=0, concat_axis=0, tiled=True)
     ids = jnp.stack([lax.axis_index(CTX), core, lax.axis_index("x")]).astype(jnp.int32)
     own = attend(ids, queries, w_kv, near, far, 4)
-    own, w_near = lax.optimization_barrier((own, w_near))
+    before, after, w_near = lax.optimization_barrier((up(own), down(own), w_near))
     w_far = swap(w_near)
-    before, after = up(own), down(own)
     half = own.shape[1] // 2
     left, right = up(before[:, :half]), down(after[:, half:])
     attn = project(ids, (own, before, after, left, right), w_near, w_far, 8, columns)

time: 190 us -> 188 us (0.989)
  blocking collectives: 40.7 us -> 63.2 us
  waiting for transfers between devices: 73.4 us -> 59 us
  local copies, waits for them, and re-layouts: 8.87 us -> 2.57 us
  starting transfers between devices: 41.5 us -> 35.5 us
  Pallas kernels: 21.3 us -> 23.3 us
    all_to_all x0 -> x1, blocking collectives: none -> 22.4 us  [local(): lax.all_to_all(jnp.broadcast_to(latents[None], (8,) + latents.shape), CTX...]
    all_to_all x1 -> x0, waiting for transfers between devices: 14.6 us -> none  [local(): lax.all_to_all(jnp.broadcast_to(latents[None], (8,) + latents.shape), CTX...]
    all_to_all x1 -> x0, starting transfers between devices: 6.2 us -> none  [local(): lax.all_to_all(jnp.broadcast_to(latents[None], (8,) + latents.shape), CTX...]
    unnamed x23 -> x14, local copies, waits for them, and re-layouts: 4.62 us -> 0.04 us
    all_to_all x1, waiting for transfers between devices: 9.91 us -> 12.9 us  [local(): lax.all_to_all(attn, EP + ('x',), split_axis=0, concat_axis=0, tiled=True)]
    all_to_all x1, waiting for transfers between devices: 4.56 us -> 1.92 us  [local(): lax.all_to_all(w_blocks, CTX_CHIPS, split_axis=0, concat_axis=0, tiled=True)]
    pallas_call x0 -> x1, Pallas kernels: none -> 2.03 us  [column_blocks(): pl.pallas_call(blocks_kernel, in_specs=[pl.BlockSpec(memory_space=pltpu.V...]
  transfers between devices with their start and end apart: 14 -> 13, of which waited for: 11 -> 11; matrix products, arithmetic and copies ran while one was open for 4% -> 1% of each run, Pallas kernels for 5% -> 6%
where the time goes in v15:
time: 188 us; the launch traced here: 186 us
  blocking collectives  63.2 us (34%)
  waiting for transfers between devices  59 us (31%)
  starting transfers between devices  35.5 us (19%)
  Pallas kernels  23.3 us (12%)
  local copies, waits for them, and re-layouts  2.57 us (1%)
    all_to_all x1, blocking collectives, exchange(): lax.all_to_all(units, CHIPS, split_axis=0, concat_axis=0, tiled=True)  40.8 us
    all_to_all x1, waiting for transfers between devices, exchange(): lax.all_to_all(units, CHIPS, split_axis=0, concat_axis=0, tiled=True)  30 us
    all_to_all x1, blocking collectives, local(): lax.all_to_all(jnp.broadcast_to(latents[None], (8,) + latents.shape), CTX...  22.4 us
    all_to_all x1, waiting for transfers between devices, local(): lax.all_to_all(attn, EP + ('x',), split_axis=0, concat_axis=0, tiled=True)  12.9 us
    ppermute x6, starting transfers between devices, swap(): return lax.ppermute(mine, 'core', SWAP)  12.3 us
    pallas_call x1, Pallas kernels, attend(): pl.pallas_call(functools.partial(attend_kernel, cuts=cuts), in_specs=[pl....  9.82 us
    all_to_all x1, starting transfers between devices, local(): lax.all_to_all(attn, EP + ('x',), split_axis=0, concat_axis=0, tiled=True)  8.18 us
    all_to_all x1, starting transfers between devices, exchange(): lax.all_to_all(units, CHIPS, split_axis=0, concat_axis=0, tiled=True)  7.35 us
  transfers between devices with their start and end apart: 13, of which 11 were waited for; matrix products, arithmetic and copies ran while one was open for 1% of the time, Pallas kernels for 6%

profile of v15, /device:TPU:1, one launch (start us, length us, event | category | flops | bytes accessed | tf_op | source)
XLA Modules:
  0.0 186.3 jit_solution(16374370788864371525)
XLA Ops:
  0.6 1.1 broadcast_in_dim.32
  1.7 22.4 %all_to_all.25.near_ref = bf16[8,576,128]{2,1,0:T(8,128)(2,1)S(1)} all-to-all(bf16[8,576,128]{2,1,0:T(8,128)(2,1)S(1)} %broadcast_in_dim.32), channel_id=1, replica_groups=mesh['z_lo'=2,'x'=4,'core'=2,'z_hi'=2,'y'=4] {'z_lo','x'}, dimensions={0} | all-to-all | bytes 2359296 | tf_op jit(solution)/shard_map/all_to_all | solution.py:361
  24.1 1.7 collective-permute-start
  25.8 2.0 %shard_map.123 = bf16[8,64,896]{2,1,0:T(8,128)(2,1)} custom-call(bf16[64,3584]{1,0:T(8,128)(2,1)} %w_ref.1), custom_call_target="tpu_custom_call" | custom-call | bytes 1376256 | tf_op jit(solution)/shard_map/pallas_call | solution.py:299
  27.8 3.6 %all-to-all-start.1 = ((bf16[8,64,896]{2,1,0:T(8,128)(2,1)}), bf16[8,64,896]{2,1,0:T(8,128)(2,1)S(1)}, u32[]{:S(2)}, u32[]{:S(2)}) async-start(bf16[8,64,896]{2,1,0:T(8,128)(2,1)} %shard_map.123), calls=%async_computation.1 | async-start | bytes 1835008 | tf_op jit(solution)/shard_map/all_to_all | solution.py:366
  31.4 0.1 pad_add_fusion.1.ids_ref
  31.5 0.0 collective-permute-done.far_ref
  31.5 9.8 %shard_map.122.own_ref = bf16[128,1024]{1,0:T(8,128)(2,1)S(1)} custom-call(s32[3]{0:T(128)S(1)} %pad_add_fusion.1.ids_ref, bf16[128,1536]{1,0:T(8,128)(2,1)} %q_hbm.1, bf16[512,2048]{1,0:T(8,128)(2,1)} %w_hbm.1, bf16[8,576,128]{2,1,0:T(8,128)(2,1)S(1)} %all_to_all.25.near_ref, bf16[8,576,128]{2,1,0:T(8,128)(2,1)S(1)} %collective-permute-done.far_ref), custom_call_target="tpu_custom_call" | custom-call | flops 4563402752 | bytes 8000000 | tf_op jit(solution)/shard_map/pallas_call | solution.py:103
  41.3 2.6 %collective-permute-start.2 = (bf16[128,1024]{1,0:T(8,128)(2,1)S(1)}, bf16[128,1024]{1,0:T(8,128)(2,1)S(1)}, u32[]{:S(2)}, u32[]{:S(2)}) collective-permute-start(bf16[128,1024]{1,0:T(8,128)(2,1)S(1)} %shard_map.122.own_ref), channel_id=1, source_target_pairs={{0,48},{16,0},{32,16},{48,32},{1,49},{17,1},{33,17},{49,33},{2,50}... | collective-permute-start | bytes 786440 | tf_op jit(solution)/shard_map/ppermute | solution.py:318
  44.0 0.0 collective-permute-start.1
  44.0 1.9 %all-to-all-done.1.near_ref = bf16[8,64,896]{2,1,0:T(8,128)(2,1)S(1)} async-done(((bf16[8,64,896]{2,1,0:T(8,128)(2,1)}), bf16[8,64,896]{2,1,0:T(8,128)(2,1)S(1)}, u32[]{:S(2)}, u32[]{:S(2)}) %all-to-all-start.1) | async-done | bytes 917536 | tf_op jit(solution)/shard_map/all_to_all | solution.py:366
  45.9 3.5 %collective-permute-done.2.after_ref = bf16[128,1024]{1,0:T(8,128)(2,1)S(1)} collective-permute-done((bf16[128,1024]{1,0:T(8,128)(2,1)S(1)}, bf16[128,1024]{1,0:T(8,128)(2,1)S(1)}, u32[]{:S(2)}, u32[]{:S(2)}) %collective-permute-start.2) | collective-permute-done | bytes 262176 | tf_op jit(solution)/shard_map/ppermute | solution.py:318
  49.4 3.1 %collective-permute-done.1.before_ref = bf16[128,1024]{1,0:T(8,128)(2,1)S(1)} collective-permute-done((bf16[128,1024]{1,0:T(8,128)(2,1)S(1)}, bf16[128,1024]{1,0:T(8,128)(2,1)S(1)}, u32[]{:S(2)}, u32[]{:S(2)}) %collective-permute-start.1) | collective-permute-done | bytes 262176 | tf_op jit(solution)/shard_map/ppermute | solution.py:314
  52.5 1.4 collective-permute-start.5
  53.9 0.0 copy-start.6
  53.9 0.1 collective-permute-start.4
  54.0 1.5 collective-permute-start.3
  55.5 3.7 %collective-permute-done.4.right_ref = bf16[128,512]{1,0:T(8,128)(2,1)S(1)} collective-permute-done((bf16[128,512]{1,0:T(8,128)(2,1)S(1)}, bf16[128,512]{1,0:T(8,128)(2,1)S(1)}, u32[]{:S(2)}, u32[]{:S(2)}) %collective-permute-start.4) | collective-permute-done | bytes 131104 | tf_op jit(solution)/shard_map/ppermute | solution.py:318
  59.1 1.1 collective-permute-done.3.left_ref
  60.2 0.0 collective-permute-done.5.far_ref
  60.2 2.9 %shard_map.124 = bf16[32,16,896]{2,1,0:T(8,128)(2,1)} custom-call(s32[3]{0:T(128)S(1)} %pad_add_fusion.1.ids_ref, bf16[128,1024]{1,0:T(8,128)(2,1)S(1)} %shard_map.122.own_ref, bf16[128,1024]{1,0:T(8,128)(2,1)S(1)} %collective-permute-done.1.before_ref, bf16[128,1024]{1,0:T(8,128)(2,1)S(1)} %collective-permute-done.2.after_ref, ...), custom_call_target="tpu_custom_call" | custom-call | flops 939524096 | bytes 1835008 | tf_op jit(solution)/shard_map/pallas_call | solution.py:272
  63.1 8.2 %all-to-all-start.2 = ((bf16[32,16,896]{2,1,0:T(8,128)(2,1)}), bf16[32,16,896]{2,1,0:T(8,128)(2,1)S(1)}, u32[]{:S(2)}, u32[]{:S(2)}) async-start(bf16[32,16,896]{2,1,0:T(8,128)(2,1)} %shard_map.124), calls=%async_computation.2 | async-start | bytes 1835008 | tf_op jit(solution)/shard_map/all_to_all | solution.py:374
  71.3 0.0 copy-done.6
  71.3 1.1 collective-permute-start.6
  72.4 0.1 and.46
  72.5 0.1 and.47
  72.6 0.7 collective-permute-done.6
  73.3 0.1 copy.46
  73.3 0.1 fusion.5
  73.5 0.1 copy.47
  73.6 0.1 copy.49
  73.7 0.1 copy.48
  73.8 12.9 %all-to-all-done.2 = bf16[32,16,896]{2,1,0:T(8,128)(2,1)S(1)} async-done(((bf16[32,16,896]{2,1,0:T(8,128)(2,1)}), bf16[32,16,896]{2,1,0:T(8,128)(2,1)S(1)}, u32[]{:S(2)}, u32[]{:S(2)}) %all-to-all-start.2) | async-done | bytes 917536 | tf_op jit(solution)/shard_map/all_to_all | solution.py:374
  86.7 0.1 convert_reduce_fusion
  86.8 0.2 fusion
  87.0 0.1 fusion.2
  87.1 2.6 %collective-permute-start.8 = (bf16[16,3584]{1,0:T(8,128)(2,1)S(1)}, bf16[16,3584]{1,0:T(8,128)(2,1)S(1)}, u32[]{:S(2)}, u32[]{:S(2)}) collective-permute-start(bf16[16,3584]{1,0:T(8,128)(2,1)S(1)} %fusion.2), channel_id=1, source_target_pairs={{0,8},{8,0},{1,9},{9,1},{2,10},{10,2},{3,11},{11,3},{4,12},{12,4},... | collective-permute-start | bytes 344072 | tf_op jit(solution)/shard_map/ppermute | solution.py:310
  89.8 0.1 bitcast_and_fusion
  89.9 0.1 copy.50
  90.0 0.1 broadcast_in_dim.33
  90.1 0.1 reshape.135
  90.3 0.5 collective-permute-done.8
  90.7 0.0 copy-start.1
  90.8 1.4 shard_map.125
  92.1 0.0 copy-start
  92.1 40.8 %all_to_all.26 = bf16[64,3,2,3584]{3,2,1,0:T(2,128)(2,1)S(1)} all-to-all(bf16[64,3,2,3584]{3,2,1,0:T(2,128)(2,1)S(1)} %bitcast.38), channel_id=1, replica_groups=mesh['z_lo'=2,'x'=4,'core'=2,'z_hi'=2,'y'=4] {'z_lo','x','z_hi','y'}, dimensions={0} | all-to-all | bytes 5505024 | tf_op jit(solution)/shard_map/all_to_all | solution.py:385
  132.9 5.8 %shard_map.126 = bf16[192,2,3584]{2,1,0:T(2,128)(2,1)} custom-call(bf16[192,2,3584]{2,1,0:T(2,128)(2,1)S(1)} %bitcast.39, bf16[3584,512]{1,0:T(8,128)(2,1)S(1)} %bitcast.40, bf16[3584,512]{1,0:T(8,128)(2,1)S(1)} %bitcast.41, bf16[512,3584]{1,0:T(8,128)(2,1)} %bitcast.44), custom_call_target="tpu_custom_call" | custom-call | flops 4227858432 | bytes 17000000 | tf_op jit(solution)/shard_map/pallas_call | solution.py:164
  138.8 0.0 copy-start.4
  138.8 7.3 %all-to-all-start.4 = ((bf16[64,3,2,3584]{3,2,1,0:T(2,128)(2,1)}), bf16[64,3,2,3584]{3,2,1,0:T(2,128)(2,1)S(1)}, u32[]{:S(2)}, u32[]{:S(2)}) async-start(bf16[64,3,2,3584]{3,2,1,0:T(2,128)(2,1)} %bitcast.42), calls=%async_computation.4 | async-start | bytes 5505024 | tf_op jit(solution)/shard_map/all_to_all | solution.py:385
  146.2 1.6 collective-permute-start.7
  147.8 0.1 copy.55
  147.9 0.7 collective-permute-done.7
  148.6 0.1 copy.51
  148.7 0.1 select_reduce_fusion
  148.8 0.1 copy.52
  148.9 0.1 copy.53
  149.0 0.1 copy.54
  149.1 0.1 broadcast_in_dim.65
  149.2 0.1 copy.56
  149.3 30.0 %all-to-all-done.4 = bf16[64,3,2,3584]{3,2,1,0:T(2,128)(2,1)S(1)} async-done(((bf16[64,3,2,3584]{3,2,1,0:T(2,128)(2,1)}), bf16[64,3,2,3584]{3,2,1,0:T(2,128)(2,1)S(1)}, u32[]{:S(2)}, u32[]{:S(2)}) %all-to-all-start.4) | async-done | bytes 2752544 | tf_op jit(solution)/shard_map/all_to_all | solution.py:385
  179.3 1.4 shard_map.127
  180.7 3.8 %collective-permute-start.9 = (f32[16,3584]{1,0:T(8,128)S(1)}, f32[16,3584]{1,0:T(8,128)S(1)}, u32[]{:S(2)}, u32[]{:S(2)}) collective-permute-start(f32[16,3584]{1,0:T(8,128)S(1)} %get-tuple-element.11), channel_id=1, source_target_pairs={{0,8},{8,0},{1,9},{9,1},{2,10},{10,2},{3,11},{11,3},{4,12},{12,4},... | collective-permute-start | bytes 688136 | tf_op jit(solution)/shard_map/ppermute | solution.py:310
  184.5 1.1 collective-permute-done.9
  185.6 0.7 fusion.4
  (30 shorter events, 0.3 us)
Async XLA Ops:
  24.1 7.4 %collective-permute-start = (bf16[8,576,128]{2,1,0:T(8,128)(2,1)S(1)}, bf16[8,576,128]{2,1,0:T(8,128)(2,1)S(1)}, u32[]{:S(2)}, u32[]{:S(2)}) collective-permute-start(bf16[8,576,128]{2,1,0:T(8,128)(2,1)S(1)} %all_to_all.25.near_ref), channel_id=1, source_target_pairs={{0,8},{8,0},{1,9},{9,1},{2,10},{10,2},{3,11},{11,3},{4,12},{12,4},... | collective-permute-start | bytes 3538952 | tf_op jit(solution)/shard_map/ppermute | solution.py:310
  27.8 18.1 %all-to-all-start.1 = ((bf16[8,64,896]{2,1,0:T(8,128)(2,1)}), bf16[8,64,896]{2,1,0:T(8,128)(2,1)S(1)}, u32[]{:S(2)}, u32[]{:S(2)}) async-start(bf16[8,64,896]{2,1,0:T(8,128)(2,1)} %shard_map.123), calls=%async_computation.1 | async-start | bytes 1835008 | tf_op jit(solution)/shard_map/all_to_all | solution.py:366
  41.3 8.1 %collective-permute-start.2 = (bf16[128,1024]{1,0:T(8,128)(2,1)S(1)}, bf16[128,1024]{1,0:T(8,128)(2,1)S(1)}, u32[]{:S(2)}, u32[]{:S(2)}) collective-permute-start(bf16[128,1024]{1,0:T(8,128)(2,1)S(1)} %shard_map.122.own_ref), channel_id=1, source_target_pairs={{0,48},{16,0},{32,16},{48,32},{1,49},{17,1},{33,17},{49,33},{2,50}... | collective-permute-start | bytes 786440 | tf_op jit(solution)/shard_map/ppermute | solution.py:318
  44.0 8.5 %collective-permute-start.1 = (bf16[128,1024]{1,0:T(8,128)(2,1)S(1)}, bf16[128,1024]{1,0:T(8,128)(2,1)S(1)}, u32[]{:S(2)}, u32[]{:S(2)}) collective-permute-start(bf16[128,1024]{1,0:T(8,128)(2,1)S(1)} %shard_map.122.own_ref), channel_id=1, source_target_pairs={{0,16},{16,32},{32,48},{48,0},{1,17},{17,33},{33,49},{49,1},{2,18}... | collective-permute-start | bytes 786440 | tf_op jit(solution)/shard_map/ppermute | solution.py:314
  52.5 7.7 %collective-permute-start.5 = (bf16[8,64,896]{2,1,0:T(8,128)(2,1)S(1)}, bf16[8,64,896]{2,1,0:T(8,128)(2,1)S(1)}, u32[]{:S(2)}, u32[]{:S(2)}) collective-permute-start(bf16[8,64,896]{2,1,0:T(8,128)(2,1)S(1)} %all-to-all-done.1.near_ref), channel_id=1, source_target_pairs={{0,8},{8,0},{1,9},{9,1},{2,10},{10,2},{3,11},{11,3},{4,12},{12,4},... | collective-permute-start | bytes 2752520 | tf_op jit(solution)/shard_map/ppermute | solution.py:310
  53.9 17.4 %copy-start.6 = (s32[16,8]{0,1:T(8,128)S(1)}, s32[16,8]{0,1:T(8,128)}, u32[]{:S(2)}) copy-start(s32[16,8]{0,1:T(8,128)} %param.17) | copy-start | bytes 1540
  53.9 5.2 %collective-permute-start.4 = (bf16[128,512]{1,0:T(8,128)(2,1)S(1)}, bf16[128,512]{1,0:T(8,128)(2,1)S(1)}, u32[]{:S(2)}, u32[]{:S(2)}) collective-permute-start(bf16[128,512]{1,0:T(8,128)(2,1)S(1)} %slice.20), channel_id=1, source_target_pairs={{0,48},{16,0},{32,16},{48,32},{1,49},{17,1},{33,17},{49,33},{2,50}... | collective-permute-start | bytes 393224 | tf_op jit(solution)/shard_map/ppermute | solution.py:318
  54.0 6.2 %collective-permute-start.3 = (bf16[128,512]{1,0:T(8,128)(2,1)S(1)}, bf16[128,512]{1,0:T(8,128)(2,1)S(1)}, u32[]{:S(2)}, u32[]{:S(2)}) collective-permute-start(bf16[128,512]{1,0:T(8,128)(2,1)S(1)} %slice.19), channel_id=1, source_target_pairs={{0,16},{16,32},{32,48},{48,0},{1,17},{17,33},{33,49},{49,1},{2,18}... | collective-permute-start | bytes 393224 | tf_op jit(solution)/shard_map/ppermute | solution.py:314
  63.1 23.7 %copy-start.3 = (bf16[16,3584]{1,0:T(8,128)(2,1)S(1)}, bf16[16,3584]{1,0:T(8,128)(2,1)}, u32[]{:S(2)}) copy-start(bf16[16,3584]{1,0:T(8,128)(2,1)} %param.15) | copy-start | bytes 344068
  63.1 23.9 %copy-start.5 = (f32[3584]{0:T(1024)S(1)}, f32[3584]{0:T(1024)}, u32[]{:S(2)}) copy-start(f32[3584]{0:T(1024)} %param.16) | copy-start | bytes 43012
  63.1 23.6 %all-to-all-start.2 = ((bf16[32,16,896]{2,1,0:T(8,128)(2,1)}), bf16[32,16,896]{2,1,0:T(8,128)(2,1)S(1)}, u32[]{:S(2)}, u32[]{:S(2)}) async-start(bf16[32,16,896]{2,1,0:T(8,128)(2,1)} %shard_map.124), calls=%async_computation.2 | async-start | bytes 1835008 | tf_op jit(solution)/shard_map/all_to_all | solution.py:374
  71.3 2.0 %collective-permute-start.6 = (s32[16,8]{0,1:T(8,128)S(1)}, s32[16,8]{0,1:T(8,128)S(1)}, u32[]{:S(2)}, u32[]{:S(2)}) collective-permute-start(s32[16,8]{0,1:T(8,128)S(1)} %copy-done.6), channel_id=1, source_target_pairs={{0,8},{8,0},{1,9},{9,1},{2,10},{10,2},{3,11},{11,3},{4,12},{12,4},... | collective-permute-start | bytes 1544 | tf_op jit(solution)/shard_map/ppermute | solution.py:310
  87.0 98.6 %copy-start.2 = (bf16[16,3584]{1,0:T(8,128)(2,1)}, bf16[16,3584]{1,0:T(8,128)(2,1)S(1)}, u32[]{:S(2)}) copy-start(bf16[16,3584]{1,0:T(8,128)(2,1)S(1)} %get-tuple-element.13) | copy-start | bytes 344068
  87.1 3.6 %collective-permute-start.8 = (bf16[16,3584]{1,0:T(8,128)(2,1)S(1)}, bf16[16,3584]{1,0:T(8,128)(2,1)S(1)}, u32[]{:S(2)}, u32[]{:S(2)}) collective-permute-start(bf16[16,3584]{1,0:T(8,128)(2,1)S(1)} %fusion.2), channel_id=1, source_target_pairs={{0,8},{8,0},{1,9},{9,1},{2,10},{10,2},{3,11},{11,3},{4,12},{12,4},... | collective-permute-start | bytes 344072 | tf_op jit(solution)/shard_map/ppermute | solution.py:310
  90.7 42.2 %copy-start.1 = (bf16[1,3584,512]{2,1,0:T(8,128)(2,1)S(1)}, bf16[1,3584,512]{2,1,0:T(8,128)(2,1)}, u32[]{:S(2)}) copy-start(bf16[1,3584,512]{2,1,0:T(8,128)(2,1)} %param.20) | copy-start | bytes 11010052
  92.1 40.8 %copy-start = (bf16[1,3584,512]{2,1,0:T(8,128)(2,1)S(1)}, bf16[1,3584,512]{2,1,0:T(8,128)(2,1)}, u32[]{:S(2)}) copy-start(bf16[1,3584,512]{2,1,0:T(8,128)(2,1)} %param.19) | copy-start | bytes 11010052
  138.8 7.4 %copy-start.4 = (s32[16,8]{0,1:T(8,128)S(1)}, s32[16,8]{0,1:T(8,128)}, u32[]{:S(2)}) copy-start(s32[16,8]{0,1:T(8,128)} %param.18) | copy-start | bytes 1540
  138.8 40.5 %all-to-all-start.4 = ((bf16[64,3,2,3584]{3,2,1,0:T(2,128)(2,1)}), bf16[64,3,2,3584]{3,2,1,0:T(2,128)(2,1)S(1)}, u32[]{:S(2)}, u32[]{:S(2)}) async-start(bf16[64,3,2,3584]{3,2,1,0:T(2,128)(2,1)} %bitcast.42), calls=%async_computation.4 | async-start | bytes 5505024 | tf_op jit(solution)/shard_map/all_to_all | solution.py:385
  146.2 2.4 %collective-permute-start.7 = (f32[16,8]{0,1:T(8,128)S(1)}, f32[16,8]{0,1:T(8,128)S(1)}, u32[]{:S(2)}, u32[]{:S(2)}) collective-permute-start(f32[16,8]{0,1:T(8,128)S(1)} %convert_divide_fusion), channel_id=1, source_target_pairs={{0,8},{8,0},{1,9},{9,1},{2,10},{10,2},{3,11},{11,3},{4,12},{12,4},... | collective-permute-start | bytes 1544 | tf_op jit(solution)/shard_map/ppermute | solution.py:310
  180.7 4.9 %collective-permute-start.9 = (f32[16,3584]{1,0:T(8,128)S(1)}, f32[16,3584]{1,0:T(8,128)S(1)}, u32[]{:S(2)}, u32[]{:S(2)}) collective-permute-start(f32[16,3584]{1,0:T(8,128)S(1)} %get-tuple-element.11), channel_id=1, source_target_pairs={{0,8},{8,0},{1,9},{9,1},{2,10},{10,2},{3,11},{11,3},{4,12},{12,4},... | collective-permute-start | bytes 688136 | tf_op jit(solution)/shard_map/ppermute | solution.py:310

commit v16 on v15

--- a/solution.py
+++ b/solution.py
@@ -242,16 +242,14 @@
     )(*[a for part in parts for a in part])
 
 
-def project_kernel(ids_ref, own_ref, before_ref, after_ref, left_ref, right_ref, near_ref, far_ref, out_ref, x_ref, w_ref):
+def project_kernel(ids_ref, own_ref, before_ref, after_ref, opposite_ref, near_ref, far_ref, out_ref, x_ref, w_ref):
     rows = own_ref.shape[0]
     group, tok = 4, out_ref.shape[1]
     parts = out_ref.shape[0] // group
     core, x = ids_ref[1], ids_ref[2]
-    half = left_ref.shape[1]
     x_ref[:rows] = own_ref[...]
     x_ref[rows : 2 * rows] = after_ref[...]
-    x_ref[2 * rows : 3 * rows, :half] = left_ref[...]
-    x_ref[2 * rows : 3 * rows, half:] = right_ref[...]
+    x_ref[2 * rows : 3 * rows] = opposite_ref[...]
     x_ref[3 * rows :] = before_ref[...]
     deep = VD // 2
     for side, ref in enumerate((near_ref, far_ref)):
@@ -366,11 +364,10 @@
     w_near = lax.all_to_all(w_blocks, CTX_CHIPS, split_axis=0, concat_axis=0, tiled=True)
     ids = jnp.stack([lax.axis_index(CTX), core, lax.axis_index("x")]).astype(jnp.int32)
     own = attend(ids, queries, w_kv, near, far, 4)
-    before, after, w_near = lax.optimization_barrier((up(own), down(own), w_near))
+    opposite = lax.ppermute(own, "x", [(i, (i + 2) % 4) for i in range(4)])
+    before, after, opposite, w_near = lax.optimization_barrier((up(own), down(own), opposite, w_near))
     w_far = swap(w_near)
-    half = own.shape[1] // 2
-    left, right = up(before[:, :half]), down(after[:, half:])
-    attn = project(ids, (own, before, after, left, right), w_near, w_far, 8, columns)
+    attn = project(ids, (own, before, after, opposite), w_near, w_far, 8, columns)
     attn = lax.all_to_all(attn, EP + ("x",), split_axis=0, concat_axis=0, tiled=True)
     attn = jnp.sum(attn.reshape(8, group, tok, columns).astype(F32), axis=0)
     attn = attn.transpose(1, 0, 2).reshape(tok, width)

time: 188 us -> 189 us (level)
    ppermute x0 -> x1, waiting for transfers between devices: none -> 5.42 us  [local(): opposite = lax.ppermute(own, 'x', [(i, (i + 2) % 4) for i in range(4)])]
    ppermute x2 -> x1, waiting for transfers between devices: 4.15 us -> 0.79 us  [up(): return lax.ppermute(a, 'x', [(i, (i + 1) % 4) for i in range(4)])]
    ppermute x0 -> x1, starting transfers between devices: none -> 2.94 us  [local(): opposite = lax.ppermute(own, 'x', [(i, (i + 2) % 4) for i in range(4)])]
    ppermute x6, waiting for transfers between devices: 2.93 us -> 5.03 us  [swap(): return lax.ppermute(mine, 'core', SWAP)]
    ppermute x2 -> x1, waiting for transfers between devices: 7.15 us -> 5.07 us  [down(): return lax.ppermute(a, 'x', [(i, (i + 3) % 4) for i in range(4)])]
  transfers between devices with their start and end apart: 13 -> 12, of which waited for: 11 -> 11; matrix products, arithmetic and copies ran while one was open for 1% -> 1% of each run, Pallas kernels for 6% -> 6%
where the time goes in v16:
time: 189 us; the launch traced here: 187 us
  blocking collectives  63 us (33%)
  waiting for transfers between devices  60.2 us (32%)
  starting transfers between devices  35.7 us (19%)
  Pallas kernels  23.3 us (12%)
  local copies, waits for them, and re-layouts  2.55 us (1%)
    all_to_all x1, blocking collectives, exchange(): lax.all_to_all(units, CHIPS, split_axis=0, concat_axis=0, tiled=True)  40.7 us
    all_to_all x1, waiting for transfers between devices, exchange(): lax.all_to_all(units, CHIPS, split_axis=0, concat_axis=0, tiled=True)  29.9 us
    all_to_all x1, blocking collectives, local(): lax.all_to_all(jnp.broadcast_to(latents[None], (8,) + latents.shape), CTX...  22.4 us
    all_to_all x1, waiting for transfers between devices, local(): lax.all_to_all(attn, EP + ('x',), split_axis=0, concat_axis=0, tiled=True)  13.8 us
    ppermute x6, starting transfers between devices, swap(): return lax.ppermute(mine, 'core', SWAP)  10.5 us
    all_to_all x1, starting transfers between devices, local(): lax.all_to_all(attn, EP + ('x',), split_axis=0, concat_axis=0, tiled=True)  9.9 us
    pallas_call x1, Pallas kernels, attend(): pl.pallas_call(functools.partial(attend_kernel, cuts=cuts), in_specs=[pl....  9.82 us
    all_to_all x1, starting transfers between devices, exchange(): lax.all_to_all(units, CHIPS, split_axis=0, concat_axis=0, tiled=True)  7.34 us
  transfers between devices with their start and end apart: 12, of which 11 were waited for; matrix products, arithmetic and copies ran while one was open for 1% of the time, Pallas kernels for 6%

profile of v16, /device:TPU:1, one launch (start us, length us, event | category | flops | bytes accessed | tf_op | source)
XLA Modules:
  0.0 187.5 jit_solution(9957699594528181296)
XLA Ops:
  0.6 1.1 broadcast_in_dim.32
  1.7 22.4 %all_to_all.25.near_ref = bf16[8,576,128]{2,1,0:T(8,128)(2,1)S(1)} all-to-all(bf16[8,576,128]{2,1,0:T(8,128)(2,1)S(1)} %broadcast_in_dim.32), channel_id=1, replica_groups=mesh['z_lo'=2,'x'=4,'core'=2,'z_hi'=2,'y'=4] {'z_lo','x'}, dimensions={0} | all-to-all | bytes 2359296 | tf_op jit(solution)/shard_map/all_to_all | solution.py:359
  24.1 1.7 collective-permute-start
  25.8 2.0 %shard_map.123 = bf16[8,64,896]{2,1,0:T(8,128)(2,1)} custom-call(bf16[64,3584]{1,0:T(8,128)(2,1)} %w_ref.1), custom_call_target="tpu_custom_call" | custom-call | bytes 1376256 | tf_op jit(solution)/shard_map/pallas_call | solution.py:297
  27.8 3.6 %all-to-all-start.1 = ((bf16[8,64,896]{2,1,0:T(8,128)(2,1)}), bf16[8,64,896]{2,1,0:T(8,128)(2,1)S(1)}, u32[]{:S(2)}, u32[]{:S(2)}) async-start(bf16[8,64,896]{2,1,0:T(8,128)(2,1)} %shard_map.123), calls=%async_computation.1 | async-start | bytes 1835008 | tf_op jit(solution)/shard_map/all_to_all | solution.py:364
  31.4 0.1 pad_add_fusion.1.ids_ref
  31.5 0.0 collective-permute-done.far_ref
  31.5 9.8 %shard_map.122.own_ref = bf16[128,1024]{1,0:T(8,128)(2,1)S(1)} custom-call(s32[3]{0:T(128)S(1)} %pad_add_fusion.1.ids_ref, bf16[128,1536]{1,0:T(8,128)(2,1)} %q_hbm.1, bf16[512,2048]{1,0:T(8,128)(2,1)} %w_hbm.1, bf16[8,576,128]{2,1,0:T(8,128)(2,1)S(1)} %all_to_all.25.near_ref, bf16[8,576,128]{2,1,0:T(8,128)(2,1)S(1)} %collective-permute-done.far_ref), custom_call_target="tpu_custom_call" | custom-call | flops 4563402752 | bytes 8000000 | tf_op jit(solution)/shard_map/pallas_call | solution.py:103
  41.3 0.0 copy-start.6
  41.3 2.9 %collective-permute-start.3 = (bf16[128,1024]{1,0:T(8,128)(2,1)S(1)}, bf16[128,1024]{1,0:T(8,128)(2,1)S(1)}, u32[]{:S(2)}, u32[]{:S(2)}) collective-permute-start(bf16[128,1024]{1,0:T(8,128)(2,1)S(1)} %shard_map.122.own_ref), channel_id=1, source_target_pairs={{0,32},{16,48},{32,0},{48,16},{1,33},{17,49},{33,1},{49,17},{2,34}... | collective-permute-start | bytes 786440 | tf_op jit(solution)/shard_map/ppermute | solution.py:367
  44.3 0.9 collective-permute-start.2
  45.2 0.6 collective-permute-start.1
  45.7 0.1 all-to-all-done.1.near_ref
  45.9 5.4 %collective-permute-done.3.opposite_ref = bf16[128,1024]{1,0:T(8,128)(2,1)S(1)} collective-permute-done((bf16[128,1024]{1,0:T(8,128)(2,1)S(1)}, bf16[128,1024]{1,0:T(8,128)(2,1)S(1)}, u32[]{:S(2)}, u32[]{:S(2)}) %collective-permute-start.3) | collective-permute-done | bytes 262176 | tf_op jit(solution)/shard_map/ppermute | solution.py:367
  51.3 5.1 %collective-permute-done.2.after_ref = bf16[128,1024]{1,0:T(8,128)(2,1)S(1)} collective-permute-done((bf16[128,1024]{1,0:T(8,128)(2,1)S(1)}, bf16[128,1024]{1,0:T(8,128)(2,1)S(1)}, u32[]{:S(2)}, u32[]{:S(2)}) %collective-permute-start.2) | collective-permute-done | bytes 262176 | tf_op jit(solution)/shard_map/ppermute | solution.py:316
  56.4 0.8 collective-permute-done.1.before_ref
  57.2 0.5 collective-permute-start.4
  57.7 2.1 %collective-permute-done.4.far_ref = bf16[8,64,896]{2,1,0:T(8,128)(2,1)S(1)} collective-permute-done((bf16[8,64,896]{2,1,0:T(8,128)(2,1)S(1)}, bf16[8,64,896]{2,1,0:T(8,128)(2,1)S(1)}, u32[]{:S(2)}, u32[]{:S(2)}) %collective-permute-start.4) | collective-permute-done | bytes 917536 | tf_op jit(solution)/shard_map/ppermute | solution.py:308
  59.8 2.9 %shard_map.124 = bf16[32,16,896]{2,1,0:T(8,128)(2,1)} custom-call(s32[3]{0:T(128)S(1)} %pad_add_fusion.1.ids_ref, bf16[128,1024]{1,0:T(8,128)(2,1)S(1)} %shard_map.122.own_ref, bf16[128,1024]{1,0:T(8,128)(2,1)S(1)} %collective-permute-done.1.before_ref, bf16[128,1024]{1,0:T(8,128)(2,1)S(1)} %collective-permute-done.2.after_ref, ...), custom_call_target="tpu_custom_call" | custom-call | flops 939524096 | bytes 1835008 | tf_op jit(solution)/shard_map/pallas_call | solution.py:270
  62.7 9.9 %all-to-all-start.2 = ((bf16[32,16,896]{2,1,0:T(8,128)(2,1)}), bf16[32,16,896]{2,1,0:T(8,128)(2,1)S(1)}, u32[]{:S(2)}, u32[]{:S(2)}) async-start(bf16[32,16,896]{2,1,0:T(8,128)(2,1)} %shard_map.124), calls=%async_computation.2 | async-start | bytes 1835008 | tf_op jit(solution)/shard_map/all_to_all | solution.py:371
  72.6 0.0 copy-done.6
  72.6 0.7 collective-permute-start.5
  73.3 0.1 and.46
  73.4 0.1 and.47
  73.5 0.7 collective-permute-done.5
  74.1 0.1 copy.46
  74.2 0.1 fusion.5
  74.3 0.1 copy.47
  74.5 0.1 copy.49
  74.6 0.1 copy.48
  74.7 13.8 %all-to-all-done.2 = bf16[32,16,896]{2,1,0:T(8,128)(2,1)S(1)} async-done(((bf16[32,16,896]{2,1,0:T(8,128)(2,1)}), bf16[32,16,896]{2,1,0:T(8,128)(2,1)S(1)}, u32[]{:S(2)}, u32[]{:S(2)}) %all-to-all-start.2) | async-done | bytes 917536 | tf_op jit(solution)/shard_map/all_to_all | solution.py:371
  88.5 0.1 convert_reduce_fusion
  88.7 0.2 fusion
  88.9 0.1 fusion.2
  89.0 2.2 %collective-permute-start.7 = (bf16[16,3584]{1,0:T(8,128)(2,1)S(1)}, bf16[16,3584]{1,0:T(8,128)(2,1)S(1)}, u32[]{:S(2)}, u32[]{:S(2)}) collective-permute-start(bf16[16,3584]{1,0:T(8,128)(2,1)S(1)} %fusion.2), channel_id=1, source_target_pairs={{0,8},{8,0},{1,9},{9,1},{2,10},{10,2},{3,11},{11,3},{4,12},{12,4},... | collective-permute-start | bytes 344072 | tf_op jit(solution)/shard_map/ppermute | solution.py:308
  91.2 0.1 bitcast_and_fusion
  91.3 0.1 copy.50
  91.4 0.1 broadcast_in_dim.33
  91.5 0.1 reshape.135
  91.7 0.5 collective-permute-done.7
  92.2 0.0 copy-start.1
  92.2 1.4 shard_map.125
  93.5 0.0 copy-start
  93.6 40.7 %all_to_all.26 = bf16[64,3,2,3584]{3,2,1,0:T(2,128)(2,1)S(1)} all-to-all(bf16[64,3,2,3584]{3,2,1,0:T(2,128)(2,1)S(1)} %bitcast.38), channel_id=1, replica_groups=mesh['z_lo'=2,'x'=4,'core'=2,'z_hi'=2,'y'=4] {'z_lo','x','z_hi','y'}, dimensions={0} | all-to-all | bytes 5505024 | tf_op jit(solution)/shard_map/all_to_all | solution.py:382
  134.2 0.0 copy-done.1
  134.2 5.8 %shard_map.126 = bf16[192,2,3584]{2,1,0:T(2,128)(2,1)} custom-call(bf16[192,2,3584]{2,1,0:T(2,128)(2,1)S(1)} %bitcast.39, bf16[3584,512]{1,0:T(8,128)(2,1)S(1)} %bitcast.40, bf16[3584,512]{1,0:T(8,128)(2,1)S(1)} %bitcast.41, bf16[512,3584]{1,0:T(8,128)(2,1)} %bitcast.44), custom_call_target="tpu_custom_call" | custom-call | flops 4227858432 | bytes 17000000 | tf_op jit(solution)/shard_map/pallas_call | solution.py:164
  140.1 0.0 copy-start.4
  140.1 7.3 %all-to-all-start.4 = ((bf16[64,3,2,3584]{3,2,1,0:T(2,128)(2,1)}), bf16[64,3,2,3584]{3,2,1,0:T(2,128)(2,1)S(1)}, u32[]{:S(2)}, u32[]{:S(2)}) async-start(bf16[64,3,2,3584]{3,2,1,0:T(2,128)(2,1)} %bitcast.42), calls=%async_computation.4 | async-start | bytes 5505024 | tf_op jit(solution)/shard_map/all_to_all | solution.py:382
  147.4 0.0 copy-done.4
  147.5 1.6 collective-permute-start.6
  149.1 0.1 copy.55
  149.2 0.7 collective-permute-done.6
  149.9 0.1 copy.51
  150.0 0.1 select_reduce_fusion
  150.1 0.1 copy.52
  150.2 0.1 copy.53
  150.3 0.1 copy.54
  150.4 0.1 broadcast_in_dim.65
  150.4 0.1 copy.56
  150.6 29.9 %all-to-all-done.4 = bf16[64,3,2,3584]{3,2,1,0:T(2,128)(2,1)S(1)} async-done(((bf16[64,3,2,3584]{3,2,1,0:T(2,128)(2,1)}), bf16[64,3,2,3584]{3,2,1,0:T(2,128)(2,1)S(1)}, u32[]{:S(2)}, u32[]{:S(2)}) %all-to-all-start.4) | async-done | bytes 2752544 | tf_op jit(solution)/shard_map/all_to_all | solution.py:382
  180.5 1.4 shard_map.127
  181.9 3.8 %collective-permute-start.8 = (f32[16,3584]{1,0:T(8,128)S(1)}, f32[16,3584]{1,0:T(8,128)S(1)}, u32[]{:S(2)}, u32[]{:S(2)}) collective-permute-start(f32[16,3584]{1,0:T(8,128)S(1)} %get-tuple-element.13), channel_id=1, source_target_pairs={{0,8},{8,0},{1,9},{9,1},{2,10},{10,2},{3,11},{11,3},{4,12},{12,4},... | collective-permute-start | bytes 688136 | tf_op jit(solution)/shard_map/ppermute | solution.py:308
  185.7 1.1 collective-permute-done.8
  186.8 0.7 fusion.4
  (26 shorter events, 0.3 us)
Async XLA Ops:
  24.1 7.4 %collective-permute-start = (bf16[8,576,128]{2,1,0:T(8,128)(2,1)S(1)}, bf16[8,576,128]{2,1,0:T(8,128)(2,1)S(1)}, u32[]{:S(2)}, u32[]{:S(2)}) collective-permute-start(bf16[8,576,128]{2,1,0:T(8,128)(2,1)S(1)} %all_to_all.25.near_ref), channel_id=1, source_target_pairs={{0,8},{8,0},{1,9},{9,1},{2,10},{10,2},{3,11},{11,3},{4,12},{12,4},... | collective-permute-start | bytes 3538952 | tf_op jit(solution)/shard_map/ppermute | solution.py:308
  27.8 18.1 %all-to-all-start.1 = ((bf16[8,64,896]{2,1,0:T(8,128)(2,1)}), bf16[8,64,896]{2,1,0:T(8,128)(2,1)S(1)}, u32[]{:S(2)}, u32[]{:S(2)}) async-start(bf16[8,64,896]{2,1,0:T(8,128)(2,1)} %shard_map.123), calls=%async_computation.1 | async-start | bytes 1835008 | tf_op jit(solution)/shard_map/all_to_all | solution.py:364
  41.3 31.2 %copy-start.6 = (s32[16,8]{0,1:T(8,128)S(1)}, s32[16,8]{0,1:T(8,128)}, u32[]{:S(2)}) copy-start(s32[16,8]{0,1:T(8,128)} %param.17) | copy-start | bytes 1540
  41.3 10.0 %collective-permute-start.3 = (bf16[128,1024]{1,0:T(8,128)(2,1)S(1)}, bf16[128,1024]{1,0:T(8,128)(2,1)S(1)}, u32[]{:S(2)}, u32[]{:S(2)}) collective-permute-start(bf16[128,1024]{1,0:T(8,128)(2,1)S(1)} %shard_map.122.own_ref), channel_id=1, source_target_pairs={{0,32},{16,48},{32,0},{48,16},{1,33},{17,49},{33,1},{49,17},{2,34}... | collective-permute-start | bytes 786440 | tf_op jit(solution)/shard_map/ppermute | solution.py:367
  44.3 12.1 %collective-permute-start.2 = (bf16[128,1024]{1,0:T(8,128)(2,1)S(1)}, bf16[128,1024]{1,0:T(8,128)(2,1)S(1)}, u32[]{:S(2)}, u32[]{:S(2)}) collective-permute-start(bf16[128,1024]{1,0:T(8,128)(2,1)S(1)} %shard_map.122.own_ref), channel_id=1, source_target_pairs={{0,48},{16,0},{32,16},{48,32},{1,49},{17,1},{33,17},{49,33},{2,50}... | collective-permute-start | bytes 786440 | tf_op jit(solution)/shard_map/ppermute | solution.py:316
  45.2 12.0 %collective-permute-start.1 = (bf16[128,1024]{1,0:T(8,128)(2,1)S(1)}, bf16[128,1024]{1,0:T(8,128)(2,1)S(1)}, u32[]{:S(2)}, u32[]{:S(2)}) collective-permute-start(bf16[128,1024]{1,0:T(8,128)(2,1)S(1)} %shard_map.122.own_ref), channel_id=1, source_target_pairs={{0,16},{16,32},{32,48},{48,0},{1,17},{17,33},{33,49},{49,1},{2,18}... | collective-permute-start | bytes 786440 | tf_op jit(solution)/shard_map/ppermute | solution.py:312
  57.2 2.6 %collective-permute-start.4 = (bf16[8,64,896]{2,1,0:T(8,128)(2,1)S(1)}, bf16[8,64,896]{2,1,0:T(8,128)(2,1)S(1)}, u32[]{:S(2)}, u32[]{:S(2)}) collective-permute-start(bf16[8,64,896]{2,1,0:T(8,128)(2,1)S(1)} %all-to-all-done.1.near_ref), channel_id=1, source_target_pairs={{0,8},{8,0},{1,9},{9,1},{2,10},{10,2},{3,11},{11,3},{4,12},{12,4},... | collective-permute-start | bytes 2752520 | tf_op jit(solution)/shard_map/ppermute | solution.py:308
  62.7 26.0 %copy-start.3 = (bf16[16,3584]{1,0:T(8,128)(2,1)S(1)}, bf16[16,3584]{1,0:T(8,128)(2,1)}, u32[]{:S(2)}) copy-start(bf16[16,3584]{1,0:T(8,128)(2,1)} %param.15) | copy-start | bytes 344068
  62.7 26.2 %copy-start.5 = (f32[3584]{0:T(1024)S(1)}, f32[3584]{0:T(1024)}, u32[]{:S(2)}) copy-start(f32[3584]{0:T(1024)} %param.16) | copy-start | bytes 43012
  62.7 25.9 %all-to-all-start.2 = ((bf16[32,16,896]{2,1,0:T(8,128)(2,1)}), bf16[32,16,896]{2,1,0:T(8,128)(2,1)S(1)}, u32[]{:S(2)}, u32[]{:S(2)}) async-start(bf16[32,16,896]{2,1,0:T(8,128)(2,1)} %shard_map.124), calls=%async_computation.2 | async-start | bytes 1835008 | tf_op jit(solution)/shard_map/all_to_all | solution.py:371
  72.6 1.6 collective-permute-start.5
  88.8 98.0 %copy-start.2 = (bf16[16,3584]{1,0:T(8,128)(2,1)}, bf16[16,3584]{1,0:T(8,128)(2,1)S(1)}, u32[]{:S(2)}) copy-start(bf16[16,3584]{1,0:T(8,128)(2,1)S(1)} %get-tuple-element.15) | copy-start | bytes 344068
  89.0 3.2 %collective-permute-start.7 = (bf16[16,3584]{1,0:T(8,128)(2,1)S(1)}, bf16[16,3584]{1,0:T(8,128)(2,1)S(1)}, u32[]{:S(2)}, u32[]{:S(2)}) collective-permute-start(bf16[16,3584]{1,0:T(8,128)(2,1)S(1)} %fusion.2), channel_id=1, source_target_pairs={{0,8},{8,0},{1,9},{9,1},{2,10},{10,2},{3,11},{11,3},{4,12},{12,4},... | collective-permute-start | bytes 344072 | tf_op jit(solution)/shard_map/ppermute | solution.py:308
  92.2 42.1 %copy-start.1 = (bf16[1,3584,512]{2,1,0:T(8,128)(2,1)S(1)}, bf16[1,3584,512]{2,1,0:T(8,128)(2,1)}, u32[]{:S(2)}) copy-start(bf16[1,3584,512]{2,1,0:T(8,128)(2,1)} %param.20) | copy-start | bytes 11010052
  93.5 40.7 %copy-start = (bf16[1,3584,512]{2,1,0:T(8,128)(2,1)S(1)}, bf16[1,3584,512]{2,1,0:T(8,128)(2,1)}, u32[]{:S(2)}) copy-start(bf16[1,3584,512]{2,1,0:T(8,128)(2,1)} %param.19) | copy-start | bytes 11010052
  140.1 7.4 %copy-start.4 = (s32[16,8]{0,1:T(8,128)S(1)}, s32[16,8]{0,1:T(8,128)}, u32[]{:S(2)}) copy-start(s32[16,8]{0,1:T(8,128)} %param.18) | copy-start | bytes 1540
  140.1 40.4 %all-to-all-start.4 = ((bf16[64,3,2,3584]{3,2,1,0:T(2,128)(2,1)}), bf16[64,3,2,3584]{3,2,1,0:T(2,128)(2,1)S(1)}, u32[]{:S(2)}, u32[]{:S(2)}) async-start(bf16[64,3,2,3584]{3,2,1,0:T(2,128)(2,1)} %bitcast.42), calls=%async_computation.4 | async-start | bytes 5505024 | tf_op jit(solution)/shard_map/all_to_all | solution.py:382
  147.5 2.4 %collective-permute-start.6 = (f32[16,8]{0,1:T(8,128)S(1)}, f32[16,8]{0,1:T(8,128)S(1)}, u32[]{:S(2)}, u32[]{:S(2)}) collective-permute-start(f32[16,8]{0,1:T(8,128)S(1)} %convert_divide_fusion), channel_id=1, source_target_pairs={{0,8},{8,0},{1,9},{9,1},{2,10},{10,2},{3,11},{11,3},{4,12},{12,4},... | collective-permute-start | bytes 1544 | tf_op jit(solution)/shard_map/ppermute | solution.py:308
  181.9 4.9 %collective-permute-start.8 = (f32[16,3584]{1,0:T(8,128)S(1)}, f32[16,3584]{1,0:T(8,128)S(1)}, u32[]{:S(2)}, u32[]{:S(2)}) collective-permute-start(f32[16,3584]{1,0:T(8,128)S(1)} %get-tuple-element.13), channel_id=1, source_target_pairs={{0,8},{8,0},{1,9},{9,1},{2,10},{10,2},{3,11},{11,3},{4,12},{12,4},... | collective-permute-start | bytes 688136 | tf_op jit(solution)/shard_map/ppermute | solution.py:308

commit v17 on v16

--- a/solution.py
+++ b/solution.py
@@ -40,16 +40,21 @@
     pairs = near_ref.shape[0]
     keys = 2 * rows * pairs
     q_copy = pltpu.make_async_copy(q_hbm, q_ref, sems.at[0])
-    w_copy = pltpu.make_async_copy(w_hbm, w_ref, sems.at[1])
     q_copy.start()
-    w_copy.start()
+    wide = w_ref.shape[1] // (sems.shape[0] - 1)
+    w_copies = []
+    for i in range(sems.shape[0] - 1):
+        part = slice(i * wide, (i + 1) * wide)
+        w_copies.append(pltpu.make_async_copy(w_hbm.at[:, part], w_ref.at[:, part], sems.at[1 + i]))
+        w_copies[-1].start()
     for i in range(pairs):
         lat_ref[:, 2 * i * rows : (2 * i + 1) * rows] = near_ref[i]
         lat_ref[:, (2 * i + 1) * rows : (2 * i + 2) * rows] = far_ref[i]
     q_copy.wait()
-    w_copy.wait()
     for h in range(heads):
         here = slice(h * rows, (h + 1) * rows)
+        if h * (NOPE + VD) % wide == 0:
+            w_copies[h * (NOPE + VD) // wide].wait()
         key_weights = w_ref[:, h * (NOPE + VD) : h * (NOPE + VD) + NOPE]
         plain = q_ref[:, h * QK : h * QK + NOPE]
         latq = lax.dot_general(plain, key_weights, (((1,), (1,)), ((), ())), preferred_element_type=F32)
@@ -112,7 +117,7 @@
             pltpu.VMEM((m, keys), F32),
             pltpu.VMEM((m, depth), BF),
             pltpu.VMEM((m, KV_RANK), F32),
-            pltpu.SemaphoreType.DMA((2,)),
+            pltpu.SemaphoreType.DMA((5,)),
         ],
         compiler_params=pltpu.CompilerParams(vmem_limit_bytes=28 * 2**20),
         cost_estimate=pl.CostEstimate(
@@ -300,7 +305,7 @@
         out_specs=pl.BlockSpec(memory_space=pltpu.HBM),
         out_shape=pltpu.HBM(shape, w.dtype),
         scratch_shapes=[pltpu.SemaphoreType.DMA((count,))],
-        cost_estimate=pl.CostEstimate(flops=0, bytes_accessed=6 * w.size, transcendentals=0),
+        cost_estimate=pl.CostEstimate(flops=0, bytes_accessed=60_000_000, transcendentals=0),
     )(w)
 
 
@@ -365,7 +370,8 @@
     ids = jnp.stack([lax.axis_index(CTX), core, lax.axis_index("x")]).astype(jnp.int32)
     own = attend(ids, queries, w_kv, near, far, 4)
     opposite = lax.ppermute(own, "x", [(i, (i + 2) % 4) for i in range(4)])
-    before, after, opposite, w_near = lax.optimization_barrier((up(own), down(own), opposite, w_near))
+    before, after = up(own), down(own)
+    opposite, w_near = lax.optimization_barrier((opposite, w_near))
     w_far = swap(w_near)
     attn = project(ids, (own, before, after, opposite), w_near, w_far, 8, columns)
     attn = lax.all_to_all(attn, EP + ("x",), split_axis=0, concat_axis=0, tiled=True)

time: 189 us -> 191 us (1.011)
    ppermute x1, waiting for transfers between devices: 0.79 us -> 3.04 us  [up(): return lax.ppermute(a, 'x', [(i, (i + 1) % 4) for i in range(4)])]
    all_to_all x1, starting transfers between devices: 9.9 us -> 7.76 us  [local(): lax.all_to_all(attn, EP + ('x',), split_axis=0, concat_axis=0, tiled=True)]
    ppermute x6, waiting for transfers between devices: 5.03 us -> 2.93 us  [swap(): return lax.ppermute(mine, 'core', SWAP)]
  transfers between devices with their start and end apart: 12 -> 12, of which waited for: 11 -> 10; matrix products, arithmetic and copies ran while one was open for 1% -> 1% of each run, Pallas kernels for 6% -> 6%
where the time goes in v17:
time: 191 us; the launch traced here: 189 us
  blocking collectives  63.3 us (33%)
  waiting for transfers between devices  60.9 us (32%)
  starting transfers between devices  35.9 us (19%)
  Pallas kernels  23.3 us (12%)
  local copies, waits for them, and re-layouts  2.55 us (1%)
    all_to_all x1, blocking collectives, exchange(): lax.all_to_all(units, CHIPS, split_axis=0, concat_axis=0, tiled=True)  40.9 us
    all_to_all x1, waiting for transfers between devices, exchange(): lax.all_to_all(units, CHIPS, split_axis=0, concat_axis=0, tiled=True)  29.9 us
    all_to_all x1, blocking collectives, local(): lax.all_to_all(jnp.broadcast_to(latents[None], (8,) + latents.shape), CTX...  22.4 us
    all_to_all x1, waiting for transfers between devices, local(): lax.all_to_all(attn, EP + ('x',), split_axis=0, concat_axis=0, tiled=True)  12.2 us
    ppermute x6, starting transfers between devices, swap(): return lax.ppermute(mine, 'core', SWAP)  12.2 us
    pallas_call x1, Pallas kernels, attend(): pl.pallas_call(functools.partial(attend_kernel, cuts=cuts), in_specs=[pl....  9.81 us
    all_to_all x1, starting transfers between devices, local(): lax.all_to_all(attn, EP + ('x',), split_axis=0, concat_axis=0, tiled=True)  7.76 us
    all_to_all x1, starting transfers between devices, exchange(): lax.all_to_all(units, CHIPS, split_axis=0, concat_axis=0, tiled=True)  7.34 us
  transfers between devices with their start and end apart: 12, of which 10 were waited for; matrix products, arithmetic and copies ran while one was open for 1% of the time, Pallas kernels for 6%

profile of v17, /device:TPU:1, one launch (start us, length us, event | category | flops | bytes accessed | tf_op | source)
XLA Modules:
  0.0 188.6 jit_solution(332780614992757770)
XLA Ops:
  0.6 1.1 broadcast_in_dim.32
  1.7 22.4 %all_to_all.25.near_ref = bf16[8,576,128]{2,1,0:T(8,128)(2,1)S(1)} all-to-all(bf16[8,576,128]{2,1,0:T(8,128)(2,1)S(1)} %broadcast_in_dim.32), channel_id=1, replica_groups=mesh['z_lo'=2,'x'=4,'core'=2,'z_hi'=2,'y'=4] {'z_lo','x'}, dimensions={0} | all-to-all | bytes 2359296 | tf_op jit(solution)/shard_map/all_to_all | solution.py:364
  24.1 1.7 collective-permute-start
  25.8 2.0 %shard_map.123 = bf16[8,64,896]{2,1,0:T(8,128)(2,1)} custom-call(bf16[64,3584]{1,0:T(8,128)(2,1)} %w_ref.1), custom_call_target="tpu_custom_call" | custom-call | bytes 60000000 | tf_op jit(solution)/shard_map/pallas_call | solution.py:302
  27.8 3.6 %all-to-all-start.1 = ((bf16[8,64,896]{2,1,0:T(8,128)(2,1)}), bf16[8,64,896]{2,1,0:T(8,128)(2,1)S(1)}, u32[]{:S(2)}, u32[]{:S(2)}) async-start(bf16[8,64,896]{2,1,0:T(8,128)(2,1)} %shard_map.123), calls=%async_computation.1 | async-start | bytes 1835008 | tf_op jit(solution)/shard_map/all_to_all | solution.py:369
  31.4 0.1 pad_add_fusion.1.ids_ref
  31.5 0.0 collective-permute-done.far_ref
  31.5 9.8 %shard_map.122.own_ref = bf16[128,1024]{1,0:T(8,128)(2,1)S(1)} custom-call(s32[3]{0:T(128)S(1)} %pad_add_fusion.1.ids_ref, bf16[128,1536]{1,0:T(8,128)(2,1)} %q_hbm.1, bf16[512,2048]{1,0:T(8,128)(2,1)} %w_hbm.1, bf16[8,576,128]{2,1,0:T(8,128)(2,1)S(1)} %all_to_all.25.near_ref, bf16[8,576,128]{2,1,0:T(8,128)(2,1)S(1)} %collective-permute-done.far_ref), custom_call_target="tpu_custom_call" | custom-call | flops 4563402752 | bytes 8000000 | tf_op jit(solution)/shard_map/pallas_call | solution.py:108
  41.3 0.0 copy-start.6
  41.3 2.9 %collective-permute-start.3 = (bf16[128,1024]{1,0:T(8,128)(2,1)S(1)}, bf16[128,1024]{1,0:T(8,128)(2,1)S(1)}, u32[]{:S(2)}, u32[]{:S(2)}) collective-permute-start(bf16[128,1024]{1,0:T(8,128)(2,1)S(1)} %shard_map.122.own_ref), channel_id=1, source_target_pairs={{0,32},{16,48},{32,0},{48,16},{1,33},{17,49},{33,1},{49,17},{2,34}... | collective-permute-start | bytes 786440 | tf_op jit(solution)/shard_map/ppermute | solution.py:372
  44.3 1.6 all-to-all-done.1.near_ref
  45.9 5.4 %collective-permute-done.3.opposite_ref = bf16[128,1024]{1,0:T(8,128)(2,1)S(1)} collective-permute-done((bf16[128,1024]{1,0:T(8,128)(2,1)S(1)}, bf16[128,1024]{1,0:T(8,128)(2,1)S(1)}, u32[]{:S(2)}, u32[]{:S(2)}) %collective-permute-start.3) | collective-permute-done | bytes 262176 | tf_op jit(solution)/shard_map/ppermute | solution.py:372
  51.3 0.8 collective-permute-start.4
  52.0 2.2 %collective-permute-start.2 = (bf16[128,1024]{1,0:T(8,128)(2,1)S(1)}, bf16[128,1024]{1,0:T(8,128)(2,1)S(1)}, u32[]{:S(2)}, u32[]{:S(2)}) collective-permute-start(bf16[128,1024]{1,0:T(8,128)(2,1)S(1)} %shard_map.122.own_ref), channel_id=1, source_target_pairs={{0,48},{16,0},{32,16},{48,32},{1,49},{17,1},{33,17},{49,33},{2,50}... | collective-permute-start | bytes 786440 | tf_op jit(solution)/shard_map/ppermute | solution.py:321
  54.2 0.0 collective-permute-start.1
  54.2 5.8 %collective-permute-done.2.after_ref = bf16[128,1024]{1,0:T(8,128)(2,1)S(1)} collective-permute-done((bf16[128,1024]{1,0:T(8,128)(2,1)S(1)}, bf16[128,1024]{1,0:T(8,128)(2,1)S(1)}, u32[]{:S(2)}, u32[]{:S(2)}) %collective-permute-start.2) | collective-permute-done | bytes 262176 | tf_op jit(solution)/shard_map/ppermute | solution.py:321
  60.0 3.0 %collective-permute-done.1.before_ref = bf16[128,1024]{1,0:T(8,128)(2,1)S(1)} collective-permute-done((bf16[128,1024]{1,0:T(8,128)(2,1)S(1)}, bf16[128,1024]{1,0:T(8,128)(2,1)S(1)}, u32[]{:S(2)}, u32[]{:S(2)}) %collective-permute-start.1) | collective-permute-done | bytes 262176 | tf_op jit(solution)/shard_map/ppermute | solution.py:317
  63.0 0.0 collective-permute-done.4.far_ref
  63.0 2.9 %shard_map.124 = bf16[32,16,896]{2,1,0:T(8,128)(2,1)} custom-call(s32[3]{0:T(128)S(1)} %pad_add_fusion.1.ids_ref, bf16[128,1024]{1,0:T(8,128)(2,1)S(1)} %shard_map.122.own_ref, bf16[128,1024]{1,0:T(8,128)(2,1)S(1)} %collective-permute-done.1.before_ref, bf16[128,1024]{1,0:T(8,128)(2,1)S(1)} %collective-permute-done.2.after_ref, ...), custom_call_target="tpu_custom_call" | custom-call | flops 939524096 | bytes 1835008 | tf_op jit(solution)/shard_map/pallas_call | solution.py:275
  65.9 7.8 %all-to-all-start.2 = ((bf16[32,16,896]{2,1,0:T(8,128)(2,1)}), bf16[32,16,896]{2,1,0:T(8,128)(2,1)S(1)}, u32[]{:S(2)}, u32[]{:S(2)}) async-start(bf16[32,16,896]{2,1,0:T(8,128)(2,1)} %shard_map.124), calls=%async_computation.2 | async-start | bytes 1835008 | tf_op jit(solution)/shard_map/all_to_all | solution.py:377
  73.7 0.0 copy-done.6
  73.7 1.4 collective-permute-start.5
  75.1 0.1 and.46
  75.2 0.1 and.47
  75.3 0.7 collective-permute-done.5
  76.0 0.1 copy.46
  76.0 0.1 fusion.5
  76.2 0.1 copy.47
  76.3 0.1 copy.49
  76.4 0.1 copy.48
  76.5 12.2 %all-to-all-done.2 = bf16[32,16,896]{2,1,0:T(8,128)(2,1)S(1)} async-done(((bf16[32,16,896]{2,1,0:T(8,128)(2,1)}), bf16[32,16,896]{2,1,0:T(8,128)(2,1)S(1)}, u32[]{:S(2)}, u32[]{:S(2)}) %all-to-all-start.2) | async-done | bytes 917536 | tf_op jit(solution)/shard_map/all_to_all | solution.py:377
  88.7 0.1 convert_reduce_fusion
  88.9 0.0 copy-done.3
  88.9 0.2 fusion
  89.1 0.0 copy-done.5
  89.1 0.1 fusion.2
  89.2 2.9 %collective-permute-start.7 = (bf16[16,3584]{1,0:T(8,128)(2,1)S(1)}, bf16[16,3584]{1,0:T(8,128)(2,1)S(1)}, u32[]{:S(2)}, u32[]{:S(2)}) collective-permute-start(bf16[16,3584]{1,0:T(8,128)(2,1)S(1)} %fusion.2), channel_id=1, source_target_pairs={{0,8},{8,0},{1,9},{9,1},{2,10},{10,2},{3,11},{11,3},{4,12},{12,4},... | collective-permute-start | bytes 344072 | tf_op jit(solution)/shard_map/ppermute | solution.py:313
  92.1 0.1 bitcast_and_fusion
  92.2 0.1 copy.50
  92.3 0.1 broadcast_in_dim.33
  92.4 0.1 reshape.135
  92.6 0.5 collective-permute-done.7
  93.0 0.0 copy-start.1
  93.1 1.3 shard_map.125
  94.4 0.0 copy-start
  94.4 40.9 %all_to_all.26 = bf16[64,3,2,3584]{3,2,1,0:T(2,128)(2,1)S(1)} all-to-all(bf16[64,3,2,3584]{3,2,1,0:T(2,128)(2,1)S(1)} %bitcast.38), channel_id=1, replica_groups=mesh['z_lo'=2,'x'=4,'core'=2,'z_hi'=2,'y'=4] {'z_lo','x','z_hi','y'}, dimensions={0} | all-to-all | bytes 5505024 | tf_op jit(solution)/shard_map/all_to_all | solution.py:388
  135.4 5.8 %shard_map.126 = bf16[192,2,3584]{2,1,0:T(2,128)(2,1)} custom-call(bf16[192,2,3584]{2,1,0:T(2,128)(2,1)S(1)} %bitcast.39, bf16[3584,512]{1,0:T(8,128)(2,1)S(1)} %bitcast.40, bf16[3584,512]{1,0:T(8,128)(2,1)S(1)} %bitcast.41, bf16[512,3584]{1,0:T(8,128)(2,1)} %bitcast.44), custom_call_target="tpu_custom_call" | custom-call | flops 4227858432 | bytes 17000000 | tf_op jit(solution)/shard_map/pallas_call | solution.py:169
  141.2 0.0 copy-start.4
  141.2 7.3 %all-to-all-start.4 = ((bf16[64,3,2,3584]{3,2,1,0:T(2,128)(2,1)}), bf16[64,3,2,3584]{3,2,1,0:T(2,128)(2,1)S(1)}, u32[]{:S(2)}, u32[]{:S(2)}) async-start(bf16[64,3,2,3584]{3,2,1,0:T(2,128)(2,1)} %bitcast.42), calls=%async_computation.4 | async-start | bytes 5505024 | tf_op jit(solution)/shard_map/all_to_all | solution.py:388
  148.6 1.6 collective-permute-start.6
  150.2 0.1 copy.55
  150.3 0.7 collective-permute-done.6
  151.0 0.1 copy.51
  151.1 0.1 select_reduce_fusion
  151.3 0.1 copy.52
  151.4 0.1 copy.53
  151.4 0.1 copy.54
  151.5 0.1 broadcast_in_dim.65
  151.6 0.1 copy.56
  151.7 29.9 %all-to-all-done.4 = bf16[64,3,2,3584]{3,2,1,0:T(2,128)(2,1)S(1)} async-done(((bf16[64,3,2,3584]{3,2,1,0:T(2,128)(2,1)}), bf16[64,3,2,3584]{3,2,1,0:T(2,128)(2,1)S(1)}, u32[]{:S(2)}, u32[]{:S(2)}) %all-to-all-start.4) | async-done | bytes 2752544 | tf_op jit(solution)/shard_map/all_to_all | solution.py:388
  181.7 1.4 shard_map.127
  183.1 3.8 %collective-permute-start.8 = (f32[16,3584]{1,0:T(8,128)S(1)}, f32[16,3584]{1,0:T(8,128)S(1)}, u32[]{:S(2)}, u32[]{:S(2)}) collective-permute-start(f32[16,3584]{1,0:T(8,128)S(1)} %get-tuple-element.9), channel_id=1, source_target_pairs={{0,8},{8,0},{1,9},{9,1},{2,10},{10,2},{3,11},{11,3},{4,12},{12,4},... | collective-permute-start | bytes 688136 | tf_op jit(solution)/shard_map/ppermute | solution.py:313
  186.8 1.1 collective-permute-done.8
  187.9 0.7 fusion.4
  (26 shorter events, 0.3 us)
Async XLA Ops:
  24.1 7.4 %collective-permute-start = (bf16[8,576,128]{2,1,0:T(8,128)(2,1)S(1)}, bf16[8,576,128]{2,1,0:T(8,128)(2,1)S(1)}, u32[]{:S(2)}, u32[]{:S(2)}) collective-permute-start(bf16[8,576,128]{2,1,0:T(8,128)(2,1)S(1)} %all_to_all.25.near_ref), channel_id=1, source_target_pairs={{0,8},{8,0},{1,9},{9,1},{2,10},{10,2},{3,11},{11,3},{4,12},{12,4},... | collective-permute-start | bytes 3538952 | tf_op jit(solution)/shard_map/ppermute | solution.py:313
  27.8 18.1 %all-to-all-start.1 = ((bf16[8,64,896]{2,1,0:T(8,128)(2,1)}), bf16[8,64,896]{2,1,0:T(8,128)(2,1)S(1)}, u32[]{:S(2)}, u32[]{:S(2)}) async-start(bf16[8,64,896]{2,1,0:T(8,128)(2,1)} %shard_map.123), calls=%async_computation.1 | async-start | bytes 1835008 | tf_op jit(solution)/shard_map/all_to_all | solution.py:369
  41.3 32.4 %copy-start.6 = (s32[16,8]{0,1:T(8,128)S(1)}, s32[16,8]{0,1:T(8,128)}, u32[]{:S(2)}) copy-start(s32[16,8]{0,1:T(8,128)} %param.17) | copy-start | bytes 1540
  41.3 9.9 %collective-permute-start.3 = (bf16[128,1024]{1,0:T(8,128)(2,1)S(1)}, bf16[128,1024]{1,0:T(8,128)(2,1)S(1)}, u32[]{:S(2)}, u32[]{:S(2)}) collective-permute-start(bf16[128,1024]{1,0:T(8,128)(2,1)S(1)} %shard_map.122.own_ref), channel_id=1, source_target_pairs={{0,32},{16,48},{32,0},{48,16},{1,33},{17,49},{33,1},{49,17},{2,34}... | collective-permute-start | bytes 786440 | tf_op jit(solution)/shard_map/ppermute | solution.py:372
  51.3 11.8 %collective-permute-start.4 = (bf16[8,64,896]{2,1,0:T(8,128)(2,1)S(1)}, bf16[8,64,896]{2,1,0:T(8,128)(2,1)S(1)}, u32[]{:S(2)}, u32[]{:S(2)}) collective-permute-start(bf16[8,64,896]{2,1,0:T(8,128)(2,1)S(1)} %all-to-all-done.1.near_ref), channel_id=1, source_target_pairs={{0,8},{8,0},{1,9},{9,1},{2,10},{10,2},{3,11},{11,3},{4,12},{12,4},... | collective-permute-start | bytes 2752520 | tf_op jit(solution)/shard_map/ppermute | solution.py:313
  52.0 7.9 %collective-permute-start.2 = (bf16[128,1024]{1,0:T(8,128)(2,1)S(1)}, bf16[128,1024]{1,0:T(8,128)(2,1)S(1)}, u32[]{:S(2)}, u32[]{:S(2)}) collective-permute-start(bf16[128,1024]{1,0:T(8,128)(2,1)S(1)} %shard_map.122.own_ref), channel_id=1, source_target_pairs={{0,48},{16,0},{32,16},{48,32},{1,49},{17,1},{33,17},{49,33},{2,50}... | collective-permute-start | bytes 786440 | tf_op jit(solution)/shard_map/ppermute | solution.py:321
  54.2 8.8 %collective-permute-start.1 = (bf16[128,1024]{1,0:T(8,128)(2,1)S(1)}, bf16[128,1024]{1,0:T(8,128)(2,1)S(1)}, u32[]{:S(2)}, u32[]{:S(2)}) collective-permute-start(bf16[128,1024]{1,0:T(8,128)(2,1)S(1)} %shard_map.122.own_ref), channel_id=1, source_target_pairs={{0,16},{16,32},{32,48},{48,0},{1,17},{17,33},{33,49},{49,1},{2,18}... | collective-permute-start | bytes 786440 | tf_op jit(solution)/shard_map/ppermute | solution.py:317
  65.9 23.0 %copy-start.3 = (bf16[16,3584]{1,0:T(8,128)(2,1)S(1)}, bf16[16,3584]{1,0:T(8,128)(2,1)}, u32[]{:S(2)}) copy-start(bf16[16,3584]{1,0:T(8,128)(2,1)} %param.15) | copy-start | bytes 344068
  65.9 23.1 %copy-start.5 = (f32[3584]{0:T(1024)S(1)}, f32[3584]{0:T(1024)}, u32[]{:S(2)}) copy-start(f32[3584]{0:T(1024)} %param.16) | copy-start | bytes 43012
  65.9 22.8 %all-to-all-start.2 = ((bf16[32,16,896]{2,1,0:T(8,128)(2,1)}), bf16[32,16,896]{2,1,0:T(8,128)(2,1)S(1)}, u32[]{:S(2)}, u32[]{:S(2)}) async-start(bf16[32,16,896]{2,1,0:T(8,128)(2,1)} %shard_map.124), calls=%async_computation.2 | async-start | bytes 1835008 | tf_op jit(solution)/shard_map/all_to_all | solution.py:377
  73.7 2.2 %collective-permute-start.5 = (s32[16,8]{0,1:T(8,128)S(1)}, s32[16,8]{0,1:T(8,128)S(1)}, u32[]{:S(2)}, u32[]{:S(2)}) collective-permute-start(s32[16,8]{0,1:T(8,128)S(1)} %copy-done.6), channel_id=1, source_target_pairs={{0,8},{8,0},{1,9},{9,1},{2,10},{10,2},{3,11},{11,3},{4,12},{12,4},... | collective-permute-start | bytes 1544 | tf_op jit(solution)/shard_map/ppermute | solution.py:313
  89.0 98.9 %copy-start.2 = (bf16[16,3584]{1,0:T(8,128)(2,1)}, bf16[16,3584]{1,0:T(8,128)(2,1)S(1)}, u32[]{:S(2)}) copy-start(bf16[16,3584]{1,0:T(8,128)(2,1)S(1)} %get-tuple-element.11) | copy-start | bytes 344068
  89.2 3.9 %collective-permute-start.7 = (bf16[16,3584]{1,0:T(8,128)(2,1)S(1)}, bf16[16,3584]{1,0:T(8,128)(2,1)S(1)}, u32[]{:S(2)}, u32[]{:S(2)}) collective-permute-start(bf16[16,3584]{1,0:T(8,128)(2,1)S(1)} %fusion.2), channel_id=1, source_target_pairs={{0,8},{8,0},{1,9},{9,1},{2,10},{10,2},{3,11},{11,3},{4,12},{12,4},... | collective-permute-start | bytes 344072 | tf_op jit(solution)/shard_map/ppermute | solution.py:313
  93.0 42.3 %copy-start.1 = (bf16[1,3584,512]{2,1,0:T(8,128)(2,1)S(1)}, bf16[1,3584,512]{2,1,0:T(8,128)(2,1)}, u32[]{:S(2)}) copy-start(bf16[1,3584,512]{2,1,0:T(8,128)(2,1)} %param.20) | copy-start | bytes 11010052
  94.4 41.0 %copy-start = (bf16[1,3584,512]{2,1,0:T(8,128)(2,1)S(1)}, bf16[1,3584,512]{2,1,0:T(8,128)(2,1)}, u32[]{:S(2)}) copy-start(bf16[1,3584,512]{2,1,0:T(8,128)(2,1)} %param.19) | copy-start | bytes 11010052
  141.2 7.4 %copy-start.4 = (s32[16,8]{0,1:T(8,128)S(1)}, s32[16,8]{0,1:T(8,128)}, u32[]{:S(2)}) copy-start(s32[16,8]{0,1:T(8,128)} %param.18) | copy-start | bytes 1540
  141.2 40.4 %all-to-all-start.4 = ((bf16[64,3,2,3584]{3,2,1,0:T(2,128)(2,1)}), bf16[64,3,2,3584]{3,2,1,0:T(2,128)(2,1)S(1)}, u32[]{:S(2)}, u32[]{:S(2)}) async-start(bf16[64,3,2,3584]{3,2,1,0:T(2,128)(2,1)} %bitcast.42), calls=%async_computation.4 | async-start | bytes 5505024 | tf_op jit(solution)/shard_map/all_to_all | solution.py:388
  148.6 2.4 %collective-permute-start.6 = (f32[16,8]{0,1:T(8,128)S(1)}, f32[16,8]{0,1:T(8,128)S(1)}, u32[]{:S(2)}, u32[]{:S(2)}) collective-permute-start(f32[16,8]{0,1:T(8,128)S(1)} %convert_divide_fusion), channel_id=1, source_target_pairs={{0,8},{8,0},{1,9},{9,1},{2,10},{10,2},{3,11},{11,3},{4,12},{12,4},... | collective-permute-start | bytes 1544 | tf_op jit(solution)/shard_map/ppermute | solution.py:313
  183.1 4.9 %collective-permute-start.8 = (f32[16,3584]{1,0:T(8,128)S(1)}, f32[16,3584]{1,0:T(8,128)S(1)}, u32[]{:S(2)}, u32[]{:S(2)}) collective-permute-start(f32[16,3584]{1,0:T(8,128)S(1)} %get-tuple-element.9), channel_id=1, source_target_pairs={{0,8},{8,0},{1,9},{9,1},{2,10},{10,2},{3,11},{11,3},{4,12},{12,4},... | collective-permute-start | bytes 688136 | tf_op jit(solution)/shard_map/ppermute | solution.py:313

commit v18 on v15

--- a/solution.py
+++ b/solution.py
@@ -16,15 +16,19 @@
 SLOTS = (slice(0, 3),)
 
 CTX = ("z_lo", "x", "core")
-CTX_CHIPS = ("z_lo", "x")
+CTX_CHIPS = ("x", "z_lo")
 EP = ("z_hi", "y")
-CHIPS = ("z_lo", "x", "z_hi", "y")
+CHIPS = ("z_hi", "z_lo", "x", "y")
 SIZES = (2, 4, 2, 2, 4)
 NAMES = ("z_lo", "x", "core", "z_hi", "y")
 SWAP = ((0, 1), (1, 0))
 BF = jnp.bfloat16
 F32 = jnp.float32
 LOG2E = 1.4426950408889634
+
+
+def chip_number(i):
+    return i % 2 * 4 + i // 2
 
 
 def in_hbm(a):
@@ -65,7 +69,7 @@
         s = jnp.dot(latq_ref[...], lat_ref[:, j * span : (j + 1) * span], preferred_element_type=F32)
         for b in range(span // rows):
             block = j * (span // rows) + b
-            pos = 2 * (block // 2) + (core if block % 2 == 0 else 1 - core)
+            pos = 2 * chip_number(block // 2) + (core if block % 2 == 0 else 1 - core)
             part = s[:, b * rows : (b + 1) * rows]
             part = jnp.where(ahead <= (ctx - pos) * rows, part, F32(-1e30))
             peak = jnp.maximum(peak, part)
@@ -257,7 +261,7 @@
     for side, ref in enumerate((near_ref, far_ref)):
         offset = (core if side == 0 else 1 - core) * deep
         for j in range(ref.shape[0]):
-            w_ref[pl.ds(pl.multiple_of(j * VD + offset, deep), deep)] = ref[j]
+            w_ref[pl.ds(pl.multiple_of(chip_number(j) * VD + offset, deep), deep)] = ref[j]
     for d in range(group):
         y = jnp.dot(x_ref[d * rows : (d + 1) * rows], w_ref[...], preferred_element_type=F32).astype(BF)
         target = lax.rem(x + d, group)
@@ -287,7 +291,7 @@
     group = w_ref.shape[1] // wide
     copies = []
     for i in range(out_ref.shape[0]):
-        first = i % group * wide
+        first = i // (out_ref.shape[0] // group) * wide
         copies.append(pltpu.make_async_copy(w_ref.at[:, first : first + wide], out_ref.at[i], sems.at[i]))
         copies[-1].start()
     for copy in copies:
@@ -330,7 +334,8 @@
 
     def of_core(a):
         a = a.reshape(2, tok, 8, 2, 4)
-        return jnp.where(core == 0, a[:, :, :, 0], a[:, :, :, 1]).reshape(2, tok, 32)
+        a = jnp.where(core == 0, a[:, :, :, 0], a[:, :, :, 1])
+        return a.reshape(2, tok, 8, 2, 2).transpose(0, 1, 3, 2, 4).reshape(2, tok, 32)
 
     weight, has = of_core(weight), of_core(has)
     count = has.astype(jnp.int32)

time: 188 us -> 186 us (0.989)
    all_to_all x1, starting transfers between devices: 7.35 us -> 5.4 us  [exchange(): lax.all_to_all(units, CHIPS, split_axis=0, concat_axis=0, tiled=True)]
where the time goes in v18:
time: 186 us; the launch traced here: 185 us
  blocking collectives  63 us (34%)
  waiting for transfers between devices  59.1 us (32%)
  starting transfers between devices  34.6 us (19%)
  Pallas kernels  23.3 us (13%)
  local copies, waits for them, and re-layouts  2.66 us (1%)
    all_to_all x1, blocking collectives, exchange(): lax.all_to_all(units, CHIPS, split_axis=0, concat_axis=0, tiled=True)  41.2 us
    all_to_all x1, waiting for transfers between devices, exchange(): lax.all_to_all(units, CHIPS, split_axis=0, concat_axis=0, tiled=True)  30.2 us
    all_to_all x1, blocking collectives, local(): lax.all_to_all(jnp.broadcast_to(latents[None], (8,) + latents.shape), CTX...  21.7 us
    ppermute x6, starting transfers between devices, swap(): return lax.ppermute(mine, 'core', SWAP)  13.3 us
    all_to_all x1, waiting for transfers between devices, local(): lax.all_to_all(attn, EP + ('x',), split_axis=0, concat_axis=0, tiled=True)  12.8 us
    pallas_call x1, Pallas kernels, attend(): pl.pallas_call(functools.partial(attend_kernel, cuts=cuts), in_specs=[pl....  9.82 us
    all_to_all x1, starting transfers between devices, local(): lax.all_to_all(attn, EP + ('x',), split_axis=0, concat_axis=0, tiled=True)  8.17 us
    ppermute x2, waiting for transfers between devices, down(): return lax.ppermute(a, 'x', [(i, (i + 3) % 4) for i in range(4)])  6.32 us
  transfers between devices with their start and end apart: 13, of which 11 were waited for; matrix products, arithmetic and copies ran while one was open for 1% of the time, Pallas kernels for 6%

profile of v18, /device:TPU:1, one launch (start us, length us, event | category | flops | bytes accessed | tf_op | source)
XLA Modules:
  0.0 185.4 jit_solution(15374529338082065170)
XLA Ops:
  0.6 1.1 broadcast_in_dim.32
  1.7 21.7 %all_to_all.25.near_ref = bf16[8,576,128]{2,1,0:T(8,128)(2,1)S(1)} all-to-all(bf16[8,576,128]{2,1,0:T(8,128)(2,1)S(1)} %broadcast_in_dim.32), channel_id=1, replica_groups=mesh['z_lo'=2,'x'=4,'core'=2,'z_hi'=2,'y'=4] {'x','z_lo'}, dimensions={0} | all-to-all | bytes 2359296 | tf_op jit(solution)/shard_map/all_to_all | solution.py:366
  23.4 2.2 %collective-permute-start = (bf16[8,576,128]{2,1,0:T(8,128)(2,1)S(1)}, bf16[8,576,128]{2,1,0:T(8,128)(2,1)S(1)}, u32[]{:S(2)}, u32[]{:S(2)}) collective-permute-start(bf16[8,576,128]{2,1,0:T(8,128)(2,1)S(1)} %all_to_all.25.near_ref), channel_id=1, source_target_pairs={{0,8},{8,0},{1,9},{9,1},{2,10},{10,2},{3,11},{11,3},{4,12},{12,4},... | collective-permute-start | bytes 3538952 | tf_op jit(solution)/shard_map/ppermute | solution.py:314
  25.6 2.0 %shard_map.123 = bf16[8,64,896]{2,1,0:T(8,128)(2,1)} custom-call(bf16[64,3584]{1,0:T(8,128)(2,1)} %w_ref.1), custom_call_target="tpu_custom_call" | custom-call | bytes 1376256 | tf_op jit(solution)/shard_map/pallas_call | solution.py:303
  27.7 3.6 %all-to-all-start.1 = ((bf16[8,64,896]{2,1,0:T(8,128)(2,1)}), bf16[8,64,896]{2,1,0:T(8,128)(2,1)S(1)}, u32[]{:S(2)}, u32[]{:S(2)}) async-start(bf16[8,64,896]{2,1,0:T(8,128)(2,1)} %shard_map.123), calls=%async_computation.1 | async-start | bytes 1835008 | tf_op jit(solution)/shard_map/all_to_all | solution.py:371
  31.2 0.1 pad_add_fusion.1.ids_ref
  31.3 0.0 collective-permute-done.far_ref
  31.3 9.8 %shard_map.122.own_ref = bf16[128,1024]{1,0:T(8,128)(2,1)S(1)} custom-call(s32[3]{0:T(128)S(1)} %pad_add_fusion.1.ids_ref, bf16[128,1536]{1,0:T(8,128)(2,1)} %q_hbm.1, bf16[512,2048]{1,0:T(8,128)(2,1)} %w_hbm.1, bf16[8,576,128]{2,1,0:T(8,128)(2,1)S(1)} %all_to_all.25.near_ref, bf16[8,576,128]{2,1,0:T(8,128)(2,1)S(1)} %collective-permute-done.far_ref), custom_call_target="tpu_custom_call" | custom-call | flops 4563402752 | bytes 8000000 | tf_op jit(solution)/shard_map/pallas_call | solution.py:107
  41.1 2.7 %collective-permute-start.2 = (bf16[128,1024]{1,0:T(8,128)(2,1)S(1)}, bf16[128,1024]{1,0:T(8,128)(2,1)S(1)}, u32[]{:S(2)}, u32[]{:S(2)}) collective-permute-start(bf16[128,1024]{1,0:T(8,128)(2,1)S(1)} %shard_map.122.own_ref), channel_id=1, source_target_pairs={{0,48},{16,0},{32,16},{48,32},{1,49},{17,1},{33,17},{49,33},{2,50}... | collective-permute-start | bytes 786440 | tf_op jit(solution)/shard_map/ppermute | solution.py:322
  43.8 0.0 collective-permute-start.1
  43.8 2.8 %all-to-all-done.1.near_ref = bf16[8,64,896]{2,1,0:T(8,128)(2,1)S(1)} async-done(((bf16[8,64,896]{2,1,0:T(8,128)(2,1)}), bf16[8,64,896]{2,1,0:T(8,128)(2,1)S(1)}, u32[]{:S(2)}, u32[]{:S(2)}) %all-to-all-start.1) | async-done | bytes 917536 | tf_op jit(solution)/shard_map/all_to_all | solution.py:371
  46.6 2.7 %collective-permute-done.2.after_ref = bf16[128,1024]{1,0:T(8,128)(2,1)S(1)} collective-permute-done((bf16[128,1024]{1,0:T(8,128)(2,1)S(1)}, bf16[128,1024]{1,0:T(8,128)(2,1)S(1)}, u32[]{:S(2)}, u32[]{:S(2)}) %collective-permute-start.2) | collective-permute-done | bytes 262176 | tf_op jit(solution)/shard_map/ppermute | solution.py:322
  49.2 3.1 %collective-permute-done.1.before_ref = bf16[128,1024]{1,0:T(8,128)(2,1)S(1)} collective-permute-done((bf16[128,1024]{1,0:T(8,128)(2,1)S(1)}, bf16[128,1024]{1,0:T(8,128)(2,1)S(1)}, u32[]{:S(2)}, u32[]{:S(2)}) %collective-permute-start.1) | collective-permute-done | bytes 262176 | tf_op jit(solution)/shard_map/ppermute | solution.py:318
  52.3 1.4 collective-permute-start.5
  53.8 0.0 copy-start.6
  53.8 0.1 collective-permute-start.4
  53.9 1.5 collective-permute-start.3
  55.3 3.7 %collective-permute-done.4.right_ref = bf16[128,512]{1,0:T(8,128)(2,1)S(1)} collective-permute-done((bf16[128,512]{1,0:T(8,128)(2,1)S(1)}, bf16[128,512]{1,0:T(8,128)(2,1)S(1)}, u32[]{:S(2)}, u32[]{:S(2)}) %collective-permute-start.4) | collective-permute-done | bytes 131104 | tf_op jit(solution)/shard_map/ppermute | solution.py:322
  59.0 1.1 collective-permute-done.3.left_ref
  60.0 0.0 collective-permute-done.5.far_ref
  60.0 2.9 %shard_map.124 = bf16[32,16,896]{2,1,0:T(8,128)(2,1)} custom-call(s32[3]{0:T(128)S(1)} %pad_add_fusion.1.ids_ref, bf16[128,1024]{1,0:T(8,128)(2,1)S(1)} %shard_map.122.own_ref, bf16[128,1024]{1,0:T(8,128)(2,1)S(1)} %collective-permute-done.1.before_ref, bf16[128,1024]{1,0:T(8,128)(2,1)S(1)} %collective-permute-done.2.after_ref, ...), custom_call_target="tpu_custom_call" | custom-call | flops 939524096 | bytes 1835008 | tf_op jit(solution)/shard_map/pallas_call | solution.py:276
  62.9 8.2 %all-to-all-start.2 = ((bf16[32,16,896]{2,1,0:T(8,128)(2,1)}), bf16[32,16,896]{2,1,0:T(8,128)(2,1)S(1)}, u32[]{:S(2)}, u32[]{:S(2)}) async-start(bf16[32,16,896]{2,1,0:T(8,128)(2,1)} %shard_map.124), calls=%async_computation.2 | async-start | bytes 1835008 | tf_op jit(solution)/shard_map/all_to_all | solution.py:379
  71.1 1.1 collective-permute-start.6
  72.3 0.1 and.49
  72.4 0.1 and.50
  72.4 0.7 collective-permute-done.6
  73.1 0.1 copy.58
  73.2 0.1 fusion.5
  73.3 0.1 copy.59
  73.5 0.1 copy.63
  73.6 0.1 copy.62
  73.7 12.8 %all-to-all-done.2 = bf16[32,16,896]{2,1,0:T(8,128)(2,1)S(1)} async-done(((bf16[32,16,896]{2,1,0:T(8,128)(2,1)}), bf16[32,16,896]{2,1,0:T(8,128)(2,1)S(1)}, u32[]{:S(2)}, u32[]{:S(2)}) %all-to-all-start.2) | async-done | bytes 917536 | tf_op jit(solution)/shard_map/all_to_all | solution.py:379
  86.5 0.1 convert_reduce_fusion
  86.7 0.0 copy-done.3
  86.7 0.2 fusion
  86.9 0.1 fusion.2
  87.0 2.6 %collective-permute-start.8 = (bf16[16,3584]{1,0:T(8,128)(2,1)S(1)}, bf16[16,3584]{1,0:T(8,128)(2,1)S(1)}, u32[]{:S(2)}, u32[]{:S(2)}) collective-permute-start(bf16[16,3584]{1,0:T(8,128)(2,1)S(1)} %fusion.2), channel_id=1, source_target_pairs={{0,8},{8,0},{1,9},{9,1},{2,10},{10,2},{3,11},{11,3},{4,12},{12,4},... | collective-permute-start | bytes 344072 | tf_op jit(solution)/shard_map/ppermute | solution.py:314
  89.6 0.1 bitcast_and_fusion
  89.7 0.1 copy.64
  89.9 0.1 broadcast_in_dim.33
  89.9 0.1 reshape.124
  90.1 0.5 collective-permute-done.8
  90.6 0.0 copy-start.1
  90.6 1.4 shard_map.125
  92.0 0.0 copy-start
  92.0 41.2 %all_to_all.26 = bf16[64,3,2,3584]{3,2,1,0:T(2,128)(2,1)S(1)} all-to-all(bf16[64,3,2,3584]{3,2,1,0:T(2,128)(2,1)S(1)} %bitcast.44), channel_id=1, replica_groups=mesh['z_lo'=2,'x'=4,'core'=2,'z_hi'=2,'y'=4] {'z_hi','z_lo','x','y'}, dimensions={0} | all-to-all | bytes 5505024 | tf_op jit(solution)/shard_map/all_to_all | solution.py:390
  133.2 5.9 %shard_map.126 = bf16[192,2,3584]{2,1,0:T(2,128)(2,1)} custom-call(bf16[192,2,3584]{2,1,0:T(2,128)(2,1)S(1)} %bitcast.45, bf16[3584,512]{1,0:T(8,128)(2,1)S(1)} %bitcast.46, bf16[3584,512]{1,0:T(8,128)(2,1)S(1)} %bitcast.47, bf16[512,3584]{1,0:T(8,128)(2,1)} %bitcast.50), custom_call_target="tpu_custom_call" | custom-call | flops 4227858432 | bytes 17000000 | tf_op jit(solution)/shard_map/pallas_call | solution.py:168
  139.1 0.0 copy-start.4
  139.1 5.4 %all-to-all-start.4 = ((bf16[64,3,2,3584]{3,2,1,0:T(2,128)(2,1)}), bf16[64,3,2,3584]{3,2,1,0:T(2,128)(2,1)S(1)}, u32[]{:S(2)}, u32[]{:S(2)}) async-start(bf16[64,3,2,3584]{3,2,1,0:T(2,128)(2,1)} %bitcast.48), calls=%async_computation.4 | async-start | bytes 5505024 | tf_op jit(solution)/shard_map/all_to_all | solution.py:390
  144.5 2.2 %collective-permute-start.7 = (f32[16,8]{0,1:T(8,128)S(1)}, f32[16,8]{0,1:T(8,128)S(1)}, u32[]{:S(2)}, u32[]{:S(2)}) collective-permute-start(f32[16,8]{0,1:T(8,128)S(1)} %convert_divide_fusion), channel_id=1, source_target_pairs={{0,8},{8,0},{1,9},{9,1},{2,10},{10,2},{3,11},{11,3},{4,12},{12,4},... | collective-permute-start | bytes 1544 | tf_op jit(solution)/shard_map/ppermute | solution.py:314
  146.7 0.1 copy.71
  146.8 0.7 collective-permute-done.7
  147.5 0.1 copy.65
  147.6 0.1 select_reduce_fusion
  147.8 0.1 copy.66
  147.9 0.1 copy.69
  148.0 0.1 copy.70
  148.1 0.1 broadcast_in_dim.65
  148.1 0.1 copy.72
  148.3 30.2 %all-to-all-done.4 = bf16[64,3,2,3584]{3,2,1,0:T(2,128)(2,1)S(1)} async-done(((bf16[64,3,2,3584]{3,2,1,0:T(2,128)(2,1)}), bf16[64,3,2,3584]{3,2,1,0:T(2,128)(2,1)S(1)}, u32[]{:S(2)}, u32[]{:S(2)}) %all-to-all-start.4) | async-done | bytes 2752544 | tf_op jit(solution)/shard_map/all_to_all | solution.py:390
  178.4 1.4 shard_map.127
  179.8 3.7 %collective-permute-start.9 = (f32[16,3584]{1,0:T(8,128)S(1)}, f32[16,3584]{1,0:T(8,128)S(1)}, u32[]{:S(2)}, u32[]{:S(2)}) collective-permute-start(f32[16,3584]{1,0:T(8,128)S(1)} %get-tuple-element.11), channel_id=1, source_target_pairs={{0,8},{8,0},{1,9},{9,1},{2,10},{10,2},{3,11},{11,3},{4,12},{12,4},... | collective-permute-start | bytes 688136 | tf_op jit(solution)/shard_map/ppermute | solution.py:314
  183.6 1.1 collective-permute-done.9
  184.7 0.7 fusion.4
  (35 shorter events, 0.4 us)
Async XLA Ops:
  23.4 7.9 %collective-permute-start = (bf16[8,576,128]{2,1,0:T(8,128)(2,1)S(1)}, bf16[8,576,128]{2,1,0:T(8,128)(2,1)S(1)}, u32[]{:S(2)}, u32[]{:S(2)}) collective-permute-start(bf16[8,576,128]{2,1,0:T(8,128)(2,1)S(1)} %all_to_all.25.near_ref), channel_id=1, source_target_pairs={{0,8},{8,0},{1,9},{9,1},{2,10},{10,2},{3,11},{11,3},{4,12},{12,4},... | collective-permute-start | bytes 3538952 | tf_op jit(solution)/shard_map/ppermute | solution.py:314
  27.7 18.9 %all-to-all-start.1 = ((bf16[8,64,896]{2,1,0:T(8,128)(2,1)}), bf16[8,64,896]{2,1,0:T(8,128)(2,1)S(1)}, u32[]{:S(2)}, u32[]{:S(2)}) async-start(bf16[8,64,896]{2,1,0:T(8,128)(2,1)} %shard_map.123), calls=%async_computation.1 | async-start | bytes 1835008 | tf_op jit(solution)/shard_map/all_to_all | solution.py:371
  41.1 8.1 %collective-permute-start.2 = (bf16[128,1024]{1,0:T(8,128)(2,1)S(1)}, bf16[128,1024]{1,0:T(8,128)(2,1)S(1)}, u32[]{:S(2)}, u32[]{:S(2)}) collective-permute-start(bf16[128,1024]{1,0:T(8,128)(2,1)S(1)} %shard_map.122.own_ref), channel_id=1, source_target_pairs={{0,48},{16,0},{32,16},{48,32},{1,49},{17,1},{33,17},{49,33},{2,50}... | collective-permute-start | bytes 786440 | tf_op jit(solution)/shard_map/ppermute | solution.py:322
  43.8 8.5 %collective-permute-start.1 = (bf16[128,1024]{1,0:T(8,128)(2,1)S(1)}, bf16[128,1024]{1,0:T(8,128)(2,1)S(1)}, u32[]{:S(2)}, u32[]{:S(2)}) collective-permute-start(bf16[128,1024]{1,0:T(8,128)(2,1)S(1)} %shard_map.122.own_ref), channel_id=1, source_target_pairs={{0,16},{16,32},{32,48},{48,0},{1,17},{17,33},{33,49},{49,1},{2,18}... | collective-permute-start | bytes 786440 | tf_op jit(solution)/shard_map/ppermute | solution.py:318
  52.3 7.7 %collective-permute-start.5 = (bf16[8,64,896]{2,1,0:T(8,128)(2,1)S(1)}, bf16[8,64,896]{2,1,0:T(8,128)(2,1)S(1)}, u32[]{:S(2)}, u32[]{:S(2)}) collective-permute-start(bf16[8,64,896]{2,1,0:T(8,128)(2,1)S(1)} %all-to-all-done.1.near_ref), channel_id=1, source_target_pairs={{0,8},{8,0},{1,9},{9,1},{2,10},{10,2},{3,11},{11,3},{4,12},{12,4},... | collective-permute-start | bytes 2752520 | tf_op jit(solution)/shard_map/ppermute | solution.py:314
  53.8 17.4 %copy-start.6 = (s32[16,8]{0,1:T(8,128)S(1)}, s32[16,8]{0,1:T(8,128)}, u32[]{:S(2)}) copy-start(s32[16,8]{0,1:T(8,128)} %param.17) | copy-start | bytes 1540
  53.8 5.2 %collective-permute-start.4 = (bf16[128,512]{1,0:T(8,128)(2,1)S(1)}, bf16[128,512]{1,0:T(8,128)(2,1)S(1)}, u32[]{:S(2)}, u32[]{:S(2)}) collective-permute-start(bf16[128,512]{1,0:T(8,128)(2,1)S(1)} %slice.20), channel_id=1, source_target_pairs={{0,48},{16,0},{32,16},{48,32},{1,49},{17,1},{33,17},{49,33},{2,50}... | collective-permute-start | bytes 393224 | tf_op jit(solution)/shard_map/ppermute | solution.py:322
  53.9 6.2 %collective-permute-start.3 = (bf16[128,512]{1,0:T(8,128)(2,1)S(1)}, bf16[128,512]{1,0:T(8,128)(2,1)S(1)}, u32[]{:S(2)}, u32[]{:S(2)}) collective-permute-start(bf16[128,512]{1,0:T(8,128)(2,1)S(1)} %slice.19), channel_id=1, source_target_pairs={{0,16},{16,32},{32,48},{48,0},{1,17},{17,33},{33,49},{49,1},{2,18}... | collective-permute-start | bytes 393224 | tf_op jit(solution)/shard_map/ppermute | solution.py:318
  62.9 23.7 %copy-start.3 = (bf16[16,3584]{1,0:T(8,128)(2,1)S(1)}, bf16[16,3584]{1,0:T(8,128)(2,1)}, u32[]{:S(2)}) copy-start(bf16[16,3584]{1,0:T(8,128)(2,1)} %param.15) | copy-start | bytes 344068
  62.9 23.9 %copy-start.5 = (f32[3584]{0:T(1024)S(1)}, f32[3584]{0:T(1024)}, u32[]{:S(2)}) copy-start(f32[3584]{0:T(1024)} %param.16) | copy-start | bytes 43012
  62.9 23.6 %all-to-all-start.2 = ((bf16[32,16,896]{2,1,0:T(8,128)(2,1)}), bf16[32,16,896]{2,1,0:T(8,128)(2,1)S(1)}, u32[]{:S(2)}, u32[]{:S(2)}) async-start(bf16[32,16,896]{2,1,0:T(8,128)(2,1)} %shard_map.124), calls=%async_computation.2 | async-start | bytes 1835008 | tf_op jit(solution)/shard_map/all_to_all | solution.py:379
  71.1 2.0 %collective-permute-start.6 = (s32[16,8]{0,1:T(8,128)S(1)}, s32[16,8]{0,1:T(8,128)S(1)}, u32[]{:S(2)}, u32[]{:S(2)}) collective-permute-start(s32[16,8]{0,1:T(8,128)S(1)} %copy-done.6), channel_id=1, source_target_pairs={{0,8},{8,0},{1,9},{9,1},{2,10},{10,2},{3,11},{11,3},{4,12},{12,4},... | collective-permute-start | bytes 1544 | tf_op jit(solution)/shard_map/ppermute | solution.py:314
  86.8 97.8 %copy-start.2 = (bf16[16,3584]{1,0:T(8,128)(2,1)}, bf16[16,3584]{1,0:T(8,128)(2,1)S(1)}, u32[]{:S(2)}) copy-start(bf16[16,3584]{1,0:T(8,128)(2,1)S(1)} %get-tuple-element.13) | copy-start | bytes 344068
  87.0 3.6 %collective-permute-start.8 = (bf16[16,3584]{1,0:T(8,128)(2,1)S(1)}, bf16[16,3584]{1,0:T(8,128)(2,1)S(1)}, u32[]{:S(2)}, u32[]{:S(2)}) collective-permute-start(bf16[16,3584]{1,0:T(8,128)(2,1)S(1)} %fusion.2), channel_id=1, source_target_pairs={{0,8},{8,0},{1,9},{9,1},{2,10},{10,2},{3,11},{11,3},{4,12},{12,4},... | collective-permute-start | bytes 344072 | tf_op jit(solution)/shard_map/ppermute | solution.py:314
  90.6 42.6 %copy-start.1 = (bf16[1,3584,512]{2,1,0:T(8,128)(2,1)S(1)}, bf16[1,3584,512]{2,1,0:T(8,128)(2,1)}, u32[]{:S(2)}) copy-start(bf16[1,3584,512]{2,1,0:T(8,128)(2,1)} %param.20) | copy-start | bytes 11010052
  92.0 41.3 %copy-start = (bf16[1,3584,512]{2,1,0:T(8,128)(2,1)S(1)}, bf16[1,3584,512]{2,1,0:T(8,128)(2,1)}, u32[]{:S(2)}) copy-start(bf16[1,3584,512]{2,1,0:T(8,128)(2,1)} %param.19) | copy-start | bytes 11010052
  139.1 5.4 %copy-start.4 = (s32[16,8]{0,1:T(8,128)S(1)}, s32[16,8]{0,1:T(8,128)}, u32[]{:S(2)}) copy-start(s32[16,8]{0,1:T(8,128)} %param.18) | copy-start | bytes 1540
  139.1 39.4 %all-to-all-start.4 = ((bf16[64,3,2,3584]{3,2,1,0:T(2,128)(2,1)}), bf16[64,3,2,3584]{3,2,1,0:T(2,128)(2,1)S(1)}, u32[]{:S(2)}, u32[]{:S(2)}) async-start(bf16[64,3,2,3584]{3,2,1,0:T(2,128)(2,1)} %bitcast.48), calls=%async_computation.4 | async-start | bytes 5505024 | tf_op jit(solution)/shard_map/all_to_all | solution.py:390
  144.5 3.0 %collective-permute-start.7 = (f32[16,8]{0,1:T(8,128)S(1)}, f32[16,8]{0,1:T(8,128)S(1)}, u32[]{:S(2)}, u32[]{:S(2)}) collective-permute-start(f32[16,8]{0,1:T(8,128)S(1)} %convert_divide_fusion), channel_id=1, source_target_pairs={{0,8},{8,0},{1,9},{9,1},{2,10},{10,2},{3,11},{11,3},{4,12},{12,4},... | collective-permute-start | bytes 1544 | tf_op jit(solution)/shard_map/ppermute | solution.py:314
  179.8 4.8 %collective-permute-start.9 = (f32[16,3584]{1,0:T(8,128)S(1)}, f32[16,3584]{1,0:T(8,128)S(1)}, u32[]{:S(2)}, u32[]{:S(2)}) collective-permute-start(f32[16,3584]{1,0:T(8,128)S(1)} %get-tuple-element.11), channel_id=1, source_target_pairs={{0,8},{8,0},{1,9},{9,1},{2,10},{10,2},{3,11},{11,3},{4,12},{12,4},... | collective-permute-start | bytes 688136 | tf_op jit(solution)/shard_map/ppermute | solution.py:314

commit v19 on v18

--- a/solution.py
+++ b/solution.py
@@ -246,7 +246,8 @@
     )(*[a for part in parts for a in part])
 
 
-def project_kernel(ids_ref, own_ref, before_ref, after_ref, left_ref, right_ref, near_ref, far_ref, out_ref, x_ref, w_ref):
+def project_kernel(ids_ref, own_ref, before_ref, after_ref, left_ref, right_ref, *refs):
+    *block_refs, out_ref, x_ref, w_ref = refs
     rows = own_ref.shape[0]
     group, tok = 4, out_ref.shape[1]
     parts = out_ref.shape[0] // group
@@ -258,10 +259,12 @@
     x_ref[2 * rows : 3 * rows, half:] = right_ref[...]
     x_ref[3 * rows :] = before_ref[...]
     deep = VD // 2
-    for side, ref in enumerate((near_ref, far_ref)):
-        offset = (core if side == 0 else 1 - core) * deep
-        for j in range(ref.shape[0]):
-            w_ref[pl.ds(pl.multiple_of(chip_number(j) * VD + offset, deep), deep)] = ref[j]
+    z = lax.div(ids_ref[0], 2 * group)
+    for i, ref in enumerate(block_refs):
+        offset = (core if i < 2 else 1 - core) * deep
+        plane = (z if i % 2 == 0 else 1 - z) * group
+        for j in range(group):
+            w_ref[pl.ds(pl.multiple_of((plane + j) * VD + offset, deep), deep)] = ref[j]
     for d in range(group):
         y = jnp.dot(x_ref[d * rows : (d + 1) * rows], w_ref[...], preferred_element_type=F32).astype(BF)
         target = lax.rem(x + d, group)
@@ -269,13 +272,13 @@
             out_ref[e * group + target] = y[e * tok : (e + 1) * tok]
 
 
-def project(ids, pieces, near, far, parts, width):
+def project(ids, pieces, blocks, parts, width):
     rows, depth = pieces[0].shape
     whole = pl.BlockSpec(memory_space=pltpu.VMEM)
     group = 4
     return pl.pallas_call(
         project_kernel,
-        in_specs=[pl.BlockSpec(memory_space=pltpu.SMEM)] + [whole] * (len(pieces) + 2),
+        in_specs=[pl.BlockSpec(memory_space=pltpu.SMEM)] + [whole] * (len(pieces) + len(blocks)),
         out_specs=whole,
         out_shape=jax.ShapeDtypeStruct((parts * group, rows // parts, width), BF),
         scratch_shapes=[pltpu.VMEM((group * rows, depth), BF), pltpu.VMEM((depth, width), BF)],
@@ -283,23 +286,22 @@
         cost_estimate=pl.CostEstimate(
             flops=2 * group * rows * depth * width, bytes_accessed=2 * depth * width, transcendentals=0
         ),
-    )(ids, *pieces, near, far)
+    )(ids, *pieces, *blocks)
 
 
 def blocks_kernel(w_ref, out_ref, sems):
     wide = out_ref.shape[2]
-    group = w_ref.shape[1] // wide
     copies = []
     for i in range(out_ref.shape[0]):
-        first = i // (out_ref.shape[0] // group) * wide
+        first = i * wide
         copies.append(pltpu.make_async_copy(w_ref.at[:, first : first + wide], out_ref.at[i], sems.at[i]))
         copies[-1].start()
     for copy in copies:
         copy.wait()
 
 
-def column_blocks(w, group, count):
-    shape = (count, w.shape[0], w.shape[1] // group)
+def column_blocks(w, count):
+    shape = (count, w.shape[0], w.shape[1] // count)
     return pl.pallas_call(
         blocks_kernel,
         in_specs=[pl.BlockSpec(memory_space=pltpu.VMEM)],
@@ -367,15 +369,17 @@
         jnp.broadcast_to(latents[None], (8,) + latents.shape), CTX_CHIPS, split_axis=0, concat_axis=0, tiled=True
     )
     far = swap(near)
-    w_blocks, _ = lax.optimization_barrier((column_blocks(w_out, group, 8), near[0, :8]))
-    w_near = lax.all_to_all(w_blocks, CTX_CHIPS, split_axis=0, concat_axis=0, tiled=True)
+    w_blocks, _ = lax.optimization_barrier((column_blocks(w_out, group), near[0, :8]))
+    w_near = lax.all_to_all(w_blocks, "x", split_axis=0, concat_axis=0, tiled=True)
     ids = jnp.stack([lax.axis_index(CTX), core, lax.axis_index("x")]).astype(jnp.int32)
     own = attend(ids, queries, w_kv, near, far, 4)
-    before, after, w_near = lax.optimization_barrier((up(own), down(own), w_near))
-    w_far = swap(w_near)
+    own, w_near = lax.optimization_barrier((own, w_near))
+    w_mate = lax.ppermute(w_near, "z_lo", SWAP)
+    before, after = up(own), down(own)
     half = own.shape[1] // 2
     left, right = up(before[:, :half]), down(after[:, half:])
-    attn = project(ids, (own, before, after, left, right), w_near, w_far, 8, columns)
+    blocks = (w_near, w_mate, swap(w_near), swap(w_mate))
+    attn = project(ids, (own, before, after, left, right), blocks, 8, columns)
     attn = lax.all_to_all(attn, EP + ("x",), split_axis=0, concat_axis=0, tiled=True)
     attn = jnp.sum(attn.reshape(8, group, tok, columns).astype(F32), axis=0)
     attn = attn.transpose(1, 0, 2).reshape(tok, width)

time: 186 us -> 196 us (1.054)
  waiting for transfers between devices: 59.1 us -> 64.8 us
  starting transfers between devices: 34.6 us -> 39.3 us
    ppermute x0 -> x1, waiting for transfers between devices: none -> 11 us  [local(): w_mate = lax.ppermute(w_near, 'z_lo', SWAP)]
    ppermute x2, starting transfers between devices: 2.74 us -> 6.11 us  [down(): return lax.ppermute(a, 'x', [(i, (i + 3) % 4) for i in range(4)])]
    all_to_all x1, waiting for transfers between devices: 12.8 us -> 9.84 us  [local(): lax.all_to_all(attn, EP + ('x',), split_axis=0, concat_axis=0, tiled=True)]
    all_to_all x1, waiting for transfers between devices: 2.76 us -> 0.01 us  [local(): lax.all_to_all(w_blocks, 'x', split_axis=0, concat_axis=0, tiled=True)]
    ppermute x6 -> x7, starting transfers between devices: 13.3 us -> 15.6 us  [swap(): return lax.ppermute(mine, 'core', SWAP)]
  transfers between devices with their start and end apart: 13 -> 15, of which waited for: 11 -> 10; matrix products, arithmetic and copies ran while one was open for 1% -> 1% of each run, Pallas kernels for 6% -> 6%
where the time goes in v19:
time: 196 us; the launch traced here: 195 us
  waiting for transfers between devices  64.8 us (33%)
  blocking collectives  62.8 us (32%)
  starting transfers between devices  39.3 us (20%)
  Pallas kernels  23.1 us (12%)
  local copies, waits for them, and re-layouts  2.65 us (1%)
    all_to_all x1, blocking collectives, exchange(): lax.all_to_all(units, CHIPS, split_axis=0, concat_axis=0, tiled=True)  41 us
    all_to_all x1, waiting for transfers between devices, exchange(): lax.all_to_all(units, CHIPS, split_axis=0, concat_axis=0, tiled=True)  30.2 us
    all_to_all x1, blocking collectives, local(): lax.all_to_all(jnp.broadcast_to(latents[None], (8,) + latents.shape), CTX...  21.7 us
    ppermute x7, starting transfers between devices, swap(): return lax.ppermute(mine, 'core', SWAP)  15.6 us
    ppermute x1, waiting for transfers between devices, local(): w_mate = lax.ppermute(w_near, 'z_lo', SWAP)  11 us
    all_to_all x1, waiting for transfers between devices, local(): lax.all_to_all(attn, EP + ('x',), split_axis=0, concat_axis=0, tiled=True)  9.84 us
    pallas_call x1, Pallas kernels, attend(): pl.pallas_call(functools.partial(attend_kernel, cuts=cuts), in_specs=[pl....  9.81 us
    all_to_all x1, starting transfers between devices, local(): lax.all_to_all(attn, EP + ('x',), split_axis=0, concat_axis=0, tiled=True)  7.78 us
  transfers between devices with their start and end apart: 15, of which 10 were waited for; matrix products, arithmetic and copies ran while one was open for 1% of the time, Pallas kernels for 6%

profile of v19, /device:TPU:1, one launch (start us, length us, event | category | flops | bytes accessed | tf_op | source)
XLA Modules:
  0.0 195.3 jit_solution(1435337626155074096)
XLA Ops:
  0.6 1.1 broadcast_in_dim.32
  1.7 21.7 %all_to_all.25.near_ref = bf16[8,576,128]{2,1,0:T(8,128)(2,1)S(1)} all-to-all(bf16[8,576,128]{2,1,0:T(8,128)(2,1)S(1)} %broadcast_in_dim.32), channel_id=1, replica_groups=mesh['z_lo'=2,'x'=4,'core'=2,'z_hi'=2,'y'=4] {'x','z_lo'}, dimensions={0} | all-to-all | bytes 2359296 | tf_op jit(solution)/shard_map/all_to_all | solution.py:368
  23.4 2.2 %collective-permute-start = (bf16[8,576,128]{2,1,0:T(8,128)(2,1)S(1)}, bf16[8,576,128]{2,1,0:T(8,128)(2,1)S(1)}, u32[]{:S(2)}, u32[]{:S(2)}) collective-permute-start(bf16[8,576,128]{2,1,0:T(8,128)(2,1)S(1)} %all_to_all.25.near_ref), channel_id=1, source_target_pairs={{0,8},{8,0},{1,9},{9,1},{2,10},{10,2},{3,11},{11,3},{4,12},{12,4},... | collective-permute-start | bytes 3538952 | tf_op jit(solution)/shard_map/ppermute | solution.py:316
  25.6 1.8 shard_map.123
  27.4 3.5 %all-to-all-start.1 = ((bf16[4,64,896]{2,1,0:T(8,128)(2,1)}), bf16[4,64,896]{2,1,0:T(8,128)(2,1)S(1)}, u32[]{:S(2)}, u32[]{:S(2)}) async-start(bf16[4,64,896]{2,1,0:T(8,128)(2,1)} %shard_map.123), calls=%async_computation.1 | async-start | bytes 917504 | tf_op jit(solution)/shard_map/all_to_all | solution.py:373
  30.9 0.1 pad_add_fusion.1.ids_ref
  31.0 0.0 collective-permute-done.far_ref
  31.0 9.8 %shard_map.122.own_ref = bf16[128,1024]{1,0:T(8,128)(2,1)S(1)} custom-call(s32[3]{0:T(128)S(1)} %pad_add_fusion.1.ids_ref, bf16[128,1536]{1,0:T(8,128)(2,1)} %q_hbm.1, bf16[512,2048]{1,0:T(8,128)(2,1)} %w_hbm.1, bf16[8,576,128]{2,1,0:T(8,128)(2,1)S(1)} %all_to_all.25.near_ref, bf16[8,576,128]{2,1,0:T(8,128)(2,1)S(1)} %collective-permute-done.far_ref), custom_call_target="tpu_custom_call" | custom-call | flops 4563402752 | bytes 8000000 | tf_op jit(solution)/shard_map/pallas_call | solution.py:107
  40.8 0.9 collective-permute-start.5
  41.8 0.3 collective-permute-start.6
  42.0 11.0 %collective-permute-done.5.refs_1_ = bf16[4,64,896]{2,1,0:T(8,128)(2,1)S(1)} collective-permute-done((bf16[4,64,896]{2,1,0:T(8,128)(2,1)S(1)}, bf16[4,64,896]{2,1,0:T(8,128)(2,1)S(1)}, u32[]{:S(2)}, u32[]{:S(2)}) %collective-permute-start.5) | collective-permute-done | bytes 458784 | tf_op jit(solution)/shard_map/ppermute | solution.py:377
  53.1 0.8 collective-permute-start.7
  53.9 2.6 %collective-permute-start.2 = (bf16[128,1024]{1,0:T(8,128)(2,1)S(1)}, bf16[128,1024]{1,0:T(8,128)(2,1)S(1)}, u32[]{:S(2)}, u32[]{:S(2)}) collective-permute-start(bf16[128,1024]{1,0:T(8,128)(2,1)S(1)} %shard_map.122.own_ref), channel_id=1, source_target_pairs={{0,48},{16,0},{32,16},{48,32},{1,49},{17,1},{33,17},{49,33},{2,50}... | collective-permute-start | bytes 786440 | tf_op jit(solution)/shard_map/ppermute | solution.py:324
  56.5 0.0 collective-permute-start.1
  56.5 5.7 %collective-permute-done.2.after_ref = bf16[128,1024]{1,0:T(8,128)(2,1)S(1)} collective-permute-done((bf16[128,1024]{1,0:T(8,128)(2,1)S(1)}, bf16[128,1024]{1,0:T(8,128)(2,1)S(1)}, u32[]{:S(2)}, u32[]{:S(2)}) %collective-permute-start.2) | collective-permute-done | bytes 262176 | tf_op jit(solution)/shard_map/ppermute | solution.py:324
  62.2 3.5 %collective-permute-start.4 = (bf16[128,512]{1,0:T(8,128)(2,1)S(1)}, bf16[128,512]{1,0:T(8,128)(2,1)S(1)}, u32[]{:S(2)}, u32[]{:S(2)}) collective-permute-start(bf16[128,512]{1,0:T(8,128)(2,1)S(1)} %slice.26), channel_id=1, source_target_pairs={{0,48},{16,0},{32,16},{48,32},{1,49},{17,1},{33,17},{49,33},{2,50}... | collective-permute-start | bytes 393224 | tf_op jit(solution)/shard_map/ppermute | solution.py:324
  65.7 0.0 collective-permute-done.1.before_ref
  65.7 0.0 copy-start.6
  65.8 0.1 collective-permute-start.3
  65.8 1.8 collective-permute-done.4.right_ref
  67.7 3.2 %collective-permute-done.3.left_ref = bf16[128,512]{1,0:T(8,128)(2,1)S(1)} collective-permute-done((bf16[128,512]{1,0:T(8,128)(2,1)S(1)}, bf16[128,512]{1,0:T(8,128)(2,1)S(1)}, u32[]{:S(2)}, u32[]{:S(2)}) %collective-permute-start.3) | collective-permute-done | bytes 131104 | tf_op jit(solution)/shard_map/ppermute | solution.py:320
  70.9 2.9 %shard_map.124 = bf16[32,16,896]{2,1,0:T(8,128)(2,1)} custom-call(s32[3]{0:T(128)S(1)} %pad_add_fusion.1.ids_ref, bf16[128,1024]{1,0:T(8,128)(2,1)S(1)} %shard_map.122.own_ref, bf16[128,1024]{1,0:T(8,128)(2,1)S(1)} %collective-permute-done.1.before_ref, bf16[128,1024]{1,0:T(8,128)(2,1)S(1)} %collective-permute-done.2.after_ref, ...), custom_call_target="tpu_custom_call" | custom-call | flops 939524096 | bytes 1835008 | tf_op jit(solution)/shard_map/pallas_call | solution.py:279
  73.7 7.8 %all-to-all-start.2 = ((bf16[32,16,896]{2,1,0:T(8,128)(2,1)}), bf16[32,16,896]{2,1,0:T(8,128)(2,1)S(1)}, u32[]{:S(2)}, u32[]{:S(2)}) async-start(bf16[32,16,896]{2,1,0:T(8,128)(2,1)} %shard_map.124), calls=%async_computation.2 | async-start | bytes 1835008 | tf_op jit(solution)/shard_map/all_to_all | solution.py:383
  81.5 2.7 %collective-permute-start.8 = (s32[16,8]{0,1:T(8,128)S(1)}, s32[16,8]{0,1:T(8,128)S(1)}, u32[]{:S(2)}, u32[]{:S(2)}) collective-permute-start(s32[16,8]{0,1:T(8,128)S(1)} %copy-done.6), channel_id=1, source_target_pairs={{0,8},{8,0},{1,9},{9,1},{2,10},{10,2},{3,11},{11,3},{4,12},{12,4},... | collective-permute-start | bytes 1544 | tf_op jit(solution)/shard_map/ppermute | solution.py:316
  84.3 0.1 and.49
  84.3 0.1 and.50
  84.4 0.7 collective-permute-done.8
  85.1 0.1 copy.58
  85.2 0.1 fusion.5
  85.3 0.1 copy.59
  85.5 0.1 copy.63
  85.6 0.1 copy.62
  85.7 9.8 %all-to-all-done.2 = bf16[32,16,896]{2,1,0:T(8,128)(2,1)S(1)} async-done(((bf16[32,16,896]{2,1,0:T(8,128)(2,1)}), bf16[32,16,896]{2,1,0:T(8,128)(2,1)S(1)}, u32[]{:S(2)}, u32[]{:S(2)}) %all-to-all-start.2) | async-done | bytes 917536 | tf_op jit(solution)/shard_map/all_to_all | solution.py:383
  95.6 0.1 convert_reduce_fusion
  95.7 0.2 fusion
  95.9 0.1 fusion.2
  96.0 3.7 %collective-permute-start.10 = (bf16[16,3584]{1,0:T(8,128)(2,1)S(1)}, bf16[16,3584]{1,0:T(8,128)(2,1)S(1)}, u32[]{:S(2)}, u32[]{:S(2)}) collective-permute-start(bf16[16,3584]{1,0:T(8,128)(2,1)S(1)} %fusion.2), channel_id=1, source_target_pairs={{0,8},{8,0},{1,9},{9,1},{2,10},{10,2},{3,11},{11,3},{4,12},{12,4},... | collective-permute-start | bytes 344072 | tf_op jit(solution)/shard_map/ppermute | solution.py:316
  99.7 0.1 bitcast_and_fusion
  99.8 0.1 copy.64
  100.0 0.1 broadcast_in_dim.33
  100.1 0.1 reshape.124
  100.2 0.5 collective-permute-done.10
  100.7 0.0 copy-start.1
  100.7 1.4 shard_map.125
  102.1 0.0 copy-start
  102.1 41.0 %all_to_all.26 = bf16[64,3,2,3584]{3,2,1,0:T(2,128)(2,1)S(1)} all-to-all(bf16[64,3,2,3584]{3,2,1,0:T(2,128)(2,1)S(1)} %bitcast.44), channel_id=1, replica_groups=mesh['z_lo'=2,'x'=4,'core'=2,'z_hi'=2,'y'=4] {'z_hi','z_lo','x','y'}, dimensions={0} | all-to-all | bytes 5505024 | tf_op jit(solution)/shard_map/all_to_all | solution.py:394
  143.1 5.8 %shard_map.126 = bf16[192,2,3584]{2,1,0:T(2,128)(2,1)} custom-call(bf16[192,2,3584]{2,1,0:T(2,128)(2,1)S(1)} %bitcast.45, bf16[3584,512]{1,0:T(8,128)(2,1)S(1)} %bitcast.46, bf16[3584,512]{1,0:T(8,128)(2,1)S(1)} %bitcast.47, bf16[512,3584]{1,0:T(8,128)(2,1)} %bitcast.50), custom_call_target="tpu_custom_call" | custom-call | flops 4227858432 | bytes 17000000 | tf_op jit(solution)/shard_map/pallas_call | solution.py:168
  149.0 0.0 copy-start.4
  149.0 5.4 %all-to-all-start.4 = ((bf16[64,3,2,3584]{3,2,1,0:T(2,128)(2,1)}), bf16[64,3,2,3584]{3,2,1,0:T(2,128)(2,1)S(1)}, u32[]{:S(2)}, u32[]{:S(2)}) async-start(bf16[64,3,2,3584]{3,2,1,0:T(2,128)(2,1)} %bitcast.48), calls=%async_computation.4 | async-start | bytes 5505024 | tf_op jit(solution)/shard_map/all_to_all | solution.py:394
  154.4 2.2 %collective-permute-start.9 = (f32[16,8]{0,1:T(8,128)S(1)}, f32[16,8]{0,1:T(8,128)S(1)}, u32[]{:S(2)}, u32[]{:S(2)}) collective-permute-start(f32[16,8]{0,1:T(8,128)S(1)} %convert_divide_fusion), channel_id=1, source_target_pairs={{0,8},{8,0},{1,9},{9,1},{2,10},{10,2},{3,11},{11,3},{4,12},{12,4},... | collective-permute-start | bytes 1544 | tf_op jit(solution)/shard_map/ppermute | solution.py:316
  156.6 0.1 copy.71
  156.7 0.7 collective-permute-done.9
  157.4 0.1 copy.65
  157.5 0.1 select_reduce_fusion
  157.7 0.1 copy.66
  157.8 0.1 copy.69
  157.9 0.1 copy.70
  158.0 0.1 broadcast_in_dim.65
  158.0 0.1 copy.72
  158.2 30.2 %all-to-all-done.4 = bf16[64,3,2,3584]{3,2,1,0:T(2,128)(2,1)S(1)} async-done(((bf16[64,3,2,3584]{3,2,1,0:T(2,128)(2,1)}), bf16[64,3,2,3584]{3,2,1,0:T(2,128)(2,1)S(1)}, u32[]{:S(2)}, u32[]{:S(2)}) %all-to-all-start.4) | async-done | bytes 2752544 | tf_op jit(solution)/shard_map/all_to_all | solution.py:394
  188.4 1.4 shard_map.127
  189.8 3.7 %collective-permute-start.11 = (f32[16,3584]{1,0:T(8,128)S(1)}, f32[16,3584]{1,0:T(8,128)S(1)}, u32[]{:S(2)}, u32[]{:S(2)}) collective-permute-start(f32[16,3584]{1,0:T(8,128)S(1)} %get-tuple-element.9), channel_id=1, source_target_pairs={{0,8},{8,0},{1,9},{9,1},{2,10},{10,2},{3,11},{11,3},{4,12},{12,4},... | collective-permute-start | bytes 688136 | tf_op jit(solution)/shard_map/ppermute | solution.py:316
  193.5 1.1 collective-permute-done.11
  194.6 0.7 fusion.4
  (39 shorter events, 0.4 us)
Async XLA Ops:
  23.4 7.6 %collective-permute-start = (bf16[8,576,128]{2,1,0:T(8,128)(2,1)S(1)}, bf16[8,576,128]{2,1,0:T(8,128)(2,1)S(1)}, u32[]{:S(2)}, u32[]{:S(2)}) collective-permute-start(bf16[8,576,128]{2,1,0:T(8,128)(2,1)S(1)} %all_to_all.25.near_ref), channel_id=1, source_target_pairs={{0,8},{8,0},{1,9},{9,1},{2,10},{10,2},{3,11},{11,3},{4,12},{12,4},... | collective-permute-start | bytes 3538952 | tf_op jit(solution)/shard_map/ppermute | solution.py:316
  27.4 13.4 %all-to-all-start.1 = ((bf16[4,64,896]{2,1,0:T(8,128)(2,1)}), bf16[4,64,896]{2,1,0:T(8,128)(2,1)S(1)}, u32[]{:S(2)}, u32[]{:S(2)}) async-start(bf16[4,64,896]{2,1,0:T(8,128)(2,1)} %shard_map.123), calls=%async_computation.1 | async-start | bytes 917504 | tf_op jit(solution)/shard_map/all_to_all | solution.py:373
  40.8 12.2 %collective-permute-start.5 = (bf16[4,64,896]{2,1,0:T(8,128)(2,1)S(1)}, bf16[4,64,896]{2,1,0:T(8,128)(2,1)S(1)}, u32[]{:S(2)}, u32[]{:S(2)}) collective-permute-start(bf16[4,64,896]{2,1,0:T(8,128)(2,1)S(1)} %all-to-all-done.1.refs_0_), channel_id=1, source_target_pairs={{0,64},{64,0},{1,65},{65,1},{2,66},{66,2},{3,67},{67,3},{4,68},{68... | collective-permute-start | bytes 1376264 | tf_op jit(solution)/shard_map/ppermute | solution.py:377
  41.8 29.1 %collective-permute-start.6 = (bf16[4,64,896]{2,1,0:T(8,128)(2,1)S(1)}, bf16[4,64,896]{2,1,0:T(8,128)(2,1)S(1)}, u32[]{:S(2)}, u32[]{:S(2)}) collective-permute-start(bf16[4,64,896]{2,1,0:T(8,128)(2,1)S(1)} %all-to-all-done.1.refs_0_), channel_id=1, source_target_pairs={{0,8},{8,0},{1,9},{9,1},{2,10},{10,2},{3,11},{11,3},{4,12},{12,4},... | collective-permute-start | bytes 1376264 | tf_op jit(solution)/shard_map/ppermute | solution.py:316
  53.1 17.8 %collective-permute-start.7 = (bf16[4,64,896]{2,1,0:T(8,128)(2,1)S(1)}, bf16[4,64,896]{2,1,0:T(8,128)(2,1)S(1)}, u32[]{:S(2)}, u32[]{:S(2)}) collective-permute-start(bf16[4,64,896]{2,1,0:T(8,128)(2,1)S(1)} %collective-permute-done.5.refs_1_), channel_id=1, source_target_pairs={{0,8},{8,0},{1,9},{9,1},{2,10},{10,2},{3,11},{11,3},{4,12},{12,4},... | collective-permute-start | bytes 1376264 | tf_op jit(solution)/shard_map/ppermute | solution.py:316
  53.9 8.4 %collective-permute-start.2 = (bf16[128,1024]{1,0:T(8,128)(2,1)S(1)}, bf16[128,1024]{1,0:T(8,128)(2,1)S(1)}, u32[]{:S(2)}, u32[]{:S(2)}) collective-permute-start(bf16[128,1024]{1,0:T(8,128)(2,1)S(1)} %shard_map.122.own_ref), channel_id=1, source_target_pairs={{0,48},{16,0},{32,16},{48,32},{1,49},{17,1},{33,17},{49,33},{2,50}... | collective-permute-start | bytes 786440 | tf_op jit(solution)/shard_map/ppermute | solution.py:324
  56.5 9.2 %collective-permute-start.1 = (bf16[128,1024]{1,0:T(8,128)(2,1)S(1)}, bf16[128,1024]{1,0:T(8,128)(2,1)S(1)}, u32[]{:S(2)}, u32[]{:S(2)}) collective-permute-start(bf16[128,1024]{1,0:T(8,128)(2,1)S(1)} %shard_map.122.own_ref), channel_id=1, source_target_pairs={{0,16},{16,32},{32,48},{48,0},{1,17},{17,33},{33,49},{49,1},{2,18}... | collective-permute-start | bytes 786440 | tf_op jit(solution)/shard_map/ppermute | solution.py:320
  62.2 5.4 %collective-permute-start.4 = (bf16[128,512]{1,0:T(8,128)(2,1)S(1)}, bf16[128,512]{1,0:T(8,128)(2,1)S(1)}, u32[]{:S(2)}, u32[]{:S(2)}) collective-permute-start(bf16[128,512]{1,0:T(8,128)(2,1)S(1)} %slice.26), channel_id=1, source_target_pairs={{0,48},{16,0},{32,16},{48,32},{1,49},{17,1},{33,17},{49,33},{2,50}... | collective-permute-start | bytes 393224 | tf_op jit(solution)/shard_map/ppermute | solution.py:324
  65.7 15.8 %copy-start.6 = (s32[16,8]{0,1:T(8,128)S(1)}, s32[16,8]{0,1:T(8,128)}, u32[]{:S(2)}) copy-start(s32[16,8]{0,1:T(8,128)} %param.17) | copy-start | bytes 1540
  65.8 5.1 %collective-permute-start.3 = (bf16[128,512]{1,0:T(8,128)(2,1)S(1)}, bf16[128,512]{1,0:T(8,128)(2,1)S(1)}, u32[]{:S(2)}, u32[]{:S(2)}) collective-permute-start(bf16[128,512]{1,0:T(8,128)(2,1)S(1)} %slice.25), channel_id=1, source_target_pairs={{0,16},{16,32},{32,48},{48,0},{1,17},{17,33},{33,49},{49,1},{2,18}... | collective-permute-start | bytes 393224 | tf_op jit(solution)/shard_map/ppermute | solution.py:320
  73.7 22.0 %copy-start.3 = (bf16[16,3584]{1,0:T(8,128)(2,1)S(1)}, bf16[16,3584]{1,0:T(8,128)(2,1)}, u32[]{:S(2)}) copy-start(bf16[16,3584]{1,0:T(8,128)(2,1)} %param.15) | copy-start | bytes 344068
  73.7 22.2 %copy-start.5 = (f32[3584]{0:T(1024)S(1)}, f32[3584]{0:T(1024)}, u32[]{:S(2)}) copy-start(f32[3584]{0:T(1024)} %param.16) | copy-start | bytes 43012
  73.7 21.8 %all-to-all-start.2 = ((bf16[32,16,896]{2,1,0:T(8,128)(2,1)}), bf16[32,16,896]{2,1,0:T(8,128)(2,1)S(1)}, u32[]{:S(2)}, u32[]{:S(2)}) async-start(bf16[32,16,896]{2,1,0:T(8,128)(2,1)} %shard_map.124), calls=%async_computation.2 | async-start | bytes 1835008 | tf_op jit(solution)/shard_map/all_to_all | solution.py:383
  81.5 3.5 %collective-permute-start.8 = (s32[16,8]{0,1:T(8,128)S(1)}, s32[16,8]{0,1:T(8,128)S(1)}, u32[]{:S(2)}, u32[]{:S(2)}) collective-permute-start(s32[16,8]{0,1:T(8,128)S(1)} %copy-done.6), channel_id=1, source_target_pairs={{0,8},{8,0},{1,9},{9,1},{2,10},{10,2},{3,11},{11,3},{4,12},{12,4},... | collective-permute-start | bytes 1544 | tf_op jit(solution)/shard_map/ppermute | solution.py:316
  95.9 98.7 %copy-start.2 = (bf16[16,3584]{1,0:T(8,128)(2,1)}, bf16[16,3584]{1,0:T(8,128)(2,1)S(1)}, u32[]{:S(2)}) copy-start(bf16[16,3584]{1,0:T(8,128)(2,1)S(1)} %get-tuple-element.11) | copy-start | bytes 344068
  96.0 4.7 %collective-permute-start.10 = (bf16[16,3584]{1,0:T(8,128)(2,1)S(1)}, bf16[16,3584]{1,0:T(8,128)(2,1)S(1)}, u32[]{:S(2)}, u32[]{:S(2)}) collective-permute-start(bf16[16,3584]{1,0:T(8,128)(2,1)S(1)} %fusion.2), channel_id=1, source_target_pairs={{0,8},{8,0},{1,9},{9,1},{2,10},{10,2},{3,11},{11,3},{4,12},{12,4},... | collective-permute-start | bytes 344072 | tf_op jit(solution)/shard_map/ppermute | solution.py:316
  100.7 42.4 %copy-start.1 = (bf16[1,3584,512]{2,1,0:T(8,128)(2,1)S(1)}, bf16[1,3584,512]{2,1,0:T(8,128)(2,1)}, u32[]{:S(2)}) copy-start(bf16[1,3584,512]{2,1,0:T(8,128)(2,1)} %param.20) | copy-start | bytes 11010052
  102.1 41.1 %copy-start = (bf16[1,3584,512]{2,1,0:T(8,128)(2,1)S(1)}, bf16[1,3584,512]{2,1,0:T(8,128)(2,1)}, u32[]{:S(2)}) copy-start(bf16[1,3584,512]{2,1,0:T(8,128)(2,1)} %param.19) | copy-start | bytes 11010052
  149.0 5.4 %copy-start.4 = (s32[16,8]{0,1:T(8,128)S(1)}, s32[16,8]{0,1:T(8,128)}, u32[]{:S(2)}) copy-start(s32[16,8]{0,1:T(8,128)} %param.18) | copy-start | bytes 1540
  149.0 39.4 %all-to-all-start.4 = ((bf16[64,3,2,3584]{3,2,1,0:T(2,128)(2,1)}), bf16[64,3,2,3584]{3,2,1,0:T(2,128)(2,1)S(1)}, u32[]{:S(2)}, u32[]{:S(2)}) async-start(bf16[64,3,2,3584]{3,2,1,0:T(2,128)(2,1)} %bitcast.48), calls=%async_computation.4 | async-start | bytes 5505024 | tf_op jit(solution)/shard_map/all_to_all | solution.py:394
  154.4 3.0 %collective-permute-start.9 = (f32[16,8]{0,1:T(8,128)S(1)}, f32[16,8]{0,1:T(8,128)S(1)}, u32[]{:S(2)}, u32[]{:S(2)}) collective-permute-start(f32[16,8]{0,1:T(8,128)S(1)} %convert_divide_fusion), channel_id=1, source_target_pairs={{0,8},{8,0},{1,9},{9,1},{2,10},{10,2},{3,11},{11,3},{4,12},{12,4},... | collective-permute-start | bytes 1544 | tf_op jit(solution)/shard_map/ppermute | solution.py:316
  189.8 4.8 %collective-permute-start.11 = (f32[16,3584]{1,0:T(8,128)S(1)}, f32[16,3584]{1,0:T(8,128)S(1)}, u32[]{:S(2)}, u32[]{:S(2)}) collective-permute-start(f32[16,3584]{1,0:T(8,128)S(1)} %get-tuple-element.9), channel_id=1, source_target_pairs={{0,8},{8,0},{1,9},{9,1},{2,10},{10,2},{3,11},{11,3},{4,12},{12,4},... | collective-permute-start | bytes 688136 | tf_op jit(solution)/shard_map/ppermute | solution.py:316

commit v20 on v19

--- a/solution.py
+++ b/solution.py
@@ -374,8 +374,7 @@
     ids = jnp.stack([lax.axis_index(CTX), core, lax.axis_index("x")]).astype(jnp.int32)
     own = attend(ids, queries, w_kv, near, far, 4)
     own, w_near = lax.optimization_barrier((own, w_near))
-    w_mate = lax.ppermute(w_near, "z_lo", SWAP)
-    before, after = up(own), down(own)
+    before, after, w_mate = lax.optimization_barrier((up(own), down(own), lax.ppermute(w_near, "z_lo", SWAP)))
     half = own.shape[1] // 2
     left, right = up(before[:, :half]), down(after[:, half:])
     blocks = (w_near, w_mate, swap(w_near), swap(w_mate))

time: 196 us -> 188 us (0.959)
  waiting for transfers between devices: 64.8 us -> 58.9 us
  starting transfers between devices: 39.3 us -> 37 us
    ppermute x1, waiting for transfers between devices: 11 us -> 0.49 us  [local(): lax.ppermute(w_near, 'z_lo', SWAP)]
    ppermute x2, waiting for transfers between devices: 3.18 us -> 6.16 us  [up(): return lax.ppermute(a, 'x', [(i, (i + 1) % 4) for i in range(4)])]
    all_to_all x1, waiting for transfers between devices: 9.84 us -> 11.9 us  [local(): lax.all_to_all(attn, EP + ('x',), split_axis=0, concat_axis=0, tiled=True)]
  transfers between devices with their start and end apart: 15 -> 15, of which waited for: 10 -> 11; matrix products, arithmetic and copies ran while one was open for 1% -> 1% of each run, Pallas kernels for 6% -> 6%
where the time goes in v20:
time: 188 us; the launch traced here: 187 us
  blocking collectives  62.8 us (33%)
  waiting for transfers between devices  58.9 us (31%)
  starting transfers between devices  37 us (20%)
  Pallas kernels  23.1 us (12%)
  local copies, waits for them, and re-layouts  2.66 us (1%)
    all_to_all x1, blocking collectives, exchange(): lax.all_to_all(units, CHIPS, split_axis=0, concat_axis=0, tiled=True)  41 us
    all_to_all x1, waiting for transfers between devices, exchange(): lax.all_to_all(units, CHIPS, split_axis=0, concat_axis=0, tiled=True)  30.2 us
    all_to_all x1, blocking collectives, local(): lax.all_to_all(jnp.broadcast_to(latents[None], (8,) + latents.shape), CTX...  21.7 us
    ppermute x7, starting transfers between devices, swap(): return lax.ppermute(mine, 'core', SWAP)  14.5 us
    all_to_all x1, waiting for transfers between devices, local(): lax.all_to_all(attn, EP + ('x',), split_axis=0, concat_axis=0, tiled=True)  11.9 us
    pallas_call x1, Pallas kernels, attend(): pl.pallas_call(functools.partial(attend_kernel, cuts=cuts), in_specs=[pl....  9.81 us
    all_to_all x1, starting transfers between devices, local(): lax.all_to_all(attn, EP + ('x',), split_axis=0, concat_axis=0, tiled=True)  7.78 us
    ppermute x2, waiting for transfers between devices, down(): return lax.ppermute(a, 'x', [(i, (i + 3) % 4) for i in range(4)])  7.2 us
  transfers between devices with their start and end apart: 15, of which 11 were waited for; matrix products, arithmetic and copies ran while one was open for 1% of the time, Pallas kernels for 6%

profile of v20, /device:TPU:1, one launch (start us, length us, event | category | flops | bytes accessed | tf_op | source)
XLA Modules:
  0.0 187.1 jit_solution(8697534224272448110)
XLA Ops:
  0.6 1.1 broadcast_in_dim.32
  1.7 21.7 %all_to_all.25.near_ref = bf16[8,576,128]{2,1,0:T(8,128)(2,1)S(1)} all-to-all(bf16[8,576,128]{2,1,0:T(8,128)(2,1)S(1)} %broadcast_in_dim.32), channel_id=1, replica_groups=mesh['z_lo'=2,'x'=4,'core'=2,'z_hi'=2,'y'=4] {'x','z_lo'}, dimensions={0} | all-to-all | bytes 2359296 | tf_op jit(solution)/shard_map/all_to_all | solution.py:368
  23.4 2.2 %collective-permute-start = (bf16[8,576,128]{2,1,0:T(8,128)(2,1)S(1)}, bf16[8,576,128]{2,1,0:T(8,128)(2,1)S(1)}, u32[]{:S(2)}, u32[]{:S(2)}) collective-permute-start(bf16[8,576,128]{2,1,0:T(8,128)(2,1)S(1)} %all_to_all.25.near_ref), channel_id=1, source_target_pairs={{0,8},{8,0},{1,9},{9,1},{2,10},{10,2},{3,11},{11,3},{4,12},{12,4},... | collective-permute-start | bytes 3538952 | tf_op jit(solution)/shard_map/ppermute | solution.py:316
  25.6 1.8 shard_map.123
  27.4 3.5 %all-to-all-start.1 = ((bf16[4,64,896]{2,1,0:T(8,128)(2,1)}), bf16[4,64,896]{2,1,0:T(8,128)(2,1)S(1)}, u32[]{:S(2)}, u32[]{:S(2)}) async-start(bf16[4,64,896]{2,1,0:T(8,128)(2,1)} %shard_map.123), calls=%async_computation.1 | async-start | bytes 917504 | tf_op jit(solution)/shard_map/all_to_all | solution.py:373
  30.9 0.1 pad_add_fusion.1.ids_ref
  31.0 0.0 collective-permute-done.far_ref
  31.0 9.8 %shard_map.122.own_ref = bf16[128,1024]{1,0:T(8,128)(2,1)S(1)} custom-call(s32[3]{0:T(128)S(1)} %pad_add_fusion.1.ids_ref, bf16[128,1536]{1,0:T(8,128)(2,1)} %q_hbm.1, bf16[512,2048]{1,0:T(8,128)(2,1)} %w_hbm.1, bf16[8,576,128]{2,1,0:T(8,128)(2,1)S(1)} %all_to_all.25.near_ref, bf16[8,576,128]{2,1,0:T(8,128)(2,1)S(1)} %collective-permute-done.far_ref), custom_call_target="tpu_custom_call" | custom-call | flops 4563402752 | bytes 8000000 | tf_op jit(solution)/shard_map/pallas_call | solution.py:107
  40.8 0.9 collective-permute-start.3
  41.8 2.6 %collective-permute-start.2 = (bf16[128,1024]{1,0:T(8,128)(2,1)S(1)}, bf16[128,1024]{1,0:T(8,128)(2,1)S(1)}, u32[]{:S(2)}, u32[]{:S(2)}) collective-permute-start(bf16[128,1024]{1,0:T(8,128)(2,1)S(1)} %shard_map.122.own_ref), channel_id=1, source_target_pairs={{0,48},{16,0},{32,16},{48,32},{1,49},{17,1},{33,17},{49,33},{2,50}... | collective-permute-start | bytes 786440 | tf_op jit(solution)/shard_map/ppermute | solution.py:324
  44.4 0.0 collective-permute-start.1
  44.4 0.8 collective-permute-start.6
  45.2 4.3 %collective-permute-done.2.after_ref = bf16[128,1024]{1,0:T(8,128)(2,1)S(1)} collective-permute-done((bf16[128,1024]{1,0:T(8,128)(2,1)S(1)}, bf16[128,1024]{1,0:T(8,128)(2,1)S(1)}, u32[]{:S(2)}, u32[]{:S(2)}) %collective-permute-start.2) | collective-permute-done | bytes 262176 | tf_op jit(solution)/shard_map/ppermute | solution.py:324
  49.5 3.1 %collective-permute-done.1.before_ref = bf16[128,1024]{1,0:T(8,128)(2,1)S(1)} collective-permute-done((bf16[128,1024]{1,0:T(8,128)(2,1)S(1)}, bf16[128,1024]{1,0:T(8,128)(2,1)S(1)}, u32[]{:S(2)}, u32[]{:S(2)}) %collective-permute-start.1) | collective-permute-done | bytes 262176 | tf_op jit(solution)/shard_map/ppermute | solution.py:320
  52.6 0.5 collective-permute-done.3.refs_1_
  53.1 1.2 collective-permute-start.7
  54.4 0.0 copy-start.6
  54.4 2.2 %collective-permute-start.5 = (bf16[128,512]{1,0:T(8,128)(2,1)S(1)}, bf16[128,512]{1,0:T(8,128)(2,1)S(1)}, u32[]{:S(2)}, u32[]{:S(2)}) collective-permute-start(bf16[128,512]{1,0:T(8,128)(2,1)S(1)} %slice.20), channel_id=1, source_target_pairs={{0,48},{16,0},{32,16},{48,32},{1,49},{17,1},{33,17},{49,33},{2,50}... | collective-permute-start | bytes 393224 | tf_op jit(solution)/shard_map/ppermute | solution.py:324
  56.6 0.0 collective-permute-start.4
  56.6 2.9 %collective-permute-done.5.right_ref = bf16[128,512]{1,0:T(8,128)(2,1)S(1)} collective-permute-done((bf16[128,512]{1,0:T(8,128)(2,1)S(1)}, bf16[128,512]{1,0:T(8,128)(2,1)S(1)}, u32[]{:S(2)}, u32[]{:S(2)}) %collective-permute-start.5) | collective-permute-done | bytes 131104 | tf_op jit(solution)/shard_map/ppermute | solution.py:324
  59.6 3.1 %collective-permute-done.4.left_ref = bf16[128,512]{1,0:T(8,128)(2,1)S(1)} collective-permute-done((bf16[128,512]{1,0:T(8,128)(2,1)S(1)}, bf16[128,512]{1,0:T(8,128)(2,1)S(1)}, u32[]{:S(2)}, u32[]{:S(2)}) %collective-permute-start.4) | collective-permute-done | bytes 131104 | tf_op jit(solution)/shard_map/ppermute | solution.py:320
  62.6 2.9 %shard_map.124 = bf16[32,16,896]{2,1,0:T(8,128)(2,1)} custom-call(s32[3]{0:T(128)S(1)} %pad_add_fusion.1.ids_ref, bf16[128,1024]{1,0:T(8,128)(2,1)S(1)} %shard_map.122.own_ref, bf16[128,1024]{1,0:T(8,128)(2,1)S(1)} %collective-permute-done.1.before_ref, bf16[128,1024]{1,0:T(8,128)(2,1)S(1)} %collective-permute-done.2.after_ref, ...), custom_call_target="tpu_custom_call" | custom-call | flops 939524096 | bytes 1835008 | tf_op jit(solution)/shard_map/pallas_call | solution.py:279
  65.5 7.8 %all-to-all-start.2 = ((bf16[32,16,896]{2,1,0:T(8,128)(2,1)}), bf16[32,16,896]{2,1,0:T(8,128)(2,1)S(1)}, u32[]{:S(2)}, u32[]{:S(2)}) async-start(bf16[32,16,896]{2,1,0:T(8,128)(2,1)} %shard_map.124), calls=%async_computation.2 | async-start | bytes 1835008 | tf_op jit(solution)/shard_map/all_to_all | solution.py:382
  73.3 1.6 collective-permute-start.8
  74.9 0.1 and.49
  75.0 0.1 and.50
  75.1 0.7 collective-permute-done.8
  75.7 0.1 copy.58
  75.8 0.1 fusion.5
  75.9 0.1 copy.59
  76.2 0.1 copy.63
  76.2 0.1 copy.62
  76.4 11.9 %all-to-all-done.2 = bf16[32,16,896]{2,1,0:T(8,128)(2,1)S(1)} async-done(((bf16[32,16,896]{2,1,0:T(8,128)(2,1)}), bf16[32,16,896]{2,1,0:T(8,128)(2,1)S(1)}, u32[]{:S(2)}, u32[]{:S(2)}) %all-to-all-start.2) | async-done | bytes 917536 | tf_op jit(solution)/shard_map/all_to_all | solution.py:382
  88.3 0.1 convert_reduce_fusion
  88.5 0.2 fusion
  88.7 0.1 fusion.2
  88.8 2.7 %collective-permute-start.10 = (bf16[16,3584]{1,0:T(8,128)(2,1)S(1)}, bf16[16,3584]{1,0:T(8,128)(2,1)S(1)}, u32[]{:S(2)}, u32[]{:S(2)}) collective-permute-start(bf16[16,3584]{1,0:T(8,128)(2,1)S(1)} %fusion.2), channel_id=1, source_target_pairs={{0,8},{8,0},{1,9},{9,1},{2,10},{10,2},{3,11},{11,3},{4,12},{12,4},... | collective-permute-start | bytes 344072 | tf_op jit(solution)/shard_map/ppermute | solution.py:316
  91.5 0.1 bitcast_and_fusion
  91.6 0.1 copy.64
  91.7 0.1 broadcast_in_dim.33
  91.8 0.1 reshape.124
  92.0 0.5 collective-permute-done.10
  92.5 0.0 copy-start.1
  92.5 1.4 shard_map.125
  93.8 0.0 copy-start
  93.9 41.0 %all_to_all.26 = bf16[64,3,2,3584]{3,2,1,0:T(2,128)(2,1)S(1)} all-to-all(bf16[64,3,2,3584]{3,2,1,0:T(2,128)(2,1)S(1)} %bitcast.44), channel_id=1, replica_groups=mesh['z_lo'=2,'x'=4,'core'=2,'z_hi'=2,'y'=4] {'z_hi','z_lo','x','y'}, dimensions={0} | all-to-all | bytes 5505024 | tf_op jit(solution)/shard_map/all_to_all | solution.py:393
  134.9 5.8 %shard_map.126 = bf16[192,2,3584]{2,1,0:T(2,128)(2,1)} custom-call(bf16[192,2,3584]{2,1,0:T(2,128)(2,1)S(1)} %bitcast.45, bf16[3584,512]{1,0:T(8,128)(2,1)S(1)} %bitcast.46, bf16[3584,512]{1,0:T(8,128)(2,1)S(1)} %bitcast.47, bf16[512,3584]{1,0:T(8,128)(2,1)} %bitcast.50), custom_call_target="tpu_custom_call" | custom-call | flops 4227858432 | bytes 17000000 | tf_op jit(solution)/shard_map/pallas_call | solution.py:168
  140.7 0.0 copy-start.4
  140.7 5.4 %all-to-all-start.4 = ((bf16[64,3,2,3584]{3,2,1,0:T(2,128)(2,1)}), bf16[64,3,2,3584]{3,2,1,0:T(2,128)(2,1)S(1)}, u32[]{:S(2)}, u32[]{:S(2)}) async-start(bf16[64,3,2,3584]{3,2,1,0:T(2,128)(2,1)} %bitcast.48), calls=%async_computation.4 | async-start | bytes 5505024 | tf_op jit(solution)/shard_map/all_to_all | solution.py:393
  146.2 2.1 %collective-permute-start.9 = (f32[16,8]{0,1:T(8,128)S(1)}, f32[16,8]{0,1:T(8,128)S(1)}, u32[]{:S(2)}, u32[]{:S(2)}) collective-permute-start(f32[16,8]{0,1:T(8,128)S(1)} %convert_divide_fusion), channel_id=1, source_target_pairs={{0,8},{8,0},{1,9},{9,1},{2,10},{10,2},{3,11},{11,3},{4,12},{12,4},... | collective-permute-start | bytes 1544 | tf_op jit(solution)/shard_map/ppermute | solution.py:316
  148.4 0.1 copy.71
  148.5 0.7 collective-permute-done.9
  149.2 0.1 copy.65
  149.3 0.1 select_reduce_fusion
  149.4 0.1 copy.66
  149.6 0.1 copy.69
  149.6 0.1 copy.70
  149.7 0.1 broadcast_in_dim.65
  149.8 0.1 copy.72
  149.9 30.2 %all-to-all-done.4 = bf16[64,3,2,3584]{3,2,1,0:T(2,128)(2,1)S(1)} async-done(((bf16[64,3,2,3584]{3,2,1,0:T(2,128)(2,1)}), bf16[64,3,2,3584]{3,2,1,0:T(2,128)(2,1)S(1)}, u32[]{:S(2)}, u32[]{:S(2)}) %all-to-all-start.4) | async-done | bytes 2752544 | tf_op jit(solution)/shard_map/all_to_all | solution.py:393
  180.1 1.4 shard_map.127
  181.5 3.7 %collective-permute-start.11 = (f32[16,3584]{1,0:T(8,128)S(1)}, f32[16,3584]{1,0:T(8,128)S(1)}, u32[]{:S(2)}, u32[]{:S(2)}) collective-permute-start(f32[16,3584]{1,0:T(8,128)S(1)} %get-tuple-element.15), channel_id=1, source_target_pairs={{0,8},{8,0},{1,9},{9,1},{2,10},{10,2},{3,11},{11,3},{4,12},{12,4},... | collective-permute-start | bytes 688136 | tf_op jit(solution)/shard_map/ppermute | solution.py:316
  185.2 1.1 collective-permute-done.11
  186.4 0.7 fusion.4
  (39 shorter events, 0.4 us)
Async XLA Ops:
  23.4 7.6 %collective-permute-start = (bf16[8,576,128]{2,1,0:T(8,128)(2,1)S(1)}, bf16[8,576,128]{2,1,0:T(8,128)(2,1)S(1)}, u32[]{:S(2)}, u32[]{:S(2)}) collective-permute-start(bf16[8,576,128]{2,1,0:T(8,128)(2,1)S(1)} %all_to_all.25.near_ref), channel_id=1, source_target_pairs={{0,8},{8,0},{1,9},{9,1},{2,10},{10,2},{3,11},{11,3},{4,12},{12,4},... | collective-permute-start | bytes 3538952 | tf_op jit(solution)/shard_map/ppermute | solution.py:316
  27.4 13.4 %all-to-all-start.1 = ((bf16[4,64,896]{2,1,0:T(8,128)(2,1)}), bf16[4,64,896]{2,1,0:T(8,128)(2,1)S(1)}, u32[]{:S(2)}, u32[]{:S(2)}) async-start(bf16[4,64,896]{2,1,0:T(8,128)(2,1)} %shard_map.123), calls=%async_computation.1 | async-start | bytes 917504 | tf_op jit(solution)/shard_map/all_to_all | solution.py:373
  40.8 12.2 %collective-permute-start.3 = (bf16[4,64,896]{2,1,0:T(8,128)(2,1)S(1)}, bf16[4,64,896]{2,1,0:T(8,128)(2,1)S(1)}, u32[]{:S(2)}, u32[]{:S(2)}) collective-permute-start(bf16[4,64,896]{2,1,0:T(8,128)(2,1)S(1)} %all-to-all-done.1.refs_0_), channel_id=1, source_target_pairs={{0,64},{64,0},{1,65},{65,1},{2,66},{66,2},{3,67},{67,3},{4,68},{68... | collective-permute-start | bytes 1376264 | tf_op jit(solution)/shard_map/ppermute | solution.py:377
  41.8 7.7 %collective-permute-start.2 = (bf16[128,1024]{1,0:T(8,128)(2,1)S(1)}, bf16[128,1024]{1,0:T(8,128)(2,1)S(1)}, u32[]{:S(2)}, u32[]{:S(2)}) collective-permute-start(bf16[128,1024]{1,0:T(8,128)(2,1)S(1)} %shard_map.122.own_ref), channel_id=1, source_target_pairs={{0,48},{16,0},{32,16},{48,32},{1,49},{17,1},{33,17},{49,33},{2,50}... | collective-permute-start | bytes 786440 | tf_op jit(solution)/shard_map/ppermute | solution.py:324
  44.4 8.2 %collective-permute-start.1 = (bf16[128,1024]{1,0:T(8,128)(2,1)S(1)}, bf16[128,1024]{1,0:T(8,128)(2,1)S(1)}, u32[]{:S(2)}, u32[]{:S(2)}) collective-permute-start(bf16[128,1024]{1,0:T(8,128)(2,1)S(1)} %shard_map.122.own_ref), channel_id=1, source_target_pairs={{0,16},{16,32},{32,48},{48,0},{1,17},{17,33},{33,49},{49,1},{2,18}... | collective-permute-start | bytes 786440 | tf_op jit(solution)/shard_map/ppermute | solution.py:320
  44.4 12.2 %collective-permute-start.6 = (bf16[4,64,896]{2,1,0:T(8,128)(2,1)S(1)}, bf16[4,64,896]{2,1,0:T(8,128)(2,1)S(1)}, u32[]{:S(2)}, u32[]{:S(2)}) collective-permute-start(bf16[4,64,896]{2,1,0:T(8,128)(2,1)S(1)} %all-to-all-done.1.refs_0_), channel_id=1, source_target_pairs={{0,8},{8,0},{1,9},{9,1},{2,10},{10,2},{3,11},{11,3},{4,12},{12,4},... | collective-permute-start | bytes 1376264 | tf_op jit(solution)/shard_map/ppermute | solution.py:316
  53.1 9.6 %collective-permute-start.7 = (bf16[4,64,896]{2,1,0:T(8,128)(2,1)S(1)}, bf16[4,64,896]{2,1,0:T(8,128)(2,1)S(1)}, u32[]{:S(2)}, u32[]{:S(2)}) collective-permute-start(bf16[4,64,896]{2,1,0:T(8,128)(2,1)S(1)} %collective-permute-done.3.refs_1_), channel_id=1, source_target_pairs={{0,8},{8,0},{1,9},{9,1},{2,10},{10,2},{3,11},{11,3},{4,12},{12,4},... | collective-permute-start | bytes 1376264 | tf_op jit(solution)/shard_map/ppermute | solution.py:316
  54.4 19.0 %copy-start.6 = (s32[16,8]{0,1:T(8,128)S(1)}, s32[16,8]{0,1:T(8,128)}, u32[]{:S(2)}) copy-start(s32[16,8]{0,1:T(8,128)} %param.17) | copy-start | bytes 1540
  54.4 5.2 %collective-permute-start.5 = (bf16[128,512]{1,0:T(8,128)(2,1)S(1)}, bf16[128,512]{1,0:T(8,128)(2,1)S(1)}, u32[]{:S(2)}, u32[]{:S(2)}) collective-permute-start(bf16[128,512]{1,0:T(8,128)(2,1)S(1)} %slice.20), channel_id=1, source_target_pairs={{0,48},{16,0},{32,16},{48,32},{1,49},{17,1},{33,17},{49,33},{2,50}... | collective-permute-start | bytes 393224 | tf_op jit(solution)/shard_map/ppermute | solution.py:324
  56.6 6.0 %collective-permute-start.4 = (bf16[128,512]{1,0:T(8,128)(2,1)S(1)}, bf16[128,512]{1,0:T(8,128)(2,1)S(1)}, u32[]{:S(2)}, u32[]{:S(2)}) collective-permute-start(bf16[128,512]{1,0:T(8,128)(2,1)S(1)} %slice.19), channel_id=1, source_target_pairs={{0,16},{16,32},{32,48},{48,0},{1,17},{17,33},{33,49},{49,1},{2,18}... | collective-permute-start | bytes 393224 | tf_op jit(solution)/shard_map/ppermute | solution.py:320
  65.5 23.0 %copy-start.3 = (bf16[16,3584]{1,0:T(8,128)(2,1)S(1)}, bf16[16,3584]{1,0:T(8,128)(2,1)}, u32[]{:S(2)}) copy-start(bf16[16,3584]{1,0:T(8,128)(2,1)} %param.15) | copy-start | bytes 344068
  65.5 23.2 %copy-start.5 = (f32[3584]{0:T(1024)S(1)}, f32[3584]{0:T(1024)}, u32[]{:S(2)}) copy-start(f32[3584]{0:T(1024)} %param.16) | copy-start | bytes 43012
  65.5 22.8 %all-to-all-start.2 = ((bf16[32,16,896]{2,1,0:T(8,128)(2,1)}), bf16[32,16,896]{2,1,0:T(8,128)(2,1)S(1)}, u32[]{:S(2)}, u32[]{:S(2)}) async-start(bf16[32,16,896]{2,1,0:T(8,128)(2,1)} %shard_map.124), calls=%async_computation.2 | async-start | bytes 1835008 | tf_op jit(solution)/shard_map/all_to_all | solution.py:382
  73.3 2.4 %collective-permute-start.8 = (s32[16,8]{0,1:T(8,128)S(1)}, s32[16,8]{0,1:T(8,128)S(1)}, u32[]{:S(2)}, u32[]{:S(2)}) collective-permute-start(s32[16,8]{0,1:T(8,128)S(1)} %copy-done.6), channel_id=1, source_target_pairs={{0,8},{8,0},{1,9},{9,1},{2,10},{10,2},{3,11},{11,3},{4,12},{12,4},... | collective-permute-start | bytes 1544 | tf_op jit(solution)/shard_map/ppermute | solution.py:316
  88.6 97.7 %copy-start.2 = (bf16[16,3584]{1,0:T(8,128)(2,1)}, bf16[16,3584]{1,0:T(8,128)(2,1)S(1)}, u32[]{:S(2)}) copy-start(bf16[16,3584]{1,0:T(8,128)(2,1)S(1)} %get-tuple-element.17) | copy-start | bytes 344068
  88.8 3.7 %collective-permute-start.10 = (bf16[16,3584]{1,0:T(8,128)(2,1)S(1)}, bf16[16,3584]{1,0:T(8,128)(2,1)S(1)}, u32[]{:S(2)}, u32[]{:S(2)}) collective-permute-start(bf16[16,3584]{1,0:T(8,128)(2,1)S(1)} %fusion.2), channel_id=1, source_target_pairs={{0,8},{8,0},{1,9},{9,1},{2,10},{10,2},{3,11},{11,3},{4,12},{12,4},... | collective-permute-start | bytes 344072 | tf_op jit(solution)/shard_map/ppermute | solution.py:316
  92.5 42.4 %copy-start.1 = (bf16[1,3584,512]{2,1,0:T(8,128)(2,1)S(1)}, bf16[1,3584,512]{2,1,0:T(8,128)(2,1)}, u32[]{:S(2)}) copy-start(bf16[1,3584,512]{2,1,0:T(8,128)(2,1)} %param.20) | copy-start | bytes 11010052
  93.8 41.1 %copy-start = (bf16[1,3584,512]{2,1,0:T(8,128)(2,1)S(1)}, bf16[1,3584,512]{2,1,0:T(8,128)(2,1)}, u32[]{:S(2)}) copy-start(bf16[1,3584,512]{2,1,0:T(8,128)(2,1)} %param.19) | copy-start | bytes 11010052
  140.7 5.5 %copy-start.4 = (s32[16,8]{0,1:T(8,128)S(1)}, s32[16,8]{0,1:T(8,128)}, u32[]{:S(2)}) copy-start(s32[16,8]{0,1:T(8,128)} %param.18) | copy-start | bytes 1540
  140.7 39.4 %all-to-all-start.4 = ((bf16[64,3,2,3584]{3,2,1,0:T(2,128)(2,1)}), bf16[64,3,2,3584]{3,2,1,0:T(2,128)(2,1)S(1)}, u32[]{:S(2)}, u32[]{:S(2)}) async-start(bf16[64,3,2,3584]{3,2,1,0:T(2,128)(2,1)} %bitcast.48), calls=%async_computation.4 | async-start | bytes 5505024 | tf_op jit(solution)/shard_map/all_to_all | solution.py:393
  146.2 3.0 %collective-permute-start.9 = (f32[16,8]{0,1:T(8,128)S(1)}, f32[16,8]{0,1:T(8,128)S(1)}, u32[]{:S(2)}, u32[]{:S(2)}) collective-permute-start(f32[16,8]{0,1:T(8,128)S(1)} %convert_divide_fusion), channel_id=1, source_target_pairs={{0,8},{8,0},{1,9},{9,1},{2,10},{10,2},{3,11},{11,3},{4,12},{12,4},... | collective-permute-start | bytes 1544 | tf_op jit(solution)/shard_map/ppermute | solution.py:316
  181.5 4.9 %collective-permute-start.11 = (f32[16,3584]{1,0:T(8,128)S(1)}, f32[16,3584]{1,0:T(8,128)S(1)}, u32[]{:S(2)}, u32[]{:S(2)}) collective-permute-start(f32[16,3584]{1,0:T(8,128)S(1)} %get-tuple-element.15), channel_id=1, source_target_pairs={{0,8},{8,0},{1,9},{9,1},{2,10},{10,2},{3,11},{11,3},{4,12},{12,4},... | collective-permute-start | bytes 688136 | tf_op jit(solution)/shard_map/ppermute | solution.py:316

commit v21 on v20

--- a/solution.py
+++ b/solution.py
@@ -246,17 +246,15 @@
     )(*[a for part in parts for a in part])
 
 
-def project_kernel(ids_ref, own_ref, before_ref, after_ref, left_ref, right_ref, *refs):
+def project_kernel(ids_ref, own_ref, before_ref, after_ref, opposite_ref, *refs):
     *block_refs, out_ref, x_ref, w_ref = refs
     rows = own_ref.shape[0]
     group, tok = 4, out_ref.shape[1]
     parts = out_ref.shape[0] // group
     core, x = ids_ref[1], ids_ref[2]
-    half = left_ref.shape[1]
     x_ref[:rows] = own_ref[...]
     x_ref[rows : 2 * rows] = after_ref[...]
-    x_ref[2 * rows : 3 * rows, :half] = left_ref[...]
-    x_ref[2 * rows : 3 * rows, half:] = right_ref[...]
+    x_ref[2 * rows : 3 * rows] = opposite_ref[...]
     x_ref[3 * rows :] = before_ref[...]
     deep = VD // 2
     z = lax.div(ids_ref[0], 2 * group)
@@ -374,11 +372,11 @@
     ids = jnp.stack([lax.axis_index(CTX), core, lax.axis_index("x")]).astype(jnp.int32)
     own = attend(ids, queries, w_kv, near, far, 4)
     own, w_near = lax.optimization_barrier((own, w_near))
-    before, after, w_mate = lax.optimization_barrier((up(own), down(own), lax.ppermute(w_near, "z_lo", SWAP)))
-    half = own.shape[1] // 2
-    left, right = up(before[:, :half]), down(after[:, half:])
+    opposite = lax.ppermute(own, "x", [(i, (i + 2) % 4) for i in range(4)])
+    mate = lax.ppermute(w_near, "z_lo", SWAP)
+    before, after, opposite, w_mate = lax.optimization_barrier((up(own), down(own), opposite, mate))
     blocks = (w_near, w_mate, swap(w_near), swap(w_mate))
-    attn = project(ids, (own, before, after, left, right), blocks, 8, columns)
+    attn = project(ids, (own, before, after, opposite), blocks, 8, columns)
     attn = lax.all_to_all(attn, EP + ("x",), split_axis=0, concat_axis=0, tiled=True)
     attn = jnp.sum(attn.reshape(8, group, tok, columns).astype(F32), axis=0)
     attn = attn.transpose(1, 0, 2).reshape(tok, width)

time: 188 us -> 187 us (level)
    ppermute x2 -> x1, waiting for transfers between devices: 6.16 us -> 0.65 us  [up(): return lax.ppermute(a, 'x', [(i, (i + 1) % 4) for i in range(4)])]
    ppermute x2 -> x1, starting transfers between devices: 4.88 us -> 0.89 us  [down(): return lax.ppermute(a, 'x', [(i, (i + 3) % 4) for i in range(4)])]
    ppermute x1 -> x2, starting transfers between devices: 0.9 us -> 3.81 us  [the longest x1 2.92 us: local(): opposite = lax.ppermute(own, 'x', [(i, (i + 2) % 4) for i in range(4)])]
    ppermute x1 -> x2, waiting for transfers between devices: 0.49 us -> 3.32 us  [the longest x1 3.32 us: local(): opposite = lax.ppermute(own, 'x', [(i, (i + 2) % 4) for i in range(4)])]
    all_to_all x1, starting transfers between devices: 7.78 us -> 10.1 us  [local(): lax.all_to_all(attn, EP + ('x',), split_axis=0, concat_axis=0, tiled=True)]
    ppermute x2 -> x1, waiting for transfers between devices: 7.2 us -> 5.58 us  [down(): return lax.ppermute(a, 'x', [(i, (i + 3) % 4) for i in range(4)])]
  transfers between devices with their start and end apart: 15 -> 14, of which waited for: 11 -> 10; matrix products, arithmetic and copies ran while one was open for 1% -> 1% of each run, Pallas kernels for 6% -> 6%
where the time goes in v21:
time: 187 us; the launch traced here: 186 us
  blocking collectives  62.5 us (33%)
  waiting for transfers between devices  57.9 us (31%)
  starting transfers between devices  37.4 us (20%)
  Pallas kernels  23.1 us (12%)
  local copies, waits for them, and re-layouts  2.64 us (1%)
    all_to_all x1, blocking collectives, exchange(): lax.all_to_all(units, CHIPS, split_axis=0, concat_axis=0, tiled=True)  40.8 us
    all_to_all x1, waiting for transfers between devices, exchange(): lax.all_to_all(units, CHIPS, split_axis=0, concat_axis=0, tiled=True)  30.2 us
    all_to_all x1, blocking collectives, local(): lax.all_to_all(jnp.broadcast_to(latents[None], (8,) + latents.shape), CTX...  21.7 us
    all_to_all x1, waiting for transfers between devices, local(): lax.all_to_all(attn, EP + ('x',), split_axis=0, concat_axis=0, tiled=True)  13.8 us
    ppermute x7, starting transfers between devices, swap(): return lax.ppermute(mine, 'core', SWAP)  13.2 us
    all_to_all x1, starting transfers between devices, local(): lax.all_to_all(attn, EP + ('x',), split_axis=0, concat_axis=0, tiled=True)  10.1 us
    pallas_call x1, Pallas kernels, attend(): pl.pallas_call(functools.partial(attend_kernel, cuts=cuts), in_specs=[pl....  9.82 us
    pallas_call x1, Pallas kernels, expert(): pl.pallas_call(expert_kernel, in_specs=[far, whole, whole, far], out_spec...  5.8 us
  transfers between devices with their start and end apart: 14, of which 10 were waited for; matrix products, arithmetic and copies ran while one was open for 1% of the time, Pallas kernels for 6%

profile of v21, /device:TPU:1, one launch (start us, length us, event | category | flops | bytes accessed | tf_op | source)
XLA Modules:
  0.0 186.2 jit_solution(9492018440750307862)
XLA Ops:
  0.6 1.1 broadcast_in_dim.32
  1.7 21.7 %all_to_all.25.near_ref = bf16[8,576,128]{2,1,0:T(8,128)(2,1)S(1)} all-to-all(bf16[8,576,128]{2,1,0:T(8,128)(2,1)S(1)} %broadcast_in_dim.32), channel_id=1, replica_groups=mesh['z_lo'=2,'x'=4,'core'=2,'z_hi'=2,'y'=4] {'x','z_lo'}, dimensions={0} | all-to-all | bytes 2359296 | tf_op jit(solution)/shard_map/all_to_all | solution.py:366
  23.4 2.2 %collective-permute-start = (bf16[8,576,128]{2,1,0:T(8,128)(2,1)S(1)}, bf16[8,576,128]{2,1,0:T(8,128)(2,1)S(1)}, u32[]{:S(2)}, u32[]{:S(2)}) collective-permute-start(bf16[8,576,128]{2,1,0:T(8,128)(2,1)S(1)} %all_to_all.25.near_ref), channel_id=1, source_target_pairs={{0,8},{8,0},{1,9},{9,1},{2,10},{10,2},{3,11},{11,3},{4,12},{12,4},... | collective-permute-start | bytes 3538952 | tf_op jit(solution)/shard_map/ppermute | solution.py:314
  25.6 1.8 shard_map.123
  27.4 3.5 %all-to-all-start.1 = ((bf16[4,64,896]{2,1,0:T(8,128)(2,1)}), bf16[4,64,896]{2,1,0:T(8,128)(2,1)S(1)}, u32[]{:S(2)}, u32[]{:S(2)}) async-start(bf16[4,64,896]{2,1,0:T(8,128)(2,1)} %shard_map.123), calls=%async_computation.1 | async-start | bytes 917504 | tf_op jit(solution)/shard_map/all_to_all | solution.py:371
  30.9 0.1 pad_add_fusion.1.ids_ref
  31.0 0.0 collective-permute-done.far_ref
  31.0 9.8 %shard_map.122.own_ref = bf16[128,1024]{1,0:T(8,128)(2,1)S(1)} custom-call(s32[3]{0:T(128)S(1)} %pad_add_fusion.1.ids_ref, bf16[128,1536]{1,0:T(8,128)(2,1)} %q_hbm.1, bf16[512,2048]{1,0:T(8,128)(2,1)} %w_hbm.1, bf16[8,576,128]{2,1,0:T(8,128)(2,1)S(1)} %all_to_all.25.near_ref, bf16[8,576,128]{2,1,0:T(8,128)(2,1)S(1)} %collective-permute-done.far_ref), custom_call_target="tpu_custom_call" | custom-call | flops 4563402752 | bytes 8000000 | tf_op jit(solution)/shard_map/pallas_call | solution.py:107
  40.8 0.0 copy-start.6
  40.9 0.0 all-to-all-done.1.refs_0_
  40.9 0.9 collective-permute-start.4
  41.8 2.9 %collective-permute-start.3 = (bf16[128,1024]{1,0:T(8,128)(2,1)S(1)}, bf16[128,1024]{1,0:T(8,128)(2,1)S(1)}, u32[]{:S(2)}, u32[]{:S(2)}) collective-permute-start(bf16[128,1024]{1,0:T(8,128)(2,1)S(1)} %shard_map.122.own_ref), channel_id=1, source_target_pairs={{0,32},{16,48},{32,0},{48,16},{1,33},{17,49},{33,1},{49,17},{2,34}... | collective-permute-start | bytes 786440 | tf_op jit(solution)/shard_map/ppermute | solution.py:375
  44.7 0.9 collective-permute-start.2
  45.6 0.6 collective-permute-start.1
  46.1 1.4 collective-permute-start.5
  47.5 3.3 %collective-permute-done.3.opposite_ref = bf16[128,1024]{1,0:T(8,128)(2,1)S(1)} collective-permute-done((bf16[128,1024]{1,0:T(8,128)(2,1)S(1)}, bf16[128,1024]{1,0:T(8,128)(2,1)S(1)}, u32[]{:S(2)}, u32[]{:S(2)}) %collective-permute-start.3) | collective-permute-done | bytes 262176 | tf_op jit(solution)/shard_map/ppermute | solution.py:375
  50.9 5.6 %collective-permute-done.2.after_ref = bf16[128,1024]{1,0:T(8,128)(2,1)S(1)} collective-permute-done((bf16[128,1024]{1,0:T(8,128)(2,1)S(1)}, bf16[128,1024]{1,0:T(8,128)(2,1)S(1)}, u32[]{:S(2)}, u32[]{:S(2)}) %collective-permute-start.2) | collective-permute-done | bytes 262176 | tf_op jit(solution)/shard_map/ppermute | solution.py:322
  56.5 0.6 collective-permute-done.1.before_ref
  57.1 0.0 collective-permute-done.4.refs_1_
  57.1 0.8 collective-permute-start.6
  57.9 1.4 collective-permute-done.6.refs_3_
  59.3 2.9 %shard_map.124 = bf16[32,16,896]{2,1,0:T(8,128)(2,1)} custom-call(s32[3]{0:T(128)S(1)} %pad_add_fusion.1.ids_ref, bf16[128,1024]{1,0:T(8,128)(2,1)S(1)} %shard_map.122.own_ref, bf16[128,1024]{1,0:T(8,128)(2,1)S(1)} %collective-permute-done.1.before_ref, bf16[128,1024]{1,0:T(8,128)(2,1)S(1)} %collective-permute-done.2.after_ref, ...), custom_call_target="tpu_custom_call" | custom-call | flops 939524096 | bytes 1835008 | tf_op jit(solution)/shard_map/pallas_call | solution.py:277
  62.2 10.1 %all-to-all-start.2 = ((bf16[32,16,896]{2,1,0:T(8,128)(2,1)}), bf16[32,16,896]{2,1,0:T(8,128)(2,1)S(1)}, u32[]{:S(2)}, u32[]{:S(2)}) async-start(bf16[32,16,896]{2,1,0:T(8,128)(2,1)} %shard_map.124), calls=%async_computation.2 | async-start | bytes 1835008 | tf_op jit(solution)/shard_map/all_to_all | solution.py:380
  72.3 0.7 collective-permute-start.7
  73.1 0.1 and.49
  73.1 0.1 and.50
  73.2 0.7 collective-permute-done.7
  73.9 0.1 copy.58
  74.0 0.1 fusion.5
  74.1 0.1 copy.59
  74.3 0.1 copy.63
  74.4 0.1 copy.62
  74.5 13.8 %all-to-all-done.2 = bf16[32,16,896]{2,1,0:T(8,128)(2,1)S(1)} async-done(((bf16[32,16,896]{2,1,0:T(8,128)(2,1)}), bf16[32,16,896]{2,1,0:T(8,128)(2,1)S(1)}, u32[]{:S(2)}, u32[]{:S(2)}) %all-to-all-start.2) | async-done | bytes 917536 | tf_op jit(solution)/shard_map/all_to_all | solution.py:380
  88.3 0.1 convert_reduce_fusion
  88.5 0.2 fusion
  88.6 0.1 fusion.2
  88.7 2.2 %collective-permute-start.9 = (bf16[16,3584]{1,0:T(8,128)(2,1)S(1)}, bf16[16,3584]{1,0:T(8,128)(2,1)S(1)}, u32[]{:S(2)}, u32[]{:S(2)}) collective-permute-start(bf16[16,3584]{1,0:T(8,128)(2,1)S(1)} %fusion.2), channel_id=1, source_target_pairs={{0,8},{8,0},{1,9},{9,1},{2,10},{10,2},{3,11},{11,3},{4,12},{12,4},... | collective-permute-start | bytes 344072 | tf_op jit(solution)/shard_map/ppermute | solution.py:314
  90.9 0.1 bitcast_and_fusion
  91.0 0.1 copy.64
  91.2 0.1 broadcast_in_dim.33
  91.3 0.1 reshape.124
  91.4 0.5 collective-permute-done.9
  91.9 0.0 copy-start.1
  91.9 1.4 shard_map.125
  93.3 0.0 copy-start
  93.3 40.8 %all_to_all.26 = bf16[64,3,2,3584]{3,2,1,0:T(2,128)(2,1)S(1)} all-to-all(bf16[64,3,2,3584]{3,2,1,0:T(2,128)(2,1)S(1)} %bitcast.44), channel_id=1, replica_groups=mesh['z_lo'=2,'x'=4,'core'=2,'z_hi'=2,'y'=4] {'z_hi','z_lo','x','y'}, dimensions={0} | all-to-all | bytes 5505024 | tf_op jit(solution)/shard_map/all_to_all | solution.py:391
  134.1 5.8 %shard_map.126 = bf16[192,2,3584]{2,1,0:T(2,128)(2,1)} custom-call(bf16[192,2,3584]{2,1,0:T(2,128)(2,1)S(1)} %bitcast.45, bf16[3584,512]{1,0:T(8,128)(2,1)S(1)} %bitcast.46, bf16[3584,512]{1,0:T(8,128)(2,1)S(1)} %bitcast.47, bf16[512,3584]{1,0:T(8,128)(2,1)} %bitcast.50), custom_call_target="tpu_custom_call" | custom-call | flops 4227858432 | bytes 17000000 | tf_op jit(solution)/shard_map/pallas_call | solution.py:168
  139.9 0.0 copy-start.4
  139.9 5.4 %all-to-all-start.4 = ((bf16[64,3,2,3584]{3,2,1,0:T(2,128)(2,1)}), bf16[64,3,2,3584]{3,2,1,0:T(2,128)(2,1)S(1)}, u32[]{:S(2)}, u32[]{:S(2)}) async-start(bf16[64,3,2,3584]{3,2,1,0:T(2,128)(2,1)} %bitcast.48), calls=%async_computation.4 | async-start | bytes 5505024 | tf_op jit(solution)/shard_map/all_to_all | solution.py:391
  145.4 2.1 %collective-permute-start.8 = (f32[16,8]{0,1:T(8,128)S(1)}, f32[16,8]{0,1:T(8,128)S(1)}, u32[]{:S(2)}, u32[]{:S(2)}) collective-permute-start(f32[16,8]{0,1:T(8,128)S(1)} %convert_divide_fusion), channel_id=1, source_target_pairs={{0,8},{8,0},{1,9},{9,1},{2,10},{10,2},{3,11},{11,3},{4,12},{12,4},... | collective-permute-start | bytes 1544 | tf_op jit(solution)/shard_map/ppermute | solution.py:314
  147.5 0.1 copy.71
  147.7 0.7 collective-permute-done.8
  148.4 0.1 copy.65
  148.4 0.1 select_reduce_fusion
  148.6 0.1 copy.66
  148.7 0.1 copy.69
  148.8 0.1 copy.70
  148.9 0.1 broadcast_in_dim.65
  149.0 0.1 copy.72
  149.1 30.2 %all-to-all-done.4 = bf16[64,3,2,3584]{3,2,1,0:T(2,128)(2,1)S(1)} async-done(((bf16[64,3,2,3584]{3,2,1,0:T(2,128)(2,1)}), bf16[64,3,2,3584]{3,2,1,0:T(2,128)(2,1)S(1)}, u32[]{:S(2)}, u32[]{:S(2)}) %all-to-all-start.4) | async-done | bytes 2752544 | tf_op jit(solution)/shard_map/all_to_all | solution.py:391
  179.3 1.4 shard_map.127
  180.7 3.7 %collective-permute-start.10 = (f32[16,3584]{1,0:T(8,128)S(1)}, f32[16,3584]{1,0:T(8,128)S(1)}, u32[]{:S(2)}, u32[]{:S(2)}) collective-permute-start(f32[16,3584]{1,0:T(8,128)S(1)} %get-tuple-element.17), channel_id=1, source_target_pairs={{0,8},{8,0},{1,9},{9,1},{2,10},{10,2},{3,11},{11,3},{4,12},{12,4},... | collective-permute-start | bytes 688136 | tf_op jit(solution)/shard_map/ppermute | solution.py:314
  184.4 1.1 collective-permute-done.10
  185.5 0.7 fusion.4
  (35 shorter events, 0.4 us)
Async XLA Ops:
  23.4 7.6 %collective-permute-start = (bf16[8,576,128]{2,1,0:T(8,128)(2,1)S(1)}, bf16[8,576,128]{2,1,0:T(8,128)(2,1)S(1)}, u32[]{:S(2)}, u32[]{:S(2)}) collective-permute-start(bf16[8,576,128]{2,1,0:T(8,128)(2,1)S(1)} %all_to_all.25.near_ref), channel_id=1, source_target_pairs={{0,8},{8,0},{1,9},{9,1},{2,10},{10,2},{3,11},{11,3},{4,12},{12,4},... | collective-permute-start | bytes 3538952 | tf_op jit(solution)/shard_map/ppermute | solution.py:314
  27.4 13.4 %all-to-all-start.1 = ((bf16[4,64,896]{2,1,0:T(8,128)(2,1)}), bf16[4,64,896]{2,1,0:T(8,128)(2,1)S(1)}, u32[]{:S(2)}, u32[]{:S(2)}) async-start(bf16[4,64,896]{2,1,0:T(8,128)(2,1)} %shard_map.123), calls=%async_computation.1 | async-start | bytes 917504 | tf_op jit(solution)/shard_map/all_to_all | solution.py:371
  40.8 31.5 %copy-start.6 = (s32[16,8]{0,1:T(8,128)S(1)}, s32[16,8]{0,1:T(8,128)}, u32[]{:S(2)}) copy-start(s32[16,8]{0,1:T(8,128)} %param.17) | copy-start | bytes 1540
  40.9 16.2 %collective-permute-start.4 = (bf16[4,64,896]{2,1,0:T(8,128)(2,1)S(1)}, bf16[4,64,896]{2,1,0:T(8,128)(2,1)S(1)}, u32[]{:S(2)}, u32[]{:S(2)}) collective-permute-start(bf16[4,64,896]{2,1,0:T(8,128)(2,1)S(1)} %all-to-all-done.1.refs_0_), channel_id=1, source_target_pairs={{0,64},{64,0},{1,65},{65,1},{2,66},{66,2},{3,67},{67,3},{4,68},{68... | collective-permute-start | bytes 1376264 | tf_op jit(solution)/shard_map/ppermute | solution.py:376
  41.8 9.1 %collective-permute-start.3 = (bf16[128,1024]{1,0:T(8,128)(2,1)S(1)}, bf16[128,1024]{1,0:T(8,128)(2,1)S(1)}, u32[]{:S(2)}, u32[]{:S(2)}) collective-permute-start(bf16[128,1024]{1,0:T(8,128)(2,1)S(1)} %shard_map.122.own_ref), channel_id=1, source_target_pairs={{0,32},{16,48},{32,0},{48,16},{1,33},{17,49},{33,1},{49,17},{2,34}... | collective-permute-start | bytes 786440 | tf_op jit(solution)/shard_map/ppermute | solution.py:375
  44.7 11.8 %collective-permute-start.2 = (bf16[128,1024]{1,0:T(8,128)(2,1)S(1)}, bf16[128,1024]{1,0:T(8,128)(2,1)S(1)}, u32[]{:S(2)}, u32[]{:S(2)}) collective-permute-start(bf16[128,1024]{1,0:T(8,128)(2,1)S(1)} %shard_map.122.own_ref), channel_id=1, source_target_pairs={{0,48},{16,0},{32,16},{48,32},{1,49},{17,1},{33,17},{49,33},{2,50}... | collective-permute-start | bytes 786440 | tf_op jit(solution)/shard_map/ppermute | solution.py:322
  45.6 11.5 %collective-permute-start.1 = (bf16[128,1024]{1,0:T(8,128)(2,1)S(1)}, bf16[128,1024]{1,0:T(8,128)(2,1)S(1)}, u32[]{:S(2)}, u32[]{:S(2)}) collective-permute-start(bf16[128,1024]{1,0:T(8,128)(2,1)S(1)} %shard_map.122.own_ref), channel_id=1, source_target_pairs={{0,16},{16,32},{32,48},{48,0},{1,17},{17,33},{33,49},{49,1},{2,18}... | collective-permute-start | bytes 786440 | tf_op jit(solution)/shard_map/ppermute | solution.py:318
  46.1 11.7 %collective-permute-start.5 = (bf16[4,64,896]{2,1,0:T(8,128)(2,1)S(1)}, bf16[4,64,896]{2,1,0:T(8,128)(2,1)S(1)}, u32[]{:S(2)}, u32[]{:S(2)}) collective-permute-start(bf16[4,64,896]{2,1,0:T(8,128)(2,1)S(1)} %all-to-all-done.1.refs_0_), channel_id=1, source_target_pairs={{0,8},{8,0},{1,9},{9,1},{2,10},{10,2},{3,11},{11,3},{4,12},{12,4},... | collective-permute-start | bytes 1376264 | tf_op jit(solution)/shard_map/ppermute | solution.py:314
  57.1 2.2 %collective-permute-start.6 = (bf16[4,64,896]{2,1,0:T(8,128)(2,1)S(1)}, bf16[4,64,896]{2,1,0:T(8,128)(2,1)S(1)}, u32[]{:S(2)}, u32[]{:S(2)}) collective-permute-start(bf16[4,64,896]{2,1,0:T(8,128)(2,1)S(1)} %collective-permute-done.4.refs_1_), channel_id=1, source_target_pairs={{0,8},{8,0},{1,9},{9,1},{2,10},{10,2},{3,11},{11,3},{4,12},{12,4},... | collective-permute-start | bytes 1376264 | tf_op jit(solution)/shard_map/ppermute | solution.py:314
  62.2 26.2 %copy-start.3 = (bf16[16,3584]{1,0:T(8,128)(2,1)S(1)}, bf16[16,3584]{1,0:T(8,128)(2,1)}, u32[]{:S(2)}) copy-start(bf16[16,3584]{1,0:T(8,128)(2,1)} %param.15) | copy-start | bytes 344068
  62.2 26.4 %copy-start.5 = (f32[3584]{0:T(1024)S(1)}, f32[3584]{0:T(1024)}, u32[]{:S(2)}) copy-start(f32[3584]{0:T(1024)} %param.16) | copy-start | bytes 43012
  62.2 26.1 %all-to-all-start.2 = ((bf16[32,16,896]{2,1,0:T(8,128)(2,1)}), bf16[32,16,896]{2,1,0:T(8,128)(2,1)S(1)}, u32[]{:S(2)}, u32[]{:S(2)}) async-start(bf16[32,16,896]{2,1,0:T(8,128)(2,1)} %shard_map.124), calls=%async_computation.2 | async-start | bytes 1835008 | tf_op jit(solution)/shard_map/all_to_all | solution.py:380
  72.3 1.6 collective-permute-start.7
  88.6 96.9 %copy-start.2 = (bf16[16,3584]{1,0:T(8,128)(2,1)}, bf16[16,3584]{1,0:T(8,128)(2,1)S(1)}, u32[]{:S(2)}) copy-start(bf16[16,3584]{1,0:T(8,128)(2,1)S(1)} %get-tuple-element.19) | copy-start | bytes 344068
  88.7 3.1 %collective-permute-start.9 = (bf16[16,3584]{1,0:T(8,128)(2,1)S(1)}, bf16[16,3584]{1,0:T(8,128)(2,1)S(1)}, u32[]{:S(2)}, u32[]{:S(2)}) collective-permute-start(bf16[16,3584]{1,0:T(8,128)(2,1)S(1)} %fusion.2), channel_id=1, source_target_pairs={{0,8},{8,0},{1,9},{9,1},{2,10},{10,2},{3,11},{11,3},{4,12},{12,4},... | collective-permute-start | bytes 344072 | tf_op jit(solution)/shard_map/ppermute | solution.py:314
  91.9 42.2 %copy-start.1 = (bf16[1,3584,512]{2,1,0:T(8,128)(2,1)S(1)}, bf16[1,3584,512]{2,1,0:T(8,128)(2,1)}, u32[]{:S(2)}) copy-start(bf16[1,3584,512]{2,1,0:T(8,128)(2,1)} %param.20) | copy-start | bytes 11010052
  93.3 40.8 %copy-start = (bf16[1,3584,512]{2,1,0:T(8,128)(2,1)S(1)}, bf16[1,3584,512]{2,1,0:T(8,128)(2,1)}, u32[]{:S(2)}) copy-start(bf16[1,3584,512]{2,1,0:T(8,128)(2,1)} %param.19) | copy-start | bytes 11010052
  139.9 5.4 %copy-start.4 = (s32[16,8]{0,1:T(8,128)S(1)}, s32[16,8]{0,1:T(8,128)}, u32[]{:S(2)}) copy-start(s32[16,8]{0,1:T(8,128)} %param.18) | copy-start | bytes 1540
  139.9 39.4 %all-to-all-start.4 = ((bf16[64,3,2,3584]{3,2,1,0:T(2,128)(2,1)}), bf16[64,3,2,3584]{3,2,1,0:T(2,128)(2,1)S(1)}, u32[]{:S(2)}, u32[]{:S(2)}) async-start(bf16[64,3,2,3584]{3,2,1,0:T(2,128)(2,1)} %bitcast.48), calls=%async_computation.4 | async-start | bytes 5505024 | tf_op jit(solution)/shard_map/all_to_all | solution.py:391
  145.4 3.0 %collective-permute-start.8 = (f32[16,8]{0,1:T(8,128)S(1)}, f32[16,8]{0,1:T(8,128)S(1)}, u32[]{:S(2)}, u32[]{:S(2)}) collective-permute-start(f32[16,8]{0,1:T(8,128)S(1)} %convert_divide_fusion), channel_id=1, source_target_pairs={{0,8},{8,0},{1,9},{9,1},{2,10},{10,2},{3,11},{11,3},{4,12},{12,4},... | collective-permute-start | bytes 1544 | tf_op jit(solution)/shard_map/ppermute | solution.py:314
  180.7 4.9 %collective-permute-start.10 = (f32[16,3584]{1,0:T(8,128)S(1)}, f32[16,3584]{1,0:T(8,128)S(1)}, u32[]{:S(2)}, u32[]{:S(2)}) collective-permute-start(f32[16,3584]{1,0:T(8,128)S(1)} %get-tuple-element.17), channel_id=1, source_target_pairs={{0,8},{8,0},{1,9},{9,1},{2,10},{10,2},{3,11},{11,3},{4,12},{12,4},... | collective-permute-start | bytes 688136 | tf_op jit(solution)/shard_map/ppermute | solution.py:314

commit v22 on v18

--- a/solution.py
+++ b/solution.py
@@ -370,6 +370,8 @@
     w_blocks, _ = lax.optimization_barrier((column_blocks(w_out, group, 8), near[0, :8]))
     w_near = lax.all_to_all(w_blocks, CTX_CHIPS, split_axis=0, concat_axis=0, tiled=True)
     ids = jnp.stack([lax.axis_index(CTX), core, lax.axis_index("x")]).astype(jnp.int32)
+    parts = routing(routes, codes)
+    ids, parts = lax.optimization_barrier((ids, parts))
     own = attend(ids, queries, w_kv, near, far, 4)
     before, after, w_near = lax.optimization_barrier((up(own), down(own), w_near))
     w_far = swap(w_near)
@@ -390,7 +392,6 @@
         units = lax.all_to_all(units, CHIPS, split_axis=0, concat_axis=0, tiled=True)
         return units.reshape(rows.shape)
 
-    parts = routing(routes, codes)
     arrived = [exchange(dispatch(place, normed2, 2)) for place, _ in parts]
     returned = [exchange(expert(rows, w_gate[0], w_up[0], w_down[0], 2, 7)) for rows in arrived]
     mine, theirs = combine([(factors, rows) for (_, factors), rows in zip(parts, returned)], 4)

time: 186 us -> 189 us (1.016)
  blocking collectives: 63 us -> 104 us
  waiting for transfers between devices: 59.1 us -> 29.9 us
  starting transfers between devices: 34.6 us -> 24.3 us
    all_to_all x1 -> x2, blocking collectives: 41.2 us -> 81.5 us  [exchange(): lax.all_to_all(units, CHIPS, split_axis=0, concat_axis=0, tiled=True)]
    all_to_all x2 -> x1, waiting for transfers between devices: 43 us -> 13.1 us  [local(): lax.all_to_all(jnp.broadcast_to(latents[None], (8,) + latents.shape), CTX...]
    all_to_all x2 -> x1, starting transfers between devices: 13.6 us -> 6.2 us  [local(): lax.all_to_all(jnp.broadcast_to(latents[None], (8,) + latents.shape), CTX...]
    ppermute x6, starting transfers between devices: 13.3 us -> 10.1 us  [swap(): return lax.ppermute(mine, 'core', SWAP)]
    all_to_all x1, waiting for transfers between devices: 2.76 us -> 0.01 us  [local(): lax.all_to_all(w_blocks, CTX_CHIPS, split_axis=0, concat_axis=0, tiled=True)]
    ppermute x2, waiting for transfers between devices: 6.32 us -> 8.97 us  [down(): return lax.ppermute(a, 'x', [(i, (i + 3) % 4) for i in range(4)])]
  transfers between devices with their start and end apart: 13 -> 12, of which waited for: 11 -> 8; matrix products, arithmetic and copies ran while one was open for 1% -> 1% of each run, Pallas kernels for 6% -> 7%
where the time goes in v22:
time: 189 us; the launch traced here: 188 us
  blocking collectives  104 us (55%)
  waiting for transfers between devices  29.9 us (16%)
  starting transfers between devices  24.3 us (13%)
  Pallas kernels  23.2 us (12%)
  local copies, waits for them, and re-layouts  3.68 us (2%)
    all_to_all x2, blocking collectives, exchange(): lax.all_to_all(units, CHIPS, split_axis=0, concat_axis=0, tiled=True)  81.5 us
    all_to_all x1, blocking collectives, local(): lax.all_to_all(attn, EP + ('x',), split_axis=0, concat_axis=0, tiled=True)  22.9 us
    all_to_all x1, waiting for transfers between devices, local(): lax.all_to_all(jnp.broadcast_to(latents[None], (8,) + latents.shape), CTX...  13.1 us
    pallas_call x1, Pallas kernels, attend(): pl.pallas_call(functools.partial(attend_kernel, cuts=cuts), in_specs=[pl....  10.6 us
    ppermute x6, starting transfers between devices, swap(): return lax.ppermute(mine, 'core', SWAP)  10.1 us
    ppermute x2, waiting for transfers between devices, down(): return lax.ppermute(a, 'x', [(i, (i + 3) % 4) for i in range(4)])  8.97 us
    all_to_all x1, starting transfers between devices, local(): lax.all_to_all(jnp.broadcast_to(latents[None], (8,) + latents.shape), CTX...  6.2 us
    pallas_call x1, Pallas kernels, expert(): pl.pallas_call(expert_kernel, in_specs=[far, whole, whole, far], out_spec...  5.87 us
  transfers between devices with their start and end apart: 12, of which 8 were waited for; matrix products, arithmetic and copies ran while one was open for 1% of the time, Pallas kernels for 7%

profile of v22, /device:TPU:1, one launch (start us, length us, event | category | flops | bytes accessed | tf_op | source)
XLA Modules:
  0.0 188.1 jit_solution(4391505314937546016)
XLA Ops:
  0.7 2.1 %broadcast_in_dim.67 = bf16[8,576,128]{2,1,0:T(8,128)(2,1)} broadcast(bf16[576,128]{1,0:T(8,128)(2,1)} %param.12), dimensions={1,2} | broadcast | bytes 1327104 | tf_op jit(solution)/shard_map/broadcast_in_dim | solution.py:367
  2.7 6.2 %all-to-all-start = ((bf16[8,576,128]{2,1,0:T(8,128)(2,1)}), bf16[8,576,128]{2,1,0:T(8,128)(2,1)S(1)}, u32[]{:S(2)}, u32[]{:S(2)}) async-start(bf16[8,576,128]{2,1,0:T(8,128)(2,1)} %broadcast_in_dim.67), calls=%async_computation | async-start | bytes 2359296 | tf_op jit(solution)/shard_map/all_to_all | solution.py:366
  9.0 1.0 collective-permute-start.1
  10.0 0.1 collective-permute-start
  10.1 0.1 pad_add_fusion.1.ids_ref
  10.2 0.1 and.49
  10.3 0.1 and.50
  10.4 2.1 %shard_map.123 = bf16[8,64,896]{2,1,0:T(8,128)(2,1)} custom-call(bf16[64,3584]{1,0:T(8,128)(2,1)} %w_ref.1), custom_call_target="tpu_custom_call" | custom-call | bytes 1376256 | tf_op jit(solution)/shard_map/pallas_call | solution.py:303
  12.5 0.0 collective-permute-done
  12.5 0.1 copy.57
  12.6 0.1 fusion.5
  12.7 0.1 copy.58
  12.9 0.1 copy.62
  13.0 0.1 copy.61
  13.1 13.1 %all-to-all-done.near_ref = bf16[8,576,128]{2,1,0:T(8,128)(2,1)S(1)} async-done(((bf16[8,576,128]{2,1,0:T(8,128)(2,1)}), bf16[8,576,128]{2,1,0:T(8,128)(2,1)S(1)}, u32[]{:S(2)}, u32[]{:S(2)}) %all-to-all-start) | async-done | bytes 1179680 | tf_op jit(solution)/shard_map/all_to_all | solution.py:366
  26.2 3.6 %all-to-all-start.1 = ((bf16[8,64,896]{2,1,0:T(8,128)(2,1)}), bf16[8,64,896]{2,1,0:T(8,128)(2,1)S(1)}, u32[]{:S(2)}, u32[]{:S(2)}) async-start(bf16[8,64,896]{2,1,0:T(8,128)(2,1)} %shard_map.123), calls=%async_computation.1 | async-start | bytes 1835008 | tf_op jit(solution)/shard_map/all_to_all | solution.py:371
  29.8 1.7 collective-permute-start.2
  31.5 0.1 bitcast_and_fusion
  31.6 0.1 copy.63
  31.7 0.1 broadcast_in_dim.36
  31.8 0.1 reshape.123
  31.9 0.1 copy.70
  32.1 0.0 collective-permute-done.1
  32.1 0.1 copy.64
  32.2 0.1 select_reduce_fusion
  32.3 0.1 copy.65
  32.5 0.1 copy.68
  32.5 0.1 copy.69
  32.6 0.1 broadcast_in_dim.64
  32.7 0.1 copy.71
  32.8 1.2 collective-permute-done.2.far_ref
  34.1 10.6 %shard_map.122.own_ref = bf16[128,1024]{1,0:T(8,128)(2,1)S(1)} custom-call(s32[3]{0:T(128)S(1)} %pad_add_fusion.1.ids_ref, bf16[128,1536]{1,0:T(8,128)(2,1)} %q_hbm.1, bf16[512,2048]{1,0:T(8,128)(2,1)} %w_hbm.1, bf16[8,576,128]{2,1,0:T(8,128)(2,1)S(1)} %all-to-all-done.near_ref, bf16[8,576,128]{2,1,0:T(8,128)(2,1)} %collective-permute-done.2.far_ref), custom_call_target="tpu_custom_call" | custom-call | flops 4563402752 | bytes 8000000 | tf_op jit(solution)/shard_map/pallas_call | solution.py:107
  44.6 2.9 %collective-permute-start.4 = (bf16[128,1024]{1,0:T(8,128)(2,1)S(1)}, bf16[128,1024]{1,0:T(8,128)(2,1)S(1)}, u32[]{:S(2)}, u32[]{:S(2)}) collective-permute-start(bf16[128,1024]{1,0:T(8,128)(2,1)S(1)} %shard_map.122.own_ref), channel_id=1, source_target_pairs={{0,48},{16,0},{32,16},{48,32},{1,49},{17,1},{33,17},{49,33},{2,50}... | collective-permute-start | bytes 786440 | tf_op jit(solution)/shard_map/ppermute | solution.py:322
  47.5 0.0 collective-permute-start.3
  47.5 0.0 all-to-all-done.1.near_ref
  47.5 5.3 %collective-permute-done.4.after_ref = bf16[128,1024]{1,0:T(8,128)(2,1)S(1)} collective-permute-done((bf16[128,1024]{1,0:T(8,128)(2,1)S(1)}, bf16[128,1024]{1,0:T(8,128)(2,1)S(1)}, u32[]{:S(2)}, u32[]{:S(2)}) %collective-permute-start.4) | collective-permute-done | bytes 262176 | tf_op jit(solution)/shard_map/ppermute | solution.py:322
  52.8 3.1 %collective-permute-done.3.before_ref = bf16[128,1024]{1,0:T(8,128)(2,1)S(1)} collective-permute-done((bf16[128,1024]{1,0:T(8,128)(2,1)S(1)}, bf16[128,1024]{1,0:T(8,128)(2,1)S(1)}, u32[]{:S(2)}, u32[]{:S(2)}) %collective-permute-start.3) | collective-permute-done | bytes 262176 | tf_op jit(solution)/shard_map/ppermute | solution.py:318
  55.9 1.5 collective-permute-start.7
  57.5 0.0 copy-start.3
  57.5 0.1 collective-permute-start.6
  57.6 1.5 collective-permute-start.5
  59.0 3.7 %collective-permute-done.6.right_ref = bf16[128,512]{1,0:T(8,128)(2,1)S(1)} collective-permute-done((bf16[128,512]{1,0:T(8,128)(2,1)S(1)}, bf16[128,512]{1,0:T(8,128)(2,1)S(1)}, u32[]{:S(2)}, u32[]{:S(2)}) %collective-permute-start.6) | collective-permute-done | bytes 131104 | tf_op jit(solution)/shard_map/ppermute | solution.py:322
  62.7 1.5 collective-permute-done.5.left_ref
  64.1 0.0 collective-permute-done.7.far_ref
  64.1 1.9 %shard_map.124 = bf16[32,16,896]{2,1,0:T(8,128)(2,1)S(1)} custom-call(s32[3]{0:T(128)S(1)} %pad_add_fusion.1.ids_ref, bf16[128,1024]{1,0:T(8,128)(2,1)S(1)} %shard_map.122.own_ref, bf16[128,1024]{1,0:T(8,128)(2,1)S(1)} %collective-permute-done.3.before_ref, bf16[128,1024]{1,0:T(8,128)(2,1)S(1)} %collective-permute-done.4.after_ref, ...), custom_call_target="tpu_custom_call" | custom-call | flops 939524096 | bytes 1835008 | tf_op jit(solution)/shard_map/pallas_call | solution.py:276
  66.1 0.0 copy-start.5
  66.1 22.9 %all_to_all.25 = bf16[32,16,896]{2,1,0:T(8,128)(2,1)S(1)} all-to-all(bf16[32,16,896]{2,1,0:T(8,128)(2,1)S(1)} %shard_map.124), channel_id=1, replica_groups=mesh['z_lo'=2,'x'=4,'core'=2,'z_hi'=2,'y'=4] {'z_hi','y','x'}, dimensions={0} | all-to-all | bytes 1835008 | tf_op jit(solution)/shard_map/all_to_all | solution.py:381
  89.0 0.1 convert_reduce_fusion
  89.1 0.2 fusion
  89.3 0.1 fusion.2
  89.4 2.5 %collective-permute-start.8 = (bf16[16,3584]{1,0:T(8,128)(2,1)S(1)}, bf16[16,3584]{1,0:T(8,128)(2,1)S(1)}, u32[]{:S(2)}, u32[]{:S(2)}) collective-permute-start(bf16[16,3584]{1,0:T(8,128)(2,1)S(1)} %fusion.2), channel_id=1, source_target_pairs={{0,8},{8,0},{1,9},{9,1},{2,10},{10,2},{3,11},{11,3},{4,12},{12,4},... | collective-permute-start | bytes 344072 | tf_op jit(solution)/shard_map/ppermute | solution.py:314
  91.9 1.0 collective-permute-done.8
  92.8 0.0 copy-start.1
  92.8 1.4 shard_map.125
  94.2 0.0 copy-start
  94.2 41.2 %all_to_all.26 = bf16[64,3,2,3584]{3,2,1,0:T(2,128)(2,1)S(1)} all-to-all(bf16[64,3,2,3584]{3,2,1,0:T(2,128)(2,1)S(1)} %bitcast.44), channel_id=1, replica_groups=mesh['z_lo'=2,'x'=4,'core'=2,'z_hi'=2,'y'=4] {'z_hi','z_lo','x','y'}, dimensions={0} | all-to-all | bytes 5505024 | tf_op jit(solution)/shard_map/all_to_all | solution.py:392
  135.5 0.0 copy-done.1
  135.5 5.9 %shard_map.126 = bf16[192,2,3584]{2,1,0:T(2,128)(2,1)} custom-call(bf16[192,2,3584]{2,1,0:T(2,128)(2,1)S(1)} %bitcast.45, bf16[3584,512]{1,0:T(8,128)(2,1)S(1)} %bitcast.46, bf16[3584,512]{1,0:T(8,128)(2,1)S(1)} %bitcast.47, bf16[512,3584]{1,0:T(8,128)(2,1)} %bitcast.50), custom_call_target="tpu_custom_call" | custom-call | flops 4227858432 | bytes 17000000 | tf_op jit(solution)/shard_map/pallas_call | solution.py:168
  141.3 40.3 %all_to_all.27 = bf16[64,3,2,3584]{3,2,1,0:T(2,128)(2,1)S(1)} all-to-all(bf16[64,3,2,3584]{3,2,1,0:T(2,128)(2,1)} %bitcast.48), channel_id=1, replica_groups=mesh['z_lo'=2,'x'=4,'core'=2,'z_hi'=2,'y'=4] {'z_hi','z_lo','x','y'}, dimensions={0} | all-to-all | bytes 5505024 | tf_op jit(solution)/shard_map/all_to_all | solution.py:392
  181.6 1.4 shard_map.127
  183.0 3.3 %collective-permute-start.9 = (f32[16,3584]{1,0:T(8,128)S(1)}, f32[16,3584]{1,0:T(8,128)S(1)}, u32[]{:S(2)}, u32[]{:S(2)}) collective-permute-start(f32[16,3584]{1,0:T(8,128)S(1)} %get-tuple-element.17), channel_id=1, source_target_pairs={{0,8},{8,0},{1,9},{9,1},{2,10},{10,2},{3,11},{11,3},{4,12},{12,4},... | collective-permute-start | bytes 688136 | tf_op jit(solution)/shard_map/ppermute | solution.py:314
  186.3 1.1 collective-permute-done.9
  187.4 0.0 copy-done.2
  187.4 0.7 fusion.4
  (34 shorter events, 0.4 us)
Async XLA Ops:
  0.6 8.3 %copy-start.4 = (s32[16,8]{0,1:T(8,128)S(1)}, s32[16,8]{0,1:T(8,128)}, u32[]{:S(2)}) copy-start(s32[16,8]{0,1:T(8,128)} %param.18) | copy-start | bytes 1540
  0.6 9.4 %copy-start.6 = (s32[16,8]{0,1:T(8,128)S(1)}, s32[16,8]{0,1:T(8,128)}, u32[]{:S(2)}) copy-start(s32[16,8]{0,1:T(8,128)} %param.17) | copy-start | bytes 1540
  2.7 23.4 %all-to-all-start = ((bf16[8,576,128]{2,1,0:T(8,128)(2,1)}), bf16[8,576,128]{2,1,0:T(8,128)(2,1)S(1)}, u32[]{:S(2)}, u32[]{:S(2)}) async-start(bf16[8,576,128]{2,1,0:T(8,128)(2,1)} %broadcast_in_dim.67), calls=%async_computation | async-start | bytes 2359296 | tf_op jit(solution)/shard_map/all_to_all | solution.py:366
  9.0 23.1 %collective-permute-start.1 = (f32[16,8]{0,1:T(8,128)S(1)}, f32[16,8]{0,1:T(8,128)S(1)}, u32[]{:S(2)}, u32[]{:S(2)}) collective-permute-start(f32[16,8]{0,1:T(8,128)S(1)} %convert_divide_fusion), channel_id=1, source_target_pairs={{0,8},{8,0},{1,9},{9,1},{2,10},{10,2},{3,11},{11,3},{4,12},{12,4},... | collective-permute-start | bytes 1544 | tf_op jit(solution)/shard_map/ppermute | solution.py:314
  10.0 2.4 %collective-permute-start = (s32[16,8]{0,1:T(8,128)S(1)}, s32[16,8]{0,1:T(8,128)S(1)}, u32[]{:S(2)}, u32[]{:S(2)}) collective-permute-start(s32[16,8]{0,1:T(8,128)S(1)} %copy-done.6), channel_id=1, source_target_pairs={{0,8},{8,0},{1,9},{9,1},{2,10},{10,2},{3,11},{11,3},{4,12},{12,4},... | collective-permute-start | bytes 1544 | tf_op jit(solution)/shard_map/ppermute | solution.py:314
  26.2 21.3 %all-to-all-start.1 = ((bf16[8,64,896]{2,1,0:T(8,128)(2,1)}), bf16[8,64,896]{2,1,0:T(8,128)(2,1)S(1)}, u32[]{:S(2)}, u32[]{:S(2)}) async-start(bf16[8,64,896]{2,1,0:T(8,128)(2,1)} %shard_map.123), calls=%async_computation.1 | async-start | bytes 1835008 | tf_op jit(solution)/shard_map/all_to_all | solution.py:371
  29.8 4.3 %collective-permute-start.2 = (bf16[8,576,128]{2,1,0:T(8,128)(2,1)S(1)}, bf16[8,576,128]{2,1,0:T(8,128)(2,1)}, u32[]{:S(2)}, u32[]{:S(2)}) collective-permute-start(bf16[8,576,128]{2,1,0:T(8,128)(2,1)S(1)} %all-to-all-done.near_ref), channel_id=1, source_target_pairs={{0,8},{8,0},{1,9},{9,1},{2,10},{10,2},{3,11},{11,3},{4,12},{12,4},... | collective-permute-start | bytes 3538952 | tf_op jit(solution)/shard_map/ppermute | solution.py:314
  44.6 8.2 %collective-permute-start.4 = (bf16[128,1024]{1,0:T(8,128)(2,1)S(1)}, bf16[128,1024]{1,0:T(8,128)(2,1)S(1)}, u32[]{:S(2)}, u32[]{:S(2)}) collective-permute-start(bf16[128,1024]{1,0:T(8,128)(2,1)S(1)} %shard_map.122.own_ref), channel_id=1, source_target_pairs={{0,48},{16,0},{32,16},{48,32},{1,49},{17,1},{33,17},{49,33},{2,50}... | collective-permute-start | bytes 786440 | tf_op jit(solution)/shard_map/ppermute | solution.py:322
  47.5 8.4 %collective-permute-start.3 = (bf16[128,1024]{1,0:T(8,128)(2,1)S(1)}, bf16[128,1024]{1,0:T(8,128)(2,1)S(1)}, u32[]{:S(2)}, u32[]{:S(2)}) collective-permute-start(bf16[128,1024]{1,0:T(8,128)(2,1)S(1)} %shard_map.122.own_ref), channel_id=1, source_target_pairs={{0,16},{16,32},{32,48},{48,0},{1,17},{17,33},{33,49},{49,1},{2,18}... | collective-permute-start | bytes 786440 | tf_op jit(solution)/shard_map/ppermute | solution.py:318
  55.9 8.2 %collective-permute-start.7 = (bf16[8,64,896]{2,1,0:T(8,128)(2,1)S(1)}, bf16[8,64,896]{2,1,0:T(8,128)(2,1)S(1)}, u32[]{:S(2)}, u32[]{:S(2)}) collective-permute-start(bf16[8,64,896]{2,1,0:T(8,128)(2,1)S(1)} %all-to-all-done.1.near_ref), channel_id=1, source_target_pairs={{0,8},{8,0},{1,9},{9,1},{2,10},{10,2},{3,11},{11,3},{4,12},{12,4},... | collective-permute-start | bytes 2752520 | tf_op jit(solution)/shard_map/ppermute | solution.py:314
  57.5 31.6 %copy-start.3 = (bf16[16,3584]{1,0:T(8,128)(2,1)S(1)}, bf16[16,3584]{1,0:T(8,128)(2,1)}, u32[]{:S(2)}) copy-start(bf16[16,3584]{1,0:T(8,128)(2,1)} %param.15) | copy-start | bytes 344068
  57.5 5.2 %collective-permute-start.6 = (bf16[128,512]{1,0:T(8,128)(2,1)S(1)}, bf16[128,512]{1,0:T(8,128)(2,1)S(1)}, u32[]{:S(2)}, u32[]{:S(2)}) collective-permute-start(bf16[128,512]{1,0:T(8,128)(2,1)S(1)} %slice.24), channel_id=1, source_target_pairs={{0,48},{16,0},{32,16},{48,32},{1,49},{17,1},{33,17},{49,33},{2,50}... | collective-permute-start | bytes 393224 | tf_op jit(solution)/shard_map/ppermute | solution.py:322
  57.6 6.6 %collective-permute-start.5 = (bf16[128,512]{1,0:T(8,128)(2,1)S(1)}, bf16[128,512]{1,0:T(8,128)(2,1)S(1)}, u32[]{:S(2)}, u32[]{:S(2)}) collective-permute-start(bf16[128,512]{1,0:T(8,128)(2,1)S(1)} %slice.23), channel_id=1, source_target_pairs={{0,16},{16,32},{32,48},{48,0},{1,17},{17,33},{33,49},{49,1},{2,18}... | collective-permute-start | bytes 393224 | tf_op jit(solution)/shard_map/ppermute | solution.py:318
  66.1 23.2 %copy-start.5 = (f32[3584]{0:T(1024)S(1)}, f32[3584]{0:T(1024)}, u32[]{:S(2)}) copy-start(f32[3584]{0:T(1024)} %param.16) | copy-start | bytes 43012
  89.3 98.2 %copy-start.2 = (bf16[16,3584]{1,0:T(8,128)(2,1)}, bf16[16,3584]{1,0:T(8,128)(2,1)S(1)}, u32[]{:S(2)}) copy-start(bf16[16,3584]{1,0:T(8,128)(2,1)S(1)} %get-tuple-element.19) | copy-start | bytes 344068
  89.4 3.4 %collective-permute-start.8 = (bf16[16,3584]{1,0:T(8,128)(2,1)S(1)}, bf16[16,3584]{1,0:T(8,128)(2,1)S(1)}, u32[]{:S(2)}, u32[]{:S(2)}) collective-permute-start(bf16[16,3584]{1,0:T(8,128)(2,1)S(1)} %fusion.2), channel_id=1, source_target_pairs={{0,8},{8,0},{1,9},{9,1},{2,10},{10,2},{3,11},{11,3},{4,12},{12,4},... | collective-permute-start | bytes 344072 | tf_op jit(solution)/shard_map/ppermute | solution.py:314
  92.8 42.6 %copy-start.1 = (bf16[1,3584,512]{2,1,0:T(8,128)(2,1)S(1)}, bf16[1,3584,512]{2,1,0:T(8,128)(2,1)}, u32[]{:S(2)}) copy-start(bf16[1,3584,512]{2,1,0:T(8,128)(2,1)} %param.20) | copy-start | bytes 11010052
  94.2 41.2 %copy-start = (bf16[1,3584,512]{2,1,0:T(8,128)(2,1)S(1)}, bf16[1,3584,512]{2,1,0:T(8,128)(2,1)}, u32[]{:S(2)}) copy-start(bf16[1,3584,512]{2,1,0:T(8,128)(2,1)} %param.19) | copy-start | bytes 11010052
  183.0 4.4 %collective-permute-start.9 = (f32[16,3584]{1,0:T(8,128)S(1)}, f32[16,3584]{1,0:T(8,128)S(1)}, u32[]{:S(2)}, u32[]{:S(2)}) collective-permute-start(f32[16,3584]{1,0:T(8,128)S(1)} %get-tuple-element.17), channel_id=1, source_target_pairs={{0,8},{8,0},{1,9},{9,1},{2,10},{10,2},{3,11},{11,3},{4,12},{12,4},... | collective-permute-start | bytes 688136 | tf_op jit(solution)/shard_map/ppermute | solution.py:314
